TPU v7x, 32 devices: a whole 2x2x4 slice. The times are simulated.
32 devices in a mesh: groups: 2 (over x), wide: 8 (over z, y), narrow: 2 (over core).
Axes of the slice: x: 2, y: 2, z: 4, core: 2. Of those that a mesh axis runs over, the one named last changes fastest.
Arguments:
- queries: bfloat16 [64, 6144], P(('groups', 'wide'), 'narrow'), parts along dimension 0
- new_keys: bfloat16 [64, 1024], P(('groups', 'wide'), 'narrow'), parts along dimension 0, may hold values from -6 to 6
- new_values: bfloat16 [64, 1024], P(('groups', 'wide'), 'narrow'), parts along dimension 0, may hold values from -6 to 6
- key_cache: bfloat16 [64, 512, 1024], P(('groups', 'wide'), None, 'narrow'), parts along dimension 0
- value_cache: bfloat16 [64, 512, 1024], P(('groups', 'wide'), None, 'narrow'), parts along dimension 0, may hold values from -6 to 6
- lengths: int32 [64], P(('groups', 'wide')), parts along dimension 0, may hold values from 32 to 512, as said below
- assignment: int32 [64], P(('groups', 'wide')), parts along dimension 0, may hold values from 0 to 31, as said below
- tokens: bfloat16 [64, 6144], P(('groups', 'wide')), parts along dimension 0, may hold values from -6 to 6
- norm_gain: float32 [6144], replicated, may hold values from 0.25 to 1.75
- routes: int32 [64, 2], P('groups'), parts along dimension 0, may hold values from 0 to 7, all different within a row; in each aligned block of 32 rows (0 to 31, 32 to 63, ...) at most 16 rows name the same one
- route_logits: float32 [64, 2], P('groups'), parts along dimension 0, may hold values from -6 to 6
- w_gate: bfloat16 [2, 6144, 8192], P('narrow', None, 'wide'), may hold values from -0.078125 to 0.078125
- w_up: bfloat16 [2, 6144, 8192], P('narrow', None, 'wide'), may hold values from -0.078125 to 0.078125
- w_down: bfloat16 [2, 8192, 6144], P('narrow', 'wide'), may hold values from -0.0625 to 0.0625
Outputs:
- context: bfloat16 [64, 6144], P(('groups', 'wide'), 'narrow'), parts along dimension 0
- mixed_out: bfloat16 [64, 6144], P(('groups', 'wide')), parts along dimension 0
There are 2 independent parts, one for each index of `groups`. A program takes and returns all parts, laid end to end along the dimension named above; an argument that names none is the same for every part. Nothing has to cross between parts.
Inputs may be any that keep to these rules, and one draw needn't show every extreme that they name: `assignment`: the requests of the micro-batch in some order, each once. `lengths`: some slot has exactly 512 and some exactly 32 positions. `routes`: each row names two different experts; no expert is named by more than 16 rows, a bound that some block reaches.
All inputs are finite; a program needn't handle non-finite values.
Results may differ from a plain program's by a relative error of at most 0.0049.
Values may be sent and summed in bfloat16 or wider, within the bound.
No kernel may reach another device: no remote copies, remote signals or barrier semaphores. Data moves between devices by JAX's collectives and lax.ppermute only.
A program may use at most 128 MiB of HBM per device.

v0:
```python
import jax
import jax.numpy as jnp
from jax import lax
from jax.sharding import PartitionSpec as P

HQ = 48
KVH = 8
HD = 128
CTX = 512


def expert_weights(routes, route_logits, expert):
    first_prob = 1.0 / (1.0 + jnp.exp(route_logits[:, 1] - route_logits[:, 0]))
    second_prob = 1.0 - first_prob
    chosen = (routes == expert).astype(jnp.float32)
    return chosen[:, 0] * first_prob + chosen[:, 1] * second_prob


def local(
    queries,
    new_keys,
    new_values,
    key_cache,
    value_cache,
    lengths,
    assignment,
    tokens,
    norm_gain,
    routes,
    route_logits,
    w_gate,
    w_up,
    w_down,
):
    row_count = tokens.shape[0]
    slot_count = key_cache.shape[0]
    head_group = HQ // KVH
    kv_local = key_cache.shape[2] // HD
    score_scale = HD ** (-0.5)
    my_index = lax.axis_index("wide")
    gathered = (
        lax.all_gather(queries, "wide", axis=0, tiled=True),
        lax.all_gather(new_keys, "wide", axis=0, tiled=True),
        lax.all_gather(new_values, "wide", axis=0, tiled=True),
    )
    query_rows = jnp.take(gathered[0], assignment, axis=0)
    key_rows = jnp.take(gathered[1], assignment, axis=0)
    value_rows = jnp.take(gathered[2], assignment, axis=0)
    query_heads = query_rows.reshape(slot_count, kv_local, head_group, HD)
    own_keys = key_rows.reshape(slot_count, kv_local, HD)
    own_values = value_rows.reshape(slot_count, kv_local, HD)
    cache_keys = key_cache.reshape(slot_count, CTX, kv_local, HD)
    cache_values = value_cache.reshape(slot_count, CTX, kv_local, HD)
    own_score = (
        jnp.einsum("rgjd,rgd->rgj", query_heads, own_keys, preferred_element_type=jnp.float32)
        * score_scale
    )
    scores = (
        jnp.einsum("rgjd,rtgd->rgjt", query_heads, cache_keys, preferred_element_type=jnp.float32)
        * score_scale
    )
    positions = jnp.arange(CTX, dtype=jnp.int32)
    is_valid = positions[None, :] < lengths[:, None]
    scores = jnp.where(is_valid[:, None, None, :], scores, -jnp.inf)
    row_max = jnp.maximum(jnp.max(scores, axis=-1), own_score)
    weights = jnp.exp(scores - row_max[..., None])
    own_weight = jnp.exp(own_score - row_max)
    denominator = jnp.sum(weights, axis=-1) + own_weight
    attn_probs = (weights / denominator[..., None]).astype(jnp.bfloat16)
    own_prob = (own_weight / denominator).astype(jnp.bfloat16)
    mixed_heads = jnp.einsum(
        "rgjt,rtgd->rgjd", attn_probs, cache_values, preferred_element_type=jnp.float32
    )
    mixed_heads = (
        mixed_heads
        + own_prob.astype(jnp.float32)[..., None] * own_values.astype(jnp.float32)[:, :, None, :]
    )
    context = mixed_heads.reshape(slot_count, kv_local * head_group * HD).astype(jnp.bfloat16)
    values = tokens.astype(jnp.float32)
    normed = (
        values * lax.rsqrt(jnp.mean(values * values, axis=-1, keepdims=True) + 1e-05) * norm_gain
    ).astype(jnp.bfloat16)
    expert = lax.axis_index("narrow")
    weight_all = expert_weights(routes, route_logits, expert)
    gate_matrix = w_gate[0]
    up_matrix = w_up[0]
    down_matrix = w_down[0]
    tok_piece = lax.all_gather(normed, "wide", axis=0, tiled=True)
    gate_out = jnp.dot(tok_piece, gate_matrix, preferred_element_type=jnp.float32)
    up_out = jnp.dot(tok_piece, up_matrix, preferred_element_type=jnp.float32)
    hidden = (weight_all[:, None] * jax.nn.silu(gate_out) * up_out).astype(jnp.bfloat16)
    term_rows = jnp.dot(hidden, down_matrix, preferred_element_type=jnp.float32)
    summed = lax.psum(term_rows, ("wide", "narrow"))
    own_rows = lax.dynamic_slice_in_dim(summed, my_index * row_count, row_count, 0)
    mixed_out = (values + own_rows).astype(jnp.bfloat16)
    return (context, mixed_out)


def solution(mesh):
    placed = (
        P(("groups", "wide"), "narrow"),
        P(("groups", "wide"), "narrow"),
        P(("groups", "wide"), "narrow"),
        P(("groups", "wide"), None, "narrow"),
        P(("groups", "wide"), None, "narrow"),
        P(("groups", "wide")),
        P(("groups", "wide")),
        P(("groups", "wide"), None),
        P(),
        P("groups", None),
        P("groups", None),
        P("narrow", None, "wide"),
        P("narrow", None, "wide"),
        P("narrow", "wide", None),
    )
    return jax.shard_map(
        local,
        mesh=mesh,
        in_specs=placed,
        out_specs=(P(("groups", "wide"), "narrow"), P(("groups", "wide"), None)),
        check_vma=False,
    )
```

profile of v0, /device:TPU:0, one launch (start us, length us, event | category | flops | bytes accessed | tf_op | source)
XLA Modules:
  0.0 170.2 jit_solution(2393751851569599377)
XLA Ops:
  7.2 0.0 copy-start
  7.2 0.0 all-reduce.2.cloned.1.call-start
  7.2 1.1 fusion.41
  8.3 0.9 fusion.47
  9.2 32.7 %all-gather.3 = bf16[8,4,6144]{2,1,0:T(4,128)(2,1)S(1)} all-gather(bf16[1,4,6144]{2,1,0:T(4,128)(2,1)S(1)} %fusion.47), channel_id=1, replica_groups=mesh['groups'=2,'wide'=8,'narrow'=2] {'wide'}, dimensions={0}, use_global_device_ids=true | all-gather | bytes 442368 | tf_op jit(solution)/shard_map/all_gather | solution.py:88
  42.0 0.1 reshape.107
  42.1 0.7 compare_convert_fusion
  42.8 0.8 add_bitcast_fusion
  43.5 6.9 %fusion.4 = f32[32,1024]{1,0:T(8,128)S(1)} fusion(bf16[32,6144]{1,0:T(8,128)(2,1)S(1)} %reshape.107, bf16[1,6144,1024]{2,1,0:T(8,128)(2,1)} %param.27), kind=kOutput, calls=%fused_computation.7 | convolution fusion | flops 402653184 | bytes 13107200 | tf_op jit(solution)/shard_map/dot_general | solution.py:89
  50.4 0.0 copy-start.6
  50.4 0.0 copy-start.5
  50.4 0.0 copy-start.3
  50.4 0.0 copy-start.4
  50.4 0.0 copy-start.2
  50.4 13.6 %fusion = f32[32,6144]{1,0:T(8,128)} fusion(bf16[1,1024,6144]{2,1,0:T(8,128)(2,1)} %param.29, bf16[32,6144]{1,0:T(8,128)(2,1)S(1)} %reshape.107, bf16[1,6144,1024]{2,1,0:T(8,128)(2,1)} %param.28, f32[32,1024]{1,0:T(8,128)S(1)} %fusion.4, f32[32]{0:T(128)S(1)} %add_bitcast_fusion), kind=kOutput, calls=%fused_computation.3 | convolution fusion | flops 805535744 | bytes 26476672 | tf_op jit(solution)/shard_map/dot_general | solution.py:92
  64.0 0.0 all-reduce.2.cloned.1.call-update
  64.0 0.0 copy-done.6
  64.1 0.0 copy-done.5
  64.1 0.1 iota_compare_fusion
  64.2 0.0 copy-done.3
  64.2 30.4 %all-gather.1 = bf16[8,4,512]{2,1,0:T(4,128)(2,1)S(1)} all-gather(bf16[1,4,512]{2,1,0:T(4,128)(2,1)S(1)} %bitcast.54), channel_id=1, replica_groups=mesh['groups'=2,'wide'=8,'narrow'=2] {'wide'}, dimensions={0}, use_global_device_ids=true | all-gather | bytes 36864 | tf_op jit(solution)/shard_map/all_gather | solution.py:43
  94.6 0.0 copy-done.4
  94.6 30.4 %all-gather.2 = bf16[8,4,512]{2,1,0:T(4,128)(2,1)S(1)} all-gather(bf16[1,4,512]{2,1,0:T(4,128)(2,1)S(1)} %bitcast.55), channel_id=1, replica_groups=mesh['groups'=2,'wide'=8,'narrow'=2] {'wide'}, dimensions={0}, use_global_device_ids=true | all-gather | bytes 36864 | tf_op jit(solution)/shard_map/all_gather | solution.py:44
  125.1 0.6 gather_fusion.1
  125.6 0.6 gather_fusion.2
  126.2 0.1 select_convert_fusion
  126.3 0.0 copy-done.2
  126.3 30.8 %all-gather = bf16[8,4,3072]{2,1,0:T(4,128)(2,1)S(1)} all-gather(bf16[1,4,3072]{2,1,0:T(4,128)(2,1)S(1)} %bitcast.53), channel_id=1, replica_groups=mesh['groups'=2,'wide'=8,'narrow'=2] {'wide'}, dimensions={0}, use_global_device_ids=true | all-gather | bytes 221184 | tf_op jit(solution)/shard_map/all_gather | solution.py:42
  157.2 0.6 gather_fusion
  157.8 0.2 fusion.48
  158.0 0.0 copy-done
  158.0 0.8 fusion.54
  158.8 0.0 copy-start.1
  158.8 0.2 fusion.32
  159.1 2.0 %fusion.27 = bf16[4,4,6,128]{3,2,1,0:T(8,128)(2,1)S(1)} fusion(f32[4,4,6,512]{3,2,1,0:T(8,128)S(1)} %get-tuple-element.8, f32[4,4,6]{2,1,0:T(4,128)S(1)} %get-tuple-element.4, f32[4,4,6]{2,1,0:T(4,128)S(1)} %multiply_maximum_fusion, f32[4,4,128]{2,1,0:T(4,128)S(1)} %reshape.72, f32[4,4,6]{2,1,0:T(4,128)S(1)} %get-tuple-element.3, ...), kind=kOutput, calls=%fused_computation.20 | convolution fusion | flops 12767232 | bytes 2327680 | tf_op jit(solution)/shard_map/rgjt,rtgd->rgjd/dot_general | solution.py:71
  161.1 0.7 convert_element_type.46
  161.8 0.0 all-reduce.2.cloned.1.call-done
  161.8 0.0 copy-done.1
  161.8 1.6 fusion.44
  (12 shorter events, 0.2 us)
Async XLA Ops:
  7.2 150.9 %copy-start = (bf16[4,512,512]{2,1,0:T(8,128)(2,1)S(1)}, bf16[4,512,512]{2,1,0:T(8,128)(2,1)}, u32[]{:S(2)}) copy-start(bf16[4,512,512]{2,1,0:T(8,128)(2,1)} %param.19) | copy-start | bytes 6291460
  7.2 154.6 %all-reduce.2.cloned.1.call-start = ((), (), s32[]{:S(2)}) async-start(), calls=%async_computation | async-start | bytes 1572864 | tf_op jit(solution)/shard_map/psum | solution.py:93
  50.4 13.6 %copy-start.6 = (s32[4]{0:T(128)S(1)}, s32[4]{0:T(128)}, u32[]{:S(2)}) copy-start(s32[4]{0:T(128)} %param.22) | copy-start | bytes 52
  50.4 13.7 %copy-start.5 = (s32[4]{0:T(128)S(1)}, s32[4]{0:T(128)}, u32[]{:S(2)}) copy-start(s32[4]{0:T(128)} %param.21) | copy-start | bytes 52
  50.4 13.8 %copy-start.3 = (bf16[4,512]{1,0:T(4,128)(2,1)S(1)}, bf16[4,512]{1,0:T(4,128)(2,1)}, u32[]{:S(2)}) copy-start(bf16[4,512]{1,0:T(4,128)(2,1)} %param.17) | copy-start | bytes 12292
  50.4 44.2 %copy-start.4 = (bf16[4,512]{1,0:T(4,128)(2,1)S(1)}, bf16[4,512]{1,0:T(4,128)(2,1)}, u32[]{:S(2)}) copy-start(bf16[4,512]{1,0:T(4,128)(2,1)} %param.18) | copy-start | bytes 12292
  50.4 75.9 %copy-start.2 = (bf16[4,3072]{1,0:T(4,128)(2,1)S(1)}, bf16[4,3072]{1,0:T(4,128)(2,1)}, u32[]{:S(2)}) copy-start(bf16[4,3072]{1,0:T(4,128)(2,1)} %param.16) | copy-start | bytes 73732
  158.8 3.0 %copy-start.1 = (bf16[4,6144]{1,0:T(4,128)(2,1)S(1)}, bf16[4,6144]{1,0:T(4,128)(2,1)}, u32[]{:S(2)}) copy-start(bf16[4,6144]{1,0:T(4,128)(2,1)} %param.23) | copy-start | bytes 147460
Sparse Core Ops, SparseCore 0:
  64.2 93.1 all-reduce.1
where the time goes:
time: 171 us; the launch traced here: 170 us
  blocking collectives  124 us (73%)
  matrix products  23.4 us (14%)
  between operations  14.2 us (8%)
  other arithmetic  5.44 us (3%)
  local copies, waits for them, and re-layouts  2.64 us (2%)
    all_gather x1, blocking collectives, local(): tok_piece = lax.all_gather(normed, 'wide', axis=0, tiled=True)  32.7 us
    all_gather x1, blocking collectives, local(): lax.all_gather(queries, 'wide', axis=0, tiled=True)  30.8 us
    all_gather x1, blocking collectives, local(): lax.all_gather(new_values, 'wide', axis=0, tiled=True)  30.4 us
    all_gather x1, blocking collectives, local(): lax.all_gather(new_keys, 'wide', axis=0, tiled=True)  30.4 us
    dot_general x1, matrix products, local(): term_rows = jnp.dot(hidden, down_matrix, preferred_element_type=jnp.float32)  13.6 us
    dot_general x1, matrix products, local(): jnp.dot(tok_piece, gate_matrix, preferred_element_type=jnp.float32)  6.86 us
  transfers between devices with their start and end apart: 1, of which 0 were waited for; matrix products, arithmetic and copies ran while one was open for 3% of the time, Pallas kernels for 0%

commit v1 on v0

v1 whole, which is shorter than its diff:
```python
import jax
import jax.numpy as jnp
from jax import lax
from jax.sharding import PartitionSpec as P

HQ = 48
KVH = 8
HD = 128
CTX = 512


def partner(index, step):
    return index ^ step


def swap(block, axis, count, step):
    return lax.ppermute(block, axis, [(i, partner(i, step)) for i in range(count)])


def expert_weights(routes, route_logits, expert):
    first_prob = 1.0 / (1.0 + jnp.exp(route_logits[:, 1] - route_logits[:, 0]))
    second_prob = 1.0 - first_prob
    chosen = (routes == expert).astype(jnp.float32)
    return chosen[:, 0] * first_prob + chosen[:, 1] * second_prob


def attention(query_rows, key_rows, value_rows, key_cache, value_cache, lengths):
    head_group = HQ // KVH
    slot_count = key_cache.shape[0]
    kv_local = key_cache.shape[2] // HD
    score_scale = HD ** (-0.5)
    query_heads = query_rows.reshape(slot_count, kv_local, head_group, HD)
    own_keys = key_rows.reshape(slot_count, kv_local, HD)
    own_values = value_rows.reshape(slot_count, kv_local, HD)
    cache_keys = key_cache.reshape(slot_count, CTX, kv_local, HD)
    cache_values = value_cache.reshape(slot_count, CTX, kv_local, HD)
    own_score = (
        jnp.einsum("rgjd,rgd->rgj", query_heads, own_keys, preferred_element_type=jnp.float32)
        * score_scale
    )
    scores = (
        jnp.einsum("rgjd,rtgd->rgjt", query_heads, cache_keys, preferred_element_type=jnp.float32)
        * score_scale
    )
    positions = jnp.arange(CTX, dtype=jnp.int32)
    is_valid = positions[None, :] < lengths[:, None]
    scores = jnp.where(is_valid[:, None, None, :], scores, -jnp.inf)
    row_max = jnp.maximum(jnp.max(scores, axis=-1), own_score)
    weights = jnp.exp(scores - row_max[..., None])
    own_weight = jnp.exp(own_score - row_max)
    denominator = jnp.sum(weights, axis=-1) + own_weight
    attn_probs = (weights / denominator[..., None]).astype(jnp.bfloat16)
    own_prob = (own_weight / denominator).astype(jnp.bfloat16)
    mixed_heads = jnp.einsum(
        "rgjt,rtgd->rgjd", attn_probs, cache_values, preferred_element_type=jnp.float32
    )
    mixed_heads = (
        mixed_heads
        + own_prob.astype(jnp.float32)[..., None] * own_values.astype(jnp.float32)[:, :, None, :]
    )
    return mixed_heads.reshape(slot_count, kv_local * head_group * HD).astype(jnp.bfloat16)


def make_local(wide):
    def local(
        queries,
        new_keys,
        new_values,
        key_cache,
        value_cache,
        lengths,
        assignment,
        tokens,
        norm_gain,
        routes,
        route_logits,
        w_gate,
        w_up,
        w_down,
    ):
        rows = tokens.shape[0]
        width = tokens.shape[1]
        half = width // 2
        me = lax.axis_index("wide")
        core = lax.axis_index("narrow")
        blocks = jnp.stack([partner(me, step) for step in range(wide)])

        token_rows = jnp.concatenate(
            [tokens] + [swap(tokens, "wide", wide, step) for step in range(1, wide)], axis=0
        )
        mine = jnp.concatenate([queries, new_keys, new_values], axis=1)
        fetched = jnp.concatenate(
            [mine] + [swap(mine, "wide", wide, step) for step in range(1, wide)], axis=0
        )

        values = token_rows.astype(jnp.float32)
        normed = (
            values
            * lax.rsqrt(jnp.mean(values * values, axis=-1, keepdims=True) + 1e-05)
            * norm_gain
        ).astype(jnp.bfloat16)
        weight_all = expert_weights(routes, route_logits, core)
        weight_all = jnp.take(weight_all.reshape(wide, rows), blocks, axis=0).reshape(-1)
        gate_out = jnp.dot(normed, w_gate[0], preferred_element_type=jnp.float32)
        up_out = jnp.dot(normed, w_up[0], preferred_element_type=jnp.float32)
        hidden = (weight_all[:, None] * jax.nn.silu(gate_out) * up_out).astype(jnp.bfloat16)
        terms = jnp.dot(hidden, w_down[0], preferred_element_type=jnp.float32)

        given = lax.dynamic_slice_in_dim(terms, (1 - core) * half, half, 1)
        kept = lax.dynamic_slice_in_dim(terms, core * half, half, 1)
        terms = kept + swap(given.astype(jnp.bfloat16), "narrow", 2, 1).astype(jnp.float32)
        sent = terms.astype(jnp.bfloat16)
        total = terms[:rows]
        for step in range(1, wide):
            block = sent[step * rows : (step + 1) * rows]
            total = total + swap(block, "wide", wide, step).astype(jnp.float32)
        own = lax.dynamic_slice_in_dim(tokens, core * half, half, 1).astype(jnp.float32)
        piece = (own + total).astype(jnp.bfloat16)
        other = swap(piece, "narrow", 2, 1)
        first = jnp.where(core == 0, piece, other)
        second = jnp.where(core == 0, other, piece)
        mixed_out = jnp.concatenate([first, second], axis=1)

        place = assignment // rows
        found = partner(place, me) * rows + assignment % rows
        slots = jnp.take(fetched, found, axis=0)
        q_width, k_width = queries.shape[1], new_keys.shape[1]
        context = attention(
            slots[:, :q_width],
            slots[:, q_width : q_width + k_width],
            slots[:, q_width + k_width :],
            key_cache,
            value_cache,
            lengths,
        )
        return (context, mixed_out)

    return local


def solution(mesh):
    placed = (
        P(("groups", "wide"), "narrow"),
        P(("groups", "wide"), "narrow"),
        P(("groups", "wide"), "narrow"),
        P(("groups", "wide"), None, "narrow"),
        P(("groups", "wide"), None, "narrow"),
        P(("groups", "wide")),
        P(("groups", "wide")),
        P(("groups", "wide"), None),
        P(),
        P("groups", None),
        P("groups", None),
        P("narrow", None, "wide"),
        P("narrow", None, "wide"),
        P("narrow", "wide", None),
    )
    return jax.shard_map(
        make_local(mesh.shape["wide"]),
        mesh=mesh,
        in_specs=placed,
        out_specs=(P(("groups", "wide"), "narrow"), P(("groups", "wide"), None)),
        check_vma=False,
    )
```

time: 171 us -> 80.7 us (0.47)
  blocking collectives: 124 us -> 0 us
  starting transfers between devices: 0.04 us -> 36.4 us
  between operations: 14.2 us -> 0.83 us
  waiting for transfers between devices: 0.02 us -> 7.16 us
  local copies, waits for them, and re-layouts: 2.64 us -> 5.78 us
    all_gather x4 -> x0, blocking collectives: 124 us -> none  [the longest x1 32.7 us: local(): tok_piece = lax.all_gather(normed, 'wide', axis=0, tiled=True)]
    ppermute x0 -> x23, starting transfers between devices: none -> 36.4 us  [swap(): lax.ppermute(block, axis, [(i, partner(i, step)) for i in range(count)])]
    ppermute x0 -> x23, waiting for transfers between devices: none -> 7.16 us  [swap(): lax.ppermute(block, axis, [(i, partner(i, step)) for i in range(count)])]
  transfers between devices with their start and end apart: 1 -> 23, of which waited for: 0 -> 7; matrix products, arithmetic and copies ran while one was open for 3% -> 14% of each run, Pallas kernels for 0% -> 0%
where the time goes in v1:
time: 80.7 us; the launch traced here: 80.3 us
  starting transfers between devices  36.4 us (45%)
  matrix products  23.8 us (29%)
  waiting for transfers between devices  7.16 us (9%)
  other arithmetic  6.33 us (8%)
  local copies, waits for them, and re-layouts  5.78 us (7%)
  between operations  0.83 us (1%)
    ppermute x23, starting transfers between devices, swap(): lax.ppermute(block, axis, [(i, partner(i, step)) for i in range(count)])  36.4 us
    dot_general x1, matrix products, local(): terms = jnp.dot(hidden, w_down[0], preferred_element_type=jnp.float32)  12.7 us
    dot_general x1, matrix products, local(): gate_out = jnp.dot(normed, w_gate[0], preferred_element_type=jnp.float32)  7.56 us
    ppermute x23, waiting for transfers between devices, swap(): lax.ppermute(block, axis, [(i, partner(i, step)) for i in range(count)])  7.16 us
    dot_general x1, matrix products, attention(): jnp.einsum('rgjt,rtgd->rgjd', attn_probs, cache_values, preferred_element...  2.03 us
    unnamed x10, local copies, waits for them, and re-layouts  1.62 us
  transfers between devices with their start and end apart: 23, of which 7 were waited for; matrix products, arithmetic and copies ran while one was open for 14% of the time, Pallas kernels for 0%

profile of v1, /device:TPU:0, one launch (start us, length us, event | category | flops | bytes accessed | tf_op | source)
XLA Modules:
  0.0 80.3 jit_solution(16123620572101854612)
XLA Ops:
  0.7 0.9 %constant_dynamic-update-slice_fusion.2 = bf16[4,4096]{1,0:T(4,128)(2,1)S(1)} fusion(bf16[4,3072]{1,0:T(4,128)(2,1)} %param.14), kind=kLoop, calls=%fused_computation.59 | loop fusion | bytes 49152
  1.6 0.7 constant_dynamic-update-slice_fusion.1
  2.3 0.7 constant_dynamic-update-slice_fusion
  2.9 3.0 %collective-permute-start = (bf16[4,4096]{1,0:T(4,128)(2,1)S(1)}, bf16[4,4096]{1,0:T(4,128)(2,1)S(1)}, u32[]{:S(2)}, u32[]{:S(2)}) collective-permute-start(bf16[4,4096]{1,0:T(4,128)(2,1)S(1)} %constant_dynamic-update-slice_fusion), channel_id=1, source_target_pairs={{0,2},{2,0},{4,6},{6,4},{8,10},{10,8},{12,14},{14,12},{1,3},{3,1},... | collective-permute-start | bytes 98312 | tf_op jit(solution)/shard_map/ppermute | solution.py:17
  5.9 1.6 %collective-permute-start.1 = (bf16[4,4096]{1,0:T(4,128)(2,1)S(1)}, bf16[4,4096]{1,0:T(4,128)(2,1)S(1)}, u32[]{:S(2)}, u32[]{:S(2)}) collective-permute-start(bf16[4,4096]{1,0:T(4,128)(2,1)S(1)} %constant_dynamic-update-slice_fusion), channel_id=1, source_target_pairs={{0,4},{2,6},{4,0},{6,2},{8,12},{10,14},{12,8},{14,10},{1,5},{3,7},... | collective-permute-start | bytes 98312 | tf_op jit(solution)/shard_map/ppermute | solution.py:17
  7.5 3.0 %collective-permute-start.3 = (bf16[4,4096]{1,0:T(4,128)(2,1)S(1)}, bf16[4,4096]{1,0:T(4,128)(2,1)S(1)}, u32[]{:S(2)}, u32[]{:S(2)}) collective-permute-start(bf16[4,4096]{1,0:T(4,128)(2,1)S(1)} %constant_dynamic-update-slice_fusion), channel_id=1, source_target_pairs={{0,8},{2,10},{4,12},{6,14},{8,0},{10,2},{12,4},{14,6},{1,9},{3,11}... | collective-permute-start | bytes 98312 | tf_op jit(solution)/shard_map/ppermute | solution.py:17
  10.5 1.3 %collective-permute-start.4 = (bf16[4,4096]{1,0:T(4,128)(2,1)S(1)}, bf16[4,4096]{1,0:T(4,128)(2,1)S(1)}, u32[]{:S(2)}, u32[]{:S(2)}) collective-permute-start(bf16[4,4096]{1,0:T(4,128)(2,1)S(1)} %constant_dynamic-update-slice_fusion), channel_id=1, source_target_pairs={{0,10},{2,8},{4,14},{6,12},{8,2},{10,0},{12,6},{14,4},{1,11},{3,9}... | collective-permute-start | bytes 98312 | tf_op jit(solution)/shard_map/ppermute | solution.py:17
  11.8 0.1 stack.62
  11.9 0.7 compare_convert_fusion
  12.6 0.8 add_reduce_fusion
  13.5 0.7 iota_compare_fusion
  14.3 0.6 gather_fusion.1
  14.9 0.7 compare_and_fusion.1
  15.6 3.7 %collective-permute-start.5 = (bf16[4,4096]{1,0:T(4,128)(2,1)S(1)}, bf16[4,4096]{1,0:T(4,128)(2,1)S(1)}, u32[]{:S(2)}, u32[]{:S(2)}) collective-permute-start(bf16[4,4096]{1,0:T(4,128)(2,1)S(1)} %constant_dynamic-update-slice_fusion), channel_id=1, source_target_pairs={{0,12},{2,14},{4,8},{6,10},{8,4},{10,6},{12,0},{14,2},{1,13},{3,15... | collective-permute-start | bytes 98312 | tf_op jit(solution)/shard_map/ppermute | solution.py:17
  19.4 1.0 %collective-permute-start.10 = (bf16[4,6144]{1,0:T(4,128)(2,1)}, bf16[4,6144]{1,0:T(4,128)(2,1)S(1)}, u32[]{:S(2)}, u32[]{:S(2)}) collective-permute-start(bf16[4,6144]{1,0:T(4,128)(2,1)} %param.21), channel_id=1, source_target_pairs={{0,8},{2,10},{4,12},{6,14},{8,0},{10,2},{12,4},{14,6},{1,9},{3,11}... | collective-permute-start | bytes 147464 | tf_op jit(solution)/shard_map/ppermute | solution.py:17
  20.4 3.1 %collective-permute-start.11 = (bf16[4,6144]{1,0:T(4,128)(2,1)}, bf16[4,6144]{1,0:T(4,128)(2,1)S(1)}, u32[]{:S(2)}, u32[]{:S(2)}) collective-permute-start(bf16[4,6144]{1,0:T(4,128)(2,1)} %param.21), channel_id=1, source_target_pairs={{0,10},{2,8},{4,14},{6,12},{8,2},{10,0},{12,6},{14,4},{1,11},{3,9}... | collective-permute-start | bytes 147464 | tf_op jit(solution)/shard_map/ppermute | solution.py:17
  23.5 3.6 %collective-permute-start.12 = (bf16[4,6144]{1,0:T(4,128)(2,1)}, bf16[4,6144]{1,0:T(4,128)(2,1)S(1)}, u32[]{:S(2)}, u32[]{:S(2)}) collective-permute-start(bf16[4,6144]{1,0:T(4,128)(2,1)} %param.21), channel_id=1, source_target_pairs={{0,12},{2,14},{4,8},{6,10},{8,4},{10,6},{12,0},{14,2},{1,13},{3,15... | collective-permute-start | bytes 147464 | tf_op jit(solution)/shard_map/ppermute | solution.py:17
  27.1 1.7 %collective-permute-start.7 = (bf16[4,6144]{1,0:T(4,128)(2,1)}, bf16[4,6144]{1,0:T(4,128)(2,1)S(1)}, u32[]{:S(2)}, u32[]{:S(2)}) collective-permute-start(bf16[4,6144]{1,0:T(4,128)(2,1)} %param.21), channel_id=1, source_target_pairs={{0,2},{2,0},{4,6},{6,4},{8,10},{10,8},{12,14},{14,12},{1,3},{3,1},... | collective-permute-start | bytes 147464 | tf_op jit(solution)/shard_map/ppermute | solution.py:17
  28.8 0.2 concatenate.34
  29.0 0.6 gather_fusion
  29.7 0.7 fusion.64
  30.4 0.6 slice_convert_fusion
  31.2 1.9 %collective-permute-start.9 = (bf16[4,6144]{1,0:T(4,128)(2,1)S(1)}, bf16[4,6144]{1,0:T(4,128)(2,1)S(1)}, u32[]{:S(2)}, u32[]{:S(2)}) collective-permute-start(bf16[4,6144]{1,0:T(4,128)(2,1)S(1)} %copy-done.2), channel_id=1, source_target_pairs={{0,6},{2,4},{4,2},{6,0},{8,14},{10,12},{12,10},{14,8},{1,7},{3,5},... | collective-permute-start | bytes 147464 | tf_op jit(solution)/shard_map/ppermute | solution.py:17
  33.0 0.7 fusion.65
  33.8 0.3 collective-permute-done.13
  34.1 1.2 %collective-permute-done.8 = bf16[4,6144]{1,0:T(4,128)(2,1)S(1)} collective-permute-done((bf16[4,6144]{1,0:T(4,128)(2,1)S(1)}, bf16[4,6144]{1,0:T(4,128)(2,1)S(1)}, u32[]{:S(2)}, u32[]{:S(2)}) %collective-permute-start.8) | collective-permute-done | bytes 49184 | tf_op jit(solution)/shard_map/ppermute | solution.py:17
  35.2 1.0 %collective-permute-done.9 = bf16[4,6144]{1,0:T(4,128)(2,1)S(1)} collective-permute-done((bf16[4,6144]{1,0:T(4,128)(2,1)S(1)}, bf16[4,6144]{1,0:T(4,128)(2,1)S(1)}, u32[]{:S(2)}, u32[]{:S(2)}) %collective-permute-start.9) | collective-permute-done | bytes 49184 | tf_op jit(solution)/shard_map/ppermute | solution.py:17
  36.2 0.3 concatenate.35
  36.5 0.2 fusion.30
  36.7 7.6 %fusion.4 = f32[32,1024]{1,0:T(8,128)} fusion(bf16[1,6144,1024]{2,1,0:T(8,128)(2,1)} %param.25, bf16[32,6144]{1,0:T(8,128)(2,1)S(1)} %concatenate.35, f32[6144]{0:T(1024)S(1)} %copy-done.1, f32[32]{0:T(128)S(1)} %add_rsqrt_fusion), kind=kOutput, calls=%fused_computation.6 | convolution fusion | flops 403439616 | bytes 13131904 | tf_op jit(solution)/shard_map/dot_general | solution.py:104
  44.3 12.7 %fusion = f32[32,6144]{1,0:T(8,128)S(1)} fusion(bf16[1,1024,6144]{2,1,0:T(8,128)(2,1)} %param.27, bf16[1,6144,1024]{2,1,0:T(8,128)(2,1)} %param.26, f32[32,1024]{1,0:T(8,128)} %fusion.4, bf16[32,6144]{1,0:T(8,128)(2,1)S(1)} %concatenate.35, f32[6144]{0:T(1024)} %param.22, f32[32]{0:T(128)S(1)} %add_rsqrt_fusion, f32[32]{0:T(128)S(1)} %select_n.80), kind=kOutput, calls=%fused_computation.2 | convolution fusion | flops 806322176 | bytes 26501376 | tf_op jit(solution)/shard_map/dot_general | solution.py:107
  57.1 0.7 multiply_maximum_fusion
  57.8 0.7 collective-permute-done.14
  58.7 1.1 %collective-permute-start.15 = (bf16[4,3072]{1,0:T(4,128)(2,1)S(1)}, bf16[4,3072]{1,0:T(4,128)(2,1)S(1)}, u32[]{:S(2)}, u32[]{:S(2)}) collective-permute-start(bf16[4,3072]{1,0:T(4,128)(2,1)S(1)} %get-tuple-element.6), channel_id=1, source_target_pairs={{0,2},{2,0},{4,6},{6,4},{8,10},{10,8},{12,14},{14,12},{1,3},{3,1},... | collective-permute-start | bytes 73736 | tf_op jit(solution)/shard_map/ppermute | solution.py:17
  59.8 1.4 %collective-permute-start.16 = (bf16[4,3072]{1,0:T(4,128)(2,1)S(1)}, bf16[4,3072]{1,0:T(4,128)(2,1)S(1)}, u32[]{:S(2)}, u32[]{:S(2)}) collective-permute-start(bf16[4,3072]{1,0:T(4,128)(2,1)S(1)} %get-tuple-element.12), channel_id=1, source_target_pairs={{0,4},{2,6},{4,0},{6,2},{8,12},{10,14},{12,8},{14,10},{1,5},{3,7},... | collective-permute-start | bytes 73736 | tf_op jit(solution)/shard_map/ppermute | solution.py:17
  61.1 0.2 fusion.35
  61.3 1.2 %collective-permute-start.17 = (bf16[4,3072]{1,0:T(4,128)(2,1)S(1)}, bf16[4,3072]{1,0:T(4,128)(2,1)S(1)}, u32[]{:S(2)}, u32[]{:S(2)}) collective-permute-start(bf16[4,3072]{1,0:T(4,128)(2,1)S(1)} %get-tuple-element.11), channel_id=1, source_target_pairs={{0,6},{2,4},{4,2},{6,0},{8,14},{10,12},{12,10},{14,8},{1,7},{3,5},... | collective-permute-start | bytes 73736 | tf_op jit(solution)/shard_map/ppermute | solution.py:17
  62.5 4.1 %collective-permute-start.18 = (bf16[4,3072]{1,0:T(4,128)(2,1)S(1)}, bf16[4,3072]{1,0:T(4,128)(2,1)S(1)}, u32[]{:S(2)}, u32[]{:S(2)}) collective-permute-start(bf16[4,3072]{1,0:T(4,128)(2,1)S(1)} %get-tuple-element.10), channel_id=1, source_target_pairs={{0,8},{2,10},{4,12},{6,14},{8,0},{10,2},{12,4},{14,6},{1,9},{3,11}... | collective-permute-start | bytes 73736 | tf_op jit(solution)/shard_map/ppermute | solution.py:17
  66.6 2.9 %collective-permute-start.20 = (bf16[4,3072]{1,0:T(4,128)(2,1)S(1)}, bf16[4,3072]{1,0:T(4,128)(2,1)S(1)}, u32[]{:S(2)}, u32[]{:S(2)}) collective-permute-start(bf16[4,3072]{1,0:T(4,128)(2,1)S(1)} %get-tuple-element.8), channel_id=1, source_target_pairs={{0,12},{2,14},{4,8},{6,10},{8,4},{10,6},{12,0},{14,2},{1,13},{3,15... | collective-permute-start | bytes 73736 | tf_op jit(solution)/shard_map/ppermute | solution.py:17
  69.5 1.8 %collective-permute-start.21 = (bf16[4,3072]{1,0:T(4,128)(2,1)S(1)}, bf16[4,3072]{1,0:T(4,128)(2,1)S(1)}, u32[]{:S(2)}, u32[]{:S(2)}) collective-permute-start(bf16[4,3072]{1,0:T(4,128)(2,1)S(1)} %get-tuple-element.7), channel_id=1, source_target_pairs={{0,14},{2,12},{4,10},{6,8},{8,6},{10,4},{12,2},{14,0},{1,15},{3,13... | collective-permute-start | bytes 73736 | tf_op jit(solution)/shard_map/ppermute | solution.py:17
  71.3 0.7 reshape.437
  72.1 0.1 collective-permute-done.19
  72.2 0.1 collective-permute-done.20
  72.3 3.7 %collective-permute-done.21 = bf16[4,3072]{1,0:T(4,128)(2,1)S(1)} collective-permute-done((bf16[4,3072]{1,0:T(4,128)(2,1)S(1)}, bf16[4,3072]{1,0:T(4,128)(2,1)S(1)}, u32[]{:S(2)}, u32[]{:S(2)}) %collective-permute-start.21) | collective-permute-done | bytes 24608 | tf_op jit(solution)/shard_map/ppermute | solution.py:17
  76.0 0.8 fusion.56
  76.9 2.0 %fusion.27 = bf16[4,4,6,128]{3,2,1,0:T(8,128)(2,1)S(1)} fusion(f32[4,4,6,512]{3,2,1,0:T(8,128)S(1)} %get-tuple-element.20, f32[4,4,6]{2,1,0:T(4,128)S(1)} %get-tuple-element.18, f32[4,4,6]{2,1,0:T(4,128)S(1)} %multiply_maximum_fusion, f32[4,4,128]{2,1,0:T(4,128)S(1)} %reshape.437, f32[4,4,6]{2,1,0:T(4,128)S(1)} %get-tuple-element.17, ...), kind=kOutput, calls=%fused_computation.19 | convolution fusion | flops 12767232 | bytes 2327680 | tf_op jit(solution)/shard_map/rgjt,rtgd->rgjd/dot_general | solution.py:54
  78.9 0.7 convert_element_type.79
  79.6 0.6 pad_maximum_fusion
  (49 shorter events, 1.0 us)
Async XLA Ops:
  0.6 29.1 %copy-start = (bf16[4,512,512]{2,1,0:T(8,128)(2,1)S(1)}, bf16[4,512,512]{2,1,0:T(8,128)(2,1)}, u32[]{:S(2)}) copy-start(bf16[4,512,512]{2,1,0:T(8,128)(2,1)} %param.17) | copy-start | bytes 6291460
  0.6 30.4 %copy-start.2 = (bf16[4,6144]{1,0:T(4,128)(2,1)S(1)}, bf16[4,6144]{1,0:T(4,128)(2,1)}, u32[]{:S(2)}) copy-start(bf16[4,6144]{1,0:T(4,128)(2,1)} %param.21) | copy-start | bytes 147460
  2.9 12.6 %collective-permute-start = (bf16[4,4096]{1,0:T(4,128)(2,1)S(1)}, bf16[4,4096]{1,0:T(4,128)(2,1)S(1)}, u32[]{:S(2)}, u32[]{:S(2)}) collective-permute-start(bf16[4,4096]{1,0:T(4,128)(2,1)S(1)} %constant_dynamic-update-slice_fusion), channel_id=1, source_target_pairs={{0,2},{2,0},{4,6},{6,4},{8,10},{10,8},{12,14},{14,12},{1,3},{3,1},... | collective-permute-start | bytes 98312 | tf_op jit(solution)/shard_map/ppermute | solution.py:17
  5.9 13.3 %collective-permute-start.1 = (bf16[4,4096]{1,0:T(4,128)(2,1)S(1)}, bf16[4,4096]{1,0:T(4,128)(2,1)S(1)}, u32[]{:S(2)}, u32[]{:S(2)}) collective-permute-start(bf16[4,4096]{1,0:T(4,128)(2,1)S(1)} %constant_dynamic-update-slice_fusion), channel_id=1, source_target_pairs={{0,4},{2,6},{4,0},{6,2},{8,12},{10,14},{12,8},{14,10},{1,5},{3,7},... | collective-permute-start | bytes 98312 | tf_op jit(solution)/shard_map/ppermute | solution.py:17
  7.5 11.9 %collective-permute-start.2 = (bf16[4,4096]{1,0:T(4,128)(2,1)S(1)}, bf16[4,4096]{1,0:T(4,128)(2,1)S(1)}, u32[]{:S(2)}, u32[]{:S(2)}) collective-permute-start(bf16[4,4096]{1,0:T(4,128)(2,1)S(1)} %constant_dynamic-update-slice_fusion), channel_id=1, source_target_pairs={{0,6},{2,4},{4,2},{6,0},{8,14},{10,12},{12,10},{14,8},{1,7},{3,5},... | collective-permute-start | bytes 98312 | tf_op jit(solution)/shard_map/ppermute | solution.py:17
  7.5 12.9 %collective-permute-start.3 = (bf16[4,4096]{1,0:T(4,128)(2,1)S(1)}, bf16[4,4096]{1,0:T(4,128)(2,1)S(1)}, u32[]{:S(2)}, u32[]{:S(2)}) collective-permute-start(bf16[4,4096]{1,0:T(4,128)(2,1)S(1)} %constant_dynamic-update-slice_fusion), channel_id=1, source_target_pairs={{0,8},{2,10},{4,12},{6,14},{8,0},{10,2},{12,4},{14,6},{1,9},{3,11}... | collective-permute-start | bytes 98312 | tf_op jit(solution)/shard_map/ppermute | solution.py:17
  10.5 13.0 %collective-permute-start.4 = (bf16[4,4096]{1,0:T(4,128)(2,1)S(1)}, bf16[4,4096]{1,0:T(4,128)(2,1)S(1)}, u32[]{:S(2)}, u32[]{:S(2)}) collective-permute-start(bf16[4,4096]{1,0:T(4,128)(2,1)S(1)} %constant_dynamic-update-slice_fusion), channel_id=1, source_target_pairs={{0,10},{2,8},{4,14},{6,12},{8,2},{10,0},{12,6},{14,4},{1,11},{3,9}... | collective-permute-start | bytes 98312 | tf_op jit(solution)/shard_map/ppermute | solution.py:17
  15.6 11.5 %collective-permute-start.5 = (bf16[4,4096]{1,0:T(4,128)(2,1)S(1)}, bf16[4,4096]{1,0:T(4,128)(2,1)S(1)}, u32[]{:S(2)}, u32[]{:S(2)}) collective-permute-start(bf16[4,4096]{1,0:T(4,128)(2,1)S(1)} %constant_dynamic-update-slice_fusion), channel_id=1, source_target_pairs={{0,12},{2,14},{4,8},{6,10},{8,4},{10,6},{12,0},{14,2},{1,13},{3,15... | collective-permute-start | bytes 98312 | tf_op jit(solution)/shard_map/ppermute | solution.py:17
  19.3 7.8 %collective-permute-start.6 = (bf16[4,4096]{1,0:T(4,128)(2,1)S(1)}, bf16[4,4096]{1,0:T(4,128)(2,1)S(1)}, u32[]{:S(2)}, u32[]{:S(2)}) collective-permute-start(bf16[4,4096]{1,0:T(4,128)(2,1)S(1)} %constant_dynamic-update-slice_fusion), channel_id=1, source_target_pairs={{0,14},{2,12},{4,10},{6,8},{8,6},{10,4},{12,2},{14,0},{1,15},{3,13... | collective-permute-start | bytes 98312 | tf_op jit(solution)/shard_map/ppermute | solution.py:17
  19.4 11.7 %collective-permute-start.10 = (bf16[4,6144]{1,0:T(4,128)(2,1)}, bf16[4,6144]{1,0:T(4,128)(2,1)S(1)}, u32[]{:S(2)}, u32[]{:S(2)}) collective-permute-start(bf16[4,6144]{1,0:T(4,128)(2,1)} %param.21), channel_id=1, source_target_pairs={{0,8},{2,10},{4,12},{6,14},{8,0},{10,2},{12,4},{14,6},{1,9},{3,11}... | collective-permute-start | bytes 147464 | tf_op jit(solution)/shard_map/ppermute | solution.py:17
  20.4 10.8 %collective-permute-start.11 = (bf16[4,6144]{1,0:T(4,128)(2,1)}, bf16[4,6144]{1,0:T(4,128)(2,1)S(1)}, u32[]{:S(2)}, u32[]{:S(2)}) collective-permute-start(bf16[4,6144]{1,0:T(4,128)(2,1)} %param.21), channel_id=1, source_target_pairs={{0,10},{2,8},{4,14},{6,12},{8,2},{10,0},{12,6},{14,4},{1,11},{3,9}... | collective-permute-start | bytes 147464 | tf_op jit(solution)/shard_map/ppermute | solution.py:17
  23.5 10.3 %collective-permute-start.12 = (bf16[4,6144]{1,0:T(4,128)(2,1)}, bf16[4,6144]{1,0:T(4,128)(2,1)S(1)}, u32[]{:S(2)}, u32[]{:S(2)}) collective-permute-start(bf16[4,6144]{1,0:T(4,128)(2,1)} %param.21), channel_id=1, source_target_pairs={{0,12},{2,14},{4,8},{6,10},{8,4},{10,6},{12,0},{14,2},{1,13},{3,15... | collective-permute-start | bytes 147464 | tf_op jit(solution)/shard_map/ppermute | solution.py:17
  27.1 7.0 %collective-permute-start.13 = (bf16[4,6144]{1,0:T(4,128)(2,1)}, bf16[4,6144]{1,0:T(4,128)(2,1)S(1)}, u32[]{:S(2)}, u32[]{:S(2)}) collective-permute-start(bf16[4,6144]{1,0:T(4,128)(2,1)} %param.21), channel_id=1, source_target_pairs={{0,14},{2,12},{4,10},{6,8},{8,6},{10,4},{12,2},{14,0},{1,15},{3,13... | collective-permute-start | bytes 147464 | tf_op jit(solution)/shard_map/ppermute | solution.py:17
  27.1 7.0 %collective-permute-start.7 = (bf16[4,6144]{1,0:T(4,128)(2,1)}, bf16[4,6144]{1,0:T(4,128)(2,1)S(1)}, u32[]{:S(2)}, u32[]{:S(2)}) collective-permute-start(bf16[4,6144]{1,0:T(4,128)(2,1)} %param.21), channel_id=1, source_target_pairs={{0,2},{2,0},{4,6},{6,4},{8,10},{10,8},{12,14},{14,12},{1,3},{3,1},... | collective-permute-start | bytes 147464 | tf_op jit(solution)/shard_map/ppermute | solution.py:17
  29.0 7.8 %copy-start.1 = (f32[6144]{0:T(1024)S(1)}, f32[6144]{0:T(1024)}, u32[]{:S(2)}) copy-start(f32[6144]{0:T(1024)} %param.22) | copy-start | bytes 73732
  31.1 4.2 %collective-permute-start.8 = (bf16[4,6144]{1,0:T(4,128)(2,1)S(1)}, bf16[4,6144]{1,0:T(4,128)(2,1)S(1)}, u32[]{:S(2)}, u32[]{:S(2)}) collective-permute-start(bf16[4,6144]{1,0:T(4,128)(2,1)S(1)} %copy-done.2), channel_id=1, source_target_pairs={{0,4},{2,6},{4,0},{6,2},{8,12},{10,14},{12,8},{14,10},{1,5},{3,7},... | collective-permute-start | bytes 147464 | tf_op jit(solution)/shard_map/ppermute | solution.py:17
  31.2 5.1 %collective-permute-start.9 = (bf16[4,6144]{1,0:T(4,128)(2,1)S(1)}, bf16[4,6144]{1,0:T(4,128)(2,1)S(1)}, u32[]{:S(2)}, u32[]{:S(2)}) collective-permute-start(bf16[4,6144]{1,0:T(4,128)(2,1)S(1)} %copy-done.2), channel_id=1, source_target_pairs={{0,6},{2,4},{4,2},{6,0},{8,14},{10,12},{12,10},{14,8},{1,7},{3,5},... | collective-permute-start | bytes 147464 | tf_op jit(solution)/shard_map/ppermute | solution.py:17
  57.0 14.3 %copy-start.3 = (f32[4,4,1,6]{3,2,1,0:T(1,128)S(1)}, f32[4,4,1,6]{3,2,1,0:T(1,128)}, u32[]{:S(2)}) copy-start(f32[4,4,1,6]{3,2,1,0:T(1,128)} %fusion.65) | copy-start | bytes 1156
  57.1 1.5 %collective-permute-start.14 = (bf16[32,3072]{1,0:T(8,128)(2,1)S(1)}, bf16[32,3072]{1,0:T(8,128)(2,1)S(1)}, u32[]{:S(2)}, u32[]{:S(2)}) collective-permute-start(bf16[32,3072]{1,0:T(8,128)(2,1)S(1)} %dynamic-slice_convert_fusion), channel_id=1, source_target_pairs={{0,1},{1,0},{2,3},{3,2},{4,5},{5,4},{6,7},{7,6},{8,9},{9,8},{10,11... | collective-permute-start | bytes 589832 | tf_op jit(solution)/shard_map/ppermute | solution.py:17
  58.7 7.9 %collective-permute-start.15 = (bf16[4,3072]{1,0:T(4,128)(2,1)S(1)}, bf16[4,3072]{1,0:T(4,128)(2,1)S(1)}, u32[]{:S(2)}, u32[]{:S(2)}) collective-permute-start(bf16[4,3072]{1,0:T(4,128)(2,1)S(1)} %get-tuple-element.6), channel_id=1, source_target_pairs={{0,2},{2,0},{4,6},{6,4},{8,10},{10,8},{12,14},{14,12},{1,3},{3,1},... | collective-permute-start | bytes 73736 | tf_op jit(solution)/shard_map/ppermute | solution.py:17
  59.8 9.7 %collective-permute-start.16 = (bf16[4,3072]{1,0:T(4,128)(2,1)S(1)}, bf16[4,3072]{1,0:T(4,128)(2,1)S(1)}, u32[]{:S(2)}, u32[]{:S(2)}) collective-permute-start(bf16[4,3072]{1,0:T(4,128)(2,1)S(1)} %get-tuple-element.12), channel_id=1, source_target_pairs={{0,4},{2,6},{4,0},{6,2},{8,12},{10,14},{12,8},{14,10},{1,5},{3,7},... | collective-permute-start | bytes 73736 | tf_op jit(solution)/shard_map/ppermute | solution.py:17
  61.3 10.8 %collective-permute-start.17 = (bf16[4,3072]{1,0:T(4,128)(2,1)S(1)}, bf16[4,3072]{1,0:T(4,128)(2,1)S(1)}, u32[]{:S(2)}, u32[]{:S(2)}) collective-permute-start(bf16[4,3072]{1,0:T(4,128)(2,1)S(1)} %get-tuple-element.11), channel_id=1, source_target_pairs={{0,6},{2,4},{4,2},{6,0},{8,14},{10,12},{12,10},{14,8},{1,7},{3,5},... | collective-permute-start | bytes 73736 | tf_op jit(solution)/shard_map/ppermute | solution.py:17
  62.5 9.6 %collective-permute-start.18 = (bf16[4,3072]{1,0:T(4,128)(2,1)S(1)}, bf16[4,3072]{1,0:T(4,128)(2,1)S(1)}, u32[]{:S(2)}, u32[]{:S(2)}) collective-permute-start(bf16[4,3072]{1,0:T(4,128)(2,1)S(1)} %get-tuple-element.10), channel_id=1, source_target_pairs={{0,8},{2,10},{4,12},{6,14},{8,0},{10,2},{12,4},{14,6},{1,9},{3,11}... | collective-permute-start | bytes 73736 | tf_op jit(solution)/shard_map/ppermute | solution.py:17
  66.6 5.6 %collective-permute-start.19 = (bf16[4,3072]{1,0:T(4,128)(2,1)S(1)}, bf16[4,3072]{1,0:T(4,128)(2,1)S(1)}, u32[]{:S(2)}, u32[]{:S(2)}) collective-permute-start(bf16[4,3072]{1,0:T(4,128)(2,1)S(1)} %get-tuple-element.9), channel_id=1, source_target_pairs={{0,10},{2,8},{4,14},{6,12},{8,2},{10,0},{12,6},{14,4},{1,11},{3,9}... | collective-permute-start | bytes 73736 | tf_op jit(solution)/shard_map/ppermute | solution.py:17
  66.6 5.7 %collective-permute-start.20 = (bf16[4,3072]{1,0:T(4,128)(2,1)S(1)}, bf16[4,3072]{1,0:T(4,128)(2,1)S(1)}, u32[]{:S(2)}, u32[]{:S(2)}) collective-permute-start(bf16[4,3072]{1,0:T(4,128)(2,1)S(1)} %get-tuple-element.8), channel_id=1, source_target_pairs={{0,12},{2,14},{4,8},{6,10},{8,4},{10,6},{12,0},{14,2},{1,13},{3,15... | collective-permute-start | bytes 73736 | tf_op jit(solution)/shard_map/ppermute | solution.py:17
  69.5 6.5 %collective-permute-start.21 = (bf16[4,3072]{1,0:T(4,128)(2,1)S(1)}, bf16[4,3072]{1,0:T(4,128)(2,1)S(1)}, u32[]{:S(2)}, u32[]{:S(2)}) collective-permute-start(bf16[4,3072]{1,0:T(4,128)(2,1)S(1)} %get-tuple-element.7), channel_id=1, source_target_pairs={{0,14},{2,12},{4,10},{6,8},{8,6},{10,4},{12,2},{14,0},{1,15},{3,13... | collective-permute-start | bytes 73736 | tf_op jit(solution)/shard_map/ppermute | solution.py:17
  76.8 2.8 %collective-permute-start.22 = (bf16[4,3072]{1,0:T(4,128)(2,1)S(1)}, bf16[4,3072]{1,0:T(4,128)(2,1)S(1)}, u32[]{:S(2)}, u32[]{:S(2)}) collective-permute-start(bf16[4,3072]{1,0:T(4,128)(2,1)S(1)} %fusion.56), channel_id=1, source_target_pairs={{0,1},{1,0},{2,3},{3,2},{4,5},{5,4},{6,7},{7,6},{8,9},{9,8},{10,11... | collective-permute-start | bytes 73736 | tf_op jit(solution)/shard_map/ppermute | solution.py:17

commit v2 on v1

--- a/solution.py
+++ b/solution.py
@@ -9,12 +9,13 @@
 CTX = 512
 
 
-def partner(index, step):
-    return index ^ step
+def swap(block, axis, count, step):
+    return lax.ppermute(block, axis, [(i, i ^ step) for i in range(count)])
 
 
-def swap(block, axis, count, step):
-    return lax.ppermute(block, axis, [(i, partner(i, step)) for i in range(count)])
+def spread(block, wide):
+    copies = jnp.broadcast_to(block[None], (wide,) + block.shape)
+    return lax.all_to_all(copies, "wide", 0, 0, tiled=True).reshape(-1, block.shape[1])
 
 
 def expert_weights(routes, route_logits, expert):
@@ -83,15 +84,18 @@
         half = width // 2
         me = lax.axis_index("wide")
         core = lax.axis_index("narrow")
-        blocks = jnp.stack([partner(me, step) for step in range(wide)])
-
+        part = lax.dynamic_slice_in_dim(tokens, core * half, half, 1)
+        part_rows = spread(part, wide)
+        other_rows = swap(part_rows, "narrow", 2, 1)
         token_rows = jnp.concatenate(
-            [tokens] + [swap(tokens, "wide", wide, step) for step in range(1, wide)], axis=0
+            [
+                jnp.where(core == 0, part_rows, other_rows),
+                jnp.where(core == 0, other_rows, part_rows),
+            ],
+            axis=1,
         )
         mine = jnp.concatenate([queries, new_keys, new_values], axis=1)
-        fetched = jnp.concatenate(
-            [mine] + [swap(mine, "wide", wide, step) for step in range(1, wide)], axis=0
-        )
+        fetched = spread(mine, wide)
 
         values = token_rows.astype(jnp.float32)
         normed = (
@@ -100,7 +104,6 @@
             * norm_gain
         ).astype(jnp.bfloat16)
         weight_all = expert_weights(routes, route_logits, core)
-        weight_all = jnp.take(weight_all.reshape(wide, rows), blocks, axis=0).reshape(-1)
         gate_out = jnp.dot(normed, w_gate[0], preferred_element_type=jnp.float32)
         up_out = jnp.dot(normed, w_up[0], preferred_element_type=jnp.float32)
         hidden = (weight_all[:, None] * jax.nn.silu(gate_out) * up_out).astype(jnp.bfloat16)
@@ -110,10 +113,8 @@
         kept = lax.dynamic_slice_in_dim(terms, core * half, half, 1)
         terms = kept + swap(given.astype(jnp.bfloat16), "narrow", 2, 1).astype(jnp.float32)
         sent = terms.astype(jnp.bfloat16)
-        total = terms[:rows]
-        for step in range(1, wide):
-            block = sent[step * rows : (step + 1) * rows]
-            total = total + swap(block, "wide", wide, step).astype(jnp.float32)
+        pieces = lax.all_to_all(sent.reshape(wide, rows, half), "wide", 0, 0, tiled=True)
+        total = jnp.sum(pieces.astype(jnp.float32), axis=0)
         own = lax.dynamic_slice_in_dim(tokens, core * half, half, 1).astype(jnp.float32)
         piece = (own + total).astype(jnp.bfloat16)
         other = swap(piece, "narrow", 2, 1)
@@ -121,9 +122,7 @@
         second = jnp.where(core == 0, other, piece)
         mixed_out = jnp.concatenate([first, second], axis=1)
 
-        place = assignment // rows
-        found = partner(place, me) * rows + assignment % rows
-        slots = jnp.take(fetched, found, axis=0)
+        slots = jnp.take(fetched, assignment, axis=0)
         q_width, k_width = queries.shape[1], new_keys.shape[1]
         context = attention(
             slots[:, :q_width],

time: 80.7 us -> 72.2 us (0.89)
  starting transfers between devices: 36.4 us -> 14.4 us
  waiting for transfers between devices: 7.16 us -> 21 us
    ppermute x23 -> x3, starting transfers between devices: 36.4 us -> 0.21 us  [swap(): return lax.ppermute(block, axis, [(i, i ^ step) for i in range(count)])]
    all_to_all x0 -> x3, waiting for transfers between devices: none -> 19.6 us  [the longest x2 11.4 us: spread(): lax.all_to_all(copies, 'wide', 0, 0, tiled=True).reshape(-1, block.shape[1])]
    all_to_all x0 -> x3, starting transfers between devices: none -> 14.2 us  [the longest x2 10.7 us: spread(): lax.all_to_all(copies, 'wide', 0, 0, tiled=True).reshape(-1, block.shape[1])]
    ppermute x23 -> x3, waiting for transfers between devices: 7.16 us -> 1.42 us  [swap(): return lax.ppermute(block, axis, [(i, i ^ step) for i in range(count)])]
    broadcast_in_dim x0 -> x2, local copies, waits for them, and re-layouts: none -> 1.49 us  [spread(): copies = jnp.broadcast_to(block[None], (wide,) + block.shape)]
    mul x0 -> x1, other arithmetic: none -> 1.28 us  [local(): weight_all[:, None] * jax.nn.silu(gate_out) * up_out]
    concatenate x3 -> x0, local copies, waits for them, and re-layouts: 1.15 us -> none  [the longest x1 0.7 us: local(): mine = jnp.concatenate([queries, new_keys, new_values], axis=1)]
    unnamed x10, local copies, waits for them, and re-layouts: 1.62 us -> 0.6 us
  transfers between devices with their start and end apart: 23 -> 6, of which waited for: 7 -> 4; matrix products, arithmetic and copies ran while one was open for 14% -> 14% of each run, Pallas kernels for 0% -> 0%
where the time goes in v2:
time: 72.2 us; the launch traced here: 71.5 us
  matrix products  23.2 us (32%)
  waiting for transfers between devices  21 us (29%)
  starting transfers between devices  14.4 us (20%)
  other arithmetic  6.2 us (9%)
  local copies, waits for them, and re-layouts  5.79 us (8%)
  between operations  0.84 us (1%)
    dot_general x1, matrix products, local(): terms = jnp.dot(hidden, w_down[0], preferred_element_type=jnp.float32)  12.8 us
    all_to_all x2, waiting for transfers between devices, spread(): lax.all_to_all(copies, 'wide', 0, 0, tiled=True).reshape(-1, block.shape[1])  11.4 us
    all_to_all x2, starting transfers between devices, spread(): lax.all_to_all(copies, 'wide', 0, 0, tiled=True).reshape(-1, block.shape[1])  10.7 us
    all_to_all x1, waiting for transfers between devices, local(): lax.all_to_all(sent.reshape(wide, rows, half), 'wide', 0, 0, tiled=True)  8.15 us
    dot_general x1, matrix products, local(): gate_out = jnp.dot(normed, w_gate[0], preferred_element_type=jnp.float32)  7.56 us
    all_to_all x1, starting transfers between devices, local(): lax.all_to_all(sent.reshape(wide, rows, half), 'wide', 0, 0, tiled=True)  3.49 us
    dot_general x1, matrix products, attention(): jnp.einsum('rgjt,rtgd->rgjd', attn_probs, cache_values, preferred_element...  2.03 us
    broadcast_in_dim x2, local copies, waits for them, and re-layouts, spread(): copies = jnp.broadcast_to(block[None], (wide,) + block.shape)  1.49 us
  transfers between devices with their start and end apart: 6, of which 4 were waited for; matrix products, arithmetic and copies ran while one was open for 14% of the time, Pallas kernels for 0%

profile of v2, /device:TPU:0, one launch (start us, length us, event | category | flops | bytes accessed | tf_op | source)
XLA Modules:
  0.0 71.5 jit_solution(14020214282643851625)
XLA Ops:
  0.6 0.0 copy-start
  0.7 0.9 %constant_dynamic-slice_fusion = bf16[4,3072]{1,0:T(4,128)(2,1)S(1)} fusion(bf16[4,6144]{1,0:T(4,128)(2,1)} %param.21, s32[]{:T(128)S(6)} %select_n.49), kind=kLoop, calls=%fused_computation.60 | loop fusion | bytes 49156 | tf_op jit(solution)/shard_map/dynamic_slice | solution.py:118
  1.6 0.7 %broadcast_in_dim.52 = bf16[8,4,3072]{2,1,0:T(4,128)(2,1)} broadcast(bf16[4,3072]{1,0:T(4,128)(2,1)S(1)} %constant_dynamic-slice_fusion), dimensions={1,2} | broadcast | bytes 221184 | tf_op jit(solution)/shard_map/broadcast_in_dim | solution.py:17
  2.3 7.3 %all-to-all-start.1 = ((bf16[8,4,3072]{2,1,0:T(4,128)(2,1)}), bf16[8,4,3072]{2,1,0:T(4,128)(2,1)S(1)}, u32[]{:S(2)}, u32[]{:S(2)}) async-start(bf16[8,4,3072]{2,1,0:T(4,128)(2,1)} %broadcast_in_dim.52), calls=%async_computation.1 | async-start | bytes 393216 | tf_op jit(solution)/shard_map/all_to_all | solution.py:18
  9.6 0.7 compare_select_fusion
  10.2 0.7 compare_and_fusion
  10.9 0.7 compare_convert_fusion
  11.6 0.8 %pad_maximum_fusion.2 = bf16[4,4096]{1,0:T(4,128)(2,1)S(1)} fusion(bf16[4,512]{1,0:T(4,128)(2,1)} %param.16, bf16[4,512]{1,0:T(4,128)(2,1)} %param.15, bf16[4,3072]{1,0:T(4,128)(2,1)} %param.14), kind=kLoop, calls=%fused_computation.45 | loop fusion | flops 98304 | bytes 65536 | tf_op jit(solution)/shard_map/concatenate | solution.py:97
  12.3 5.2 %all-to-all-done.1 = bf16[8,4,3072]{2,1,0:T(4,128)(2,1)S(1)} async-done(((bf16[8,4,3072]{2,1,0:T(4,128)(2,1)}), bf16[8,4,3072]{2,1,0:T(4,128)(2,1)S(1)}, u32[]{:S(2)}, u32[]{:S(2)}) %all-to-all-start.1) | async-done | bytes 196640 | tf_op jit(solution)/shard_map/all_to_all | solution.py:18
  17.5 0.8 %broadcast_in_dim.30 = bf16[8,4,4096]{2,1,0:T(4,128)(2,1)} broadcast(bf16[4,4096]{1,0:T(4,128)(2,1)S(1)} %pad_maximum_fusion.2), dimensions={1,2} | broadcast | bytes 294912 | tf_op jit(solution)/shard_map/broadcast_in_dim | solution.py:17
  18.3 3.4 %all-to-all-start = ((bf16[8,4,4096]{2,1,0:T(4,128)(2,1)}), bf16[8,4,4096]{2,1,0:T(4,128)(2,1)S(1)}, u32[]{:S(2)}, u32[]{:S(2)}) async-start(bf16[8,4,4096]{2,1,0:T(4,128)(2,1)} %broadcast_in_dim.30), calls=%async_computation | async-start | bytes 524288 | tf_op jit(solution)/shard_map/all_to_all | solution.py:18
  21.7 0.7 %iota_compare_fusion = pred[4,512]{1,0:T(4,128)(4,1)S(1)} fusion(s32[4]{0:T(128)} %param.19), kind=kLoop, calls=%fused_computation.50 | loop fusion | flops 2048 | bytes 2064 | tf_op jit(solution)/shard_map/lt | solution.py:47
  22.4 1.3 %add_bitcast_fusion = f32[32]{0:T(128)} fusion(f32[32,2]{0,1:T(2,128)S(1)} %compare_convert_fusion, f32[32,2]{0,1:T(2,128)} %param.24), kind=kLoop, calls=%fused_computation.62 | loop fusion | flops 224 | bytes 640 | tf_op jit(solution)/shard_map/mul | solution.py:109
  23.8 0.1 collective-permute-start
  23.9 6.3 %all-to-all-done = bf16[8,4,4096]{2,1,0:T(4,128)(2,1)S(1)} async-done(((bf16[8,4,4096]{2,1,0:T(4,128)(2,1)}), bf16[8,4,4096]{2,1,0:T(4,128)(2,1)S(1)}, u32[]{:S(2)}, u32[]{:S(2)}) %all-to-all-start) | async-done | bytes 262176 | tf_op jit(solution)/shard_map/all_to_all | solution.py:18
  30.1 0.1 reshape.71
  30.2 0.0 copy-start.1
  30.2 0.6 gather_fusion
  30.8 0.1 broadcast_select_fusion.2
  31.0 0.6 reshape.78
  31.6 0.0 copy-done
  31.6 0.7 %fusion.52 = (f32[4,4,6]{2,1,0:T(4,128)S(1)}, f32[4,4,6,512]{3,2,1,0:T(8,128)S(1)}) fusion(bf16[4,4,6,128]{3,2,1,0:T(8,128)(2,1)S(1)} %reshape.72, pred[4,512]{1,0:T(4,128)(4,1)S(1)} %iota_compare_fusion, bf16[4,512,512]{2,1,0:T(8,128)(2,1)S(1)} %copy-done), kind=kOutput, calls=%fused_computation.64 | convolution fusion | flops 12730272 | bytes 2320768 | tf_op jit(solution)/shard_map/rgjd,rtgd->rgjt/dot_general | solution.py:43
  32.3 0.1 fusion.53
  32.5 0.0 collective-permute-done
  32.5 0.2 fusion.30
  32.7 0.0 copy-start.4
  32.8 0.6 copy-done.4
  33.3 0.0 copy-done.1
  33.3 7.6 %fusion.4 = f32[32,1024]{1,0:T(8,128)} fusion(bf16[1,6144,1024]{2,1,0:T(8,128)(2,1)} %param.25, f32[6144]{0:T(1024)S(1)} %copy-done.1, f32[32]{0:T(128)S(1)} %add_rsqrt_fusion, bf16[32,3072]{1,0:T(8,128)(2,1)S(1)} %get-tuple-element.3, bf16[32,3072]{1,0:T(8,128)(2,1)S(1)} %get-tuple-element.2), kind=kOutput, calls=%fused_computation.5 | convolution fusion | flops 404029440 | bytes 13131904 | tf_op jit(solution)/shard_map/dot_general | solution.py:107
  40.9 12.8 %fusion = f32[32,6144]{1,0:T(8,128)S(1)} fusion(bf16[1,1024,6144]{2,1,0:T(8,128)(2,1)} %param.27, bf16[1,6144,1024]{2,1,0:T(8,128)(2,1)} %param.26, f32[32,1024]{1,0:T(8,128)} %fusion.4, f32[32]{0:T(128)} %add_bitcast_fusion, f32[6144]{0:T(1024)} %param.22, f32[32]{0:T(128)} %copy-done.4, bf16[32,3072]{1,0:T(8,128)(2,1)S(1)} %get-tuple-element.3, ...), kind=kOutput, calls=%fused_computation.1 | convolution fusion | flops 806912000 | bytes 26501376 | tf_op jit(solution)/shard_map/dot_general | solution.py:110
  53.7 0.0 copy-start.2
  53.7 0.0 copy-start.3
  53.7 0.1 collective-permute-start.1
  53.8 1.4 %collective-permute-done.1 = bf16[32,3072]{1,0:T(8,128)(2,1)S(1)} collective-permute-done((bf16[32,3072]{1,0:T(8,128)(2,1)S(1)}, bf16[32,3072]{1,0:T(8,128)(2,1)S(1)}, u32[]{:S(2)}, u32[]{:S(2)}) %collective-permute-start.1) | collective-permute-done | bytes 196640 | tf_op jit(solution)/shard_map/ppermute | solution.py:13
  55.3 0.8 %reshape.77 = bf16[8,4,3072]{2,1,0:T(4,128)(2,1)} reshape(bf16[32,3072]{1,0:T(8,128)(2,1)S(1)} %add_convert_fusion) | data formatting | bytes 393216 | tf_op jit(solution)/shard_map/reshape | solution.py:116
  56.0 3.5 %all-to-all-start.2 = ((bf16[8,4,3072]{2,1,0:T(4,128)(2,1)}), bf16[8,4,3072]{2,1,0:T(4,128)(2,1)S(1)}, u32[]{:S(2)}, u32[]{:S(2)}) async-start(bf16[8,4,3072]{2,1,0:T(4,128)(2,1)} %reshape.77), calls=%async_computation.2 | async-start | bytes 393216 | tf_op jit(solution)/shard_map/all_to_all | solution.py:116
  59.5 0.2 fusion.35
  59.8 8.2 %all-to-all-done.2 = bf16[8,4,3072]{2,1,0:T(4,128)(2,1)S(1)} async-done(((bf16[8,4,3072]{2,1,0:T(4,128)(2,1)}), bf16[8,4,3072]{2,1,0:T(4,128)(2,1)S(1)}, u32[]{:S(2)}, u32[]{:S(2)}) %all-to-all-start.2) | async-done | bytes 196640 | tf_op jit(solution)/shard_map/all_to_all | solution.py:116
  67.9 0.1 convert_reduce_fusion
  68.0 0.0 copy-done.2
  68.0 0.1 collective-permute-start.2
  68.1 0.0 copy-done.3
  68.1 2.0 %fusion.27 = bf16[4,4,6,128]{3,2,1,0:T(8,128)(2,1)S(1)} fusion(f32[4,4,6,512]{3,2,1,0:T(8,128)S(1)} %get-tuple-element.11, f32[4,4,6]{2,1,0:T(4,128)S(1)} %get-tuple-element.9, f32[4,4,6]{2,1,0:T(4,128)S(1)} %multiply_maximum_fusion, f32[4,4,128]{2,1,0:T(4,128)S(1)} %copy-done.3, f32[4,4,6]{2,1,0:T(4,128)S(1)} %get-tuple-element.8, ...), kind=kOutput, calls=%fused_computation.18 | convolution fusion | flops 12767232 | bytes 2327680 | tf_op jit(solution)/shard_map/rgjt,rtgd->rgjd/dot_general | solution.py:55
  70.2 0.7 convert_element_type.61
  70.8 0.0 collective-permute-done.2
  70.8 0.6 pad_maximum_fusion.1
  (14 shorter events, 0.3 us)
Async XLA Ops:
  0.6 31.0 %copy-start = (bf16[4,512,512]{2,1,0:T(8,128)(2,1)S(1)}, bf16[4,512,512]{2,1,0:T(8,128)(2,1)}, u32[]{:S(2)}) copy-start(bf16[4,512,512]{2,1,0:T(8,128)(2,1)} %param.17) | copy-start | bytes 6291460
  2.3 15.2 %all-to-all-start.1 = ((bf16[8,4,3072]{2,1,0:T(4,128)(2,1)}), bf16[8,4,3072]{2,1,0:T(4,128)(2,1)S(1)}, u32[]{:S(2)}, u32[]{:S(2)}) async-start(bf16[8,4,3072]{2,1,0:T(4,128)(2,1)} %broadcast_in_dim.52), calls=%async_computation.1 | async-start | bytes 393216 | tf_op jit(solution)/shard_map/all_to_all | solution.py:18
  18.3 11.9 %all-to-all-start = ((bf16[8,4,4096]{2,1,0:T(4,128)(2,1)}), bf16[8,4,4096]{2,1,0:T(4,128)(2,1)S(1)}, u32[]{:S(2)}, u32[]{:S(2)}) async-start(bf16[8,4,4096]{2,1,0:T(4,128)(2,1)} %broadcast_in_dim.30), calls=%async_computation | async-start | bytes 524288 | tf_op jit(solution)/shard_map/all_to_all | solution.py:18
  23.8 8.7 %collective-permute-start = (bf16[32,3072]{1,0:T(8,128)(2,1)S(1)}, bf16[32,3072]{1,0:T(8,128)(2,1)S(1)}, u32[]{:S(2)}, u32[]{:S(2)}) collective-permute-start(bf16[32,3072]{1,0:T(8,128)(2,1)S(1)} %reshape.76), channel_id=1, source_target_pairs={{0,1},{1,0},{2,3},{3,2},{4,5},{5,4},{6,7},{7,6},{8,9},{9,8},{10,11... | collective-permute-start | bytes 589832 | tf_op jit(solution)/shard_map/ppermute | solution.py:13
  30.2 3.1 %copy-start.1 = (f32[6144]{0:T(1024)S(1)}, f32[6144]{0:T(1024)}, u32[]{:S(2)}) copy-start(f32[6144]{0:T(1024)} %param.22) | copy-start | bytes 73732
  32.7 0.6 copy-start.4
  53.7 14.3 %copy-start.2 = (bf16[4,6144]{1,0:T(4,128)(2,1)S(1)}, bf16[4,6144]{1,0:T(4,128)(2,1)}, u32[]{:S(2)}) copy-start(bf16[4,6144]{1,0:T(4,128)(2,1)} %param.21) | copy-start | bytes 147460
  53.7 14.4 %copy-start.3 = (f32[4,4,128]{2,1,0:T(4,128)S(1)}, f32[4,4,128]{2,1,0:T(4,128)}, u32[]{:S(2)}) copy-start(f32[4,4,128]{2,1,0:T(4,128)} %reshape.78) | copy-start | bytes 24580
  53.7 1.5 %collective-permute-start.1 = (bf16[32,3072]{1,0:T(8,128)(2,1)S(1)}, bf16[32,3072]{1,0:T(8,128)(2,1)S(1)}, u32[]{:S(2)}, u32[]{:S(2)}) collective-permute-start(bf16[32,3072]{1,0:T(8,128)(2,1)S(1)} %dynamic-slice_convert_fusion), channel_id=1, source_target_pairs={{0,1},{1,0},{2,3},{3,2},{4,5},{5,4},{6,7},{7,6},{8,9},{9,8},{10,11... | collective-permute-start | bytes 589832 | tf_op jit(solution)/shard_map/ppermute | solution.py:13
  56.0 11.9 %all-to-all-start.2 = ((bf16[8,4,3072]{2,1,0:T(4,128)(2,1)}), bf16[8,4,3072]{2,1,0:T(4,128)(2,1)S(1)}, u32[]{:S(2)}, u32[]{:S(2)}) async-start(bf16[8,4,3072]{2,1,0:T(4,128)(2,1)} %reshape.77), calls=%async_computation.2 | async-start | bytes 393216 | tf_op jit(solution)/shard_map/all_to_all | solution.py:116
  68.0 2.8 %collective-permute-start.2 = (bf16[4,3072]{1,0:T(4,128)(2,1)S(1)}, bf16[4,3072]{1,0:T(4,128)(2,1)S(1)}, u32[]{:S(2)}, u32[]{:S(2)}) collective-permute-start(bf16[4,3072]{1,0:T(4,128)(2,1)S(1)} %add_convert_fusion.1), channel_id=1, source_target_pairs={{0,1},{1,0},{2,3},{3,2},{4,5},{5,4},{6,7},{7,6},{8,9},{9,8},{10,11... | collective-permute-start | bytes 73736 | tf_op jit(solution)/shard_map/ppermute | solution.py:13

commit v3 on v2

v3 whole, which is shorter than its diff:
```python
import functools
import math

import jax
import jax.numpy as jnp
from jax import lax
from jax.experimental import pallas as pl
from jax.experimental.pallas import tpu as pltpu
from jax.sharding import PartitionSpec as P

HQ = 48
KVH = 8
HD = 128
GROUP = HQ // KVH
SCALE = HD ** (-0.5)
TILE = 256
CUTS = 4
MIB = 1024 * 1024


def steps_of(wide):
    return [wide >> (i + 1) for i in range(int(math.log2(wide)))]


def swap(block, axis, count, step):
    return lax.ppermute(block, axis, [(i, i ^ step) for i in range(count)])


def owner_of(place, me, steps):
    found = me
    for bit, step in enumerate(steps):
        found = found ^ (((place >> bit) & 1) * step)
    return found


def place_of(owner, me, steps):
    differ = owner ^ me
    found = 0
    for bit, step in enumerate(steps):
        shift = int(math.log2(step))
        found = found | (((differ >> shift) & 1) << bit)
    return found


def call(kernel, outs, ins, scratch=(), flops=0, size=0, limit=16, smem=(), far=()):
    spaces = [pltpu.SMEM if i in smem else pl.ANY if i in far else pltpu.VMEM for i in range(len(ins))]
    return pl.pallas_call(
        kernel,
        name=getattr(kernel, "func", kernel).__name__,
        out_shape=outs,
        in_specs=[pl.BlockSpec(memory_space=space) for space in spaces],
        out_specs=jax.tree.map(lambda _: pl.BlockSpec(memory_space=pltpu.VMEM), outs),
        scratch_shapes=list(scratch),
        compiler_params=pltpu.CompilerParams(vmem_limit_bytes=limit * MIB),
        cost_estimate=pl.CostEstimate(flops=flops, bytes_accessed=size, transcendentals=0),
    )(*ins)


def row_copies(source, target, sems, first):
    rows = target.shape[0] // CUTS
    return [
        pltpu.make_async_copy(
            source.at[0, pl.ds(pl.multiple_of(first + i * rows, rows), rows), :],
            target.at[pl.ds(i * rows, rows), :],
            sems.at[i],
        )
        for i in range(CUTS)
    ]


def column_copies(source, target, sems, first):
    columns = target.shape[1] // CUTS
    return [
        pltpu.make_async_copy(
            source.at[0, :, pl.ds(pl.multiple_of(first + i * columns, columns), columns)],
            target.at[:, pl.ds(i * columns, columns)],
            sems.at[i],
        )
        for i in range(CUTS)
    ]


def load(other, source, after, target, sems):
    core = lax.axis_index("narrow")
    side = 1 - core if other else core
    copies = row_copies(source, target, sems, side * target.shape[0])
    for copy in copies:
        copy.start()
    for copy in copies:
        copy.wait()


def shape(dims, dtype):
    return jax.ShapeDtypeStruct(dims, dtype)


def near(array):
    return pltpu.with_memory_space_constraint(array, pltpu.VMEM)


def distant(array):
    return pltpu.with_memory_space_constraint(array, pltpu.HBM)


def prepare(far_tokens, far_gain, far_query, far_key, far_value, out_ref, heads_ref, *held):
    *near_refs, packed, sems = held
    far_refs = (far_tokens, far_gain, far_query, far_key, far_value)
    copies = [
        pltpu.make_async_copy(far, ref, sems.at[i])
        for i, (far, ref) in enumerate(zip(far_refs, near_refs))
    ]
    for copy in copies:
        copy.start()
    for copy in copies:
        copy.wait()
    tokens_ref, gain_ref, *head_refs = near_refs
    half = out_ref.shape[1]
    core = lax.axis_index("narrow")
    values = tokens_ref[...].astype(jnp.float32)
    scale = lax.rsqrt(jnp.mean(values * values, axis=-1, keepdims=True) + 1e-05)
    normed = (values * scale * gain_ref[...]).astype(jnp.bfloat16)
    out_ref[...] = jnp.where(core == 0, normed[:, :half], normed[:, half:])
    rows = tokens_ref.shape[0]
    at = 0
    each = heads_ref.shape[0] // rows
    for ref in head_refs:
        block = ref[...].astype(jnp.float32)
        for head in range(ref.shape[1] // HD):
            packed[pl.ds(at, rows, stride=each), :] = block[:, head * HD : (head + 1) * HD]
            at += 1
    heads_ref[...] = packed[...].astype(jnp.bfloat16)


def grow(own_ref, got_ref, after, out_ref):
    both = [own_ref[...].astype(jnp.float32), got_ref[...].astype(jnp.float32)]
    out_ref[...] = jnp.concatenate(both, axis=0).astype(jnp.bfloat16)


def gate_first(x_ref, gate_ref, up_ref, far_up, gate_out, up_out, up_rest, sems):
    core = lax.axis_index("narrow")
    copies = row_copies(far_up, up_rest, sems, (1 - core) * up_rest.shape[0])
    for copy in copies:
        copy.start()
    tile = min(TILE, gate_ref.shape[1])

    @pl.loop(0, gate_ref.shape[1] // tile)
    def _(i):
        columns = pl.ds(pl.multiple_of(i * tile, tile), tile)
        x = x_ref[...]
        gate_out[:, columns] = jnp.dot(x, gate_ref[:, columns], preferred_element_type=jnp.float32)
        up_out[:, columns] = jnp.dot(x, up_ref[:, columns], preferred_element_type=jnp.float32)

    for copy in copies:
        copy.wait()


def gate_second(
    steps,
    rows,
    x_ref,
    gate_ref,
    up_ref,
    gate_part,
    up_part,
    routes_ref,
    logits_ref,
    far_down,
    hidden_out,
    given_out,
    down_own,
    down_other,
    sems,
):
    count, depth = x_ref.shape
    core = lax.axis_index("narrow")
    me = lax.axis_index("wide")
    other_copies = column_copies(far_down, down_other, sems.at[0], (1 - core) * depth)
    own_copies = column_copies(far_down, down_own, sems.at[1], core * depth)
    for copy in other_copies + own_copies:
        copy.start()
    tile = min(TILE, gate_ref.shape[1])

    logits = logits_ref[...]
    first = 1.0 / (1.0 + jnp.exp(logits[1:2] - logits[0:1]))
    second = 1.0 - first
    chosen = (routes_ref[...] == core).astype(jnp.float32)
    weight_row = chosen[0:1] * first + chosen[1:2] * second
    row = lax.broadcasted_iota(jnp.int32, (count, count), 0)
    column = lax.broadcasted_iota(jnp.int32, (count, count), 1)
    shift = int(math.log2(rows))
    token = (owner_of(row >> shift, me, steps) << shift) | (row & (rows - 1))
    weight = jnp.sum(jnp.where(token == column, weight_row, 0.0), axis=1, keepdims=True)

    @pl.loop(0, gate_ref.shape[1] // tile)
    def _(i):
        columns = pl.ds(pl.multiple_of(i * tile, tile), tile)
        x = x_ref[...]
        gate = gate_part[:, columns] + jnp.dot(
            x, gate_ref[:, columns], preferred_element_type=jnp.float32
        )
        up = up_part[:, columns] + jnp.dot(
            x, up_ref[:, columns], preferred_element_type=jnp.float32
        )
        hidden_out[:, columns] = (weight * (gate * jax.nn.sigmoid(gate)) * up).astype(jnp.bfloat16)

    span = depth // CUTS
    for cut, copy in enumerate(other_copies):
        copy.wait()
        columns = slice(cut * span, (cut + 1) * span)
        given_out[:, columns] = jnp.dot(
            hidden_out[...], down_other[:, columns], preferred_element_type=jnp.float32
        ).astype(jnp.bfloat16)
    for copy in own_copies:
        copy.wait()


def down_first(hidden_ref, down_ref, out_ref):
    @pl.loop(0, out_ref.shape[1] // TILE)
    def _(i):
        columns = pl.ds(pl.multiple_of(i * TILE, TILE), TILE)
        out_ref[:, columns] = jnp.dot(
            hidden_ref[...], down_ref[:, columns], preferred_element_type=jnp.float32
        )


def combine(terms_ref, taken_ref, after, kept_ref, sent_ref):
    total = terms_ref[...] + taken_ref[...].astype(jnp.float32)
    kept = kept_ref.shape[0]
    kept_ref[...] = total[:kept]
    sent_ref[...] = total[kept:].astype(jnp.bfloat16)


def finish(terms_ref, taken_ref, tokens_ref, out_ref):
    half = out_ref.shape[1]
    core = lax.axis_index("narrow")
    own = tokens_ref[...].astype(jnp.float32)
    own = jnp.where(core == 0, own[:, :half], own[:, half:])
    total = terms_ref[...] + taken_ref[...].astype(jnp.float32)
    out_ref[...] = (own + total).astype(jnp.bfloat16)


def join(own_ref, other_ref, out_ref):
    half = own_ref.shape[1]
    core = lax.axis_index("narrow")
    own, other = own_ref[...], other_ref[...]
    out_ref[:, :half] = jnp.where(core == 0, own, other)
    out_ref[:, half:] = jnp.where(core == 0, other, own)


def attend(
    steps, taking, near_ref, far_ref, keys_ref, values_ref, lengths_ref, place_ref, after, out_ref
):
    slots, span, width = keys_ref.shape
    rows = slots
    kv_local = width // HD
    heads = kv_local * GROUP
    each = heads + 2 * kv_local
    me = lax.axis_index("wide")
    shift = int(math.log2(rows))
    half = near_ref.shape[0]
    head_of = lax.broadcasted_iota(jnp.int32, (heads, 1), 0)
    positions = lax.broadcasted_iota(jnp.int32, (heads, span), 1)

    def by_group(pieces):
        result = pieces[0]
        for g in range(1, kv_local):
            result = jnp.where(head_of >= g * GROUP, pieces[g], result)
        return result

    for order, slot in enumerate(taking):
        request = place_ref[slot]
        at = (place_of(request >> shift, me, steps) << shift) | (request & (rows - 1))
        at = at * each
        inside = pl.ds(pl.multiple_of(jnp.where(at < half, at, at - half), each), each)
        block = jnp.where(at < half, near_ref[inside, :], far_ref[inside, :])
        query = block[:heads]
        own = block[heads:].astype(jnp.float32)
        own_key = by_group([own[g : g + 1] for g in range(kv_local)])
        own_value = by_group([own[kv_local + g : kv_local + g + 1] for g in range(kv_local)])
        own_score = jnp.sum(query.astype(jnp.float32) * own_key, axis=1, keepdims=True) * SCALE
        scores = by_group(
            [
                lax.dot_general(
                    query,
                    keys_ref[slot, :, g * HD : (g + 1) * HD],
                    (((1,), (1,)), ((), ())),
                    preferred_element_type=jnp.float32,
                )
                for g in range(kv_local)
            ]
        )
        scores = jnp.where(positions < lengths_ref[slot], scores * SCALE, -jnp.inf)
        row_max = jnp.maximum(jnp.max(scores, axis=1, keepdims=True), own_score)
        weights = jnp.exp(scores - row_max)
        own_weight = jnp.exp(own_score - row_max)
        total = jnp.sum(weights, axis=1, keepdims=True) + own_weight
        probs = (weights / total).astype(jnp.bfloat16)
        own_prob = (own_weight / total).astype(jnp.bfloat16).astype(jnp.float32)
        mixed = by_group(
            [
                jnp.dot(
                    probs,
                    values_ref[slot, :, g * HD : (g + 1) * HD],
                    preferred_element_type=jnp.float32,
                )
                for g in range(kv_local)
            ]
        )
        out_ref[order * heads : (order + 1) * heads, :] = mixed + own_prob * own_value


def lay_out(heads, pieces, out_ref, held):
    at = 0
    for piece in pieces:
        held[at : at + piece.shape[0], :] = piece[...]
        at += piece.shape[0]
    for head in range(heads):
        out_ref[:, head * HD : (head + 1) * HD] = held[
            pl.ds(head, out_ref.shape[0], stride=heads), :
        ].astype(jnp.bfloat16)


def attend_last(steps, taking, heads, *refs):
    *ins, early, out_ref, late, held = refs
    attend(steps, taking, *ins, late)
    lay_out(heads, [early, late], out_ref, held)


def make_local(wide):
    steps = steps_of(wide)

    def local(
        queries,
        new_keys,
        new_values,
        key_cache,
        value_cache,
        lengths,
        assignment,
        tokens,
        norm_gain,
        routes,
        route_logits,
        w_gate,
        w_up,
        w_down,
    ):
        rows, width = tokens.shape
        half = width // 2
        units = w_gate.shape[2]
        count = rows * wide
        each = (queries.shape[1] + 2 * new_keys.shape[1]) // HD
        core = lax.axis_index("narrow")
        bf16, f32 = jnp.bfloat16, jnp.float32
        heads_local = queries.shape[1] // HD
        dma = pltpu.SemaphoreType.DMA
        piece_bytes = 2 * half * units

        firsts = [tokens, norm_gain[None], queries, new_keys, new_values]
        x, heads = call(
            prepare,
            [shape((rows, half), bf16), shape((rows * each, HD), bf16)],
            [distant(a) for a in firsts],
            [pltpu.VMEM(a.shape, a.dtype) for a in firsts]
            + [pltpu.VMEM((rows * each, HD), f32), dma((len(firsts),))],
            size=100000,
            far=range(len(firsts)),
        )

        def loaded(weights, other, after):
            return call(
                functools.partial(load, other),
                pltpu.VMEM((half, units), bf16),
                [distant(weights), after],
                [dma((CUTS,))],
                size=piece_bytes,
                far=(0, 1),
            )

        pieces = []
        far_heads = None
        for order, step in enumerate(steps):
            got = swap(x, "wide", wide, step)
            got_heads = swap(heads, "wide", wide, step)
            if order < 3:
                pieces.append(loaded((w_gate, w_up, w_gate)[order], order == 2, x))
            x = call(
                grow,
                shape((2 * x.shape[0], half), bf16),
                [x, got, near(pieces[-1])],
                size=8 * x.size,
                far=(2,),
            )
            if order < len(steps) - 1:
                heads = jnp.concatenate([heads, got_heads], axis=0)
            else:
                far_heads = got_heads

        product = 2 * count * half * units
        other_x = swap(x, "narrow", 2, 1)
        part = shape((count, units), f32)
        gate_part, up_part, up_rest = call(
            gate_first,
            [part, part, pltpu.VMEM((half, units), bf16)],
            [x, near(pieces[0]), near(pieces[1]), distant(w_up)],
            [dma((CUTS,))],
            flops=2 * product,
            size=3 * piece_bytes,
            far=(3,),
        )
        hidden, given, down_piece = call(
            functools.partial(gate_second, steps, rows),
            [shape((count, units), bf16), shape((count, half), bf16), pltpu.VMEM((units, half), bf16)],
            [
                other_x,
                near(pieces[2]),
                near(up_rest),
                gate_part,
                up_part,
                routes.T,
                route_logits.T,
                distant(w_down),
            ],
            [pltpu.VMEM((units, half), bf16), dma((2, CUTS))],
            flops=3 * product,
            size=4 * piece_bytes,
            far=(7,),
        )
        taken = swap(given, "narrow", 2, 1)
        terms = call(
            down_first,
            shape((count, half), f32),
            [hidden, near(down_piece)],
            flops=product,
            size=piece_bytes,
        )

        caches = [near(key_cache), near(value_cache), lengths, assignment]
        slots = queries.shape[0]
        early = None
        context = None
        after = hidden
        for order, step in enumerate(reversed(steps)):
            kept = terms.shape[0] // 2
            terms, sent = call(
                combine,
                [shape((kept, half), f32), shape((kept, half), bf16)],
                [terms, taken, after],
                size=terms.size * 8,
                far=(2,),
            )
            taken = swap(sent, "wide", wide, step)
            if order == 0:
                early = call(
                    functools.partial(attend, steps, list(range(slots // 2))),
                    shape((slots // 2 * heads_local, HD), f32),
                    [heads, far_heads, *caches, sent],
                    flops=2 * key_cache.size * GROUP,
                    size=2 * key_cache.size,
                    smem=(4, 5),
                    far=(6,),
                )
                after = early
            elif order == 1:
                context = call(
                    functools.partial(attend_last, steps, list(range(slots // 2, slots)), heads_local),
                    shape(queries.shape, bf16),
                    [heads, far_heads, *caches, sent, early],
                    [
                        pltpu.VMEM(((slots - slots // 2) * heads_local, HD), f32),
                        pltpu.VMEM((slots * heads_local, HD), f32),
                    ],
                    flops=2 * key_cache.size * GROUP,
                    size=2 * key_cache.size,
                    smem=(4, 5),
                    far=(6,),
                )
                after = distant(context)

        piece = call(finish, shape((rows, half), bf16), [terms, taken, tokens], size=terms.size * 8)
        other = swap(piece, "narrow", 2, 1)
        mixed_out = call(join, shape((rows, width), bf16), [piece, other], size=terms.size * 4)
        return (context, mixed_out)

    return local


def solution(mesh):
    placed = (
        P(("groups", "wide"), "narrow"),
        P(("groups", "wide"), "narrow"),
        P(("groups", "wide"), "narrow"),
        P(("groups", "wide"), None, "narrow"),
        P(("groups", "wide"), None, "narrow"),
        P(("groups", "wide")),
        P(("groups", "wide")),
        P(("groups", "wide"), None),
        P(),
        P("groups", None),
        P("groups", None),
        P("narrow", None, "wide"),
        P("narrow", None, "wide"),
        P("narrow", "wide", None),
    )
    return jax.shard_map(
        make_local(mesh.shape["wide"]),
        mesh=mesh,
        in_specs=placed,
        out_specs=(P(("groups", "wide"), "narrow"), P(("groups", "wide"), None)),
        check_vma=False,
    )
```

time: 72.2 us -> 48.1 us (0.67)
  Pallas kernels: 0 us -> 24.5 us
  matrix products: 23.2 us -> 0 us
  waiting for transfers between devices: 21 us -> 6.59 us
  other arithmetic: 6.2 us -> 0.01 us
  local copies, waits for them, and re-layouts: 5.79 us -> 0.07 us
  starting transfers between devices: 14.4 us -> 15.9 us
    pallas_call x0 -> x17, Pallas kernels: none -> 24.5 us  [call(): pl.pallas_call(kernel, name=getattr(kernel, 'func', kernel).__name__, out...]
    dot_general x5 -> x0, matrix products: 23.2 us -> none  [the longest x1 12.8 us: local(): terms = jnp.dot(hidden, w_down[0], preferred_element_type=jnp.float32)]
    all_to_all x3 -> x0, waiting for transfers between devices: 19.6 us -> none  [the longest x2 11.4 us: spread(): lax.all_to_all(copies, 'wide', 0, 0, tiled=True).reshape(-1, block.shape[1])]
    ppermute x3 -> x12, starting transfers between devices: 0.21 us -> 15.9 us  [swap(): return lax.ppermute(block, axis, [(i, i ^ step) for i in range(count)])]
    all_to_all x3 -> x0, starting transfers between devices: 14.2 us -> none  [the longest x2 10.7 us: spread(): lax.all_to_all(copies, 'wide', 0, 0, tiled=True).reshape(-1, block.shape[1])]
    ppermute x3 -> x12, waiting for transfers between devices: 1.42 us -> 6.59 us  [swap(): return lax.ppermute(block, axis, [(i, i ^ step) for i in range(count)])]
    broadcast_in_dim x2 -> x0, local copies, waits for them, and re-layouts: 1.49 us -> none  [spread(): copies = jnp.broadcast_to(block[None], (wide,) + block.shape)]
    concatenate x2 -> x1, other arithmetic: 1.43 us -> 0.01 us  [local(): heads = jnp.concatenate([heads, got_heads], axis=0)]
  transfers between devices with their start and end apart: 6 -> 12, of which waited for: 4 -> 5; matrix products, arithmetic and copies ran while one was open for 14% -> 0% of each run, Pallas kernels for 0% -> 47%
where the time goes in v3:
time: 48.1 us; the launch traced here: 48 us
  Pallas kernels  24.5 us (51%)
  starting transfers between devices  15.9 us (33%)
  waiting for transfers between devices  6.59 us (14%)
  between operations  0.9 us (2%)
    pallas_call x17, Pallas kernels, call(): pl.pallas_call(kernel, name=getattr(kernel, 'func', kernel).__name__, out...  24.5 us
    ppermute x12, starting transfers between devices, swap(): return lax.ppermute(block, axis, [(i, i ^ step) for i in range(count)])  15.9 us
    ppermute x12, waiting for transfers between devices, swap(): return lax.ppermute(block, axis, [(i, i ^ step) for i in range(count)])  6.59 us
  transfers between devices with their start and end apart: 12, of which 5 were waited for; matrix products, arithmetic and copies ran while one was open for 0% of the time, Pallas kernels for 47%

profile of v3, /device:TPU:0, one launch (start us, length us, event | category | flops | bytes accessed | tf_op | source)
XLA Modules:
  0.0 48.0 jit_solution(9117881867814178975)
XLA Ops:
  0.6 1.0 %prepare.1 = (bf16[4,3072]{1,0:T(4,128)(2,1)S(1)}, bf16[128,128]{1,0:T(8,128)(2,1)S(1)}) custom-call(bf16[4,6144]{1,0:T(4,128)(2,1)} %tokens_ref.1, f32[1,6144]{1,0:T(1,128)} %bitcast.5, bf16[4,3072]{1,0:T(4,128)(2,1)} %far_query.1, bf16[4,512]{1,0:T(4,128)(2,1)} %far_key.1, bf16[4,512]{1,0:T(4,128)(2,1)} %far_value.1), custom_call_target="tpu_custom_call" | custom-call | bytes 100000 | tf_op jit(solution)/shard_map/prepare/pallas_call | solution.py:47
  1.7 4.1 %collective-permute-start.3 = (bf16[4,3072]{1,0:T(4,128)(2,1)S(1)}, bf16[4,3072]{1,0:T(4,128)(2,1)S(1)}, u32[]{:S(2)}, u32[]{:S(2)}) collective-permute-start(bf16[4,3072]{1,0:T(4,128)(2,1)S(1)} %get-tuple-element.17.after.own_ref), channel_id=1, source_target_pairs={{0,8},{2,10},{4,12},{6,14},{8,0},{10,2},{12,4},{14,6},{1,9},{3,11}... | collective-permute-start | bytes 73736 | tf_op jit(solution)/shard_map/ppermute | solution.py:26
  5.8 2.9 %load.3.after.gate_ref = bf16[3072,1024]{1,0:T(8,128)(2,1)S(1)} custom-call(bf16[1,6144,1024]{2,1,0:T(8,128)(2,1)} %source.5, bf16[4,3072]{1,0:T(4,128)(2,1)S(1)} %get-tuple-element.17.after.own_ref), custom_call_target="tpu_custom_call" | custom-call | bytes 6291456 | tf_op jit(solution)/shard_map/load/pallas_call | solution.py:47
  8.6 0.0 collective-permute-done.3.got_ref
  8.7 1.6 %collective-permute-start.4 = (bf16[8,3072]{1,0:T(8,128)(2,1)S(1)}, bf16[8,3072]{1,0:T(8,128)(2,1)S(1)}, u32[]{:S(2)}, u32[]{:S(2)}) collective-permute-start(bf16[8,3072]{1,0:T(8,128)(2,1)S(1)} %grow.3.after.own_ref), channel_id=1, source_target_pairs={{0,4},{2,6},{4,0},{6,2},{8,12},{10,14},{12,8},{14,10},{1,5},{3,7},... | collective-permute-start | bytes 147464 | tf_op jit(solution)/shard_map/ppermute | solution.py:26
  10.3 2.9 %load.4.after.up_ref = bf16[3072,1024]{1,0:T(8,128)(2,1)S(1)} custom-call(bf16[1,6144,1024]{2,1,0:T(8,128)(2,1)} %far_up.1, bf16[8,3072]{1,0:T(8,128)(2,1)S(1)} %grow.3.after.own_ref), custom_call_target="tpu_custom_call" | custom-call | bytes 6291456 | tf_op jit(solution)/shard_map/load/pallas_call | solution.py:47
  13.2 0.0 collective-permute-done.4.got_ref
  13.2 1.6 %collective-permute-start.5 = (bf16[16,3072]{1,0:T(8,128)(2,1)S(1)}, bf16[16,3072]{1,0:T(8,128)(2,1)S(1)}, u32[]{:S(2)}, u32[]{:S(2)}) collective-permute-start(bf16[16,3072]{1,0:T(8,128)(2,1)S(1)} %grow.4.after.own_ref), channel_id=1, source_target_pairs={{0,2},{2,0},{4,6},{6,4},{8,10},{10,8},{12,14},{14,12},{1,3},{3,1},... | collective-permute-start | bytes 294920 | tf_op jit(solution)/shard_map/ppermute | solution.py:26
  14.8 2.0 %collective-permute-start = (bf16[128,128]{1,0:T(8,128)(2,1)S(1)}, bf16[128,128]{1,0:T(8,128)(2,1)S(1)}, u32[]{:S(2)}, u32[]{:S(2)}) collective-permute-start(bf16[128,128]{1,0:T(8,128)(2,1)S(1)} %get-tuple-element.16), channel_id=1, source_target_pairs={{0,8},{2,10},{4,12},{6,14},{8,0},{10,2},{12,4},{14,6},{1,9},{3,11}... | collective-permute-start | bytes 98312 | tf_op jit(solution)/shard_map/ppermute | solution.py:26
  16.8 2.9 %load.5.after.gate_ref = bf16[3072,1024]{1,0:T(8,128)(2,1)S(1)} custom-call(bf16[1,6144,1024]{2,1,0:T(8,128)(2,1)} %source.5, bf16[16,3072]{1,0:T(8,128)(2,1)S(1)} %grow.4.after.own_ref), custom_call_target="tpu_custom_call" | custom-call | bytes 6291456 | tf_op jit(solution)/shard_map/load/pallas_call | solution.py:47
  19.6 0.0 collective-permute-done.5.got_ref
  19.7 0.1 collective-permute-start.6
  19.8 0.0 collective-permute-done
  19.8 0.0 copy-start.5
  19.8 0.0 copy-start.6
  19.8 1.3 %collective-permute-start.1 = (bf16[256,128]{1,0:T(8,128)(2,1)S(1)}, bf16[256,128]{1,0:T(8,128)(2,1)S(1)}, u32[]{:S(2)}, u32[]{:S(2)}) collective-permute-start(bf16[256,128]{1,0:T(8,128)(2,1)S(1)} %pad_maximum_fusion), channel_id=1, source_target_pairs={{0,4},{2,6},{4,0},{6,2},{8,12},{10,14},{12,8},{14,10},{1,5},{3,7},... | collective-permute-start | bytes 196616 | tf_op jit(solution)/shard_map/ppermute | solution.py:26
  21.1 2.9 %gate_first.1 = (f32[32,1024]{1,0:T(8,128)S(1)}, f32[32,1024]{1,0:T(8,128)S(1)}, bf16[3072,1024]{1,0:T(8,128)(2,1)S(1)}) custom-call(bf16[32,3072]{1,0:T(8,128)(2,1)S(1)} %grow.5.x_ref, bf16[3072,1024]{1,0:T(8,128)(2,1)S(1)} %load.3.after.gate_ref, bf16[3072,1024]{1,0:T(8,128)(2,1)S(1)} %load.4.after.up_ref, bf16[1,6144,1024]{2,1,0:T(8,128)(2,1)} %far_up.1), custom_call_target="tpu_custom_call" | custom-call | flops 402653184 | bytes 18874368 | tf_op jit(solution)/shard_map/gate_first/pallas_call | solution.py:47
  24.0 0.0 collective-permute-done.6.x_ref
  24.0 0.0 copy-done.5
  24.0 0.0 copy-done.6
  24.0 4.8 %gate_second.1 = (bf16[32,1024]{1,0:T(8,128)(2,1)S(1)}, bf16[32,3072]{1,0:T(8,128)(2,1)S(1)}, bf16[1024,3072]{1,0:T(8,128)(2,1)S(1)}) custom-call(bf16[32,3072]{1,0:T(8,128)(2,1)S(1)} %collective-permute-done.6.x_ref, bf16[3072,1024]{1,0:T(8,128)(2,1)S(1)} %load.5.after.gate_ref, bf16[3072,1024]{1,0:T(8,128)(2,1)S(1)} %get-tuple-element.18.up_ref, ...), custom_call_target="tpu_custom_call" | custom-call | flops 603979776 | bytes 25165824 | tf_op jit(solution)/shard_map/gate_second/pallas_call | solution.py:47
  28.8 0.0 copy-start
  28.8 0.0 copy-start.1
  28.8 0.0 copy-start.3
  28.8 0.0 copy-start.4
  28.8 0.3 collective-permute-start.7
  29.1 0.0 collective-permute-done.1
  29.1 0.6 %collective-permute-start.2 = (bf16[512,128]{1,0:T(8,128)(2,1)S(1)}, bf16[512,128]{1,0:T(8,128)(2,1)S(1)}, u32[]{:S(2)}, u32[]{:S(2)}) collective-permute-start(bf16[512,128]{1,0:T(8,128)(2,1)S(1)} %constant_dynamic-update-slice_fusion.near_ref.refs_0_), channel_id=1, source_target_pairs={{0,2},{2,0},{4,6},{6,4},{8,10},{10,8},{12,14},{14,12},{1,3},{3,1},... | collective-permute-start | bytes 393224 | tf_op jit(solution)/shard_map/ppermute | solution.py:26
  29.7 2.5 %down_first.1.terms_ref = f32[32,3072]{1,0:T(8,128)S(1)} custom-call(bf16[32,1024]{1,0:T(8,128)(2,1)S(1)} %get-tuple-element.21.hidden_ref.after, bf16[1024,3072]{1,0:T(8,128)(2,1)S(1)} %get-tuple-element.22.down_ref), custom_call_target="tpu_custom_call" | custom-call | flops 201326592 | bytes 6291456 | tf_op jit(solution)/shard_map/down_first/pallas_call | solution.py:47
  32.2 0.0 copy-start.2
  32.2 0.0 collective-permute-done.7.taken_ref
  32.2 0.1 combine.3
  32.2 1.6 %collective-permute-start.8 = (bf16[16,3072]{1,0:T(8,128)(2,1)S(1)}, bf16[16,3072]{1,0:T(8,128)(2,1)S(1)}, u32[]{:S(2)}, u32[]{:S(2)}) collective-permute-start(bf16[16,3072]{1,0:T(8,128)(2,1)S(1)} %get-tuple-element.25.after), channel_id=1, source_target_pairs={{0,2},{2,0},{4,6},{6,4},{8,10},{10,8},{12,14},{14,12},{1,3},{3,1},... | collective-permute-start | bytes 294920 | tf_op jit(solution)/shard_map/ppermute | solution.py:26
  33.8 1.1 %collective-permute-done.2.far_ref.refs_1_ = bf16[512,128]{1,0:T(8,128)(2,1)S(1)} collective-permute-done((bf16[512,128]{1,0:T(8,128)(2,1)S(1)}, bf16[512,128]{1,0:T(8,128)(2,1)S(1)}, u32[]{:S(2)}, u32[]{:S(2)}) %collective-permute-start.2) | collective-permute-done | bytes 131104 | tf_op jit(solution)/shard_map/ppermute | solution.py:26
  34.9 0.0 copy-done
  34.9 0.0 copy-done.1
  34.9 0.0 copy-done.3
  34.9 1.7 %attend.1.after.refs_7_ = f32[48,128]{1,0:T(8,128)S(1)} custom-call(bf16[512,128]{1,0:T(8,128)(2,1)S(1)} %constant_dynamic-update-slice_fusion.near_ref.refs_0_, bf16[512,128]{1,0:T(8,128)(2,1)S(1)} %collective-permute-done.2.far_ref.refs_1_, bf16[4,512,512]{2,1,0:T(8,128)(2,1)S(1)} %copy-done, bf16[4,512,512]{2,1,0:T(8,128)(2,1)S(1)} %copy-done.1, ...), custom_call_target="tpu_custom_call" | custom-call | flops 12582912 | bytes 2097152 | tf_op jit(solution)/shard_map/attend/pallas_call | solution.py:47
  36.6 0.4 collective-permute-done.8.taken_ref
  37.1 0.9 %collective-permute-start.9 = (bf16[8,3072]{1,0:T(8,128)(2,1)S(1)}, bf16[8,3072]{1,0:T(8,128)(2,1)S(1)}, u32[]{:S(2)}, u32[]{:S(2)}) collective-permute-start(bf16[8,3072]{1,0:T(8,128)(2,1)S(1)} %get-tuple-element.26.refs_6_), channel_id=1, source_target_pairs={{0,4},{2,6},{4,0},{6,2},{8,12},{10,14},{12,8},{14,10},{1,5},{3,7},... | collective-permute-start | bytes 147464 | tf_op jit(solution)/shard_map/ppermute | solution.py:26
  38.0 2.3 %attend_last.1.after = bf16[4,3072]{1,0:T(4,128)(2,1)} custom-call(bf16[512,128]{1,0:T(8,128)(2,1)S(1)} %constant_dynamic-update-slice_fusion.near_ref.refs_0_, bf16[512,128]{1,0:T(8,128)(2,1)S(1)} %collective-permute-done.2.far_ref.refs_1_, bf16[4,512,512]{2,1,0:T(8,128)(2,1)S(1)} %copy-done, bf16[4,512,512]{2,1,0:T(8,128)(2,1)S(1)} %copy-done.1, ...), custom_call_target="tpu_custom_call" | custom-call | flops 12582912 | bytes 2097152 | tf_op jit(solution)/shard_map/attend_last/pallas_call | solution.py:47
  40.3 1.0 %collective-permute-done.9.taken_ref = bf16[8,3072]{1,0:T(8,128)(2,1)S(1)} collective-permute-done((bf16[8,3072]{1,0:T(8,128)(2,1)S(1)}, bf16[8,3072]{1,0:T(8,128)(2,1)S(1)}, u32[]{:S(2)}, u32[]{:S(2)}) %collective-permute-start.9) | collective-permute-done | bytes 49184 | tf_op jit(solution)/shard_map/ppermute | solution.py:26
  41.2 1.9 %collective-permute-start.10 = (bf16[4,3072]{1,0:T(4,128)(2,1)S(1)}, bf16[4,3072]{1,0:T(4,128)(2,1)S(1)}, u32[]{:S(2)}, u32[]{:S(2)}) collective-permute-start(bf16[4,3072]{1,0:T(4,128)(2,1)S(1)} %get-tuple-element.29), channel_id=1, source_target_pairs={{0,8},{2,10},{4,12},{6,14},{8,0},{10,2},{12,4},{14,6},{1,9},{3,11}... | collective-permute-start | bytes 73736 | tf_op jit(solution)/shard_map/ppermute | solution.py:26
  43.1 2.9 %collective-permute-done.10.taken_ref = bf16[4,3072]{1,0:T(4,128)(2,1)S(1)} collective-permute-done((bf16[4,3072]{1,0:T(4,128)(2,1)S(1)}, bf16[4,3072]{1,0:T(4,128)(2,1)S(1)}, u32[]{:S(2)}, u32[]{:S(2)}) %collective-permute-start.10) | collective-permute-done | bytes 24608 | tf_op jit(solution)/shard_map/ppermute | solution.py:26
  46.0 0.0 copy-done.2
  46.1 0.1 collective-permute-start.11
  46.1 1.2 %collective-permute-done.11.other_ref = bf16[4,3072]{1,0:T(4,128)(2,1)S(1)} collective-permute-done((bf16[4,3072]{1,0:T(4,128)(2,1)S(1)}, bf16[4,3072]{1,0:T(4,128)(2,1)S(1)}, u32[]{:S(2)}, u32[]{:S(2)}) %collective-permute-start.11) | collective-permute-done | bytes 24608 | tf_op jit(solution)/shard_map/ppermute | solution.py:26
  47.3 0.6 %join.1 = bf16[4,6144]{1,0:T(4,128)(2,1)} custom-call(bf16[4,3072]{1,0:T(4,128)(2,1)S(1)} %finish.1.own_ref, bf16[4,3072]{1,0:T(4,128)(2,1)S(1)} %collective-permute-done.11.other_ref), custom_call_target="tpu_custom_call" | custom-call | bytes 49152 | tf_op jit(solution)/shard_map/join/pallas_call | solution.py:47
  (11 shorter events, 0.1 us)
Async XLA Ops:
  1.7 7.0 %collective-permute-start.3 = (bf16[4,3072]{1,0:T(4,128)(2,1)S(1)}, bf16[4,3072]{1,0:T(4,128)(2,1)S(1)}, u32[]{:S(2)}, u32[]{:S(2)}) collective-permute-start(bf16[4,3072]{1,0:T(4,128)(2,1)S(1)} %get-tuple-element.17.after.own_ref), channel_id=1, source_target_pairs={{0,8},{2,10},{4,12},{6,14},{8,0},{10,2},{12,4},{14,6},{1,9},{3,11}... | collective-permute-start | bytes 73736 | tf_op jit(solution)/shard_map/ppermute | solution.py:26
  8.7 4.5 %collective-permute-start.4 = (bf16[8,3072]{1,0:T(8,128)(2,1)S(1)}, bf16[8,3072]{1,0:T(8,128)(2,1)S(1)}, u32[]{:S(2)}, u32[]{:S(2)}) collective-permute-start(bf16[8,3072]{1,0:T(8,128)(2,1)S(1)} %grow.3.after.own_ref), channel_id=1, source_target_pairs={{0,4},{2,6},{4,0},{6,2},{8,12},{10,14},{12,8},{14,10},{1,5},{3,7},... | collective-permute-start | bytes 147464 | tf_op jit(solution)/shard_map/ppermute | solution.py:26
  13.2 6.4 %collective-permute-start.5 = (bf16[16,3072]{1,0:T(8,128)(2,1)S(1)}, bf16[16,3072]{1,0:T(8,128)(2,1)S(1)}, u32[]{:S(2)}, u32[]{:S(2)}) collective-permute-start(bf16[16,3072]{1,0:T(8,128)(2,1)S(1)} %grow.4.after.own_ref), channel_id=1, source_target_pairs={{0,2},{2,0},{4,6},{6,4},{8,10},{10,8},{12,14},{14,12},{1,3},{3,1},... | collective-permute-start | bytes 294920 | tf_op jit(solution)/shard_map/ppermute | solution.py:26
  14.8 5.0 %collective-permute-start = (bf16[128,128]{1,0:T(8,128)(2,1)S(1)}, bf16[128,128]{1,0:T(8,128)(2,1)S(1)}, u32[]{:S(2)}, u32[]{:S(2)}) collective-permute-start(bf16[128,128]{1,0:T(8,128)(2,1)S(1)} %get-tuple-element.16), channel_id=1, source_target_pairs={{0,8},{2,10},{4,12},{6,14},{8,0},{10,2},{12,4},{14,6},{1,9},{3,11}... | collective-permute-start | bytes 98312 | tf_op jit(solution)/shard_map/ppermute | solution.py:26
  19.7 4.3 %collective-permute-start.6 = (bf16[32,3072]{1,0:T(8,128)(2,1)S(1)}, bf16[32,3072]{1,0:T(8,128)(2,1)S(1)}, u32[]{:S(2)}, u32[]{:S(2)}) collective-permute-start(bf16[32,3072]{1,0:T(8,128)(2,1)S(1)} %grow.5.x_ref), channel_id=1, source_target_pairs={{0,1},{1,0},{2,3},{3,2},{4,5},{5,4},{6,7},{7,6},{8,9},{9,8},{10,11... | collective-permute-start | bytes 589832 | tf_op jit(solution)/shard_map/ppermute | solution.py:26
  19.8 4.2 %copy-start.5 = (s32[32,2]{0,1:T(2,128)S(1)}, s32[32,2]{0,1:T(2,128)}, u32[]{:S(2)}) copy-start(s32[32,2]{0,1:T(2,128)} %param.23) | copy-start | bytes 772
  19.8 4.2 %copy-start.6 = (f32[32,2]{0,1:T(2,128)S(1)}, f32[32,2]{0,1:T(2,128)}, u32[]{:S(2)}) copy-start(f32[32,2]{0,1:T(2,128)} %param.24) | copy-start | bytes 772
  19.8 9.3 %collective-permute-start.1 = (bf16[256,128]{1,0:T(8,128)(2,1)S(1)}, bf16[256,128]{1,0:T(8,128)(2,1)S(1)}, u32[]{:S(2)}, u32[]{:S(2)}) collective-permute-start(bf16[256,128]{1,0:T(8,128)(2,1)S(1)} %pad_maximum_fusion), channel_id=1, source_target_pairs={{0,4},{2,6},{4,0},{6,2},{8,12},{10,14},{12,8},{14,10},{1,5},{3,7},... | collective-permute-start | bytes 196616 | tf_op jit(solution)/shard_map/ppermute | solution.py:26
  28.8 6.1 %copy-start = (bf16[4,512,512]{2,1,0:T(8,128)(2,1)S(1)}, bf16[4,512,512]{2,1,0:T(8,128)(2,1)}, u32[]{:S(2)}) copy-start(bf16[4,512,512]{2,1,0:T(8,128)(2,1)} %refs_2_.1) | copy-start | bytes 6291460
  28.8 6.1 %copy-start.1 = (bf16[4,512,512]{2,1,0:T(8,128)(2,1)S(1)}, bf16[4,512,512]{2,1,0:T(8,128)(2,1)}, u32[]{:S(2)}) copy-start(bf16[4,512,512]{2,1,0:T(8,128)(2,1)} %refs_3_.1) | copy-start | bytes 6291460
  28.8 6.1 %copy-start.3 = (s32[4]{0:T(128)S(1)}, s32[4]{0:T(128)}, u32[]{:S(2)}) copy-start(s32[4]{0:T(128)} %refs_4_.1) | copy-start | bytes 52
  28.8 6.1 %copy-start.4 = (s32[4]{0:T(128)S(1)}, s32[4]{0:T(128)}, u32[]{:S(2)}) copy-start(s32[4]{0:T(128)} %refs_5_.1) | copy-start | bytes 52
  28.8 3.4 %collective-permute-start.7 = (bf16[32,3072]{1,0:T(8,128)(2,1)S(1)}, bf16[32,3072]{1,0:T(8,128)(2,1)S(1)}, u32[]{:S(2)}, u32[]{:S(2)}) collective-permute-start(bf16[32,3072]{1,0:T(8,128)(2,1)S(1)} %get-tuple-element.23), channel_id=1, source_target_pairs={{0,1},{1,0},{2,3},{3,2},{4,5},{5,4},{6,7},{7,6},{8,9},{9,8},{10,11... | collective-permute-start | bytes 589832 | tf_op jit(solution)/shard_map/ppermute | solution.py:26
  29.1 5.8 %collective-permute-start.2 = (bf16[512,128]{1,0:T(8,128)(2,1)S(1)}, bf16[512,128]{1,0:T(8,128)(2,1)S(1)}, u32[]{:S(2)}, u32[]{:S(2)}) collective-permute-start(bf16[512,128]{1,0:T(8,128)(2,1)S(1)} %constant_dynamic-update-slice_fusion.near_ref.refs_0_), channel_id=1, source_target_pairs={{0,2},{2,0},{4,6},{6,4},{8,10},{10,8},{12,14},{14,12},{1,3},{3,1},... | collective-permute-start | bytes 393224 | tf_op jit(solution)/shard_map/ppermute | solution.py:26
  32.2 13.9 %copy-start.2 = (bf16[4,6144]{1,0:T(4,128)(2,1)S(1)}, bf16[4,6144]{1,0:T(4,128)(2,1)}, u32[]{:S(2)}) copy-start(bf16[4,6144]{1,0:T(4,128)(2,1)} %tokens_ref.1) | copy-start | bytes 147460
  32.2 4.8 %collective-permute-start.8 = (bf16[16,3072]{1,0:T(8,128)(2,1)S(1)}, bf16[16,3072]{1,0:T(8,128)(2,1)S(1)}, u32[]{:S(2)}, u32[]{:S(2)}) collective-permute-start(bf16[16,3072]{1,0:T(8,128)(2,1)S(1)} %get-tuple-element.25.after), channel_id=1, source_target_pairs={{0,2},{2,0},{4,6},{6,4},{8,10},{10,8},{12,14},{14,12},{1,3},{3,1},... | collective-permute-start | bytes 294920 | tf_op jit(solution)/shard_map/ppermute | solution.py:26
  37.1 4.2 %collective-permute-start.9 = (bf16[8,3072]{1,0:T(8,128)(2,1)S(1)}, bf16[8,3072]{1,0:T(8,128)(2,1)S(1)}, u32[]{:S(2)}, u32[]{:S(2)}) collective-permute-start(bf16[8,3072]{1,0:T(8,128)(2,1)S(1)} %get-tuple-element.26.refs_6_), channel_id=1, source_target_pairs={{0,4},{2,6},{4,0},{6,2},{8,12},{10,14},{12,8},{14,10},{1,5},{3,7},... | collective-permute-start | bytes 147464 | tf_op jit(solution)/shard_map/ppermute | solution.py:26
  41.2 4.8 %collective-permute-start.10 = (bf16[4,3072]{1,0:T(4,128)(2,1)S(1)}, bf16[4,3072]{1,0:T(4,128)(2,1)S(1)}, u32[]{:S(2)}, u32[]{:S(2)}) collective-permute-start(bf16[4,3072]{1,0:T(4,128)(2,1)S(1)} %get-tuple-element.29), channel_id=1, source_target_pairs={{0,8},{2,10},{4,12},{6,14},{8,0},{10,2},{12,4},{14,6},{1,9},{3,11}... | collective-permute-start | bytes 73736 | tf_op jit(solution)/shard_map/ppermute | solution.py:26
  46.1 1.3 %collective-permute-start.11 = (bf16[4,3072]{1,0:T(4,128)(2,1)S(1)}, bf16[4,3072]{1,0:T(4,128)(2,1)S(1)}, u32[]{:S(2)}, u32[]{:S(2)}) collective-permute-start(bf16[4,3072]{1,0:T(4,128)(2,1)S(1)} %finish.1.own_ref), channel_id=1, source_target_pairs={{0,1},{1,0},{2,3},{3,2},{4,5},{5,4},{6,7},{7,6},{8,9},{9,8},{10,11... | collective-permute-start | bytes 73736 | tf_op jit(solution)/shard_map/ppermute | solution.py:26

commit v4 on v3

--- a/solution.py
+++ b/solution.py
@@ -14,6 +14,7 @@
 GROUP = HQ // KVH
 SCALE = HD ** (-0.5)
 TILE = 256
+WIDE_TILE = 768
 CUTS = 4
 MIB = 1024 * 1024
 
@@ -56,18 +57,6 @@
     )(*ins)
 
 
-def row_copies(source, target, sems, first):
-    rows = target.shape[0] // CUTS
-    return [
-        pltpu.make_async_copy(
-            source.at[0, pl.ds(pl.multiple_of(first + i * rows, rows), rows), :],
-            target.at[pl.ds(i * rows, rows), :],
-            sems.at[i],
-        )
-        for i in range(CUTS)
-    ]
-
-
 def column_copies(source, target, sems, first):
     columns = target.shape[1] // CUTS
     return [
@@ -78,16 +67,6 @@
         )
         for i in range(CUTS)
     ]
-
-
-def load(other, source, after, target, sems):
-    core = lax.axis_index("narrow")
-    side = 1 - core if other else core
-    copies = row_copies(source, target, sems, side * target.shape[0])
-    for copy in copies:
-        copy.start()
-    for copy in copies:
-        copy.wait()
 
 
 def shape(dims, dtype):
@@ -131,37 +110,27 @@
     heads_ref[...] = packed[...].astype(jnp.bfloat16)
 
 
-def grow(own_ref, got_ref, after, out_ref):
+def stacked(own_ref, got_ref):
     both = [own_ref[...].astype(jnp.float32), got_ref[...].astype(jnp.float32)]
-    out_ref[...] = jnp.concatenate(both, axis=0).astype(jnp.bfloat16)
-
-
-def gate_first(x_ref, gate_ref, up_ref, far_up, gate_out, up_out, up_rest, sems):
-    core = lax.axis_index("narrow")
-    copies = row_copies(far_up, up_rest, sems, (1 - core) * up_rest.shape[0])
-    for copy in copies:
-        copy.start()
-    tile = min(TILE, gate_ref.shape[1])
-
-    @pl.loop(0, gate_ref.shape[1] // tile)
-    def _(i):
-        columns = pl.ds(pl.multiple_of(i * tile, tile), tile)
-        x = x_ref[...]
-        gate_out[:, columns] = jnp.dot(x, gate_ref[:, columns], preferred_element_type=jnp.float32)
-        up_out[:, columns] = jnp.dot(x, up_ref[:, columns], preferred_element_type=jnp.float32)
-
-    for copy in copies:
-        copy.wait()
-
-
-def gate_second(
+    return jnp.concatenate(both, axis=0).astype(jnp.bfloat16)
+
+
+def grow(own_ref, got_ref, *refs):
+    refs[-1][...] = stacked(own_ref, got_ref)
+
+
+def grow_both(own_ref, got_ref, own_heads, got_heads, *refs):
+    refs[-2][...] = stacked(own_ref, got_ref)
+    refs[-1][...] = stacked(own_heads, got_heads)
+
+
+def gate_all(
     steps,
     rows,
     x_ref,
+    other_ref,
     gate_ref,
     up_ref,
-    gate_part,
-    up_part,
     routes_ref,
     logits_ref,
     far_down,
@@ -178,7 +147,9 @@
     own_copies = column_copies(far_down, down_own, sems.at[1], core * depth)
     for copy in other_copies + own_copies:
         copy.start()
-    tile = min(TILE, gate_ref.shape[1])
+    tile = min(TILE, gate_ref.shape[2])
+    own = pl.ds(pl.multiple_of(core * depth, depth), depth)
+    other = pl.ds(pl.multiple_of((1 - core) * depth, depth), depth)
 
     logits = logits_ref[...]
     first = 1.0 / (1.0 + jnp.exp(logits[1:2] - logits[0:1]))
@@ -191,16 +162,14 @@
     token = (owner_of(row >> shift, me, steps) << shift) | (row & (rows - 1))
     weight = jnp.sum(jnp.where(token == column, weight_row, 0.0), axis=1, keepdims=True)
 
-    @pl.loop(0, gate_ref.shape[1] // tile)
+    @pl.loop(0, gate_ref.shape[2] // tile)
     def _(i):
         columns = pl.ds(pl.multiple_of(i * tile, tile), tile)
-        x = x_ref[...]
-        gate = gate_part[:, columns] + jnp.dot(
-            x, gate_ref[:, columns], preferred_element_type=jnp.float32
-        )
-        up = up_part[:, columns] + jnp.dot(
-            x, up_ref[:, columns], preferred_element_type=jnp.float32
-        )
+        x, y = x_ref[...], other_ref[...]
+        gate = jnp.dot(x, gate_ref[0, own, columns], preferred_element_type=jnp.float32)
+        gate += jnp.dot(y, gate_ref[0, other, columns], preferred_element_type=jnp.float32)
+        up = jnp.dot(x, up_ref[0, own, columns], preferred_element_type=jnp.float32)
+        up += jnp.dot(y, up_ref[0, other, columns], preferred_element_type=jnp.float32)
         hidden_out[:, columns] = (weight * (gate * jax.nn.sigmoid(gate)) * up).astype(jnp.bfloat16)
 
     span = depth // CUTS
@@ -215,9 +184,9 @@
 
 
 def down_first(hidden_ref, down_ref, out_ref):
-    @pl.loop(0, out_ref.shape[1] // TILE)
+    @pl.loop(0, out_ref.shape[1] // WIDE_TILE)
     def _(i):
-        columns = pl.ds(pl.multiple_of(i * TILE, TILE), TILE)
+        columns = pl.ds(pl.multiple_of(i * WIDE_TILE, WIDE_TILE), WIDE_TILE)
         out_ref[:, columns] = jnp.dot(
             hidden_ref[...], down_ref[:, columns], preferred_element_type=jnp.float32
         )
@@ -230,21 +199,23 @@
     sent_ref[...] = total[kept:].astype(jnp.bfloat16)
 
 
-def finish(terms_ref, taken_ref, tokens_ref, out_ref):
-    half = out_ref.shape[1]
+def part_last(terms_ref, taken_ref, after, kept_ref, sent_ref):
+    total = (terms_ref[...] + taken_ref[...].astype(jnp.float32)).astype(jnp.bfloat16)
+    kept = kept_ref.shape[0]
+    kept_ref[...] = total[:kept]
+    sent_ref[...] = total[kept:]
+
+
+def finish(kept_ref, taken_ref, other_kept, other_taken, tokens_ref, out_ref):
+    half = kept_ref.shape[1]
     core = lax.axis_index("narrow")
-    own = tokens_ref[...].astype(jnp.float32)
-    own = jnp.where(core == 0, own[:, :half], own[:, half:])
-    total = terms_ref[...] + taken_ref[...].astype(jnp.float32)
-    out_ref[...] = (own + total).astype(jnp.bfloat16)
-
-
-def join(own_ref, other_ref, out_ref):
-    half = own_ref.shape[1]
-    core = lax.axis_index("narrow")
-    own, other = own_ref[...], other_ref[...]
-    out_ref[:, :half] = jnp.where(core == 0, own, other)
-    out_ref[:, half:] = jnp.where(core == 0, other, own)
+    own = kept_ref[...].astype(jnp.float32) + taken_ref[...].astype(jnp.float32)
+    other = other_kept[...].astype(jnp.float32) + other_taken[...].astype(jnp.float32)
+    tokens = tokens_ref[...].astype(jnp.float32)
+    first = tokens[:, :half] + jnp.where(core == 0, own, other)
+    second = tokens[:, half:] + jnp.where(core == 0, other, own)
+    out_ref[:, :half] = first.astype(jnp.bfloat16)
+    out_ref[:, half:] = second.astype(jnp.bfloat16)
 
 
 def attend(
@@ -367,64 +338,38 @@
             far=range(len(firsts)),
         )
 
-        def loaded(weights, other, after):
-            return call(
-                functools.partial(load, other),
-                pltpu.VMEM((half, units), bf16),
-                [distant(weights), after],
-                [dma((CUTS,))],
-                size=piece_bytes,
-                far=(0, 1),
-            )
-
-        pieces = []
-        far_heads = None
         for order, step in enumerate(steps):
-            got = swap(x, "wide", wide, step)
-            got_heads = swap(heads, "wide", wide, step)
-            if order < 3:
-                pieces.append(loaded((w_gate, w_up, w_gate)[order], order == 2, x))
-            x = call(
-                grow,
-                shape((2 * x.shape[0], half), bf16),
-                [x, got, near(pieces[-1])],
-                size=8 * x.size,
-                far=(2,),
-            )
-            if order < len(steps) - 1:
-                heads = jnp.concatenate([heads, got_heads], axis=0)
+            ins = [x, swap(x, "wide", wide, step)]
+            outs = [shape((2 * x.shape[0], half), bf16)]
+            if order > 0:
+                ins += [heads, swap(heads, "wide", wide, steps[order - 1])]
+                outs += [shape((2 * heads.shape[0], HD), bf16)]
+            far = (len(ins),)
+            ins += [distant(w_gate)]
+            if order == 0:
+                x = call(grow, outs[0], ins, size=8 * x.size, far=far)
             else:
-                far_heads = got_heads
+                x, heads = call(grow_both, outs, ins, size=8 * (x.size + heads.size), far=far)
+        far_heads = swap(heads, "wide", wide, steps[-1])
 
         product = 2 * count * half * units
         other_x = swap(x, "narrow", 2, 1)
-        part = shape((count, units), f32)
-        gate_part, up_part, up_rest = call(
-            gate_first,
-            [part, part, pltpu.VMEM((half, units), bf16)],
-            [x, near(pieces[0]), near(pieces[1]), distant(w_up)],
-            [dma((CUTS,))],
-            flops=2 * product,
-            size=3 * piece_bytes,
-            far=(3,),
-        )
         hidden, given, down_piece = call(
-            functools.partial(gate_second, steps, rows),
+            functools.partial(gate_all, steps, rows),
             [shape((count, units), bf16), shape((count, half), bf16), pltpu.VMEM((units, half), bf16)],
             [
+                x,
                 other_x,
-                near(pieces[2]),
-                near(up_rest),
-                gate_part,
-                up_part,
+                near(w_gate),
+                near(w_up),
                 routes.T,
                 route_logits.T,
                 distant(w_down),
             ],
             [pltpu.VMEM((units, half), bf16), dma((2, CUTS))],
-            flops=3 * product,
-            size=4 * piece_bytes,
-            far=(7,),
+            flops=5 * product,
+            size=6 * piece_bytes,
+            far=(6,),
         )
         taken = swap(given, "narrow", 2, 1)
         terms = call(
@@ -442,9 +387,10 @@
         after = hidden
         for order, step in enumerate(reversed(steps)):
             kept = terms.shape[0] // 2
+            last = order == len(steps) - 1
             terms, sent = call(
-                combine,
-                [shape((kept, half), f32), shape((kept, half), bf16)],
+                part_last if last else combine,
+                [shape((kept, half), bf16 if last else f32), shape((kept, half), bf16)],
                 [terms, taken, after],
                 size=terms.size * 8,
                 far=(2,),
@@ -477,9 +423,15 @@
                 )
                 after = distant(context)
 
-        piece = call(finish, shape((rows, half), bf16), [terms, taken, tokens], size=terms.size * 8)
-        other = swap(piece, "narrow", 2, 1)
-        mixed_out = call(join, shape((rows, width), bf16), [piece, other], size=terms.size * 4)
+        crossed = [(i, ((i >> 1) ^ steps[0]) * 2 + (1 - (i & 1))) for i in range(2 * wide)]
+        other_taken = lax.ppermute(sent, ("wide", "narrow"), crossed)
+        other_kept = swap(terms, "narrow", 2, 1)
+        mixed_out = call(
+            finish,
+            shape((rows, width), bf16),
+            [terms, taken, other_kept, other_taken, tokens],
+            size=terms.size * 8,
+        )
         return (context, mixed_out)
 
     return local

time: 48.1 us -> 49.4 us (1.027)
  waiting for transfers between devices: 6.59 us -> 17.4 us
  Pallas kernels: 24.5 us -> 14.1 us
  starting transfers between devices: 15.9 us -> 16.7 us
    pallas_call x17 -> x12, Pallas kernels: 24.5 us -> 14.1 us  [call(): pl.pallas_call(kernel, name=getattr(kernel, 'func', kernel).__name__, out...]
    ppermute x12, waiting for transfers between devices: 6.59 us -> 15.4 us  [swap(): return lax.ppermute(block, axis, [(i, i ^ step) for i in range(count)])]
    ppermute x0 -> x1, waiting for transfers between devices: none -> 2.04 us  [local(): other_taken = lax.ppermute(sent, ('wide', 'narrow'), crossed)]
  transfers between devices with their start and end apart: 12 -> 13, of which waited for: 5 -> 8; matrix products, arithmetic and copies ran while one was open for 0% -> 0% of each run, Pallas kernels for 47% -> 11%
where the time goes in v4:
time: 49.4 us; the launch traced here: 49.1 us
  waiting for transfers between devices  17.4 us (35%)
  starting transfers between devices  16.7 us (34%)
  Pallas kernels  14.1 us (29%)
  between operations  0.82 us (2%)
    ppermute x12, starting transfers between devices, swap(): return lax.ppermute(block, axis, [(i, i ^ step) for i in range(count)])  16.3 us
    ppermute x12, waiting for transfers between devices, swap(): return lax.ppermute(block, axis, [(i, i ^ step) for i in range(count)])  15.4 us
    pallas_call x12, Pallas kernels, call(): pl.pallas_call(kernel, name=getattr(kernel, 'func', kernel).__name__, out...  14.1 us
    ppermute x1, waiting for transfers between devices, local(): other_taken = lax.ppermute(sent, ('wide', 'narrow'), crossed)  2.04 us
  transfers between devices with their start and end apart: 13, of which 8 were waited for; matrix products, arithmetic and copies ran while one was open for 0% of the time, Pallas kernels for 11%

profile of v4, /device:TPU:0, one launch (start us, length us, event | category | flops | bytes accessed | tf_op | source)
XLA Modules:
  0.0 49.1 jit_solution(3483555739680396924)
XLA Ops:
  0.6 1.0 %prepare.1 = (bf16[4,3072]{1,0:T(4,128)(2,1)S(1)}, bf16[128,128]{1,0:T(8,128)(2,1)S(1)}) custom-call(bf16[4,6144]{1,0:T(4,128)(2,1)} %tokens_ref.1, f32[1,6144]{1,0:T(1,128)} %bitcast.7, bf16[4,3072]{1,0:T(4,128)(2,1)} %far_query.1, bf16[4,512]{1,0:T(4,128)(2,1)} %far_key.1, bf16[4,512]{1,0:T(4,128)(2,1)} %far_value.1), custom_call_target="tpu_custom_call" | custom-call | bytes 100000 | tf_op jit(solution)/shard_map/prepare/pallas_call | solution.py:48
  1.7 4.1 %collective-permute-start = (bf16[4,3072]{1,0:T(4,128)(2,1)S(1)}, bf16[4,3072]{1,0:T(4,128)(2,1)S(1)}, u32[]{:S(2)}, u32[]{:S(2)}) collective-permute-start(bf16[4,3072]{1,0:T(4,128)(2,1)S(1)} %get-tuple-element.17.own_ref), channel_id=1, source_target_pairs={{0,8},{2,10},{4,12},{6,14},{8,0},{10,2},{12,4},{14,6},{1,9},{3,11}... | collective-permute-start | bytes 73736 | tf_op jit(solution)/shard_map/ppermute | solution.py:27
  5.8 1.8 %collective-permute-done.got_ref = bf16[4,3072]{1,0:T(4,128)(2,1)S(1)} collective-permute-done((bf16[4,3072]{1,0:T(4,128)(2,1)S(1)}, bf16[4,3072]{1,0:T(4,128)(2,1)S(1)}, u32[]{:S(2)}, u32[]{:S(2)}) %collective-permute-start) | collective-permute-done | bytes 24608 | tf_op jit(solution)/shard_map/ppermute | solution.py:27
  7.6 2.0 %collective-permute-start.1 = (bf16[8,3072]{1,0:T(8,128)(2,1)S(1)}, bf16[8,3072]{1,0:T(8,128)(2,1)S(1)}, u32[]{:S(2)}, u32[]{:S(2)}) collective-permute-start(bf16[8,3072]{1,0:T(8,128)(2,1)S(1)} %grow.1.own_ref), channel_id=1, source_target_pairs={{0,4},{2,6},{4,0},{6,2},{8,12},{10,14},{12,8},{14,10},{1,5},{3,7},... | collective-permute-start | bytes 147464 | tf_op jit(solution)/shard_map/ppermute | solution.py:27
  9.6 0.0 copy-start.7
  9.6 2.8 %collective-permute-start.2 = (bf16[128,128]{1,0:T(8,128)(2,1)S(1)}, bf16[128,128]{1,0:T(8,128)(2,1)S(1)}, u32[]{:S(2)}, u32[]{:S(2)}) collective-permute-start(bf16[128,128]{1,0:T(8,128)(2,1)S(1)} %get-tuple-element.18.own_heads), channel_id=1, source_target_pairs={{0,8},{2,10},{4,12},{6,14},{8,0},{10,2},{12,4},{14,6},{1,9},{3,11}... | collective-permute-start | bytes 98312 | tf_op jit(solution)/shard_map/ppermute | solution.py:27
  12.4 2.4 %collective-permute-done.2.got_heads = bf16[128,128]{1,0:T(8,128)(2,1)S(1)} collective-permute-done((bf16[128,128]{1,0:T(8,128)(2,1)S(1)}, bf16[128,128]{1,0:T(8,128)(2,1)S(1)}, u32[]{:S(2)}, u32[]{:S(2)}) %collective-permute-start.2) | collective-permute-done | bytes 32800 | tf_op jit(solution)/shard_map/ppermute | solution.py:27
  14.8 0.0 collective-permute-done.1.got_ref
  14.8 1.6 %collective-permute-start.3 = (bf16[16,3072]{1,0:T(8,128)(2,1)S(1)}, bf16[16,3072]{1,0:T(8,128)(2,1)S(1)}, u32[]{:S(2)}, u32[]{:S(2)}) collective-permute-start(bf16[16,3072]{1,0:T(8,128)(2,1)S(1)} %get-tuple-element.19.own_ref), channel_id=1, source_target_pairs={{0,2},{2,0},{4,6},{6,4},{8,10},{10,8},{12,14},{14,12},{1,3},{3,1},... | collective-permute-start | bytes 294920 | tf_op jit(solution)/shard_map/ppermute | solution.py:27
  16.4 0.3 collective-permute-start.4
  16.8 3.9 %collective-permute-done.4.got_heads = bf16[256,128]{1,0:T(8,128)(2,1)S(1)} collective-permute-done((bf16[256,128]{1,0:T(8,128)(2,1)S(1)}, bf16[256,128]{1,0:T(8,128)(2,1)S(1)}, u32[]{:S(2)}, u32[]{:S(2)}) %collective-permute-start.4) | collective-permute-done | bytes 65568 | tf_op jit(solution)/shard_map/ppermute | solution.py:27
  20.7 0.0 collective-permute-done.3.got_ref
  20.7 0.1 collective-permute-start.6
  20.8 1.4 %collective-permute-done.6.other_ref = bf16[32,3072]{1,0:T(8,128)(2,1)S(1)} collective-permute-done((bf16[32,3072]{1,0:T(8,128)(2,1)S(1)}, bf16[32,3072]{1,0:T(8,128)(2,1)S(1)}, u32[]{:S(2)}, u32[]{:S(2)}) %collective-permute-start.6) | collective-permute-done | bytes 196640 | tf_op jit(solution)/shard_map/ppermute | solution.py:27
  22.2 0.0 slice-done
  22.2 0.0 slice-done.1
  22.2 0.0 copy-done
  22.2 0.0 copy-done.6
  22.3 0.0 copy-done.7
  22.3 0.0 slice-done.2
  22.3 0.0 copy-start.1
  22.3 0.0 copy-start.2
  22.3 0.0 copy-start.4
  22.3 0.0 copy-start.5
  22.3 6.8 %gate_all.1 = (bf16[32,1024]{1,0:T(8,128)(2,1)S(1)}, bf16[32,3072]{1,0:T(8,128)(2,1)S(1)}, bf16[1024,3072]{1,0:T(8,128)(2,1)S(1)}) custom-call(bf16[32,3072]{1,0:T(8,128)(2,1)S(1)} %get-tuple-element.22.x_ref, bf16[32,3072]{1,0:T(8,128)(2,1)S(1)} %collective-permute-done.6.other_ref, bf16[1,6144,1024]{2,1,0:T(8,128)(2,1)S(1)} %bitcast.4, ...), custom_call_target="tpu_custom_call" | custom-call | flops 1006632960 | bytes 37748736 | tf_op jit(solution)/shard_map/gate_all/pallas_call | solution.py:48
  29.1 0.0 copy-start.3
  29.1 0.2 collective-permute-start.7
  29.3 0.5 %collective-permute-start.5 = (bf16[512,128]{1,0:T(8,128)(2,1)S(1)}, bf16[512,128]{1,0:T(8,128)(2,1)S(1)}, u32[]{:S(2)}, u32[]{:S(2)}) collective-permute-start(bf16[512,128]{1,0:T(8,128)(2,1)S(1)} %get-tuple-element.21.near_ref.refs_0_), channel_id=1, source_target_pairs={{0,2},{2,0},{4,6},{6,4},{8,10},{10,8},{12,14},{14,12},{1,3},{3,1},... | collective-permute-start | bytes 393224 | tf_op jit(solution)/shard_map/ppermute | solution.py:27
  29.9 1.5 %down_first.1.terms_ref = f32[32,3072]{1,0:T(8,128)S(1)} custom-call(bf16[32,1024]{1,0:T(8,128)(2,1)S(1)} %get-tuple-element.23.hidden_ref.after, bf16[1024,3072]{1,0:T(8,128)(2,1)S(1)} %get-tuple-element.24.down_ref), custom_call_target="tpu_custom_call" | custom-call | flops 201326592 | bytes 6291456 | tf_op jit(solution)/shard_map/down_first/pallas_call | solution.py:48
  31.4 0.0 collective-permute-done.7.taken_ref
  31.5 1.6 %collective-permute-start.8 = (bf16[16,3072]{1,0:T(8,128)(2,1)S(1)}, bf16[16,3072]{1,0:T(8,128)(2,1)S(1)}, u32[]{:S(2)}, u32[]{:S(2)}) collective-permute-start(bf16[16,3072]{1,0:T(8,128)(2,1)S(1)} %get-tuple-element.27.after), channel_id=1, source_target_pairs={{0,2},{2,0},{4,6},{6,4},{8,10},{10,8},{12,14},{14,12},{1,3},{3,1},... | collective-permute-start | bytes 294920 | tf_op jit(solution)/shard_map/ppermute | solution.py:27
  33.0 2.6 %collective-permute-done.5.far_ref.refs_1_ = bf16[512,128]{1,0:T(8,128)(2,1)S(1)} collective-permute-done((bf16[512,128]{1,0:T(8,128)(2,1)S(1)}, bf16[512,128]{1,0:T(8,128)(2,1)S(1)}, u32[]{:S(2)}, u32[]{:S(2)}) %collective-permute-start.5) | collective-permute-done | bytes 131104 | tf_op jit(solution)/shard_map/ppermute | solution.py:27
  35.7 0.0 copy-done.1
  35.7 0.0 copy-done.2
  35.7 0.0 copy-done.4
  35.7 0.0 copy-done.5
  35.7 1.7 %attend.1.after.refs_7_ = f32[48,128]{1,0:T(8,128)S(1)} custom-call(bf16[512,128]{1,0:T(8,128)(2,1)S(1)} %get-tuple-element.21.near_ref.refs_0_, bf16[512,128]{1,0:T(8,128)(2,1)S(1)} %collective-permute-done.5.far_ref.refs_1_, bf16[4,512,512]{2,1,0:T(8,128)(2,1)S(1)} %copy-done.1, bf16[4,512,512]{2,1,0:T(8,128)(2,1)S(1)} %copy-done.2, s32[4]{0:T(128)S(1)} %copy-done.4, ...), custom_call_target="tpu_custom_call" | custom-call | flops 12582912 | bytes 2097152 | tf_op jit(solution)/shard_map/attend/pallas_call | solution.py:48
  37.4 0.0 collective-permute-done.8.taken_ref
  37.4 0.4 collective-permute-start.9
  37.8 2.3 %attend_last.1.after = bf16[4,3072]{1,0:T(4,128)(2,1)} custom-call(bf16[512,128]{1,0:T(8,128)(2,1)S(1)} %get-tuple-element.21.near_ref.refs_0_, bf16[512,128]{1,0:T(8,128)(2,1)S(1)} %collective-permute-done.5.far_ref.refs_1_, bf16[4,512,512]{2,1,0:T(8,128)(2,1)S(1)} %copy-done.1, bf16[4,512,512]{2,1,0:T(8,128)(2,1)S(1)} %copy-done.2, s32[4]{0:T(128)S(1)} %copy-done.4, ...), custom_call_target="tpu_custom_call" | custom-call | flops 12582912 | bytes 2097152 | tf_op jit(solution)/shard_map/attend_last/pallas_call | solution.py:48
  40.1 1.4 %collective-permute-done.9.taken_ref = bf16[8,3072]{1,0:T(8,128)(2,1)S(1)} collective-permute-done((bf16[8,3072]{1,0:T(8,128)(2,1)S(1)}, bf16[8,3072]{1,0:T(8,128)(2,1)S(1)}, u32[]{:S(2)}, u32[]{:S(2)}) %collective-permute-start.9) | collective-permute-done | bytes 49184 | tf_op jit(solution)/shard_map/ppermute | solution.py:27
  41.6 2.7 %collective-permute-start.10 = (bf16[4,3072]{1,0:T(4,128)(2,1)S(1)}, bf16[4,3072]{1,0:T(4,128)(2,1)S(1)}, u32[]{:S(2)}, u32[]{:S(2)}) collective-permute-start(bf16[4,3072]{1,0:T(4,128)(2,1)S(1)} %get-tuple-element.31), channel_id=1, source_target_pairs={{0,8},{2,10},{4,12},{6,14},{8,0},{10,2},{12,4},{14,6},{1,9},{3,11}... | collective-permute-start | bytes 73736 | tf_op jit(solution)/shard_map/ppermute | solution.py:27
  44.3 0.0 collective-permute-start.11
  44.3 0.4 collective-permute-start.12
  44.7 1.7 %collective-permute-done.10.taken_ref = bf16[4,3072]{1,0:T(4,128)(2,1)S(1)} collective-permute-done((bf16[4,3072]{1,0:T(4,128)(2,1)S(1)}, bf16[4,3072]{1,0:T(4,128)(2,1)S(1)}, u32[]{:S(2)}, u32[]{:S(2)}) %collective-permute-start.10) | collective-permute-done | bytes 24608 | tf_op jit(solution)/shard_map/ppermute | solution.py:27
  46.4 0.0 collective-permute-done.11.other_kept
  46.4 2.0 %collective-permute-done.12.other_taken = bf16[4,3072]{1,0:T(4,128)(2,1)S(1)} collective-permute-done((bf16[4,3072]{1,0:T(4,128)(2,1)S(1)}, bf16[4,3072]{1,0:T(4,128)(2,1)S(1)}, u32[]{:S(2)}, u32[]{:S(2)}) %collective-permute-start.12) | collective-permute-done | bytes 24608 | tf_op jit(solution)/shard_map/ppermute | solution.py:427
  48.5 0.7 %finish.1 = bf16[4,6144]{1,0:T(4,128)(2,1)} custom-call(bf16[4,3072]{1,0:T(4,128)(2,1)S(1)} %get-tuple-element.30.kept_ref, bf16[4,3072]{1,0:T(4,128)(2,1)S(1)} %collective-permute-done.10.taken_ref, bf16[4,3072]{1,0:T(4,128)(2,1)S(1)} %collective-permute-done.11.other_kept, bf16[4,3072]{1,0:T(4,128)(2,1)S(1)} %collective-permute-done.12.other_taken, ...), custom_call_target="tpu_custom_call" | custom-call | bytes 98304 | tf_op jit(solution)/shard_map/finish/pallas_call | solution.py:48
  (13 shorter events, 0.2 us)
Async XLA Ops:
  1.7 5.9 %collective-permute-start = (bf16[4,3072]{1,0:T(4,128)(2,1)S(1)}, bf16[4,3072]{1,0:T(4,128)(2,1)S(1)}, u32[]{:S(2)}, u32[]{:S(2)}) collective-permute-start(bf16[4,3072]{1,0:T(4,128)(2,1)S(1)} %get-tuple-element.17.own_ref), channel_id=1, source_target_pairs={{0,8},{2,10},{4,12},{6,14},{8,0},{10,2},{12,4},{14,6},{1,9},{3,11}... | collective-permute-start | bytes 73736 | tf_op jit(solution)/shard_map/ppermute | solution.py:27
  7.6 7.2 %collective-permute-start.1 = (bf16[8,3072]{1,0:T(8,128)(2,1)S(1)}, bf16[8,3072]{1,0:T(8,128)(2,1)S(1)}, u32[]{:S(2)}, u32[]{:S(2)}) collective-permute-start(bf16[8,3072]{1,0:T(8,128)(2,1)S(1)} %grow.1.own_ref), channel_id=1, source_target_pairs={{0,4},{2,6},{4,0},{6,2},{8,12},{10,14},{12,8},{14,10},{1,5},{3,7},... | collective-permute-start | bytes 147464 | tf_op jit(solution)/shard_map/ppermute | solution.py:27
  9.6 12.7 %slice-start = ((s8[12582912]{0:T(1024)(128)(4,1)}), s8[4194304]{0:T(1024)(128)(4,1)S(1)}, s32[]{:S(2)}) async-start(s8[12582912]{0:T(1024)(128)(4,1)} %bitcast.3), calls=%async_computation | async-start | bytes 8388608
  9.6 12.7 %slice-start.1 = ((s8[12582912]{0:T(1024)(128)(4,1)}), s8[4194304]{0:T(1024)(128)(4,1)S(1)}, s32[]{:S(2)}) async-start(s8[12582912]{0:T(1024)(128)(4,1)} %bitcast.3), calls=%async_computation.1 | async-start | bytes 8388608
  9.6 12.7 %copy-start = (bf16[1,6144,1024]{2,1,0:T(8,128)(2,1)S(1)}, bf16[1,6144,1024]{2,1,0:T(8,128)(2,1)}, u32[]{:S(2)}) copy-start(bf16[1,6144,1024]{2,1,0:T(8,128)(2,1)} %up_ref.1) | copy-start | bytes 37748740
  9.6 12.7 %copy-start.6 = (s32[32,2]{0,1:T(2,128)S(1)}, s32[32,2]{0,1:T(2,128)}, u32[]{:S(2)}) copy-start(s32[32,2]{0,1:T(2,128)} %param.23) | copy-start | bytes 772
  9.6 12.7 %copy-start.7 = (f32[32,2]{0,1:T(2,128)S(1)}, f32[32,2]{0,1:T(2,128)}, u32[]{:S(2)}) copy-start(f32[32,2]{0,1:T(2,128)} %param.24) | copy-start | bytes 772
  9.6 5.2 %collective-permute-start.2 = (bf16[128,128]{1,0:T(8,128)(2,1)S(1)}, bf16[128,128]{1,0:T(8,128)(2,1)S(1)}, u32[]{:S(2)}, u32[]{:S(2)}) collective-permute-start(bf16[128,128]{1,0:T(8,128)(2,1)S(1)} %get-tuple-element.18.own_heads), channel_id=1, source_target_pairs={{0,8},{2,10},{4,12},{6,14},{8,0},{10,2},{12,4},{14,6},{1,9},{3,11}... | collective-permute-start | bytes 98312 | tf_op jit(solution)/shard_map/ppermute | solution.py:27
  14.8 5.9 %collective-permute-start.3 = (bf16[16,3072]{1,0:T(8,128)(2,1)S(1)}, bf16[16,3072]{1,0:T(8,128)(2,1)S(1)}, u32[]{:S(2)}, u32[]{:S(2)}) collective-permute-start(bf16[16,3072]{1,0:T(8,128)(2,1)S(1)} %get-tuple-element.19.own_ref), channel_id=1, source_target_pairs={{0,2},{2,0},{4,6},{6,4},{8,10},{10,8},{12,14},{14,12},{1,3},{3,1},... | collective-permute-start | bytes 294920 | tf_op jit(solution)/shard_map/ppermute | solution.py:27
  16.4 5.9 %slice-start.2 = ((s8[12582912]{0:T(1024)(128)(4,1)}), s8[4194304]{0:T(1024)(128)(4,1)S(1)}, s32[]{:S(2)}) async-start(s8[12582912]{0:T(1024)(128)(4,1)} %bitcast.3), calls=%async_computation.2 | async-start | bytes 8388608
  16.4 4.3 %collective-permute-start.4 = (bf16[256,128]{1,0:T(8,128)(2,1)S(1)}, bf16[256,128]{1,0:T(8,128)(2,1)S(1)}, u32[]{:S(2)}, u32[]{:S(2)}) collective-permute-start(bf16[256,128]{1,0:T(8,128)(2,1)S(1)} %get-tuple-element.20.own_heads), channel_id=1, source_target_pairs={{0,4},{2,6},{4,0},{6,2},{8,12},{10,14},{12,8},{14,10},{1,5},{3,7},... | collective-permute-start | bytes 196616 | tf_op jit(solution)/shard_map/ppermute | solution.py:27
  20.7 1.5 %collective-permute-start.6 = (bf16[32,3072]{1,0:T(8,128)(2,1)S(1)}, bf16[32,3072]{1,0:T(8,128)(2,1)S(1)}, u32[]{:S(2)}, u32[]{:S(2)}) collective-permute-start(bf16[32,3072]{1,0:T(8,128)(2,1)S(1)} %get-tuple-element.22.x_ref), channel_id=1, source_target_pairs={{0,1},{1,0},{2,3},{3,2},{4,5},{5,4},{6,7},{7,6},{8,9},{9,8},{10,11... | collective-permute-start | bytes 589832 | tf_op jit(solution)/shard_map/ppermute | solution.py:27
  22.3 13.4 %copy-start.1 = (bf16[4,512,512]{2,1,0:T(8,128)(2,1)S(1)}, bf16[4,512,512]{2,1,0:T(8,128)(2,1)}, u32[]{:S(2)}) copy-start(bf16[4,512,512]{2,1,0:T(8,128)(2,1)} %refs_2_.1) | copy-start | bytes 6291460
  22.3 13.4 %copy-start.2 = (bf16[4,512,512]{2,1,0:T(8,128)(2,1)S(1)}, bf16[4,512,512]{2,1,0:T(8,128)(2,1)}, u32[]{:S(2)}) copy-start(bf16[4,512,512]{2,1,0:T(8,128)(2,1)} %refs_3_.1) | copy-start | bytes 6291460
  22.3 13.4 %copy-start.4 = (s32[4]{0:T(128)S(1)}, s32[4]{0:T(128)}, u32[]{:S(2)}) copy-start(s32[4]{0:T(128)} %refs_4_.1) | copy-start | bytes 52
  22.3 13.4 %copy-start.5 = (s32[4]{0:T(128)S(1)}, s32[4]{0:T(128)}, u32[]{:S(2)}) copy-start(s32[4]{0:T(128)} %refs_5_.1) | copy-start | bytes 52
  29.1 19.3 %copy-start.3 = (bf16[4,6144]{1,0:T(4,128)(2,1)S(1)}, bf16[4,6144]{1,0:T(4,128)(2,1)}, u32[]{:S(2)}) copy-start(bf16[4,6144]{1,0:T(4,128)(2,1)} %tokens_ref.1) | copy-start | bytes 147460
  29.1 2.2 %collective-permute-start.7 = (bf16[32,3072]{1,0:T(8,128)(2,1)S(1)}, bf16[32,3072]{1,0:T(8,128)(2,1)S(1)}, u32[]{:S(2)}, u32[]{:S(2)}) collective-permute-start(bf16[32,3072]{1,0:T(8,128)(2,1)S(1)} %get-tuple-element.25), channel_id=1, source_target_pairs={{0,1},{1,0},{2,3},{3,2},{4,5},{5,4},{6,7},{7,6},{8,9},{9,8},{10,11... | collective-permute-start | bytes 589832 | tf_op jit(solution)/shard_map/ppermute | solution.py:27
  29.3 6.3 %collective-permute-start.5 = (bf16[512,128]{1,0:T(8,128)(2,1)S(1)}, bf16[512,128]{1,0:T(8,128)(2,1)S(1)}, u32[]{:S(2)}, u32[]{:S(2)}) collective-permute-start(bf16[512,128]{1,0:T(8,128)(2,1)S(1)} %get-tuple-element.21.near_ref.refs_0_), channel_id=1, source_target_pairs={{0,2},{2,0},{4,6},{6,4},{8,10},{10,8},{12,14},{14,12},{1,3},{3,1},... | collective-permute-start | bytes 393224 | tf_op jit(solution)/shard_map/ppermute | solution.py:27
  31.5 5.9 %collective-permute-start.8 = (bf16[16,3072]{1,0:T(8,128)(2,1)S(1)}, bf16[16,3072]{1,0:T(8,128)(2,1)S(1)}, u32[]{:S(2)}, u32[]{:S(2)}) collective-permute-start(bf16[16,3072]{1,0:T(8,128)(2,1)S(1)} %get-tuple-element.27.after), channel_id=1, source_target_pairs={{0,2},{2,0},{4,6},{6,4},{8,10},{10,8},{12,14},{14,12},{1,3},{3,1},... | collective-permute-start | bytes 294920 | tf_op jit(solution)/shard_map/ppermute | solution.py:27
  37.4 4.2 %collective-permute-start.9 = (bf16[8,3072]{1,0:T(8,128)(2,1)S(1)}, bf16[8,3072]{1,0:T(8,128)(2,1)S(1)}, u32[]{:S(2)}, u32[]{:S(2)}) collective-permute-start(bf16[8,3072]{1,0:T(8,128)(2,1)S(1)} %get-tuple-element.28.refs_6_), channel_id=1, source_target_pairs={{0,4},{2,6},{4,0},{6,2},{8,12},{10,14},{12,8},{14,10},{1,5},{3,7},... | collective-permute-start | bytes 147464 | tf_op jit(solution)/shard_map/ppermute | solution.py:27
  41.6 4.8 %collective-permute-start.10 = (bf16[4,3072]{1,0:T(4,128)(2,1)S(1)}, bf16[4,3072]{1,0:T(4,128)(2,1)S(1)}, u32[]{:S(2)}, u32[]{:S(2)}) collective-permute-start(bf16[4,3072]{1,0:T(4,128)(2,1)S(1)} %get-tuple-element.31), channel_id=1, source_target_pairs={{0,8},{2,10},{4,12},{6,14},{8,0},{10,2},{12,4},{14,6},{1,9},{3,11}... | collective-permute-start | bytes 73736 | tf_op jit(solution)/shard_map/ppermute | solution.py:27
  44.3 2.1 %collective-permute-start.11 = (bf16[4,3072]{1,0:T(4,128)(2,1)S(1)}, bf16[4,3072]{1,0:T(4,128)(2,1)S(1)}, u32[]{:S(2)}, u32[]{:S(2)}) collective-permute-start(bf16[4,3072]{1,0:T(4,128)(2,1)S(1)} %get-tuple-element.30.kept_ref), channel_id=1, source_target_pairs={{0,1},{1,0},{2,3},{3,2},{4,5},{5,4},{6,7},{7,6},{8,9},{9,8},{10,11... | collective-permute-start | bytes 73736 | tf_op jit(solution)/shard_map/ppermute | solution.py:27
  44.3 4.2 %collective-permute-start.12 = (bf16[4,3072]{1,0:T(4,128)(2,1)S(1)}, bf16[4,3072]{1,0:T(4,128)(2,1)S(1)}, u32[]{:S(2)}, u32[]{:S(2)}) collective-permute-start(bf16[4,3072]{1,0:T(4,128)(2,1)S(1)} %get-tuple-element.31), channel_id=1, source_target_pairs={{0,9},{1,8},{2,11},{3,10},{4,13},{5,12},{6,15},{7,14},{8,1},{9,0},... | collective-permute-start | bytes 73736 | tf_op jit(solution)/shard_map/ppermute | solution.py:427

commit v5 on v4

--- a/solution.py
+++ b/solution.py
@@ -43,7 +43,7 @@
     return found
 
 
-def call(kernel, outs, ins, scratch=(), flops=0, size=0, limit=16, smem=(), far=()):
+def call(kernel, outs, ins, scratch=(), flops=0, size=0, limit=4, smem=(), far=()):
     spaces = [pltpu.SMEM if i in smem else pl.ANY if i in far else pltpu.VMEM for i in range(len(ins))]
     return pl.pallas_call(
         kernel,
@@ -81,7 +81,7 @@
     return pltpu.with_memory_space_constraint(array, pltpu.HBM)
 
 
-def prepare(far_tokens, far_gain, far_query, far_key, far_value, out_ref, heads_ref, *held):
+def prepare(far_tokens, far_gain, far_query, far_key, far_value, out_ref, both_ref, *held):
     *near_refs, packed, sems = held
     far_refs = (far_tokens, far_gain, far_query, far_key, far_value)
     copies = [
@@ -93,64 +93,63 @@
     for copy in copies:
         copy.wait()
     tokens_ref, gain_ref, *head_refs = near_refs
-    half = out_ref.shape[1]
+    rows, half = out_ref.shape
     core = lax.axis_index("narrow")
     values = tokens_ref[...].astype(jnp.float32)
     scale = lax.rsqrt(jnp.mean(values * values, axis=-1, keepdims=True) + 1e-05)
-    normed = (values * scale * gain_ref[...]).astype(jnp.bfloat16)
-    out_ref[...] = jnp.where(core == 0, normed[:, :half], normed[:, half:])
-    rows = tokens_ref.shape[0]
-    at = 0
-    each = heads_ref.shape[0] // rows
+    normed = values * scale * gain_ref[...]
+    normed = jnp.where(core == 0, normed[:, :half], normed[:, half:])
+    out_ref[...] = normed.astype(jnp.bfloat16)
+    pieces = half // HD
+    for piece in range(pieces):
+        packed[pl.ds(piece, rows, stride=pieces), :] = normed[:, piece * HD : (piece + 1) * HD]
+    at = rows * pieces
+    each = (both_ref.shape[0] - at) // rows
     for ref in head_refs:
         block = ref[...].astype(jnp.float32)
         for head in range(ref.shape[1] // HD):
             packed[pl.ds(at, rows, stride=each), :] = block[:, head * HD : (head + 1) * HD]
             at += 1
-    heads_ref[...] = packed[...].astype(jnp.bfloat16)
-
-
-def stacked(own_ref, got_ref):
-    both = [own_ref[...].astype(jnp.float32), got_ref[...].astype(jnp.float32)]
-    return jnp.concatenate(both, axis=0).astype(jnp.bfloat16)
-
-
-def grow(own_ref, got_ref, *refs):
-    refs[-1][...] = stacked(own_ref, got_ref)
+    both_ref[...] = packed[...].astype(jnp.bfloat16)
+
+
+def stacked(refs):
+    return jnp.concatenate([ref[...].astype(jnp.float32) for ref in refs], axis=0)
+
+
+def gather_line(own_ref, far_both, next_ref, last_ref, own_both, *refs):
+    *_, out_ref, heads_ref, packed = refs
+    rows, half = own_ref.shape
+    pieces = half // HD
+    tokens = rows * pieces
+    packed[...] = far_both[:tokens, :].astype(jnp.float32)
+    far = [packed[pl.ds(piece, rows, stride=pieces), :] for piece in range(pieces)]
+    far = jnp.concatenate(far, axis=1)
+    own, near_rows, last = (r[...].astype(jnp.float32) for r in (own_ref, next_ref, last_ref))
+    out_ref[...] = jnp.concatenate([own, far, near_rows, last], axis=0).astype(jnp.bfloat16)
+    count = heads_ref.shape[0] // 2
+    heads_ref[:count, :] = own_both[tokens:, :]
+    heads_ref[count:, :] = far_both[tokens:, :]
 
 
 def grow_both(own_ref, got_ref, own_heads, got_heads, *refs):
-    refs[-2][...] = stacked(own_ref, got_ref)
-    refs[-1][...] = stacked(own_heads, got_heads)
-
-
-def gate_all(
-    steps,
-    rows,
-    x_ref,
-    other_ref,
-    gate_ref,
-    up_ref,
-    routes_ref,
-    logits_ref,
-    far_down,
-    hidden_out,
-    given_out,
-    down_own,
-    down_other,
-    sems,
-):
-    count, depth = x_ref.shape
+    refs[-2][...] = stacked([own_ref, got_ref]).astype(jnp.bfloat16)
+    refs[-1][...] = stacked([own_heads, got_heads]).astype(jnp.bfloat16)
+
+
+def shares(steps, rows, far_routes, far_logits, *refs):
+    *_, out_ref, routes_ref, logits_ref, sems = refs
+    copies = [
+        pltpu.make_async_copy(far_routes, routes_ref, sems.at[0]),
+        pltpu.make_async_copy(far_logits, logits_ref, sems.at[1]),
+    ]
+    for copy in copies:
+        copy.start()
+    for copy in copies:
+        copy.wait()
+    count = out_ref.shape[0]
     core = lax.axis_index("narrow")
     me = lax.axis_index("wide")
-    other_copies = column_copies(far_down, down_other, sems.at[0], (1 - core) * depth)
-    own_copies = column_copies(far_down, down_own, sems.at[1], core * depth)
-    for copy in other_copies + own_copies:
-        copy.start()
-    tile = min(TILE, gate_ref.shape[2])
-    own = pl.ds(pl.multiple_of(core * depth, depth), depth)
-    other = pl.ds(pl.multiple_of((1 - core) * depth, depth), depth)
-
     logits = logits_ref[...]
     first = 1.0 / (1.0 + jnp.exp(logits[1:2] - logits[0:1]))
     second = 1.0 - first
@@ -161,6 +160,32 @@
     shift = int(math.log2(rows))
     token = (owner_of(row >> shift, me, steps) << shift) | (row & (rows - 1))
     weight = jnp.sum(jnp.where(token == column, weight_row, 0.0), axis=1, keepdims=True)
+    out_ref[...] = jnp.broadcast_to(weight, out_ref.shape)
+
+
+def gate_all(
+    x_ref,
+    other_ref,
+    gate_ref,
+    up_ref,
+    share_ref,
+    far_down,
+    hidden_out,
+    down_own,
+    down_other,
+    sems,
+):
+    count, depth = x_ref.shape
+    core = lax.axis_index("narrow")
+    other_copies = column_copies(far_down, down_other, sems.at[0], (1 - core) * depth)
+    own_copies = column_copies(far_down, down_own, sems.at[1], core * depth)
+    for copy in other_copies + own_copies:
+        copy.start()
+    tile = min(TILE, gate_ref.shape[2])
+    own = pl.ds(pl.multiple_of(core * depth, depth), depth)
+    other = pl.ds(pl.multiple_of((1 - core) * depth, depth), depth)
+
+    weight = share_ref[:, 0:1]
 
     @pl.loop(0, gate_ref.shape[2] // tile)
     def _(i):
@@ -172,24 +197,17 @@
         up += jnp.dot(y, up_ref[0, other, columns], preferred_element_type=jnp.float32)
         hidden_out[:, columns] = (weight * (gate * jax.nn.sigmoid(gate)) * up).astype(jnp.bfloat16)
 
-    span = depth // CUTS
-    for cut, copy in enumerate(other_copies):
+    for copy in other_copies + own_copies:
         copy.wait()
-        columns = slice(cut * span, (cut + 1) * span)
-        given_out[:, columns] = jnp.dot(
-            hidden_out[...], down_other[:, columns], preferred_element_type=jnp.float32
-        ).astype(jnp.bfloat16)
-    for copy in own_copies:
-        copy.wait()
-
-
-def down_first(hidden_ref, down_ref, out_ref):
+
+
+def down(hidden_ref, down_ref, after, out_ref):
     @pl.loop(0, out_ref.shape[1] // WIDE_TILE)
     def _(i):
         columns = pl.ds(pl.multiple_of(i * WIDE_TILE, WIDE_TILE), WIDE_TILE)
         out_ref[:, columns] = jnp.dot(
             hidden_ref[...], down_ref[:, columns], preferred_element_type=jnp.float32
-        )
+        ).astype(out_ref.dtype)
 
 
 def combine(terms_ref, taken_ref, after, kept_ref, sent_ref):
@@ -199,23 +217,31 @@
     sent_ref[...] = total[kept:].astype(jnp.bfloat16)
 
 
-def part_last(terms_ref, taken_ref, after, kept_ref, sent_ref):
-    total = (terms_ref[...] + taken_ref[...].astype(jnp.float32)).astype(jnp.bfloat16)
-    kept = kept_ref.shape[0]
-    kept_ref[...] = total[:kept]
-    sent_ref[...] = total[kept:]
-
-
-def finish(kept_ref, taken_ref, other_kept, other_taken, tokens_ref, out_ref):
+def part_line(terms_ref, taken_ref, after, kept_ref, far_ref, next_ref, last_ref):
+    total = terms_ref[...] + taken_ref[...].astype(jnp.float32)
+    rows = kept_ref.shape[0]
+    kept_ref[...] = total[:rows]
+    for i, ref in enumerate((far_ref, next_ref, last_ref)):
+        ref[...] = total[(i + 1) * rows : (i + 2) * rows].astype(jnp.bfloat16)
+
+
+def finish(kept_ref, far_ref, next_ref, last_ref, tokens_ref, after, out_ref):
     half = kept_ref.shape[1]
     core = lax.axis_index("narrow")
-    own = kept_ref[...].astype(jnp.float32) + taken_ref[...].astype(jnp.float32)
-    other = other_kept[...].astype(jnp.float32) + other_taken[...].astype(jnp.float32)
-    tokens = tokens_ref[...].astype(jnp.float32)
-    first = tokens[:, :half] + jnp.where(core == 0, own, other)
-    second = tokens[:, half:] + jnp.where(core == 0, other, own)
-    out_ref[:, :half] = first.astype(jnp.bfloat16)
-    out_ref[:, half:] = second.astype(jnp.bfloat16)
+    own = tokens_ref[...].astype(jnp.float32)
+    own = jnp.where(core == 0, own[:, :half], own[:, half:])
+    total = kept_ref[...]
+    for ref in (far_ref, next_ref, last_ref):
+        total = total + ref[...].astype(jnp.float32)
+    out_ref[...] = (own + total).astype(jnp.bfloat16)
+
+
+def join(own_ref, other_ref, out_ref):
+    half = own_ref.shape[1]
+    core = lax.axis_index("narrow")
+    own, other = own_ref[...], other_ref[...]
+    out_ref[:, :half] = jnp.where(core == 0, own, other)
+    out_ref[:, half:] = jnp.where(core == 0, other, own)
 
 
 def attend(
@@ -328,78 +354,109 @@
         piece_bytes = 2 * half * units
 
         firsts = [tokens, norm_gain[None], queries, new_keys, new_values]
-        x, heads = call(
+        both_rows = rows * (half // HD + each)
+        weights = [distant(w_gate), distant(w_up)]
+        x, both = call(
             prepare,
-            [shape((rows, half), bf16), shape((rows * each, HD), bf16)],
+            [shape((rows, half), bf16), shape((both_rows, HD), bf16)],
             [distant(a) for a in firsts],
             [pltpu.VMEM(a.shape, a.dtype) for a in firsts]
-            + [pltpu.VMEM((rows * each, HD), f32), dma((len(firsts),))],
+            + [pltpu.VMEM((both_rows, HD), f32), dma((len(firsts),))],
             size=100000,
             far=range(len(firsts)),
         )
-
-        for order, step in enumerate(steps):
+        line = [swap(both, "wide", wide, steps[0])]
+        line += [swap(x, "wide", wide, step) for step in (steps[1], steps[0] ^ steps[1])]
+        share = call(
+            functools.partial(shares, steps, rows),
+            shape((count, HD), f32),
+            [distant(routes.T), distant(route_logits.T), x, *weights],
+            [
+                pltpu.VMEM(routes.T.shape, jnp.int32),
+                pltpu.VMEM(route_logits.T.shape, f32),
+                dma((2,)),
+            ],
+            size=100000,
+            far=range(5),
+        )
+        x, heads = call(
+            gather_line,
+            [shape((4 * rows, half), bf16), shape((2 * rows * each, HD), bf16)],
+            [
+                x,
+                *line,
+                both,
+                share,
+                *weights,
+            ],
+            [pltpu.VMEM((rows * half // HD, HD), f32)],
+            size=100000,
+            far=(5, 6, 7),
+        )
+        for order, step in enumerate(steps[2:]):
             ins = [x, swap(x, "wide", wide, step)]
-            outs = [shape((2 * x.shape[0], half), bf16)]
-            if order > 0:
-                ins += [heads, swap(heads, "wide", wide, steps[order - 1])]
-                outs += [shape((2 * heads.shape[0], HD), bf16)]
-            far = (len(ins),)
-            ins += [distant(w_gate)]
-            if order == 0:
-                x = call(grow, outs[0], ins, size=8 * x.size, far=far)
-            else:
-                x, heads = call(grow_both, outs, ins, size=8 * (x.size + heads.size), far=far)
+            ins += [heads, swap(heads, "wide", wide, steps[order + 1])]
+            outs = [shape((2 * x.shape[0], half), bf16), shape((2 * heads.shape[0], HD), bf16)]
+            x, heads = call(grow_both, outs, ins, size=8 * (x.size + heads.size))
         far_heads = swap(heads, "wide", wide, steps[-1])
 
         product = 2 * count * half * units
         other_x = swap(x, "narrow", 2, 1)
-        hidden, given, down_piece = call(
-            functools.partial(gate_all, steps, rows),
-            [shape((count, units), bf16), shape((count, half), bf16), pltpu.VMEM((units, half), bf16)],
+        whole = pltpu.VMEM((units, half), bf16)
+        hidden, down_own, down_other = call(
+            gate_all,
+            [shape((count, units), bf16), whole, whole],
             [
                 x,
                 other_x,
                 near(w_gate),
                 near(w_up),
-                routes.T,
-                route_logits.T,
+                share,
                 distant(w_down),
             ],
-            [pltpu.VMEM((units, half), bf16), dma((2, CUTS))],
-            flops=5 * product,
+            [dma((2, CUTS))],
+            flops=4 * product,
             size=6 * piece_bytes,
-            far=(6,),
+            far=(5,),
+        )
+        given = call(
+            down,
+            shape((count, half), bf16),
+            [hidden, near(down_other), far_heads],
+            flops=product,
+            size=piece_bytes,
+            far=(2,),
         )
         taken = swap(given, "narrow", 2, 1)
         terms = call(
-            down_first,
+            down,
             shape((count, half), f32),
-            [hidden, near(down_piece)],
+            [hidden, near(down_own), given],
             flops=product,
             size=piece_bytes,
+            far=(2,),
         )
 
         caches = [near(key_cache), near(value_cache), lengths, assignment]
         slots = queries.shape[0]
+        early_slots = list(range(slots - 1))
+        late_slots = list(range(slots - 1, slots))
         early = None
-        context = None
         after = hidden
-        for order, step in enumerate(reversed(steps)):
+        for step in reversed(steps[2:]):
             kept = terms.shape[0] // 2
-            last = order == len(steps) - 1
             terms, sent = call(
-                part_last if last else combine,
-                [shape((kept, half), bf16 if last else f32), shape((kept, half), bf16)],
+                combine,
+                [shape((kept, half), f32), shape((kept, half), bf16)],
                 [terms, taken, after],
                 size=terms.size * 8,
                 far=(2,),
             )
             taken = swap(sent, "wide", wide, step)
-            if order == 0:
+            if early is None:
                 early = call(
-                    functools.partial(attend, steps, list(range(slots // 2))),
-                    shape((slots // 2 * heads_local, HD), f32),
+                    functools.partial(attend, steps, early_slots),
+                    shape((len(early_slots) * heads_local, HD), f32),
                     [heads, far_heads, *caches, sent],
                     flops=2 * key_cache.size * GROUP,
                     size=2 * key_cache.size,
@@ -407,31 +464,37 @@
                     far=(6,),
                 )
                 after = early
-            elif order == 1:
-                context = call(
-                    functools.partial(attend_last, steps, list(range(slots // 2, slots)), heads_local),
-                    shape(queries.shape, bf16),
-                    [heads, far_heads, *caches, sent, early],
-                    [
-                        pltpu.VMEM(((slots - slots // 2) * heads_local, HD), f32),
-                        pltpu.VMEM((slots * heads_local, HD), f32),
-                    ],
-                    flops=2 * key_cache.size * GROUP,
-                    size=2 * key_cache.size,
-                    smem=(4, 5),
-                    far=(6,),
-                )
-                after = distant(context)
-
-        crossed = [(i, ((i >> 1) ^ steps[0]) * 2 + (1 - (i & 1))) for i in range(2 * wide)]
-        other_taken = lax.ppermute(sent, ("wide", "narrow"), crossed)
-        other_kept = swap(terms, "narrow", 2, 1)
-        mixed_out = call(
-            finish,
-            shape((rows, width), bf16),
-            [terms, taken, other_kept, other_taken, tokens],
+        block = shape((rows, half), bf16)
+        terms, far_sent, next_sent, last_sent = call(
+            part_line,
+            [shape((rows, half), f32), block, block, block],
+            [terms, taken, after],
             size=terms.size * 8,
-        )
+            far=(2,),
+        )
+        got = [
+            swap(far_sent, "wide", wide, steps[0]),
+            swap(next_sent, "wide", wide, steps[1]),
+            swap(last_sent, "wide", wide, steps[0] ^ steps[1]),
+        ]
+        context = call(
+            functools.partial(attend_last, steps, late_slots, heads_local),
+            shape(queries.shape, bf16),
+            [heads, far_heads, *caches, next_sent, early],
+            [
+                pltpu.VMEM((len(late_slots) * heads_local, HD), f32),
+                pltpu.VMEM((slots * heads_local, HD), f32),
+            ],
+            flops=2 * key_cache.size * GROUP,
+            size=2 * key_cache.size,
+            smem=(4, 5),
+            far=(6,),
+        )
+        piece = call(
+            finish, block, [terms, *got, tokens, distant(context)], size=terms.size * 8, far=(5,)
+        )
+        other = swap(piece, "narrow", 2, 1)
+        mixed_out = call(join, shape((rows, width), bf16), [piece, other], size=terms.size * 4)
         return (context, mixed_out)
 
     return local

time: 49.4 us -> 42.4 us (0.86)
  starting transfers between devices: 16.7 us -> 12.4 us
  waiting for transfers between devices: 17.4 us -> 14 us
  Pallas kernels: 14.1 us -> 14.8 us
    ppermute x12 -> x13, starting transfers between devices: 16.3 us -> 12.4 us  [swap(): return lax.ppermute(block, axis, [(i, i ^ step) for i in range(count)])]
    ppermute x1 -> x0, waiting for transfers between devices: 2.04 us -> none  [local(): other_taken = lax.ppermute(sent, ('wide', 'narrow'), crossed)]
    ppermute x12 -> x13, waiting for transfers between devices: 15.4 us -> 14 us  [swap(): return lax.ppermute(block, axis, [(i, i ^ step) for i in range(count)])]
    pallas_call x12 -> x13, Pallas kernels: 14.1 us -> 14.8 us  [call(): pl.pallas_call(kernel, name=getattr(kernel, 'func', kernel).__name__, out...]
  transfers between devices with their start and end apart: 13 -> 13, of which waited for: 8 -> 8; matrix products, arithmetic and copies ran while one was open for 0% -> 0% of each run, Pallas kernels for 11% -> 27%
where the time goes in v5:
time: 42.4 us; the launch traced here: 42.2 us
  Pallas kernels  14.8 us (35%)
  waiting for transfers between devices  14 us (33%)
  starting transfers between devices  12.4 us (29%)
  between operations  0.85 us (2%)
    pallas_call x13, Pallas kernels, call(): pl.pallas_call(kernel, name=getattr(kernel, 'func', kernel).__name__, out...  14.8 us
    ppermute x13, waiting for transfers between devices, swap(): return lax.ppermute(block, axis, [(i, i ^ step) for i in range(count)])  14 us
    ppermute x13, starting transfers between devices, swap(): return lax.ppermute(block, axis, [(i, i ^ step) for i in range(count)])  12.4 us
  transfers between devices with their start and end apart: 13, of which 8 were waited for; matrix products, arithmetic and copies ran while one was open for 0% of the time, Pallas kernels for 27%

profile of v5, /device:TPU:0, one launch (start us, length us, event | category | flops | bytes accessed | tf_op | source)
XLA Modules:
  0.0 42.2 jit_solution(16875132928278908242)
XLA Ops:
  0.6 1.0 %prepare.1 = (bf16[4,3072]{1,0:T(4,128)(2,1)S(1)}, bf16[224,128]{1,0:T(8,128)(2,1)S(1)}) custom-call(bf16[4,6144]{1,0:T(4,128)(2,1)} %tokens_ref.1, f32[1,6144]{1,0:T(1,128)} %bitcast.7, bf16[4,3072]{1,0:T(4,128)(2,1)} %far_query.1, bf16[4,512]{1,0:T(4,128)(2,1)} %far_key.1, bf16[4,512]{1,0:T(4,128)(2,1)} %far_value.1), custom_call_target="tpu_custom_call" | custom-call | bytes 100000 | tf_op jit(solution)/shard_map/prepare/pallas_call | solution.py:48
  1.6 4.1 %collective-permute-start = (bf16[224,128]{1,0:T(8,128)(2,1)S(1)}, bf16[224,128]{1,0:T(8,128)(2,1)S(1)}, u32[]{:S(2)}, u32[]{:S(2)}) collective-permute-start(bf16[224,128]{1,0:T(8,128)(2,1)S(1)} %get-tuple-element.18.own_both), channel_id=1, source_target_pairs={{0,8},{2,10},{4,12},{6,14},{8,0},{10,2},{12,4},{14,6},{1,9},{3,11}... | collective-permute-start | bytes 172040 | tf_op jit(solution)/shard_map/ppermute | solution.py:27
  5.8 1.6 %collective-permute-start.1 = (bf16[4,3072]{1,0:T(4,128)(2,1)S(1)}, bf16[4,3072]{1,0:T(4,128)(2,1)S(1)}, u32[]{:S(2)}, u32[]{:S(2)}) collective-permute-start(bf16[4,3072]{1,0:T(4,128)(2,1)S(1)} %get-tuple-element.17.refs_0_.own_ref), channel_id=1, source_target_pairs={{0,4},{2,6},{4,0},{6,2},{8,12},{10,14},{12,8},{14,10},{1,5},{3,7},... | collective-permute-start | bytes 73736 | tf_op jit(solution)/shard_map/ppermute | solution.py:27
  7.3 0.0 collective-permute-start.2
  7.3 0.0 slice-start.4
  7.4 1.0 %shares.1.refs_0_.share_ref = f32[32,128]{1,0:T(8,128)S(1)} custom-call(s32[2,32]{1,0:T(2,128)} %bitcast.8, f32[2,32]{1,0:T(2,128)} %bitcast.9, bf16[4,3072]{1,0:T(4,128)(2,1)S(1)} %get-tuple-element.17.refs_0_.own_ref, bf16[1,6144,1024]{2,1,0:T(8,128)(2,1)} %gate_ref.1, bf16[1,6144,1024]{2,1,0:T(8,128)(2,1)} %up_ref.1), custom_call_target="tpu_custom_call" | custom-call | bytes 100000 | tf_op jit(solution)/shard_map/shares/pallas_call | solution.py:48
  8.3 0.0 slice-start.2
  8.3 0.0 slice-start.5
  8.4 1.2 %collective-permute-done.1.next_ref = bf16[4,3072]{1,0:T(4,128)(2,1)S(1)} collective-permute-done((bf16[4,3072]{1,0:T(4,128)(2,1)S(1)}, bf16[4,3072]{1,0:T(4,128)(2,1)S(1)}, u32[]{:S(2)}, u32[]{:S(2)}) %collective-permute-start.1) | collective-permute-done | bytes 24608 | tf_op jit(solution)/shard_map/ppermute | solution.py:27
  9.6 3.4 %collective-permute-done.2.last_ref = bf16[4,3072]{1,0:T(4,128)(2,1)S(1)} collective-permute-done((bf16[4,3072]{1,0:T(4,128)(2,1)S(1)}, bf16[4,3072]{1,0:T(4,128)(2,1)S(1)}, u32[]{:S(2)}, u32[]{:S(2)}) %collective-permute-start.2) | collective-permute-done | bytes 24608 | tf_op jit(solution)/shard_map/ppermute | solution.py:27
  13.0 0.0 collective-permute-done.far_both
  13.0 1.6 %collective-permute-start.3 = (bf16[16,3072]{1,0:T(8,128)(2,1)S(1)}, bf16[16,3072]{1,0:T(8,128)(2,1)S(1)}, u32[]{:S(2)}, u32[]{:S(2)}) collective-permute-start(bf16[16,3072]{1,0:T(8,128)(2,1)S(1)} %get-tuple-element.19.own_ref), channel_id=1, source_target_pairs={{0,2},{2,0},{4,6},{6,4},{8,10},{10,8},{12,14},{14,12},{1,3},{3,1},... | collective-permute-start | bytes 294920 | tf_op jit(solution)/shard_map/ppermute | solution.py:27
  14.6 0.0 collective-permute-start.4
  14.6 4.3 %collective-permute-done.4.got_heads = bf16[256,128]{1,0:T(8,128)(2,1)S(1)} collective-permute-done((bf16[256,128]{1,0:T(8,128)(2,1)S(1)}, bf16[256,128]{1,0:T(8,128)(2,1)S(1)}, u32[]{:S(2)}, u32[]{:S(2)}) %collective-permute-start.4) | collective-permute-done | bytes 65568 | tf_op jit(solution)/shard_map/ppermute | solution.py:27
  18.8 0.0 collective-permute-done.3.got_ref
  18.9 0.1 collective-permute-start.6
  19.0 0.6 %collective-permute-start.5 = (bf16[512,128]{1,0:T(8,128)(2,1)S(1)}, bf16[512,128]{1,0:T(8,128)(2,1)S(1)}, u32[]{:S(2)}, u32[]{:S(2)}) collective-permute-start(bf16[512,128]{1,0:T(8,128)(2,1)S(1)} %get-tuple-element.21.near_ref.refs_0_), channel_id=1, source_target_pairs={{0,2},{2,0},{4,6},{6,4},{8,10},{10,8},{12,14},{14,12},{1,3},{3,1},... | collective-permute-start | bytes 393224 | tf_op jit(solution)/shard_map/ppermute | solution.py:27
  19.5 0.9 %collective-permute-done.6.other_ref = bf16[32,3072]{1,0:T(8,128)(2,1)S(1)} collective-permute-done((bf16[32,3072]{1,0:T(8,128)(2,1)S(1)}, bf16[32,3072]{1,0:T(8,128)(2,1)S(1)}, u32[]{:S(2)}, u32[]{:S(2)}) %collective-permute-start.6) | collective-permute-done | bytes 196640 | tf_op jit(solution)/shard_map/ppermute | solution.py:27
  20.4 0.0 slice-done
  20.4 0.0 slice-done.1
  20.4 0.0 slice-done.3
  20.4 0.0 slice-done.4
  20.4 0.0 slice-done.2
  20.4 0.0 slice-done.5
  20.5 5.0 %gate_all.1 = (bf16[32,1024]{1,0:T(8,128)(2,1)S(1)}, bf16[1024,3072]{1,0:T(8,128)(2,1)S(1)}, bf16[1024,3072]{1,0:T(8,128)(2,1)S(1)}) custom-call(bf16[32,3072]{1,0:T(8,128)(2,1)S(1)} %get-tuple-element.22.x_ref, bf16[32,3072]{1,0:T(8,128)(2,1)S(1)} %collective-permute-done.6.other_ref, bf16[1,6144,1024]{2,1,0:T(8,128)(2,1)S(1)} %bitcast.4, ...), custom_call_target="tpu_custom_call" | custom-call | flops 805306368 | bytes 37748736 | tf_op jit(solution)/shard_map/gate_all/pallas_call | solution.py:48
  25.5 0.0 collective-permute-done.5.after.far_ref.refs_1_
  25.5 0.0 copy-start
  25.5 0.0 copy-start.1
  25.5 0.0 copy-start.3
  25.5 0.0 copy-start.4
  25.5 1.5 %down.2.after = bf16[32,3072]{1,0:T(8,128)(2,1)S(1)} custom-call(bf16[32,1024]{1,0:T(8,128)(2,1)S(1)} %get-tuple-element.23.hidden_ref.after, bf16[1024,3072]{1,0:T(8,128)(2,1)S(1)} %get-tuple-element.25.down_ref, bf16[512,128]{1,0:T(8,128)(2,1)S(1)} %collective-permute-done.5.after.far_ref.refs_1_), custom_call_target="tpu_custom_call" | custom-call | flops 201326592 | bytes 6291456 | tf_op jit(solution)/shard_map/down/pallas_call | solution.py:48
  27.1 0.2 collective-permute-start.7
  27.2 1.5 %down.3.terms_ref = f32[32,3072]{1,0:T(8,128)S(1)} custom-call(bf16[32,1024]{1,0:T(8,128)(2,1)S(1)} %get-tuple-element.23.hidden_ref.after, bf16[1024,3072]{1,0:T(8,128)(2,1)S(1)} %get-tuple-element.24.down_ref, bf16[32,3072]{1,0:T(8,128)(2,1)S(1)} %down.2.after), custom_call_target="tpu_custom_call" | custom-call | flops 201326592 | bytes 6291456 | tf_op jit(solution)/shard_map/down/pallas_call | solution.py:48
  28.8 0.0 collective-permute-done.7.taken_ref
  28.8 0.8 %collective-permute-start.8 = (bf16[16,3072]{1,0:T(8,128)(2,1)S(1)}, bf16[16,3072]{1,0:T(8,128)(2,1)S(1)}, u32[]{:S(2)}, u32[]{:S(2)}) collective-permute-start(bf16[16,3072]{1,0:T(8,128)(2,1)S(1)} %get-tuple-element.27.after), channel_id=1, source_target_pairs={{0,2},{2,0},{4,6},{6,4},{8,10},{10,8},{12,14},{14,12},{1,3},{3,1},... | collective-permute-start | bytes 294920 | tf_op jit(solution)/shard_map/ppermute | solution.py:27
  29.6 0.0 copy-done
  29.6 2.2 %attend.1.after.refs_7_ = f32[72,128]{1,0:T(8,128)S(1)} custom-call(bf16[512,128]{1,0:T(8,128)(2,1)S(1)} %get-tuple-element.21.near_ref.refs_0_, bf16[512,128]{1,0:T(8,128)(2,1)S(1)} %collective-permute-done.5.after.far_ref.refs_1_, bf16[4,512,512]{2,1,0:T(8,128)(2,1)S(1)} %copy-done, bf16[4,512,512]{2,1,0:T(8,128)(2,1)S(1)} %copy-done.1, s32[4]{0:T(128)S(1)} %copy-done.3, ...), custom_call_target="tpu_custom_call" | custom-call | flops 12582912 | bytes 2097152 | tf_op jit(solution)/shard_map/attend/pallas_call | solution.py:48
  31.8 2.2 %collective-permute-done.8.taken_ref = bf16[16,3072]{1,0:T(8,128)(2,1)S(1)} collective-permute-done((bf16[16,3072]{1,0:T(8,128)(2,1)S(1)}, bf16[16,3072]{1,0:T(8,128)(2,1)S(1)}, u32[]{:S(2)}, u32[]{:S(2)}) %collective-permute-start.8) | collective-permute-done | bytes 98336 | tf_op jit(solution)/shard_map/ppermute | solution.py:27
  34.0 0.1 collective-permute-start.10
  34.1 1.1 %collective-permute-start.11 = (bf16[4,3072]{1,0:T(4,128)(2,1)S(1)}, bf16[4,3072]{1,0:T(4,128)(2,1)S(1)}, u32[]{:S(2)}, u32[]{:S(2)}) collective-permute-start(bf16[4,3072]{1,0:T(4,128)(2,1)S(1)} %get-tuple-element.31), channel_id=1, source_target_pairs={{0,12},{2,14},{4,8},{6,10},{8,4},{10,6},{12,0},{14,2},{1,13},{3,15... | collective-permute-start | bytes 73736 | tf_op jit(solution)/shard_map/ppermute | solution.py:27
  35.2 2.4 %collective-permute-start.9 = (bf16[4,3072]{1,0:T(4,128)(2,1)S(1)}, bf16[4,3072]{1,0:T(4,128)(2,1)S(1)}, u32[]{:S(2)}, u32[]{:S(2)}) collective-permute-start(bf16[4,3072]{1,0:T(4,128)(2,1)S(1)} %get-tuple-element.30), channel_id=1, source_target_pairs={{0,8},{2,10},{4,12},{6,14},{8,0},{10,2},{12,4},{14,6},{1,9},{3,11}... | collective-permute-start | bytes 73736 | tf_op jit(solution)/shard_map/ppermute | solution.py:27
  37.5 1.8 %attend_last.1.after = bf16[4,3072]{1,0:T(4,128)(2,1)} custom-call(bf16[512,128]{1,0:T(8,128)(2,1)S(1)} %get-tuple-element.21.near_ref.refs_0_, bf16[512,128]{1,0:T(8,128)(2,1)S(1)} %collective-permute-done.5.after.far_ref.refs_1_, bf16[4,512,512]{2,1,0:T(8,128)(2,1)S(1)} %copy-done, bf16[4,512,512]{2,1,0:T(8,128)(2,1)S(1)} %copy-done.1, s32[4]{0:T(128)S(1)} %copy-done.3, ...), custom_call_target="tpu_custom_call" | custom-call | flops 12582912 | bytes 2097152 | tf_op jit(solution)/shard_map/attend_last/pallas_call | solution.py:48
  39.3 0.0 collective-permute-done.10.next_ref
  39.3 0.4 %collective-permute-done.11.last_ref = bf16[4,3072]{1,0:T(4,128)(2,1)S(1)} collective-permute-done((bf16[4,3072]{1,0:T(4,128)(2,1)S(1)}, bf16[4,3072]{1,0:T(4,128)(2,1)S(1)}, u32[]{:S(2)}, u32[]{:S(2)}) %collective-permute-start.11) | collective-permute-done | bytes 24608 | tf_op jit(solution)/shard_map/ppermute | solution.py:27
  39.8 0.5 %collective-permute-done.9.far_ref = bf16[4,3072]{1,0:T(4,128)(2,1)S(1)} collective-permute-done((bf16[4,3072]{1,0:T(4,128)(2,1)S(1)}, bf16[4,3072]{1,0:T(4,128)(2,1)S(1)}, u32[]{:S(2)}, u32[]{:S(2)}) %collective-permute-start.9) | collective-permute-done | bytes 24608 | tf_op jit(solution)/shard_map/ppermute | solution.py:27
  40.3 0.1 collective-permute-start.12
  40.4 1.2 %collective-permute-done.12.other_ref = bf16[4,3072]{1,0:T(4,128)(2,1)S(1)} collective-permute-done((bf16[4,3072]{1,0:T(4,128)(2,1)S(1)}, bf16[4,3072]{1,0:T(4,128)(2,1)S(1)}, u32[]{:S(2)}, u32[]{:S(2)}) %collective-permute-start.12) | collective-permute-done | bytes 24608 | tf_op jit(solution)/shard_map/ppermute | solution.py:27
  41.6 0.6 %join.1 = bf16[4,6144]{1,0:T(4,128)(2,1)} custom-call(bf16[4,3072]{1,0:T(4,128)(2,1)S(1)} %finish.1.own_ref, bf16[4,3072]{1,0:T(4,128)(2,1)S(1)} %collective-permute-done.12.other_ref), custom_call_target="tpu_custom_call" | custom-call | bytes 49152 | tf_op jit(solution)/shard_map/join/pallas_call | solution.py:48
  (15 shorter events, 0.2 us)
Async XLA Ops:
  1.6 11.3 %collective-permute-start = (bf16[224,128]{1,0:T(8,128)(2,1)S(1)}, bf16[224,128]{1,0:T(8,128)(2,1)S(1)}, u32[]{:S(2)}, u32[]{:S(2)}) collective-permute-start(bf16[224,128]{1,0:T(8,128)(2,1)S(1)} %get-tuple-element.18.own_both), channel_id=1, source_target_pairs={{0,8},{2,10},{4,12},{6,14},{8,0},{10,2},{12,4},{14,6},{1,9},{3,11}... | collective-permute-start | bytes 172040 | tf_op jit(solution)/shard_map/ppermute | solution.py:27
  5.8 3.8 %collective-permute-start.1 = (bf16[4,3072]{1,0:T(4,128)(2,1)S(1)}, bf16[4,3072]{1,0:T(4,128)(2,1)S(1)}, u32[]{:S(2)}, u32[]{:S(2)}) collective-permute-start(bf16[4,3072]{1,0:T(4,128)(2,1)S(1)} %get-tuple-element.17.refs_0_.own_ref), channel_id=1, source_target_pairs={{0,4},{2,6},{4,0},{6,2},{8,12},{10,14},{12,8},{14,10},{1,5},{3,7},... | collective-permute-start | bytes 73736 | tf_op jit(solution)/shard_map/ppermute | solution.py:27
  7.3 5.6 %collective-permute-start.2 = (bf16[4,3072]{1,0:T(4,128)(2,1)S(1)}, bf16[4,3072]{1,0:T(4,128)(2,1)S(1)}, u32[]{:S(2)}, u32[]{:S(2)}) collective-permute-start(bf16[4,3072]{1,0:T(4,128)(2,1)S(1)} %get-tuple-element.17.refs_0_.own_ref), channel_id=1, source_target_pairs={{0,12},{2,14},{4,8},{6,10},{8,4},{10,6},{12,0},{14,2},{1,13},{3,15... | collective-permute-start | bytes 73736 | tf_op jit(solution)/shard_map/ppermute | solution.py:27
  7.3 13.1 %slice-start = ((s8[12582912]{0:T(1024)(128)(4,1)}), s8[4194304]{0:T(1024)(128)(4,1)S(1)}, s32[]{:S(2)}) async-start(s8[12582912]{0:T(1024)(128)(4,1)} %bitcast.3), calls=%async_computation | async-start | bytes 8388608
  7.3 13.1 %slice-start.1 = ((s8[12582912]{0:T(1024)(128)(4,1)}), s8[4194304]{0:T(1024)(128)(4,1)S(1)}, s32[]{:S(2)}) async-start(s8[12582912]{0:T(1024)(128)(4,1)} %bitcast.3), calls=%async_computation.1 | async-start | bytes 8388608
  7.3 13.1 %slice-start.3 = ((s8[12582912]{0:T(1024)(128)(4,1)}), s8[4194304]{0:T(1024)(128)(4,1)S(1)}, s32[]{:S(2)}) async-start(s8[12582912]{0:T(1024)(128)(4,1)} %bitcast.5), calls=%async_computation.3 | async-start | bytes 8388608
  7.3 13.1 %slice-start.4 = ((s8[12582912]{0:T(1024)(128)(4,1)}), s8[4194304]{0:T(1024)(128)(4,1)S(1)}, s32[]{:S(2)}) async-start(s8[12582912]{0:T(1024)(128)(4,1)} %bitcast.5), calls=%async_computation.4 | async-start | bytes 8388608
  8.3 12.1 %slice-start.2 = ((s8[12582912]{0:T(1024)(128)(4,1)}), s8[4194304]{0:T(1024)(128)(4,1)S(1)}, s32[]{:S(2)}) async-start(s8[12582912]{0:T(1024)(128)(4,1)} %bitcast.3), calls=%async_computation.2 | async-start | bytes 8388608
  8.3 12.1 %slice-start.5 = ((s8[12582912]{0:T(1024)(128)(4,1)}), s8[4194304]{0:T(1024)(128)(4,1)S(1)}, s32[]{:S(2)}) async-start(s8[12582912]{0:T(1024)(128)(4,1)} %bitcast.5), calls=%async_computation.5 | async-start | bytes 8388608
  13.0 5.9 %collective-permute-start.3 = (bf16[16,3072]{1,0:T(8,128)(2,1)S(1)}, bf16[16,3072]{1,0:T(8,128)(2,1)S(1)}, u32[]{:S(2)}, u32[]{:S(2)}) collective-permute-start(bf16[16,3072]{1,0:T(8,128)(2,1)S(1)} %get-tuple-element.19.own_ref), channel_id=1, source_target_pairs={{0,2},{2,0},{4,6},{6,4},{8,10},{10,8},{12,14},{14,12},{1,3},{3,1},... | collective-permute-start | bytes 294920 | tf_op jit(solution)/shard_map/ppermute | solution.py:27
  14.6 4.3 %collective-permute-start.4 = (bf16[256,128]{1,0:T(8,128)(2,1)S(1)}, bf16[256,128]{1,0:T(8,128)(2,1)S(1)}, u32[]{:S(2)}, u32[]{:S(2)}) collective-permute-start(bf16[256,128]{1,0:T(8,128)(2,1)S(1)} %get-tuple-element.20.own_heads), channel_id=1, source_target_pairs={{0,4},{2,6},{4,0},{6,2},{8,12},{10,14},{12,8},{14,10},{1,5},{3,7},... | collective-permute-start | bytes 196616 | tf_op jit(solution)/shard_map/ppermute | solution.py:27
  18.9 1.5 %collective-permute-start.6 = (bf16[32,3072]{1,0:T(8,128)(2,1)S(1)}, bf16[32,3072]{1,0:T(8,128)(2,1)S(1)}, u32[]{:S(2)}, u32[]{:S(2)}) collective-permute-start(bf16[32,3072]{1,0:T(8,128)(2,1)S(1)} %get-tuple-element.22.x_ref), channel_id=1, source_target_pairs={{0,1},{1,0},{2,3},{3,2},{4,5},{5,4},{6,7},{7,6},{8,9},{9,8},{10,11... | collective-permute-start | bytes 589832 | tf_op jit(solution)/shard_map/ppermute | solution.py:27
  19.0 6.5 %collective-permute-start.5 = (bf16[512,128]{1,0:T(8,128)(2,1)S(1)}, bf16[512,128]{1,0:T(8,128)(2,1)S(1)}, u32[]{:S(2)}, u32[]{:S(2)}) collective-permute-start(bf16[512,128]{1,0:T(8,128)(2,1)S(1)} %get-tuple-element.21.near_ref.refs_0_), channel_id=1, source_target_pairs={{0,2},{2,0},{4,6},{6,4},{8,10},{10,8},{12,14},{14,12},{1,3},{3,1},... | collective-permute-start | bytes 393224 | tf_op jit(solution)/shard_map/ppermute | solution.py:27
  25.5 4.1 %copy-start = (bf16[4,512,512]{2,1,0:T(8,128)(2,1)S(1)}, bf16[4,512,512]{2,1,0:T(8,128)(2,1)}, u32[]{:S(2)}) copy-start(bf16[4,512,512]{2,1,0:T(8,128)(2,1)} %refs_2_.5) | copy-start | bytes 6291460
  25.5 4.1 %copy-start.1 = (bf16[4,512,512]{2,1,0:T(8,128)(2,1)S(1)}, bf16[4,512,512]{2,1,0:T(8,128)(2,1)}, u32[]{:S(2)}) copy-start(bf16[4,512,512]{2,1,0:T(8,128)(2,1)} %refs_3_.1) | copy-start | bytes 6291460
  25.5 4.1 %copy-start.3 = (s32[4]{0:T(128)S(1)}, s32[4]{0:T(128)}, u32[]{:S(2)}) copy-start(s32[4]{0:T(128)} %refs_4_.1) | copy-start | bytes 52
  25.5 4.1 %copy-start.4 = (s32[4]{0:T(128)S(1)}, s32[4]{0:T(128)}, u32[]{:S(2)}) copy-start(s32[4]{0:T(128)} %refs_5_.1) | copy-start | bytes 52
  27.1 1.7 %collective-permute-start.7 = (bf16[32,3072]{1,0:T(8,128)(2,1)S(1)}, bf16[32,3072]{1,0:T(8,128)(2,1)S(1)}, u32[]{:S(2)}, u32[]{:S(2)}) collective-permute-start(bf16[32,3072]{1,0:T(8,128)(2,1)S(1)} %down.2.after), channel_id=1, source_target_pairs={{0,1},{1,0},{2,3},{3,2},{4,5},{5,4},{6,7},{7,6},{8,9},{9,8},{10,11... | collective-permute-start | bytes 589832 | tf_op jit(solution)/shard_map/ppermute | solution.py:27
  28.8 11.5 %copy-start.2 = (bf16[4,6144]{1,0:T(4,128)(2,1)S(1)}, bf16[4,6144]{1,0:T(4,128)(2,1)}, u32[]{:S(2)}) copy-start(bf16[4,6144]{1,0:T(4,128)(2,1)} %tokens_ref.1) | copy-start | bytes 147460
  28.8 5.1 %collective-permute-start.8 = (bf16[16,3072]{1,0:T(8,128)(2,1)S(1)}, bf16[16,3072]{1,0:T(8,128)(2,1)S(1)}, u32[]{:S(2)}, u32[]{:S(2)}) collective-permute-start(bf16[16,3072]{1,0:T(8,128)(2,1)S(1)} %get-tuple-element.27.after), channel_id=1, source_target_pairs={{0,2},{2,0},{4,6},{6,4},{8,10},{10,8},{12,14},{14,12},{1,3},{3,1},... | collective-permute-start | bytes 294920 | tf_op jit(solution)/shard_map/ppermute | solution.py:27
  34.0 5.3 %collective-permute-start.10 = (bf16[4,3072]{1,0:T(4,128)(2,1)S(1)}, bf16[4,3072]{1,0:T(4,128)(2,1)S(1)}, u32[]{:S(2)}, u32[]{:S(2)}) collective-permute-start(bf16[4,3072]{1,0:T(4,128)(2,1)S(1)} %get-tuple-element.28.refs_6_), channel_id=1, source_target_pairs={{0,4},{2,6},{4,0},{6,2},{8,12},{10,14},{12,8},{14,10},{1,5},{3,7},... | collective-permute-start | bytes 73736 | tf_op jit(solution)/shard_map/ppermute | solution.py:27
  34.1 5.7 %collective-permute-start.11 = (bf16[4,3072]{1,0:T(4,128)(2,1)S(1)}, bf16[4,3072]{1,0:T(4,128)(2,1)S(1)}, u32[]{:S(2)}, u32[]{:S(2)}) collective-permute-start(bf16[4,3072]{1,0:T(4,128)(2,1)S(1)} %get-tuple-element.31), channel_id=1, source_target_pairs={{0,12},{2,14},{4,8},{6,10},{8,4},{10,6},{12,0},{14,2},{1,13},{3,15... | collective-permute-start | bytes 73736 | tf_op jit(solution)/shard_map/ppermute | solution.py:27
  35.2 5.1 %collective-permute-start.9 = (bf16[4,3072]{1,0:T(4,128)(2,1)S(1)}, bf16[4,3072]{1,0:T(4,128)(2,1)S(1)}, u32[]{:S(2)}, u32[]{:S(2)}) collective-permute-start(bf16[4,3072]{1,0:T(4,128)(2,1)S(1)} %get-tuple-element.30), channel_id=1, source_target_pairs={{0,8},{2,10},{4,12},{6,14},{8,0},{10,2},{12,4},{14,6},{1,9},{3,11}... | collective-permute-start | bytes 73736 | tf_op jit(solution)/shard_map/ppermute | solution.py:27
  40.3 1.3 %collective-permute-start.12 = (bf16[4,3072]{1,0:T(4,128)(2,1)S(1)}, bf16[4,3072]{1,0:T(4,128)(2,1)S(1)}, u32[]{:S(2)}, u32[]{:S(2)}) collective-permute-start(bf16[4,3072]{1,0:T(4,128)(2,1)S(1)} %finish.1.own_ref), channel_id=1, source_target_pairs={{0,1},{1,0},{2,3},{3,2},{4,5},{5,4},{6,7},{7,6},{8,9},{9,8},{10,11... | collective-permute-start | bytes 73736 | tf_op jit(solution)/shard_map/ppermute | solution.py:27

commit v6 on v5

--- a/solution.py
+++ b/solution.py
@@ -20,7 +20,8 @@
 
 
 def steps_of(wide):
-    return [wide >> (i + 1) for i in range(int(math.log2(wide)))]
+    bits = int(math.log2(wide))
+    return [1 << i for i in range(bits - 2)] + [wide >> 1, wide >> 2]
 
 
 def swap(block, axis, count, step):
@@ -117,19 +118,30 @@
     return jnp.concatenate([ref[...].astype(jnp.float32) for ref in refs], axis=0)
 
 
-def gather_line(own_ref, far_both, next_ref, last_ref, own_both, *refs):
-    *_, out_ref, heads_ref, packed = refs
+def grow_first(own_ref, far_both, own_both, after, out_ref, heads_ref, packed):
     rows, half = own_ref.shape
     pieces = half // HD
     tokens = rows * pieces
     packed[...] = far_both[:tokens, :].astype(jnp.float32)
     far = [packed[pl.ds(piece, rows, stride=pieces), :] for piece in range(pieces)]
     far = jnp.concatenate(far, axis=1)
-    own, near_rows, last = (r[...].astype(jnp.float32) for r in (own_ref, next_ref, last_ref))
-    out_ref[...] = jnp.concatenate([own, far, near_rows, last], axis=0).astype(jnp.bfloat16)
+    own = own_ref[...].astype(jnp.float32)
+    out_ref[...] = jnp.concatenate([own, far], axis=0).astype(jnp.bfloat16)
     count = heads_ref.shape[0] // 2
     heads_ref[:count, :] = own_both[tokens:, :]
     heads_ref[count:, :] = far_both[tokens:, :]
+
+
+def stack(*refs):
+    refs[-1][...] = stacked(refs[:-1]).astype(refs[-1].dtype)
+
+
+def stack_line(own_ref, last_ref, far_ref, next_ref, out_ref):
+    stack(own_ref, far_ref, next_ref, last_ref, out_ref)
+
+
+def stack_after(own_ref, got_ref, after, out_ref):
+    stack(own_ref, got_ref, out_ref)
 
 
 def grow_both(own_ref, got_ref, own_heads, got_heads, *refs):
@@ -210,14 +222,7 @@
         ).astype(out_ref.dtype)
 
 
-def combine(terms_ref, taken_ref, after, kept_ref, sent_ref):
-    total = terms_ref[...] + taken_ref[...].astype(jnp.float32)
-    kept = kept_ref.shape[0]
-    kept_ref[...] = total[:kept]
-    sent_ref[...] = total[kept:].astype(jnp.bfloat16)
-
-
-def part_line(terms_ref, taken_ref, after, kept_ref, far_ref, next_ref, last_ref):
+def part_line(terms_ref, taken_ref, kept_ref, far_ref, next_ref, last_ref):
     total = terms_ref[...] + taken_ref[...].astype(jnp.float32)
     rows = kept_ref.shape[0]
     kept_ref[...] = total[:rows]
@@ -225,14 +230,22 @@
         ref[...] = total[(i + 1) * rows : (i + 2) * rows].astype(jnp.bfloat16)
 
 
-def finish(kept_ref, far_ref, next_ref, last_ref, tokens_ref, after, out_ref):
+def combine(*refs):
+    terms_ref, *taken, after, kept_ref, sent_ref = refs
+    total = terms_ref[...]
+    for ref in taken:
+        total = total + ref[...].astype(jnp.float32)
+    kept = kept_ref.shape[0]
+    kept_ref[...] = total[:kept]
+    sent_ref[...] = total[kept:].astype(jnp.bfloat16)
+
+
+def finish(kept_ref, taken_ref, tokens_ref, after, out_ref):
     half = kept_ref.shape[1]
     core = lax.axis_index("narrow")
     own = tokens_ref[...].astype(jnp.float32)
     own = jnp.where(core == 0, own[:, :half], own[:, half:])
-    total = kept_ref[...]
-    for ref in (far_ref, next_ref, last_ref):
-        total = total + ref[...].astype(jnp.float32)
+    total = kept_ref[...] + taken_ref[...].astype(jnp.float32)
     out_ref[...] = (own + total).astype(jnp.bfloat16)
 
 
@@ -365,8 +378,7 @@
             size=100000,
             far=range(len(firsts)),
         )
-        line = [swap(both, "wide", wide, steps[0])]
-        line += [swap(x, "wide", wide, step) for step in (steps[1], steps[0] ^ steps[1])]
+        far_both = swap(both, "wide", wide, steps[0])
         share = call(
             functools.partial(shares, steps, rows),
             shape((count, HD), f32),
@@ -380,25 +392,24 @@
             far=range(5),
         )
         x, heads = call(
-            gather_line,
-            [shape((4 * rows, half), bf16), shape((2 * rows * each, HD), bf16)],
-            [
-                x,
-                *line,
-                both,
-                share,
-                *weights,
-            ],
+            grow_first,
+            [shape((2 * rows, half), bf16), shape((2 * rows * each, HD), bf16)],
+            [x, far_both, both, share],
             [pltpu.VMEM((rows * half // HD, HD), f32)],
             size=100000,
-            far=(5, 6, 7),
-        )
-        for order, step in enumerate(steps[2:]):
-            ins = [x, swap(x, "wide", wide, step)]
-            ins += [heads, swap(heads, "wide", wide, steps[order + 1])]
+            far=(3,),
+        )
+        for step in steps[1:-2]:
+            ins = [x, swap(x, "wide", wide, step), heads, swap(heads, "wide", wide, step)]
             outs = [shape((2 * x.shape[0], half), bf16), shape((2 * heads.shape[0], HD), bf16)]
             x, heads = call(grow_both, outs, ins, size=8 * (x.size + heads.size))
-        far_heads = swap(heads, "wide", wide, steps[-1])
+        line_steps = [steps[-2], steps[-1], steps[-2] ^ steps[-1]]
+        last = swap(x, "wide", wide, line_steps[2])
+        line = [swap(x, "wide", wide, step) for step in line_steps[:2]]
+        got_heads = swap(heads, "wide", wide, steps[-2])
+        x = call(
+            stack_line, shape((count, half), bf16), [x, last, *line], size=8 * count * half
+        )
 
         product = 2 * count * half * units
         other_x = swap(x, "narrow", 2, 1)
@@ -419,15 +430,23 @@
             size=6 * piece_bytes,
             far=(5,),
         )
+        heads = call(
+            stack_after,
+            shape((2 * heads.shape[0], HD), bf16),
+            [heads, got_heads, hidden],
+            size=8 * heads.size,
+            far=(2,),
+        )
         given = call(
             down,
             shape((count, half), bf16),
-            [hidden, near(down_other), far_heads],
+            [hidden, near(down_other), heads],
             flops=product,
             size=piece_bytes,
             far=(2,),
         )
         taken = swap(given, "narrow", 2, 1)
+        far_heads = swap(heads, "wide", wide, steps[-1])
         terms = call(
             down,
             shape((count, half), f32),
@@ -441,46 +460,38 @@
         slots = queries.shape[0]
         early_slots = list(range(slots - 1))
         late_slots = list(range(slots - 1, slots))
-        early = None
-        after = hidden
-        for step in reversed(steps[2:]):
+        quarter = count // 4
+        block = shape((quarter, half), bf16)
+        terms, *sent = call(
+            part_line,
+            [shape((quarter, half), f32), block, block, block],
+            [terms, taken],
+            size=terms.size * 8,
+        )
+        taken = [swap(part, "wide", wide, step) for part, step in zip(sent, line_steps)]
+        early = call(
+            functools.partial(attend, steps, early_slots),
+            shape((len(early_slots) * heads_local, HD), f32),
+            [heads, far_heads, *caches, sent[0]],
+            flops=2 * key_cache.size * GROUP,
+            size=2 * key_cache.size,
+            smem=(4, 5),
+            far=(6,),
+        )
+        for step in reversed(steps[:-2]):
             kept = terms.shape[0] // 2
             terms, sent = call(
                 combine,
                 [shape((kept, half), f32), shape((kept, half), bf16)],
-                [terms, taken, after],
+                [terms, *taken, early],
                 size=terms.size * 8,
-                far=(2,),
+                far=(1 + len(taken),),
             )
-            taken = swap(sent, "wide", wide, step)
-            if early is None:
-                early = call(
-                    functools.partial(attend, steps, early_slots),
-                    shape((len(early_slots) * heads_local, HD), f32),
-                    [heads, far_heads, *caches, sent],
-                    flops=2 * key_cache.size * GROUP,
-                    size=2 * key_cache.size,
-                    smem=(4, 5),
-                    far=(6,),
-                )
-                after = early
-        block = shape((rows, half), bf16)
-        terms, far_sent, next_sent, last_sent = call(
-            part_line,
-            [shape((rows, half), f32), block, block, block],
-            [terms, taken, after],
-            size=terms.size * 8,
-            far=(2,),
-        )
-        got = [
-            swap(far_sent, "wide", wide, steps[0]),
-            swap(next_sent, "wide", wide, steps[1]),
-            swap(last_sent, "wide", wide, steps[0] ^ steps[1]),
-        ]
+            taken = [swap(sent, "wide", wide, step)]
         context = call(
             functools.partial(attend_last, steps, late_slots, heads_local),
             shape(queries.shape, bf16),
-            [heads, far_heads, *caches, next_sent, early],
+            [heads, far_heads, *caches, sent, early],
             [
                 pltpu.VMEM((len(late_slots) * heads_local, HD), f32),
                 pltpu.VMEM((slots * heads_local, HD), f32),
@@ -491,7 +502,11 @@
             far=(6,),
         )
         piece = call(
-            finish, block, [terms, *got, tokens, distant(context)], size=terms.size * 8, far=(5,)
+            finish,
+            shape((rows, half), bf16),
+            [terms, *taken, tokens, distant(context)],
+            size=terms.size * 8,
+            far=(3,),
         )
         other = swap(piece, "narrow", 2, 1)
         mixed_out = call(join, shape((rows, width), bf16), [piece, other], size=terms.size * 4)

time: 42.4 us -> 41.4 us (0.976)
  waiting for transfers between devices: 14 us -> 9.24 us
  starting transfers between devices: 12.4 us -> 16.3 us
    ppermute x13, waiting for transfers between devices: 14 us -> 9.24 us  [swap(): return lax.ppermute(block, axis, [(i, i ^ step) for i in range(count)])]
    ppermute x13, starting transfers between devices: 12.4 us -> 16.3 us  [swap(): return lax.ppermute(block, axis, [(i, i ^ step) for i in range(count)])]
    pallas_call x13 -> x14, Pallas kernels: 14.8 us -> 14.8 us  [call(): pl.pallas_call(kernel, name=getattr(kernel, 'func', kernel).__name__, out...]
  transfers between devices with their start and end apart: 13 -> 13, of which waited for: 8 -> 6; matrix products, arithmetic and copies ran while one was open for 0% -> 0% of each run, Pallas kernels for 27% -> 28%
where the time goes in v6:
time: 41.4 us; the launch traced here: 41.2 us
  starting transfers between devices  16.3 us (39%)
  Pallas kernels  14.8 us (36%)
  waiting for transfers between devices  9.24 us (22%)
  between operations  0.83 us (2%)
    ppermute x13, starting transfers between devices, swap(): return lax.ppermute(block, axis, [(i, i ^ step) for i in range(count)])  16.3 us
    pallas_call x14, Pallas kernels, call(): pl.pallas_call(kernel, name=getattr(kernel, 'func', kernel).__name__, out...  14.8 us
    ppermute x13, waiting for transfers between devices, swap(): return lax.ppermute(block, axis, [(i, i ^ step) for i in range(count)])  9.24 us
  transfers between devices with their start and end apart: 13, of which 6 were waited for; matrix products, arithmetic and copies ran while one was open for 0% of the time, Pallas kernels for 28%

profile of v6, /device:TPU:0, one launch (start us, length us, event | category | flops | bytes accessed | tf_op | source)
XLA Modules:
  0.0 41.2 jit_solution(12933974759260655749)
XLA Ops:
  0.6 1.0 %prepare.1 = (bf16[4,3072]{1,0:T(4,128)(2,1)S(1)}, bf16[224,128]{1,0:T(8,128)(2,1)S(1)}) custom-call(bf16[4,6144]{1,0:T(4,128)(2,1)} %tokens_ref.1, f32[1,6144]{1,0:T(1,128)} %bitcast.5, bf16[4,3072]{1,0:T(4,128)(2,1)} %far_query.1, bf16[4,512]{1,0:T(4,128)(2,1)} %far_key.1, bf16[4,512]{1,0:T(4,128)(2,1)} %far_value.1), custom_call_target="tpu_custom_call" | custom-call | bytes 100000 | tf_op jit(solution)/shard_map/prepare/pallas_call | solution.py:49
  1.6 3.0 %collective-permute-start = (bf16[224,128]{1,0:T(8,128)(2,1)S(1)}, bf16[224,128]{1,0:T(8,128)(2,1)S(1)}, u32[]{:S(2)}, u32[]{:S(2)}) collective-permute-start(bf16[224,128]{1,0:T(8,128)(2,1)S(1)} %get-tuple-element.16.own_both), channel_id=1, source_target_pairs={{0,2},{2,0},{4,6},{6,4},{8,10},{10,8},{12,14},{14,12},{1,3},{3,1},... | collective-permute-start | bytes 172040 | tf_op jit(solution)/shard_map/ppermute | solution.py:28
  4.7 0.0 slice-start
  4.7 1.0 %shares.1.after.share_ref = f32[32,128]{1,0:T(8,128)S(1)} custom-call(s32[2,32]{1,0:T(2,128)} %bitcast.6, f32[2,32]{1,0:T(2,128)} %bitcast.7, bf16[4,3072]{1,0:T(4,128)(2,1)S(1)} %get-tuple-element.15.refs_0_.own_ref, bf16[1,6144,1024]{2,1,0:T(8,128)(2,1)} %gate_ref.1, bf16[1,6144,1024]{2,1,0:T(8,128)(2,1)} %up_ref.1), custom_call_target="tpu_custom_call" | custom-call | bytes 100000 | tf_op jit(solution)/shard_map/shares/pallas_call | solution.py:49
  5.7 1.2 %collective-permute-done.far_both = bf16[224,128]{1,0:T(8,128)(2,1)S(1)} collective-permute-done((bf16[224,128]{1,0:T(8,128)(2,1)S(1)}, bf16[224,128]{1,0:T(8,128)(2,1)S(1)}, u32[]{:S(2)}, u32[]{:S(2)}) %collective-permute-start) | collective-permute-done | bytes 57376 | tf_op jit(solution)/shard_map/ppermute | solution.py:28
  6.9 4.2 %collective-permute-start.2 = (bf16[8,3072]{1,0:T(8,128)(2,1)S(1)}, bf16[8,3072]{1,0:T(8,128)(2,1)S(1)}, u32[]{:S(2)}, u32[]{:S(2)}) collective-permute-start(bf16[8,3072]{1,0:T(8,128)(2,1)S(1)} %get-tuple-element.18.own_ref), channel_id=1, source_target_pairs={{0,12},{2,14},{4,8},{6,10},{8,4},{10,6},{12,0},{14,2},{1,13},{3,15... | collective-permute-start | bytes 147464 | tf_op jit(solution)/shard_map/ppermute | solution.py:28
  11.0 0.0 collective-permute-start.3
  11.0 0.6 %collective-permute-start.4 = (bf16[8,3072]{1,0:T(8,128)(2,1)S(1)}, bf16[8,3072]{1,0:T(8,128)(2,1)S(1)}, u32[]{:S(2)}, u32[]{:S(2)}) collective-permute-start(bf16[8,3072]{1,0:T(8,128)(2,1)S(1)} %get-tuple-element.18.own_ref), channel_id=1, source_target_pairs={{0,4},{2,6},{4,0},{6,2},{8,12},{10,14},{12,8},{14,10},{1,5},{3,7},... | collective-permute-start | bytes 147464 | tf_op jit(solution)/shard_map/ppermute | solution.py:28
  11.7 1.5 %collective-permute-done.2.last_ref = bf16[8,3072]{1,0:T(8,128)(2,1)S(1)} collective-permute-done((bf16[8,3072]{1,0:T(8,128)(2,1)S(1)}, bf16[8,3072]{1,0:T(8,128)(2,1)S(1)}, u32[]{:S(2)}, u32[]{:S(2)}) %collective-permute-start.2) | collective-permute-done | bytes 49184 | tf_op jit(solution)/shard_map/ppermute | solution.py:28
  13.1 2.9 %collective-permute-done.3.far_ref = bf16[8,3072]{1,0:T(8,128)(2,1)S(1)} collective-permute-done((bf16[8,3072]{1,0:T(8,128)(2,1)S(1)}, bf16[8,3072]{1,0:T(8,128)(2,1)S(1)}, u32[]{:S(2)}, u32[]{:S(2)}) %collective-permute-start.3) | collective-permute-done | bytes 49184 | tf_op jit(solution)/shard_map/ppermute | solution.py:28
  16.0 0.0 collective-permute-done.4.next_ref
  16.0 0.1 collective-permute-start.5
  16.1 2.1 %collective-permute-start.1 = (bf16[256,128]{1,0:T(8,128)(2,1)S(1)}, bf16[256,128]{1,0:T(8,128)(2,1)S(1)}, u32[]{:S(2)}, u32[]{:S(2)}) collective-permute-start(bf16[256,128]{1,0:T(8,128)(2,1)S(1)} %get-tuple-element.17.own_ref), channel_id=1, source_target_pairs={{0,8},{2,10},{4,12},{6,14},{8,0},{10,2},{12,4},{14,6},{1,9},{3,11}... | collective-permute-start | bytes 196616 | tf_op jit(solution)/shard_map/ppermute | solution.py:28
  18.2 0.0 collective-permute-done.5.other_ref
  18.2 0.0 slice-done
  18.2 0.0 slice-done.1
  18.2 0.0 slice-done.2
  18.2 0.0 copy-done
  18.3 5.0 %gate_all.1 = (bf16[32,1024]{1,0:T(8,128)(2,1)S(1)}, bf16[1024,3072]{1,0:T(8,128)(2,1)S(1)}, bf16[1024,3072]{1,0:T(8,128)(2,1)S(1)}) custom-call(bf16[32,3072]{1,0:T(8,128)(2,1)S(1)} %stack_line.1.x_ref, bf16[32,3072]{1,0:T(8,128)(2,1)S(1)} %collective-permute-done.5.other_ref, bf16[1,6144,1024]{2,1,0:T(8,128)(2,1)S(1)} %bitcast.4, ...), custom_call_target="tpu_custom_call" | custom-call | flops 805306368 | bytes 37748736 | tf_op jit(solution)/shard_map/gate_all/pallas_call | solution.py:49
  23.3 0.0 collective-permute-done.1.got_ref
  23.3 0.0 copy-start.1
  23.3 0.0 copy-start.2
  23.4 0.0 copy-start.4
  23.4 0.0 copy-start.5
  23.4 1.5 %down.2.after = bf16[32,3072]{1,0:T(8,128)(2,1)S(1)} custom-call(bf16[32,1024]{1,0:T(8,128)(2,1)S(1)} %get-tuple-element.19.after.hidden_ref, bf16[1024,3072]{1,0:T(8,128)(2,1)S(1)} %get-tuple-element.21.down_ref, bf16[512,128]{1,0:T(8,128)(2,1)S(1)} %stack_after.1.after.near_ref.refs_0_), custom_call_target="tpu_custom_call" | custom-call | flops 201326592 | bytes 6291456 | tf_op jit(solution)/shard_map/down/pallas_call | solution.py:49
  24.9 0.2 collective-permute-start.7
  25.1 0.0 collective-permute-start.6
  25.1 1.5 %down.3.terms_ref = f32[32,3072]{1,0:T(8,128)S(1)} custom-call(bf16[32,1024]{1,0:T(8,128)(2,1)S(1)} %get-tuple-element.19.after.hidden_ref, bf16[1024,3072]{1,0:T(8,128)(2,1)S(1)} %get-tuple-element.20.down_ref, bf16[32,3072]{1,0:T(8,128)(2,1)S(1)} %down.2.after), custom_call_target="tpu_custom_call" | custom-call | flops 201326592 | bytes 6291456 | tf_op jit(solution)/shard_map/down/pallas_call | solution.py:49
  26.6 0.0 collective-permute-done.7.taken_ref
  26.7 2.9 %collective-permute-start.10 = (bf16[8,3072]{1,0:T(8,128)(2,1)S(1)}, bf16[8,3072]{1,0:T(8,128)(2,1)S(1)}, u32[]{:S(2)}, u32[]{:S(2)}) collective-permute-start(bf16[8,3072]{1,0:T(8,128)(2,1)S(1)} %get-tuple-element.25), channel_id=1, source_target_pairs={{0,12},{2,14},{4,8},{6,10},{8,4},{10,6},{12,0},{14,2},{1,13},{3,15... | collective-permute-start | bytes 147464 | tf_op jit(solution)/shard_map/ppermute | solution.py:28
  29.6 0.7 %collective-permute-start.8 = (bf16[8,3072]{1,0:T(8,128)(2,1)S(1)}, bf16[8,3072]{1,0:T(8,128)(2,1)S(1)}, u32[]{:S(2)}, u32[]{:S(2)}) collective-permute-start(bf16[8,3072]{1,0:T(8,128)(2,1)S(1)} %get-tuple-element.23.after), channel_id=1, source_target_pairs={{0,8},{2,10},{4,12},{6,14},{8,0},{10,2},{12,4},{14,6},{1,9},{3,11}... | collective-permute-start | bytes 147464 | tf_op jit(solution)/shard_map/ppermute | solution.py:28
  30.2 0.9 %collective-permute-start.9 = (bf16[8,3072]{1,0:T(8,128)(2,1)S(1)}, bf16[8,3072]{1,0:T(8,128)(2,1)S(1)}, u32[]{:S(2)}, u32[]{:S(2)}) collective-permute-start(bf16[8,3072]{1,0:T(8,128)(2,1)S(1)} %get-tuple-element.24), channel_id=1, source_target_pairs={{0,4},{2,6},{4,0},{6,2},{8,12},{10,14},{12,8},{14,10},{1,5},{3,7},... | collective-permute-start | bytes 147464 | tf_op jit(solution)/shard_map/ppermute | solution.py:28
  31.1 0.0 collective-permute-done.6.far_ref.refs_1_
  31.2 0.0 copy-done.1
  31.2 0.0 copy-done.2
  31.2 0.0 copy-done.4
  31.2 0.0 copy-done.5
  31.2 2.2 %attend.1.refs_4_.refs_7_ = f32[72,128]{1,0:T(8,128)S(1)} custom-call(bf16[512,128]{1,0:T(8,128)(2,1)S(1)} %stack_after.1.after.near_ref.refs_0_, bf16[512,128]{1,0:T(8,128)(2,1)S(1)} %collective-permute-done.6.far_ref.refs_1_, bf16[4,512,512]{2,1,0:T(8,128)(2,1)S(1)} %copy-done.1, bf16[4,512,512]{2,1,0:T(8,128)(2,1)S(1)} %copy-done.2, s32[4]{0:T(128)S(1)} %copy-done.4, ...), custom_call_target="tpu_custom_call" | custom-call | flops 12582912 | bytes 2097152 | tf_op jit(solution)/shard_map/attend/pallas_call | solution.py:49
  33.4 0.0 collective-permute-done.10.refs_3_
  33.4 2.0 %collective-permute-done.8.refs_1_ = bf16[8,3072]{1,0:T(8,128)(2,1)S(1)} collective-permute-done((bf16[8,3072]{1,0:T(8,128)(2,1)S(1)}, bf16[8,3072]{1,0:T(8,128)(2,1)S(1)}, u32[]{:S(2)}, u32[]{:S(2)}) %collective-permute-start.8) | collective-permute-done | bytes 49184 | tf_op jit(solution)/shard_map/ppermute | solution.py:28
  35.4 0.0 collective-permute-done.9.refs_2_
  35.4 1.6 %collective-permute-start.11 = (bf16[4,3072]{1,0:T(4,128)(2,1)S(1)}, bf16[4,3072]{1,0:T(4,128)(2,1)S(1)}, u32[]{:S(2)}, u32[]{:S(2)}) collective-permute-start(bf16[4,3072]{1,0:T(4,128)(2,1)S(1)} %get-tuple-element.26.refs_6_), channel_id=1, source_target_pairs={{0,2},{2,0},{4,6},{6,4},{8,10},{10,8},{12,14},{14,12},{1,3},{3,1},... | collective-permute-start | bytes 73736 | tf_op jit(solution)/shard_map/ppermute | solution.py:28
  37.0 1.8 %attend_last.1.after = bf16[4,3072]{1,0:T(4,128)(2,1)} custom-call(bf16[512,128]{1,0:T(8,128)(2,1)S(1)} %stack_after.1.after.near_ref.refs_0_, bf16[512,128]{1,0:T(8,128)(2,1)S(1)} %collective-permute-done.6.far_ref.refs_1_, bf16[4,512,512]{2,1,0:T(8,128)(2,1)S(1)} %copy-done.1, bf16[4,512,512]{2,1,0:T(8,128)(2,1)S(1)} %copy-done.2, s32[4]{0:T(128)S(1)} %copy-done.4, ...), custom_call_target="tpu_custom_call" | custom-call | flops 12582912 | bytes 2097152 | tf_op jit(solution)/shard_map/attend_last/pallas_call | solution.py:49
  38.8 0.5 %collective-permute-done.11.taken_ref = bf16[4,3072]{1,0:T(4,128)(2,1)S(1)} collective-permute-done((bf16[4,3072]{1,0:T(4,128)(2,1)S(1)}, bf16[4,3072]{1,0:T(4,128)(2,1)S(1)}, u32[]{:S(2)}, u32[]{:S(2)}) %collective-permute-start.11) | collective-permute-done | bytes 24608 | tf_op jit(solution)/shard_map/ppermute | solution.py:28
  39.3 0.0 copy-done.3
  39.3 0.1 collective-permute-start.12
  39.4 1.2 %collective-permute-done.12.other_ref = bf16[4,3072]{1,0:T(4,128)(2,1)S(1)} collective-permute-done((bf16[4,3072]{1,0:T(4,128)(2,1)S(1)}, bf16[4,3072]{1,0:T(4,128)(2,1)S(1)}, u32[]{:S(2)}, u32[]{:S(2)}) %collective-permute-start.12) | collective-permute-done | bytes 24608 | tf_op jit(solution)/shard_map/ppermute | solution.py:28
  40.6 0.6 %join.1 = bf16[4,6144]{1,0:T(4,128)(2,1)} custom-call(bf16[4,3072]{1,0:T(4,128)(2,1)S(1)} %finish.1.own_ref, bf16[4,3072]{1,0:T(4,128)(2,1)S(1)} %collective-permute-done.12.other_ref), custom_call_target="tpu_custom_call" | custom-call | bytes 49152 | tf_op jit(solution)/shard_map/join/pallas_call | solution.py:49
  (11 shorter events, 0.2 us)
Async XLA Ops:
  1.6 5.2 %collective-permute-start = (bf16[224,128]{1,0:T(8,128)(2,1)S(1)}, bf16[224,128]{1,0:T(8,128)(2,1)S(1)}, u32[]{:S(2)}, u32[]{:S(2)}) collective-permute-start(bf16[224,128]{1,0:T(8,128)(2,1)S(1)} %get-tuple-element.16.own_both), channel_id=1, source_target_pairs={{0,2},{2,0},{4,6},{6,4},{8,10},{10,8},{12,14},{14,12},{1,3},{3,1},... | collective-permute-start | bytes 172040 | tf_op jit(solution)/shard_map/ppermute | solution.py:28
  4.7 13.5 %slice-start = ((s8[12582912]{0:T(1024)(128)(4,1)}), s8[4194304]{0:T(1024)(128)(4,1)S(1)}, s32[]{:S(2)}) async-start(s8[12582912]{0:T(1024)(128)(4,1)} %bitcast.3), calls=%async_computation | async-start | bytes 8388608
  4.7 13.5 %slice-start.1 = ((s8[12582912]{0:T(1024)(128)(4,1)}), s8[4194304]{0:T(1024)(128)(4,1)S(1)}, s32[]{:S(2)}) async-start(s8[12582912]{0:T(1024)(128)(4,1)} %bitcast.3), calls=%async_computation.1 | async-start | bytes 8388608
  4.7 13.5 %slice-start.2 = ((s8[12582912]{0:T(1024)(128)(4,1)}), s8[4194304]{0:T(1024)(128)(4,1)S(1)}, s32[]{:S(2)}) async-start(s8[12582912]{0:T(1024)(128)(4,1)} %bitcast.3), calls=%async_computation.2 | async-start | bytes 8388608
  4.7 13.6 %copy-start = (bf16[1,6144,1024]{2,1,0:T(8,128)(2,1)S(1)}, bf16[1,6144,1024]{2,1,0:T(8,128)(2,1)}, u32[]{:S(2)}) copy-start(bf16[1,6144,1024]{2,1,0:T(8,128)(2,1)} %up_ref.1) | copy-start | bytes 37748740
  6.9 6.3 %collective-permute-start.2 = (bf16[8,3072]{1,0:T(8,128)(2,1)S(1)}, bf16[8,3072]{1,0:T(8,128)(2,1)S(1)}, u32[]{:S(2)}, u32[]{:S(2)}) collective-permute-start(bf16[8,3072]{1,0:T(8,128)(2,1)S(1)} %get-tuple-element.18.own_ref), channel_id=1, source_target_pairs={{0,12},{2,14},{4,8},{6,10},{8,4},{10,6},{12,0},{14,2},{1,13},{3,15... | collective-permute-start | bytes 147464 | tf_op jit(solution)/shard_map/ppermute | solution.py:28
  11.0 5.0 %collective-permute-start.3 = (bf16[8,3072]{1,0:T(8,128)(2,1)S(1)}, bf16[8,3072]{1,0:T(8,128)(2,1)S(1)}, u32[]{:S(2)}, u32[]{:S(2)}) collective-permute-start(bf16[8,3072]{1,0:T(8,128)(2,1)S(1)} %get-tuple-element.18.own_ref), channel_id=1, source_target_pairs={{0,8},{2,10},{4,12},{6,14},{8,0},{10,2},{12,4},{14,6},{1,9},{3,11}... | collective-permute-start | bytes 147464 | tf_op jit(solution)/shard_map/ppermute | solution.py:28
  11.0 5.0 %collective-permute-start.4 = (bf16[8,3072]{1,0:T(8,128)(2,1)S(1)}, bf16[8,3072]{1,0:T(8,128)(2,1)S(1)}, u32[]{:S(2)}, u32[]{:S(2)}) collective-permute-start(bf16[8,3072]{1,0:T(8,128)(2,1)S(1)} %get-tuple-element.18.own_ref), channel_id=1, source_target_pairs={{0,4},{2,6},{4,0},{6,2},{8,12},{10,14},{12,8},{14,10},{1,5},{3,7},... | collective-permute-start | bytes 147464 | tf_op jit(solution)/shard_map/ppermute | solution.py:28
  16.0 2.2 %collective-permute-start.5 = (bf16[32,3072]{1,0:T(8,128)(2,1)S(1)}, bf16[32,3072]{1,0:T(8,128)(2,1)S(1)}, u32[]{:S(2)}, u32[]{:S(2)}) collective-permute-start(bf16[32,3072]{1,0:T(8,128)(2,1)S(1)} %stack_line.1.x_ref), channel_id=1, source_target_pairs={{0,1},{1,0},{2,3},{3,2},{4,5},{5,4},{6,7},{7,6},{8,9},{9,8},{10,11... | collective-permute-start | bytes 589832 | tf_op jit(solution)/shard_map/ppermute | solution.py:28
  16.1 7.2 %collective-permute-start.1 = (bf16[256,128]{1,0:T(8,128)(2,1)S(1)}, bf16[256,128]{1,0:T(8,128)(2,1)S(1)}, u32[]{:S(2)}, u32[]{:S(2)}) collective-permute-start(bf16[256,128]{1,0:T(8,128)(2,1)S(1)} %get-tuple-element.17.own_ref), channel_id=1, source_target_pairs={{0,8},{2,10},{4,12},{6,14},{8,0},{10,2},{12,4},{14,6},{1,9},{3,11}... | collective-permute-start | bytes 196616 | tf_op jit(solution)/shard_map/ppermute | solution.py:28
  23.3 7.8 %copy-start.1 = (bf16[4,512,512]{2,1,0:T(8,128)(2,1)S(1)}, bf16[4,512,512]{2,1,0:T(8,128)(2,1)}, u32[]{:S(2)}) copy-start(bf16[4,512,512]{2,1,0:T(8,128)(2,1)} %refs_2_.3) | copy-start | bytes 6291460
  23.3 7.8 %copy-start.2 = (bf16[4,512,512]{2,1,0:T(8,128)(2,1)S(1)}, bf16[4,512,512]{2,1,0:T(8,128)(2,1)}, u32[]{:S(2)}) copy-start(bf16[4,512,512]{2,1,0:T(8,128)(2,1)} %refs_3_.1) | copy-start | bytes 6291460
  23.4 7.8 %copy-start.4 = (s32[4]{0:T(128)S(1)}, s32[4]{0:T(128)}, u32[]{:S(2)}) copy-start(s32[4]{0:T(128)} %refs_4_.1) | copy-start | bytes 52
  23.4 7.8 %copy-start.5 = (s32[4]{0:T(128)S(1)}, s32[4]{0:T(128)}, u32[]{:S(2)}) copy-start(s32[4]{0:T(128)} %refs_5_.1) | copy-start | bytes 52
  24.9 1.7 %collective-permute-start.7 = (bf16[32,3072]{1,0:T(8,128)(2,1)S(1)}, bf16[32,3072]{1,0:T(8,128)(2,1)S(1)}, u32[]{:S(2)}, u32[]{:S(2)}) collective-permute-start(bf16[32,3072]{1,0:T(8,128)(2,1)S(1)} %down.2.after), channel_id=1, source_target_pairs={{0,1},{1,0},{2,3},{3,2},{4,5},{5,4},{6,7},{7,6},{8,9},{9,8},{10,11... | collective-permute-start | bytes 589832 | tf_op jit(solution)/shard_map/ppermute | solution.py:28
  25.1 6.1 %collective-permute-start.6 = (bf16[512,128]{1,0:T(8,128)(2,1)S(1)}, bf16[512,128]{1,0:T(8,128)(2,1)S(1)}, u32[]{:S(2)}, u32[]{:S(2)}) collective-permute-start(bf16[512,128]{1,0:T(8,128)(2,1)S(1)} %stack_after.1.after.near_ref.refs_0_), channel_id=1, source_target_pairs={{0,4},{2,6},{4,0},{6,2},{8,12},{10,14},{12,8},{14,10},{1,5},{3,7},... | collective-permute-start | bytes 393224 | tf_op jit(solution)/shard_map/ppermute | solution.py:28
  26.6 12.7 %copy-start.3 = (bf16[4,6144]{1,0:T(4,128)(2,1)S(1)}, bf16[4,6144]{1,0:T(4,128)(2,1)}, u32[]{:S(2)}) copy-start(bf16[4,6144]{1,0:T(4,128)(2,1)} %tokens_ref.1) | copy-start | bytes 147460
  26.7 6.7 %collective-permute-start.10 = (bf16[8,3072]{1,0:T(8,128)(2,1)S(1)}, bf16[8,3072]{1,0:T(8,128)(2,1)S(1)}, u32[]{:S(2)}, u32[]{:S(2)}) collective-permute-start(bf16[8,3072]{1,0:T(8,128)(2,1)S(1)} %get-tuple-element.25), channel_id=1, source_target_pairs={{0,12},{2,14},{4,8},{6,10},{8,4},{10,6},{12,0},{14,2},{1,13},{3,15... | collective-permute-start | bytes 147464 | tf_op jit(solution)/shard_map/ppermute | solution.py:28
  29.6 5.8 %collective-permute-start.8 = (bf16[8,3072]{1,0:T(8,128)(2,1)S(1)}, bf16[8,3072]{1,0:T(8,128)(2,1)S(1)}, u32[]{:S(2)}, u32[]{:S(2)}) collective-permute-start(bf16[8,3072]{1,0:T(8,128)(2,1)S(1)} %get-tuple-element.23.after), channel_id=1, source_target_pairs={{0,8},{2,10},{4,12},{6,14},{8,0},{10,2},{12,4},{14,6},{1,9},{3,11}... | collective-permute-start | bytes 147464 | tf_op jit(solution)/shard_map/ppermute | solution.py:28
  30.2 5.1 %collective-permute-start.9 = (bf16[8,3072]{1,0:T(8,128)(2,1)S(1)}, bf16[8,3072]{1,0:T(8,128)(2,1)S(1)}, u32[]{:S(2)}, u32[]{:S(2)}) collective-permute-start(bf16[8,3072]{1,0:T(8,128)(2,1)S(1)} %get-tuple-element.24), channel_id=1, source_target_pairs={{0,4},{2,6},{4,0},{6,2},{8,12},{10,14},{12,8},{14,10},{1,5},{3,7},... | collective-permute-start | bytes 147464 | tf_op jit(solution)/shard_map/ppermute | solution.py:28
  35.4 3.9 %collective-permute-start.11 = (bf16[4,3072]{1,0:T(4,128)(2,1)S(1)}, bf16[4,3072]{1,0:T(4,128)(2,1)S(1)}, u32[]{:S(2)}, u32[]{:S(2)}) collective-permute-start(bf16[4,3072]{1,0:T(4,128)(2,1)S(1)} %get-tuple-element.26.refs_6_), channel_id=1, source_target_pairs={{0,2},{2,0},{4,6},{6,4},{8,10},{10,8},{12,14},{14,12},{1,3},{3,1},... | collective-permute-start | bytes 73736 | tf_op jit(solution)/shard_map/ppermute | solution.py:28
  39.3 1.3 %collective-permute-start.12 = (bf16[4,3072]{1,0:T(4,128)(2,1)S(1)}, bf16[4,3072]{1,0:T(4,128)(2,1)S(1)}, u32[]{:S(2)}, u32[]{:S(2)}) collective-permute-start(bf16[4,3072]{1,0:T(4,128)(2,1)S(1)} %finish.1.own_ref), channel_id=1, source_target_pairs={{0,1},{1,0},{2,3},{3,2},{4,5},{5,4},{6,7},{7,6},{8,9},{9,8},{10,11... | collective-permute-start | bytes 73736 | tf_op jit(solution)/shard_map/ppermute | solution.py:28

commit v7 on v5

v7 whole, which is shorter than its diff:
```python
import functools
import math

import jax
import jax.numpy as jnp
from jax import lax
from jax.experimental import pallas as pl
from jax.experimental.pallas import tpu as pltpu
from jax.sharding import PartitionSpec as P

HQ = 48
KVH = 8
HD = 128
GROUP = HQ // KVH
SCALE = HD ** (-0.5)
TILE = 256
WIDE_TILE = 768
CUTS = 4
MIB = 1024 * 1024


def steps_of(wide):
    bits = int(math.log2(wide))
    return [1 << i for i in range(bits - 2)], wide >> 1, wide >> 2


def swap(block, axis, count, step):
    return lax.ppermute(block, axis, [(i, i ^ step) for i in range(count)])


def swap_by_core(block, wide, steps):
    pairs = [(2 * i + c, 2 * (i ^ step) + c) for c, step in enumerate(steps) if step for i in range(wide)]
    return lax.ppermute(block, ("wide", "narrow"), pairs)


def owner_of(place, me, steps):
    found = me
    for bit, step in enumerate(steps):
        found = found ^ (((place >> bit) & 1) * step)
    return found


def place_of(owner, me, steps):
    differ = owner ^ me
    found = 0
    for bit, step in enumerate(steps):
        shift = int(math.log2(step))
        found = found | (((differ >> shift) & 1) << bit)
    return found


def call(kernel, outs, ins, scratch=(), flops=0, size=0, limit=4, smem=(), far=()):
    spaces = [pltpu.SMEM if i in smem else pl.ANY if i in far else pltpu.VMEM for i in range(len(ins))]
    return pl.pallas_call(
        kernel,
        name=getattr(kernel, "func", kernel).__name__,
        out_shape=outs,
        in_specs=[pl.BlockSpec(memory_space=space) for space in spaces],
        out_specs=jax.tree.map(lambda _: pl.BlockSpec(memory_space=pltpu.VMEM), outs),
        scratch_shapes=list(scratch),
        compiler_params=pltpu.CompilerParams(vmem_limit_bytes=limit * MIB),
        cost_estimate=pl.CostEstimate(flops=flops, bytes_accessed=size, transcendentals=0),
    )(*ins)


def shape(dims, dtype):
    return jax.ShapeDtypeStruct(dims, dtype)


def near(array):
    return pltpu.with_memory_space_constraint(array, pltpu.VMEM)


def distant(array):
    return pltpu.with_memory_space_constraint(array, pltpu.HBM)


def prepare(far_tokens, far_gain, far_query, far_key, far_value, out_ref, heads_ref, *held):
    *near_refs, packed, sems = held
    far_refs = (far_tokens, far_gain, far_query, far_key, far_value)
    copies = [
        pltpu.make_async_copy(far, ref, sems.at[i])
        for i, (far, ref) in enumerate(zip(far_refs, near_refs))
    ]
    for copy in copies:
        copy.start()
    for copy in copies:
        copy.wait()
    tokens_ref, gain_ref, *head_refs = near_refs
    rows = out_ref.shape[0]
    values = tokens_ref[...].astype(jnp.float32)
    scale = lax.rsqrt(jnp.mean(values * values, axis=-1, keepdims=True) + 1e-05)
    out_ref[...] = (values * scale * gain_ref[...]).astype(jnp.bfloat16)
    at = 0
    each = heads_ref.shape[0] // rows
    for ref in head_refs:
        block = ref[...].astype(jnp.float32)
        for head in range(ref.shape[1] // HD):
            packed[pl.ds(at, rows, stride=each), :] = block[:, head * HD : (head + 1) * HD]
            at += 1
    heads_ref[...] = packed[...].astype(jnp.bfloat16)


def stacked(refs):
    return jnp.concatenate([ref[...].astype(jnp.float32) for ref in refs], axis=0)


def stack(own_ref, got_ref, out_ref):
    out_ref[...] = stacked([own_ref, got_ref]).astype(out_ref.dtype)


def stack_after(own_ref, got_ref, after, out_ref):
    stack(own_ref, got_ref, out_ref)


def stack_line(own_ref, second_ref, first_ref, after, out_ref):
    first = lax.axis_index("narrow") == 0
    own, one, two = (r[...].astype(jnp.float32) for r in (own_ref, first_ref, second_ref))
    both = [jnp.where(first, own, one), jnp.where(first, one, two)]
    out_ref[...] = jnp.concatenate(both, axis=0).astype(jnp.bfloat16)


def shares(steps, rows, far_routes, far_logits, *refs):
    *_, out_ref, routes_ref, logits_ref, sems = refs
    copies = [
        pltpu.make_async_copy(far_routes, routes_ref, sems.at[0]),
        pltpu.make_async_copy(far_logits, logits_ref, sems.at[1]),
    ]
    for copy in copies:
        copy.start()
    for copy in copies:
        copy.wait()
    count = out_ref.shape[0]
    core = lax.axis_index("narrow")
    me = lax.axis_index("wide") ^ (core * steps[-1])
    logits = logits_ref[...]
    first = 1.0 / (1.0 + jnp.exp(logits[1:2] - logits[0:1]))
    second = 1.0 - first
    chosen = (routes_ref[...] == core).astype(jnp.float32)
    weight_row = chosen[0:1] * first + chosen[1:2] * second
    row = lax.broadcasted_iota(jnp.int32, (count, count), 0)
    column = lax.broadcasted_iota(jnp.int32, (count, count), 1)
    shift = int(math.log2(rows))
    token = (owner_of(row >> shift, me, steps) << shift) | (row & (rows - 1))
    weight = jnp.sum(jnp.where(token == column, weight_row, 0.0), axis=1, keepdims=True)
    out_ref[...] = jnp.broadcast_to(weight, out_ref.shape)


def gate_all(
    own_ref,
    other_ref,
    gate_ref,
    up_ref,
    share_ref,
    far_down,
    hidden_out,
    near_down,
    x_ref,
    sems,
):
    span = near_down.shape[0] // CUTS
    copies = [
        pltpu.make_async_copy(
            far_down.at[0, pl.ds(i * span, span), :],
            near_down.at[pl.ds(i * span, span), :],
            sems.at[i],
        )
        for i in range(CUTS)
    ]
    for copy in copies:
        copy.start()
    tile = min(TILE, gate_ref.shape[2])
    held = own_ref.shape[0]
    x_ref[:held, :] = own_ref[...]
    x_ref[held:, :] = other_ref[...]
    weight = share_ref[:, 0:1]

    @pl.loop(0, gate_ref.shape[2] // tile)
    def _(i):
        columns = pl.ds(pl.multiple_of(i * tile, tile), tile)
        x = x_ref[...]
        gate = jnp.dot(x, gate_ref[0, :, columns], preferred_element_type=jnp.float32)
        up = jnp.dot(x, up_ref[0, :, columns], preferred_element_type=jnp.float32)
        hidden_out[:, columns] = (weight * (gate * jax.nn.sigmoid(gate)) * up).astype(jnp.bfloat16)

    for copy in copies:
        copy.wait()


def down(hidden_ref, down_ref, after, kept_ref, given_ref):
    kept = kept_ref.shape[0]

    @pl.loop(0, kept_ref.shape[1] // WIDE_TILE)
    def _(i):
        columns = pl.ds(pl.multiple_of(i * WIDE_TILE, WIDE_TILE), WIDE_TILE)
        terms = jnp.dot(
            hidden_ref[...], down_ref[:, columns], preferred_element_type=jnp.float32
        )
        kept_ref[:, columns] = terms[:kept]
        given_ref[:, columns] = terms[kept:].astype(jnp.bfloat16)


def combine(terms_ref, taken_ref, after, kept_ref, sent_ref):
    total = terms_ref[...] + taken_ref[...].astype(jnp.float32)
    kept = kept_ref.shape[0]
    kept_ref[...] = total[:kept]
    sent_ref[...] = total[kept:].astype(jnp.bfloat16)


def part_line(terms_ref, taken_ref, after, kept_ref, first_ref, second_ref):
    first = lax.axis_index("narrow") == 0
    total = terms_ref[...] + taken_ref[...].astype(jnp.float32)
    rows = kept_ref.shape[0]
    one, two = total[:rows], total[rows:]
    kept_ref[...] = jnp.where(first, one, 0.0)
    first_ref[...] = jnp.where(first, two, one).astype(jnp.bfloat16)
    second_ref[...] = two.astype(jnp.bfloat16)


def merge(kept_ref, second_ref, first_ref, after, out_ref):
    second = second_ref[...].astype(jnp.float32)
    second = jnp.where(lax.axis_index("narrow") == 0, 0.0, second)
    total = kept_ref[...] + first_ref[...].astype(jnp.float32) + second
    out_ref[...] = total.astype(jnp.bfloat16)


def finish(own_ref, other_ref, tokens_ref, out_ref):
    total = own_ref[...].astype(jnp.float32) + other_ref[...].astype(jnp.float32)
    out_ref[...] = (tokens_ref[...].astype(jnp.float32) + total).astype(jnp.bfloat16)


def attend(
    steps, taking, near_ref, far_ref, keys_ref, values_ref, lengths_ref, place_ref, after, out_ref
):
    slots, span, width = keys_ref.shape
    rows = slots
    kv_local = width // HD
    heads = kv_local * GROUP
    each = heads + 2 * kv_local
    me = lax.axis_index("wide")
    shift = int(math.log2(rows))
    half = near_ref.shape[0]
    head_of = lax.broadcasted_iota(jnp.int32, (heads, 1), 0)
    positions = lax.broadcasted_iota(jnp.int32, (heads, span), 1)

    def by_group(pieces):
        result = pieces[0]
        for g in range(1, kv_local):
            result = jnp.where(head_of >= g * GROUP, pieces[g], result)
        return result

    for order, slot in enumerate(taking):
        request = place_ref[slot]
        at = (place_of(request >> shift, me, steps) << shift) | (request & (rows - 1))
        at = at * each
        inside = pl.ds(pl.multiple_of(jnp.where(at < half, at, at - half), each), each)
        block = jnp.where(at < half, near_ref[inside, :], far_ref[inside, :])
        query = block[:heads]
        own = block[heads:].astype(jnp.float32)
        own_key = by_group([own[g : g + 1] for g in range(kv_local)])
        own_value = by_group([own[kv_local + g : kv_local + g + 1] for g in range(kv_local)])
        own_score = jnp.sum(query.astype(jnp.float32) * own_key, axis=1, keepdims=True) * SCALE
        scores = by_group(
            [
                lax.dot_general(
                    query,
                    keys_ref[slot, :, g * HD : (g + 1) * HD],
                    (((1,), (1,)), ((), ())),
                    preferred_element_type=jnp.float32,
                )
                for g in range(kv_local)
            ]
        )
        scores = jnp.where(positions < lengths_ref[slot], scores * SCALE, -jnp.inf)
        row_max = jnp.maximum(jnp.max(scores, axis=1, keepdims=True), own_score)
        weights = jnp.exp(scores - row_max)
        own_weight = jnp.exp(own_score - row_max)
        total = jnp.sum(weights, axis=1, keepdims=True) + own_weight
        probs = (weights / total).astype(jnp.bfloat16)
        own_prob = (own_weight / total).astype(jnp.bfloat16).astype(jnp.float32)
        mixed = by_group(
            [
                jnp.dot(
                    probs,
                    values_ref[slot, :, g * HD : (g + 1) * HD],
                    preferred_element_type=jnp.float32,
                )
                for g in range(kv_local)
            ]
        )
        out_ref[order * heads : (order + 1) * heads, :] = mixed + own_prob * own_value


def lay_out(heads, pieces, out_ref, held):
    at = 0
    for piece in pieces:
        held[at : at + piece.shape[0], :] = piece[...]
        at += piece.shape[0]
    for head in range(heads):
        out_ref[:, head * HD : (head + 1) * HD] = held[
            pl.ds(head, out_ref.shape[0], stride=heads), :
        ].astype(jnp.bfloat16)


def attend_last(steps, taking, heads, *refs):
    *ins, early, out_ref, late, held = refs
    attend(steps, taking, *ins, late)
    lay_out(heads, [early, late], out_ref, held)


def make_local(wide):
    short, far_step, near_step = steps_of(wide)
    steps = [far_step, *short, near_step]
    head_steps = [*short, far_step, near_step]

    def local(
        queries,
        new_keys,
        new_values,
        key_cache,
        value_cache,
        lengths,
        assignment,
        tokens,
        norm_gain,
        routes,
        route_logits,
        w_gate,
        w_up,
        w_down,
    ):
        rows, width = tokens.shape
        half = width // 2
        units = w_gate.shape[2]
        count = rows * wide
        each = (queries.shape[1] + 2 * new_keys.shape[1]) // HD
        bf16, f32 = jnp.bfloat16, jnp.float32
        heads_local = queries.shape[1] // HD
        slots = queries.shape[0]
        dma = pltpu.SemaphoreType.DMA
        piece_bytes = 2 * half * units
        product = 2 * count * half * units

        firsts = [tokens, norm_gain[None], queries, new_keys, new_values]
        x, heads = call(
            prepare,
            [shape((rows, width), bf16), shape((rows * each, HD), bf16)],
            [distant(a) for a in firsts],
            [pltpu.VMEM(a.shape, a.dtype) for a in firsts]
            + [pltpu.VMEM((rows * each, HD), f32), dma((len(firsts),))],
            size=100000,
            far=range(len(firsts)),
        )
        share = call(
            functools.partial(shares, steps, rows),
            shape((count, HD), f32),
            [distant(routes.T), distant(route_logits.T), x, distant(w_gate), distant(w_up)],
            [
                pltpu.VMEM(routes.T.shape, jnp.int32),
                pltpu.VMEM(route_logits.T.shape, f32),
                dma((2,)),
            ],
            size=100000,
            far=range(5),
        )
        second = swap_by_core(x, wide, [0, far_step ^ near_step])
        first = swap_by_core(x, wide, [far_step, near_step])
        x = call(
            stack_line,
            shape((2 * rows, width), bf16),
            [x, second, first, share],
            size=8 * rows * width,
            far=(3,),
        )
        for step in short:
            got_heads = swap(heads, "wide", wide, step)
            heads = call(
                stack, shape((2 * heads.shape[0], HD), bf16), [heads, got_heads], size=4 * heads.size
            )
            x = call(
                stack_after,
                shape((2 * x.shape[0], width), bf16),
                [x, swap(x, "wide", wide, step), heads],
                size=8 * x.size,
                far=(2,),
            )
        got_heads = swap(heads, "wide", wide, far_step)
        other_x = swap(x, "narrow", 2, 1)
        hidden, near_down = call(
            gate_all,
            [shape((count, units), bf16), pltpu.VMEM((units, width), bf16)],
            [x, other_x, near(w_gate), near(w_up), share, distant(w_down)],
            [pltpu.VMEM((count, width), bf16), dma((CUTS,))],
            flops=4 * product,
            size=6 * piece_bytes,
            far=(5,),
        )
        heads = call(
            stack_after,
            shape((2 * heads.shape[0], HD), bf16),
            [heads, got_heads, hidden],
            size=8 * heads.size,
            far=(2,),
        )
        terms, given = call(
            down,
            [shape((count // 2, width), f32), shape((count // 2, width), bf16)],
            [hidden, near(near_down), heads],
            flops=2 * product,
            size=2 * piece_bytes,
            far=(2,),
        )
        taken = swap(given, "narrow", 2, 1)
        far_heads = swap(heads, "wide", wide, near_step)

        caches = [near(key_cache), near(value_cache), lengths, assignment]
        early_slots = list(range(slots - 1))
        late_slots = list(range(slots - 1, slots))
        early = hidden
        for step in reversed(short):
            kept = terms.shape[0] // 2
            terms, sent = call(
                combine,
                [shape((kept, width), f32), shape((kept, width), bf16)],
                [terms, taken, early],
                size=12 * kept * width,
                far=(2,),
            )
            taken = swap(sent, "wide", wide, step)
            if early is hidden:
                early = call(
                    functools.partial(attend, head_steps, early_slots),
                    shape((len(early_slots) * heads_local, HD), f32),
                    [heads, far_heads, *caches, sent],
                    flops=2 * key_cache.size * GROUP,
                    size=2 * key_cache.size,
                    smem=(4, 5),
                    far=(6,),
                )
        block = shape((rows, width), bf16)
        terms, first, second = call(
            part_line,
            [shape((rows, width), f32), block, block],
            [terms, taken, early],
            size=12 * rows * width,
            far=(2,),
        )
        second_taken = swap_by_core(second, wide, [0, far_step ^ near_step])
        first_taken = swap_by_core(first, wide, [far_step, near_step])
        context = call(
            functools.partial(attend_last, head_steps, late_slots, heads_local),
            shape(queries.shape, bf16),
            [heads, far_heads, *caches, first, early],
            [
                pltpu.VMEM((len(late_slots) * heads_local, HD), f32),
                pltpu.VMEM((slots * heads_local, HD), f32),
            ],
            flops=2 * key_cache.size * GROUP,
            size=2 * key_cache.size,
            smem=(4, 5),
            far=(6,),
        )
        part = call(
            merge,
            block,
            [terms, second_taken, first_taken, distant(context)],
            size=12 * rows * width,
            far=(3,),
        )
        other = swap(part, "narrow", 2, 1)
        mixed_out = call(finish, block, [part, other, tokens], size=8 * rows * width)
        return (context, mixed_out)

    return local


def solution(mesh):
    placed = (
        P(("groups", "wide"), "narrow"),
        P(("groups", "wide"), "narrow"),
        P(("groups", "wide"), "narrow"),
        P(("groups", "wide"), None, "narrow"),
        P(("groups", "wide"), None, "narrow"),
        P(("groups", "wide")),
        P(("groups", "wide")),
        P(("groups", "wide"), None),
        P(),
        P("groups", None),
        P("groups", None),
        P("narrow", None, "wide"),
        P("narrow", None, "wide"),
        P("narrow", "wide", None),
    )
    return jax.shard_map(
        make_local(mesh.shape["wide"]),
        mesh=mesh,
        in_specs=placed,
        out_specs=(P(("groups", "wide"), "narrow"), P(("groups", "wide"), None)),
        check_vma=False,
    )
```

time: 42.4 us -> 43.1 us (1.017)
  starting transfers between devices: 12.4 us -> 16.1 us
  waiting for transfers between devices: 14 us -> 11 us
    ppermute x0 -> x4, starting transfers between devices: none -> 6.78 us  [swap_by_core(): return lax.ppermute(block, ('wide', 'narrow'), pairs)]
    ppermute x13 -> x8, waiting for transfers between devices: 14 us -> 7.42 us  [swap(): return lax.ppermute(block, axis, [(i, i ^ step) for i in range(count)])]
    ppermute x0 -> x4, waiting for transfers between devices: none -> 3.56 us  [swap_by_core(): return lax.ppermute(block, ('wide', 'narrow'), pairs)]
    ppermute x13 -> x8, starting transfers between devices: 12.4 us -> 9.34 us  [swap(): return lax.ppermute(block, axis, [(i, i ^ step) for i in range(count)])]
    pallas_call x13 -> x14, Pallas kernels: 14.8 us -> 14.9 us  [call(): pl.pallas_call(kernel, name=getattr(kernel, 'func', kernel).__name__, out...]
  transfers between devices with their start and end apart: 13 -> 12, of which waited for: 8 -> 5; matrix products, arithmetic and copies ran while one was open for 0% -> 0% of each run, Pallas kernels for 27% -> 23%
where the time goes in v7:
time: 43.1 us; the launch traced here: 42.9 us
  starting transfers between devices  16.1 us (37%)
  Pallas kernels  14.9 us (35%)
  waiting for transfers between devices  11 us (26%)
  between operations  0.82 us (2%)
    pallas_call x14, Pallas kernels, call(): pl.pallas_call(kernel, name=getattr(kernel, 'func', kernel).__name__, out...  14.9 us
    ppermute x8, starting transfers between devices, swap(): return lax.ppermute(block, axis, [(i, i ^ step) for i in range(count)])  9.34 us
    ppermute x8, waiting for transfers between devices, swap(): return lax.ppermute(block, axis, [(i, i ^ step) for i in range(count)])  7.42 us
    ppermute x4, starting transfers between devices, swap_by_core(): return lax.ppermute(block, ('wide', 'narrow'), pairs)  6.78 us
    ppermute x4, waiting for transfers between devices, swap_by_core(): return lax.ppermute(block, ('wide', 'narrow'), pairs)  3.56 us
  transfers between devices with their start and end apart: 12, of which 5 were waited for; matrix products, arithmetic and copies ran while one was open for 0% of the time, Pallas kernels for 23%

profile of v7, /device:TPU:0, one launch (start us, length us, event | category | flops | bytes accessed | tf_op | source)
XLA Modules:
  0.0 42.9 jit_solution(1541412242062301736)
XLA Ops:
  0.6 1.0 %prepare.1 = (bf16[4,6144]{1,0:T(4,128)(2,1)S(1)}, bf16[128,128]{1,0:T(8,128)(2,1)S(1)}) custom-call(bf16[4,6144]{1,0:T(4,128)(2,1)} %tokens_ref.1, f32[1,6144]{1,0:T(1,128)} %bitcast.3, bf16[4,3072]{1,0:T(4,128)(2,1)} %far_query.1, bf16[4,512]{1,0:T(4,128)(2,1)} %far_key.1, bf16[4,512]{1,0:T(4,128)(2,1)} %far_value.1), custom_call_target="tpu_custom_call" | custom-call | bytes 100000 | tf_op jit(solution)/shard_map/prepare/pallas_call | solution.py:54
  1.6 4.1 %collective-permute-start.3 = (bf16[4,6144]{1,0:T(4,128)(2,1)S(1)}, bf16[4,6144]{1,0:T(4,128)(2,1)S(1)}, u32[]{:S(2)}, u32[]{:S(2)}) collective-permute-start(bf16[4,6144]{1,0:T(4,128)(2,1)S(1)} %get-tuple-element.14.refs_0_.own_ref), channel_id=1, source_target_pairs={{0,8},{2,10},{4,12},{6,14},{8,0},{10,2},{12,4},{14,6},{1,5},{3,7},... | collective-permute-start | bytes 147464 | tf_op jit(solution)/shard_map/ppermute | solution.py:33
  5.7 0.7 %collective-permute-start.2 = (bf16[4,6144]{1,0:T(4,128)(2,1)S(1)}, bf16[4,6144]{1,0:T(4,128)(2,1)S(1)}, u32[]{:S(2)}, u32[]{:S(2)}) collective-permute-start(bf16[4,6144]{1,0:T(4,128)(2,1)S(1)} %get-tuple-element.14.refs_0_.own_ref), channel_id=1, source_target_pairs={{1,13},{3,15},{5,9},{7,11},{9,5},{11,7},{13,1},{15,3},{17,29},{19,... | collective-permute-start | bytes 147464 | tf_op jit(solution)/shard_map/ppermute | solution.py:33
  6.4 0.0 copy-start
  6.4 0.0 copy-start.1
  6.4 1.0 %shares.1.after.share_ref = f32[32,128]{1,0:T(8,128)S(1)} custom-call(s32[2,32]{1,0:T(2,128)} %bitcast.4, f32[2,32]{1,0:T(2,128)} %bitcast.5, bf16[4,6144]{1,0:T(4,128)(2,1)S(1)} %get-tuple-element.14.refs_0_.own_ref, bf16[1,6144,1024]{2,1,0:T(8,128)(2,1)} %gate_ref.1, bf16[1,6144,1024]{2,1,0:T(8,128)(2,1)} %up_ref.1), custom_call_target="tpu_custom_call" | custom-call | bytes 100000 | tf_op jit(solution)/shard_map/shares/pallas_call | solution.py:54
  7.4 0.4 collective-permute-done.3.first_ref
  7.8 0.0 collective-permute-done.2.second_ref
  7.9 1.9 %collective-permute-start.4 = (bf16[8,6144]{1,0:T(8,128)(2,1)S(1)}, bf16[8,6144]{1,0:T(8,128)(2,1)S(1)}, u32[]{:S(2)}, u32[]{:S(2)}) collective-permute-start(bf16[8,6144]{1,0:T(8,128)(2,1)S(1)} %stack_line.1.own_ref), channel_id=1, source_target_pairs={{0,2},{2,0},{4,6},{6,4},{8,10},{10,8},{12,14},{14,12},{1,3},{3,1},... | collective-permute-start | bytes 294920 | tf_op jit(solution)/shard_map/ppermute | solution.py:28
  9.8 0.2 collective-permute-start
  10.0 3.8 %collective-permute-done.got_ref = bf16[128,128]{1,0:T(8,128)(2,1)S(1)} collective-permute-done((bf16[128,128]{1,0:T(8,128)(2,1)S(1)}, bf16[128,128]{1,0:T(8,128)(2,1)S(1)}, u32[]{:S(2)}, u32[]{:S(2)}) %collective-permute-start) | collective-permute-done | bytes 32800 | tf_op jit(solution)/shard_map/ppermute | solution.py:28
  13.8 0.0 collective-permute-done.4.got_ref
  13.8 1.3 %collective-permute-start.5 = (bf16[16,6144]{1,0:T(8,128)(2,1)S(1)}, bf16[16,6144]{1,0:T(8,128)(2,1)S(1)}, u32[]{:S(2)}, u32[]{:S(2)}) collective-permute-start(bf16[16,6144]{1,0:T(8,128)(2,1)S(1)} %stack_after.2.own_ref), channel_id=1, source_target_pairs={{0,1},{1,0},{2,3},{3,2},{4,5},{5,4},{6,7},{7,6},{8,9},{9,8},{10,11... | collective-permute-start | bytes 589832 | tf_op jit(solution)/shard_map/ppermute | solution.py:28
  15.1 2.3 %collective-permute-start.1 = (bf16[256,128]{1,0:T(8,128)(2,1)S(1)}, bf16[256,128]{1,0:T(8,128)(2,1)S(1)}, u32[]{:S(2)}, u32[]{:S(2)}) collective-permute-start(bf16[256,128]{1,0:T(8,128)(2,1)S(1)} %stack.1.after.own_ref), channel_id=1, source_target_pairs={{0,8},{2,10},{4,12},{6,14},{8,0},{10,2},{12,4},{14,6},{1,9},{3,11}... | collective-permute-start | bytes 196616 | tf_op jit(solution)/shard_map/ppermute | solution.py:28
  17.4 0.0 collective-permute-done.5.other_ref
  17.4 0.0 copy-done
  17.4 0.0 copy-done.1
  17.4 5.0 %gate_all.1 = (bf16[32,1024]{1,0:T(8,128)(2,1)S(1)}, bf16[1024,6144]{1,0:T(8,128)(2,1)S(1)}) custom-call(bf16[16,6144]{1,0:T(8,128)(2,1)S(1)} %stack_after.2.own_ref, bf16[16,6144]{1,0:T(8,128)(2,1)S(1)} %collective-permute-done.5.other_ref, bf16[1,6144,1024]{2,1,0:T(8,128)(2,1)S(1)} %copy-done, bf16[1,6144,1024]{2,1,0:T(8,128)(2,1)S(1)} %copy-done.1, ...), custom_call_target="tpu_custom_call" | custom-call | flops 805306368 | bytes 37748736 | tf_op jit(solution)/shard_map/gate_all/pallas_call | solution.py:54
  22.4 0.0 copy-start.2
  22.4 0.0 copy-start.3
  22.4 0.0 copy-start.5
  22.5 0.0 copy-start.6
  22.5 0.0 copy-start.4
  22.5 0.0 collective-permute-done.1.got_ref
  22.5 3.1 %down.1 = (f32[16,6144]{1,0:T(8,128)S(1)}, bf16[16,6144]{1,0:T(8,128)(2,1)S(1)}) custom-call(bf16[32,1024]{1,0:T(8,128)(2,1)S(1)} %get-tuple-element.15.after.hidden_ref, bf16[1024,6144]{1,0:T(8,128)(2,1)S(1)} %get-tuple-element.16.down_ref, bf16[512,128]{1,0:T(8,128)(2,1)S(1)} %stack_after.3.after.near_ref.refs_0_), custom_call_target="tpu_custom_call" | custom-call | flops 402653184 | bytes 12582912 | tf_op jit(solution)/shard_map/down/pallas_call | solution.py:54
  25.6 0.2 collective-permute-start.7
  25.8 1.7 %collective-permute-start.6 = (bf16[512,128]{1,0:T(8,128)(2,1)S(1)}, bf16[512,128]{1,0:T(8,128)(2,1)S(1)}, u32[]{:S(2)}, u32[]{:S(2)}) collective-permute-start(bf16[512,128]{1,0:T(8,128)(2,1)S(1)} %stack_after.3.after.near_ref.refs_0_), channel_id=1, source_target_pairs={{0,4},{2,6},{4,0},{6,2},{8,12},{10,14},{12,8},{14,10},{1,5},{3,7},... | collective-permute-start | bytes 393224 | tf_op jit(solution)/shard_map/ppermute | solution.py:28
  27.5 0.0 collective-permute-done.7.taken_ref
  27.6 1.6 %collective-permute-start.8 = (bf16[8,6144]{1,0:T(8,128)(2,1)S(1)}, bf16[8,6144]{1,0:T(8,128)(2,1)S(1)}, u32[]{:S(2)}, u32[]{:S(2)}) collective-permute-start(bf16[8,6144]{1,0:T(8,128)(2,1)S(1)} %get-tuple-element.20.after), channel_id=1, source_target_pairs={{0,2},{2,0},{4,6},{6,4},{8,10},{10,8},{12,14},{14,12},{1,3},{3,1},... | collective-permute-start | bytes 294920 | tf_op jit(solution)/shard_map/ppermute | solution.py:28
  29.1 2.5 %collective-permute-done.6.far_ref.refs_1_ = bf16[512,128]{1,0:T(8,128)(2,1)S(1)} collective-permute-done((bf16[512,128]{1,0:T(8,128)(2,1)S(1)}, bf16[512,128]{1,0:T(8,128)(2,1)S(1)}, u32[]{:S(2)}, u32[]{:S(2)}) %collective-permute-start.6) | collective-permute-done | bytes 131104 | tf_op jit(solution)/shard_map/ppermute | solution.py:28
  31.6 0.0 copy-done.2
  31.6 0.0 copy-done.3
  31.6 0.0 copy-done.5
  31.6 0.0 copy-done.6
  31.6 2.2 %attend.1.after.refs_7_ = f32[72,128]{1,0:T(8,128)S(1)} custom-call(bf16[512,128]{1,0:T(8,128)(2,1)S(1)} %stack_after.3.after.near_ref.refs_0_, bf16[512,128]{1,0:T(8,128)(2,1)S(1)} %collective-permute-done.6.far_ref.refs_1_, bf16[4,512,512]{2,1,0:T(8,128)(2,1)S(1)} %copy-done.2, bf16[4,512,512]{2,1,0:T(8,128)(2,1)S(1)} %copy-done.3, s32[4]{0:T(128)S(1)} %copy-done.5, ...), custom_call_target="tpu_custom_call" | custom-call | flops 12582912 | bytes 2097152 | tf_op jit(solution)/shard_map/attend/pallas_call | solution.py:54
  33.8 0.0 collective-permute-done.8.taken_ref
  33.8 0.1 part_line.1
  33.9 0.7 %collective-permute-start.9 = (bf16[4,6144]{1,0:T(4,128)(2,1)S(1)}, bf16[4,6144]{1,0:T(4,128)(2,1)S(1)}, u32[]{:S(2)}, u32[]{:S(2)}) collective-permute-start(bf16[4,6144]{1,0:T(4,128)(2,1)S(1)} %get-tuple-element.23), channel_id=1, source_target_pairs={{1,13},{3,15},{5,9},{7,11},{9,5},{11,7},{13,1},{15,3},{17,29},{19,... | collective-permute-start | bytes 147464 | tf_op jit(solution)/shard_map/ppermute | solution.py:33
  34.6 1.4 %collective-permute-start.10 = (bf16[4,6144]{1,0:T(4,128)(2,1)S(1)}, bf16[4,6144]{1,0:T(4,128)(2,1)S(1)}, u32[]{:S(2)}, u32[]{:S(2)}) collective-permute-start(bf16[4,6144]{1,0:T(4,128)(2,1)S(1)} %get-tuple-element.21.refs_6_), channel_id=1, source_target_pairs={{0,8},{2,10},{4,12},{6,14},{8,0},{10,2},{12,4},{14,6},{1,5},{3,7},... | collective-permute-start | bytes 147464 | tf_op jit(solution)/shard_map/ppermute | solution.py:33
  35.9 1.8 %attend_last.1.after = bf16[4,3072]{1,0:T(4,128)(2,1)} custom-call(bf16[512,128]{1,0:T(8,128)(2,1)S(1)} %stack_after.3.after.near_ref.refs_0_, bf16[512,128]{1,0:T(8,128)(2,1)S(1)} %collective-permute-done.6.far_ref.refs_1_, bf16[4,512,512]{2,1,0:T(8,128)(2,1)S(1)} %copy-done.2, bf16[4,512,512]{2,1,0:T(8,128)(2,1)S(1)} %copy-done.3, s32[4]{0:T(128)S(1)} %copy-done.5, ...), custom_call_target="tpu_custom_call" | custom-call | flops 12582912 | bytes 2097152 | tf_op jit(solution)/shard_map/attend_last/pallas_call | solution.py:54
  37.7 0.0 collective-permute-done.9.second_ref
  37.7 3.1 %collective-permute-done.10.first_ref = bf16[4,6144]{1,0:T(4,128)(2,1)S(1)} collective-permute-done((bf16[4,6144]{1,0:T(4,128)(2,1)S(1)}, bf16[4,6144]{1,0:T(4,128)(2,1)S(1)}, u32[]{:S(2)}, u32[]{:S(2)}) %collective-permute-start.10) | collective-permute-done | bytes 49184 | tf_op jit(solution)/shard_map/ppermute | solution.py:33
  40.9 0.2 collective-permute-start.11
  41.1 1.1 %collective-permute-done.11.other_ref = bf16[4,6144]{1,0:T(4,128)(2,1)S(1)} collective-permute-done((bf16[4,6144]{1,0:T(4,128)(2,1)S(1)}, bf16[4,6144]{1,0:T(4,128)(2,1)S(1)}, u32[]{:S(2)}, u32[]{:S(2)}) %collective-permute-start.11) | collective-permute-done | bytes 49184 | tf_op jit(solution)/shard_map/ppermute | solution.py:28
  42.2 0.0 copy-done.4
  42.2 0.7 %finish.1 = bf16[4,6144]{1,0:T(4,128)(2,1)} custom-call(bf16[4,6144]{1,0:T(4,128)(2,1)S(1)} %merge.1.own_ref, bf16[4,6144]{1,0:T(4,128)(2,1)S(1)} %collective-permute-done.11.other_ref, bf16[4,6144]{1,0:T(4,128)(2,1)S(1)} %copy-done.4), custom_call_target="tpu_custom_call" | custom-call | bytes 196608 | tf_op jit(solution)/shard_map/finish/pallas_call | solution.py:54
  (6 shorter events, 0.2 us)
Async XLA Ops:
  1.6 6.2 %collective-permute-start.3 = (bf16[4,6144]{1,0:T(4,128)(2,1)S(1)}, bf16[4,6144]{1,0:T(4,128)(2,1)S(1)}, u32[]{:S(2)}, u32[]{:S(2)}) collective-permute-start(bf16[4,6144]{1,0:T(4,128)(2,1)S(1)} %get-tuple-element.14.refs_0_.own_ref), channel_id=1, source_target_pairs={{0,8},{2,10},{4,12},{6,14},{8,0},{10,2},{12,4},{14,6},{1,5},{3,7},... | collective-permute-start | bytes 147464 | tf_op jit(solution)/shard_map/ppermute | solution.py:33
  5.7 2.1 %collective-permute-start.2 = (bf16[4,6144]{1,0:T(4,128)(2,1)S(1)}, bf16[4,6144]{1,0:T(4,128)(2,1)S(1)}, u32[]{:S(2)}, u32[]{:S(2)}) collective-permute-start(bf16[4,6144]{1,0:T(4,128)(2,1)S(1)} %get-tuple-element.14.refs_0_.own_ref), channel_id=1, source_target_pairs={{1,13},{3,15},{5,9},{7,11},{9,5},{11,7},{13,1},{15,3},{17,29},{19,... | collective-permute-start | bytes 147464 | tf_op jit(solution)/shard_map/ppermute | solution.py:33
  6.4 11.0 %copy-start = (bf16[1,6144,1024]{2,1,0:T(8,128)(2,1)S(1)}, bf16[1,6144,1024]{2,1,0:T(8,128)(2,1)}, u32[]{:S(2)}) copy-start(bf16[1,6144,1024]{2,1,0:T(8,128)(2,1)} %gate_ref.1) | copy-start | bytes 37748740
  6.4 11.0 %copy-start.1 = (bf16[1,6144,1024]{2,1,0:T(8,128)(2,1)S(1)}, bf16[1,6144,1024]{2,1,0:T(8,128)(2,1)}, u32[]{:S(2)}) copy-start(bf16[1,6144,1024]{2,1,0:T(8,128)(2,1)} %up_ref.1) | copy-start | bytes 37748740
  7.9 5.9 %collective-permute-start.4 = (bf16[8,6144]{1,0:T(8,128)(2,1)S(1)}, bf16[8,6144]{1,0:T(8,128)(2,1)S(1)}, u32[]{:S(2)}, u32[]{:S(2)}) collective-permute-start(bf16[8,6144]{1,0:T(8,128)(2,1)S(1)} %stack_line.1.own_ref), channel_id=1, source_target_pairs={{0,2},{2,0},{4,6},{6,4},{8,10},{10,8},{12,14},{14,12},{1,3},{3,1},... | collective-permute-start | bytes 294920 | tf_op jit(solution)/shard_map/ppermute | solution.py:28
  9.8 4.0 %collective-permute-start = (bf16[128,128]{1,0:T(8,128)(2,1)S(1)}, bf16[128,128]{1,0:T(8,128)(2,1)S(1)}, u32[]{:S(2)}, u32[]{:S(2)}) collective-permute-start(bf16[128,128]{1,0:T(8,128)(2,1)S(1)} %get-tuple-element.13.own_ref), channel_id=1, source_target_pairs={{0,2},{2,0},{4,6},{6,4},{8,10},{10,8},{12,14},{14,12},{1,3},{3,1},... | collective-permute-start | bytes 98312 | tf_op jit(solution)/shard_map/ppermute | solution.py:28
  13.8 3.6 %collective-permute-start.5 = (bf16[16,6144]{1,0:T(8,128)(2,1)S(1)}, bf16[16,6144]{1,0:T(8,128)(2,1)S(1)}, u32[]{:S(2)}, u32[]{:S(2)}) collective-permute-start(bf16[16,6144]{1,0:T(8,128)(2,1)S(1)} %stack_after.2.own_ref), channel_id=1, source_target_pairs={{0,1},{1,0},{2,3},{3,2},{4,5},{5,4},{6,7},{7,6},{8,9},{9,8},{10,11... | collective-permute-start | bytes 589832 | tf_op jit(solution)/shard_map/ppermute | solution.py:28
  15.1 7.3 %collective-permute-start.1 = (bf16[256,128]{1,0:T(8,128)(2,1)S(1)}, bf16[256,128]{1,0:T(8,128)(2,1)S(1)}, u32[]{:S(2)}, u32[]{:S(2)}) collective-permute-start(bf16[256,128]{1,0:T(8,128)(2,1)S(1)} %stack.1.after.own_ref), channel_id=1, source_target_pairs={{0,8},{2,10},{4,12},{6,14},{8,0},{10,2},{12,4},{14,6},{1,9},{3,11}... | collective-permute-start | bytes 196616 | tf_op jit(solution)/shard_map/ppermute | solution.py:28
  22.4 9.2 %copy-start.2 = (bf16[4,512,512]{2,1,0:T(8,128)(2,1)S(1)}, bf16[4,512,512]{2,1,0:T(8,128)(2,1)}, u32[]{:S(2)}) copy-start(bf16[4,512,512]{2,1,0:T(8,128)(2,1)} %refs_2_.3) | copy-start | bytes 6291460
  22.4 9.2 %copy-start.3 = (bf16[4,512,512]{2,1,0:T(8,128)(2,1)S(1)}, bf16[4,512,512]{2,1,0:T(8,128)(2,1)}, u32[]{:S(2)}) copy-start(bf16[4,512,512]{2,1,0:T(8,128)(2,1)} %refs_3_.1) | copy-start | bytes 6291460
  22.4 9.2 %copy-start.5 = (s32[4]{0:T(128)S(1)}, s32[4]{0:T(128)}, u32[]{:S(2)}) copy-start(s32[4]{0:T(128)} %refs_4_.1) | copy-start | bytes 52
  22.5 9.2 %copy-start.6 = (s32[4]{0:T(128)S(1)}, s32[4]{0:T(128)}, u32[]{:S(2)}) copy-start(s32[4]{0:T(128)} %refs_5_.1) | copy-start | bytes 52
  22.5 19.8 %copy-start.4 = (bf16[4,6144]{1,0:T(4,128)(2,1)S(1)}, bf16[4,6144]{1,0:T(4,128)(2,1)}, u32[]{:S(2)}) copy-start(bf16[4,6144]{1,0:T(4,128)(2,1)} %tokens_ref.1) | copy-start | bytes 147460
  25.6 1.9 %collective-permute-start.7 = (bf16[16,6144]{1,0:T(8,128)(2,1)S(1)}, bf16[16,6144]{1,0:T(8,128)(2,1)S(1)}, u32[]{:S(2)}, u32[]{:S(2)}) collective-permute-start(bf16[16,6144]{1,0:T(8,128)(2,1)S(1)} %get-tuple-element.18), channel_id=1, source_target_pairs={{0,1},{1,0},{2,3},{3,2},{4,5},{5,4},{6,7},{7,6},{8,9},{9,8},{10,11... | collective-permute-start | bytes 589832 | tf_op jit(solution)/shard_map/ppermute | solution.py:28
  25.8 5.8 %collective-permute-start.6 = (bf16[512,128]{1,0:T(8,128)(2,1)S(1)}, bf16[512,128]{1,0:T(8,128)(2,1)S(1)}, u32[]{:S(2)}, u32[]{:S(2)}) collective-permute-start(bf16[512,128]{1,0:T(8,128)(2,1)S(1)} %stack_after.3.after.near_ref.refs_0_), channel_id=1, source_target_pairs={{0,4},{2,6},{4,0},{6,2},{8,12},{10,14},{12,8},{14,10},{1,5},{3,7},... | collective-permute-start | bytes 393224 | tf_op jit(solution)/shard_map/ppermute | solution.py:28
  27.6 6.3 %collective-permute-start.8 = (bf16[8,6144]{1,0:T(8,128)(2,1)S(1)}, bf16[8,6144]{1,0:T(8,128)(2,1)S(1)}, u32[]{:S(2)}, u32[]{:S(2)}) collective-permute-start(bf16[8,6144]{1,0:T(8,128)(2,1)S(1)} %get-tuple-element.20.after), channel_id=1, source_target_pairs={{0,2},{2,0},{4,6},{6,4},{8,10},{10,8},{12,14},{14,12},{1,3},{3,1},... | collective-permute-start | bytes 294920 | tf_op jit(solution)/shard_map/ppermute | solution.py:28
  33.9 3.8 %collective-permute-start.9 = (bf16[4,6144]{1,0:T(4,128)(2,1)S(1)}, bf16[4,6144]{1,0:T(4,128)(2,1)S(1)}, u32[]{:S(2)}, u32[]{:S(2)}) collective-permute-start(bf16[4,6144]{1,0:T(4,128)(2,1)S(1)} %get-tuple-element.23), channel_id=1, source_target_pairs={{1,13},{3,15},{5,9},{7,11},{9,5},{11,7},{13,1},{15,3},{17,29},{19,... | collective-permute-start | bytes 147464 | tf_op jit(solution)/shard_map/ppermute | solution.py:33
  34.6 6.3 %collective-permute-start.10 = (bf16[4,6144]{1,0:T(4,128)(2,1)S(1)}, bf16[4,6144]{1,0:T(4,128)(2,1)S(1)}, u32[]{:S(2)}, u32[]{:S(2)}) collective-permute-start(bf16[4,6144]{1,0:T(4,128)(2,1)S(1)} %get-tuple-element.21.refs_6_), channel_id=1, source_target_pairs={{0,8},{2,10},{4,12},{6,14},{8,0},{10,2},{12,4},{14,6},{1,5},{3,7},... | collective-permute-start | bytes 147464 | tf_op jit(solution)/shard_map/ppermute | solution.py:33
  40.9 1.3 %collective-permute-start.11 = (bf16[4,6144]{1,0:T(4,128)(2,1)S(1)}, bf16[4,6144]{1,0:T(4,128)(2,1)S(1)}, u32[]{:S(2)}, u32[]{:S(2)}) collective-permute-start(bf16[4,6144]{1,0:T(4,128)(2,1)S(1)} %merge.1.own_ref), channel_id=1, source_target_pairs={{0,1},{1,0},{2,3},{3,2},{4,5},{5,4},{6,7},{7,6},{8,9},{9,8},{10,11... | collective-permute-start | bytes 147464 | tf_op jit(solution)/shard_map/ppermute | solution.py:28

commit v8 on v7

--- a/solution.py
+++ b/solution.py
@@ -113,7 +113,7 @@
     stack(own_ref, got_ref, out_ref)
 
 
-def stack_line(own_ref, second_ref, first_ref, after, out_ref):
+def stack_line(own_ref, second_ref, first_ref, share, heads, out_ref):
     first = lax.axis_index("narrow") == 0
     own, one, two = (r[...].astype(jnp.float32) for r in (own_ref, first_ref, second_ref))
     both = [jnp.where(first, own, one), jnp.where(first, one, two)]
@@ -187,7 +187,7 @@
         copy.wait()
 
 
-def down(hidden_ref, down_ref, after, kept_ref, given_ref):
+def down_most(hidden_ref, down_ref, kept_ref, given_ref):
     kept = kept_ref.shape[0]
 
     @pl.loop(0, kept_ref.shape[1] // WIDE_TILE)
@@ -198,6 +198,15 @@
         )
         kept_ref[:, columns] = terms[:kept]
         given_ref[:, columns] = terms[kept:].astype(jnp.bfloat16)
+
+
+def down_rest(hidden_ref, down_ref, most_kept, most_given, after, kept_ref, given_ref):
+    kept, most = most_kept.shape
+    terms = jnp.dot(hidden_ref[...], down_ref[:, most:], preferred_element_type=jnp.float32)
+    kept_ref[:, :most] = most_kept[...]
+    given_ref[:, :most] = most_given[...]
+    kept_ref[:, most:] = terms[:kept]
+    given_ref[:, most:] = terms[kept:].astype(jnp.bfloat16)
 
 
 def combine(terms_ref, taken_ref, after, kept_ref, sent_ref):
@@ -310,8 +319,9 @@
 
 def make_local(wide):
     short, far_step, near_step = steps_of(wide)
-    steps = [far_step, *short, near_step]
-    head_steps = [*short, far_step, near_step]
+    cross_step = far_step ^ near_step
+    steps = [cross_step, *short, near_step]
+    head_steps = [*short, near_step, far_step]
 
     def local(
         queries,
@@ -363,20 +373,25 @@
             size=100000,
             far=range(5),
         )
-        second = swap_by_core(x, wide, [0, far_step ^ near_step])
-        first = swap_by_core(x, wide, [far_step, near_step])
+        first = swap_by_core(x, wide, [cross_step, near_step])
+        second = swap_by_core(x, wide, [0, far_step])
+
+        def grown(heads, step):
+            got = swap(heads, "wide", wide, step)
+            return call(
+                stack, shape((2 * heads.shape[0], HD), bf16), [heads, got], size=4 * heads.size
+            )
+
+        heads = grown(heads, head_steps[0])
         x = call(
             stack_line,
             shape((2 * rows, width), bf16),
-            [x, second, first, share],
+            [x, second, first, share, heads],
             size=8 * rows * width,
-            far=(3,),
-        )
-        for step in short:
-            got_heads = swap(heads, "wide", wide, step)
-            heads = call(
-                stack, shape((2 * heads.shape[0], HD), bf16), [heads, got_heads], size=4 * heads.size
-            )
+            far=(3, 4),
+        )
+        for order, step in enumerate(short):
+            heads = grown(heads, head_steps[order + 1])
             x = call(
                 stack_after,
                 shape((2 * x.shape[0], width), bf16),
@@ -384,7 +399,7 @@
                 size=8 * x.size,
                 far=(2,),
             )
-        got_heads = swap(heads, "wide", wide, far_step)
+        far_heads = swap(heads, "wide", wide, far_step)
         other_x = swap(x, "narrow", 2, 1)
         hidden, near_down = call(
             gate_all,
@@ -395,23 +410,21 @@
             size=6 * piece_bytes,
             far=(5,),
         )
-        heads = call(
-            stack_after,
-            shape((2 * heads.shape[0], HD), bf16),
-            [heads, got_heads, hidden],
-            size=8 * heads.size,
-            far=(2,),
+        most = width - WIDE_TILE
+        parts = call(
+            down_most,
+            [shape((count // 2, most), f32), shape((count // 2, most), bf16)],
+            [hidden, near(near_down)],
         )
         terms, given = call(
-            down,
+            down_rest,
             [shape((count // 2, width), f32), shape((count // 2, width), bf16)],
-            [hidden, near(near_down), heads],
+            [hidden, near(near_down), *parts, far_heads],
             flops=2 * product,
             size=2 * piece_bytes,
-            far=(2,),
+            far=(4,),
         )
         taken = swap(given, "narrow", 2, 1)
-        far_heads = swap(heads, "wide", wide, near_step)
 
         caches = [near(key_cache), near(value_cache), lengths, assignment]
         early_slots = list(range(slots - 1))
@@ -445,12 +458,12 @@
             size=12 * rows * width,
             far=(2,),
         )
-        second_taken = swap_by_core(second, wide, [0, far_step ^ near_step])
-        first_taken = swap_by_core(first, wide, [far_step, near_step])
+        first_taken = swap_by_core(first, wide, [cross_step, near_step])
+        second_taken = swap_by_core(second, wide, [0, far_step])
         context = call(
             functools.partial(attend_last, head_steps, late_slots, heads_local),
             shape(queries.shape, bf16),
-            [heads, far_heads, *caches, first, early],
+            [heads, far_heads, *caches, second, early],
             [
                 pltpu.VMEM((len(late_slots) * heads_local, HD), f32),
                 pltpu.VMEM((slots * heads_local, HD), f32),

time: 43.1 us -> 42 us (0.974)
  starting transfers between devices: 16.1 us -> 12.2 us
  waiting for transfers between devices: 11 us -> 13.8 us
    ppermute x8, starting transfers between devices: 9.34 us -> 4.31 us  [swap(): return lax.ppermute(block, axis, [(i, i ^ step) for i in range(count)])]
    ppermute x8, waiting for transfers between devices: 7.42 us -> 11.7 us  [swap(): return lax.ppermute(block, axis, [(i, i ^ step) for i in range(count)])]
    ppermute x4, waiting for transfers between devices: 3.56 us -> 2.09 us  [swap_by_core(): return lax.ppermute(block, ('wide', 'narrow'), pairs)]
    ppermute x4, starting transfers between devices: 6.78 us -> 7.93 us  [swap_by_core(): return lax.ppermute(block, ('wide', 'narrow'), pairs)]
    pallas_call x14 -> x15, Pallas kernels: 14.9 us -> 14.9 us  [call(): pl.pallas_call(kernel, name=getattr(kernel, 'func', kernel).__name__, out...]
  transfers between devices with their start and end apart: 12 -> 12, of which waited for: 5 -> 7; matrix products, arithmetic and copies ran while one was open for 0% -> 0% of each run, Pallas kernels for 23% -> 30%
where the time goes in v8:
time: 42 us; the launch traced here: 41.8 us
  Pallas kernels  14.9 us (35%)
  waiting for transfers between devices  13.8 us (33%)
  starting transfers between devices  12.2 us (29%)
  between operations  0.82 us (2%)
    pallas_call x15, Pallas kernels, call(): pl.pallas_call(kernel, name=getattr(kernel, 'func', kernel).__name__, out...  14.9 us
    ppermute x8, waiting for transfers between devices, swap(): return lax.ppermute(block, axis, [(i, i ^ step) for i in range(count)])  11.7 us
    ppermute x4, starting transfers between devices, swap_by_core(): return lax.ppermute(block, ('wide', 'narrow'), pairs)  7.93 us
    ppermute x8, starting transfers between devices, swap(): return lax.ppermute(block, axis, [(i, i ^ step) for i in range(count)])  4.31 us
    ppermute x4, waiting for transfers between devices, swap_by_core(): return lax.ppermute(block, ('wide', 'narrow'), pairs)  2.09 us
  transfers between devices with their start and end apart: 12, of which 7 were waited for; matrix products, arithmetic and copies ran while one was open for 0% of the time, Pallas kernels for 30%

profile of v8, /device:TPU:0, one launch (start us, length us, event | category | flops | bytes accessed | tf_op | source)
XLA Modules:
  0.0 41.8 jit_solution(6579114566383149857)
XLA Ops:
  0.6 1.0 %prepare.1 = (bf16[4,6144]{1,0:T(4,128)(2,1)S(1)}, bf16[128,128]{1,0:T(8,128)(2,1)S(1)}) custom-call(bf16[4,6144]{1,0:T(4,128)(2,1)} %tokens_ref.1, f32[1,6144]{1,0:T(1,128)} %bitcast.3, bf16[4,3072]{1,0:T(4,128)(2,1)} %far_query.1, bf16[4,512]{1,0:T(4,128)(2,1)} %far_key.1, bf16[4,512]{1,0:T(4,128)(2,1)} %far_value.1), custom_call_target="tpu_custom_call" | custom-call | bytes 100000 | tf_op jit(solution)/shard_map/prepare/pallas_call | solution.py:54
  1.6 5.1 %collective-permute-start.4 = (bf16[4,6144]{1,0:T(4,128)(2,1)S(1)}, bf16[4,6144]{1,0:T(4,128)(2,1)S(1)}, u32[]{:S(2)}, u32[]{:S(2)}) collective-permute-start(bf16[4,6144]{1,0:T(4,128)(2,1)S(1)} %get-tuple-element.16.refs_0_.own_ref), channel_id=1, source_target_pairs={{0,12},{2,14},{4,8},{6,10},{8,4},{10,6},{12,0},{14,2},{1,5},{3,7},... | collective-permute-start | bytes 147464 | tf_op jit(solution)/shard_map/ppermute | solution.py:33
  6.8 0.7 %collective-permute-start.3 = (bf16[4,6144]{1,0:T(4,128)(2,1)S(1)}, bf16[4,6144]{1,0:T(4,128)(2,1)S(1)}, u32[]{:S(2)}, u32[]{:S(2)}) collective-permute-start(bf16[4,6144]{1,0:T(4,128)(2,1)S(1)} %get-tuple-element.16.refs_0_.own_ref), channel_id=1, source_target_pairs={{1,9},{3,11},{5,13},{7,15},{9,1},{11,3},{13,5},{15,7},{17,25},{19,... | collective-permute-start | bytes 147464 | tf_op jit(solution)/shard_map/ppermute | solution.py:33
  7.4 1.6 %collective-permute-start = (bf16[128,128]{1,0:T(8,128)(2,1)S(1)}, bf16[128,128]{1,0:T(8,128)(2,1)S(1)}, u32[]{:S(2)}, u32[]{:S(2)}) collective-permute-start(bf16[128,128]{1,0:T(8,128)(2,1)S(1)} %get-tuple-element.15.own_ref), channel_id=1, source_target_pairs={{0,2},{2,0},{4,6},{6,4},{8,10},{10,8},{12,14},{14,12},{1,3},{3,1},... | collective-permute-start | bytes 98312 | tf_op jit(solution)/shard_map/ppermute | solution.py:28
  9.0 0.0 copy-start
  9.0 0.0 copy-start.1
  9.0 1.0 %shares.1.share.share_ref = f32[32,128]{1,0:T(8,128)S(1)} custom-call(s32[2,32]{1,0:T(2,128)} %bitcast.4, f32[2,32]{1,0:T(2,128)} %bitcast.5, bf16[4,6144]{1,0:T(4,128)(2,1)S(1)} %get-tuple-element.16.refs_0_.own_ref, bf16[1,6144,1024]{2,1,0:T(8,128)(2,1)} %gate_ref.1, bf16[1,6144,1024]{2,1,0:T(8,128)(2,1)} %up_ref.1), custom_call_target="tpu_custom_call" | custom-call | bytes 100000 | tf_op jit(solution)/shard_map/shares/pallas_call | solution.py:54
  10.0 1.7 %collective-permute-done.got_ref = bf16[128,128]{1,0:T(8,128)(2,1)S(1)} collective-permute-done((bf16[128,128]{1,0:T(8,128)(2,1)S(1)}, bf16[128,128]{1,0:T(8,128)(2,1)S(1)}, u32[]{:S(2)}, u32[]{:S(2)}) %collective-permute-start) | collective-permute-done | bytes 32800 | tf_op jit(solution)/shard_map/ppermute | solution.py:28
  11.7 0.0 collective-permute-done.4.first_ref
  11.7 0.0 collective-permute-done.3.second_ref
  11.7 1.6 %collective-permute-start.5 = (bf16[8,6144]{1,0:T(8,128)(2,1)S(1)}, bf16[8,6144]{1,0:T(8,128)(2,1)S(1)}, u32[]{:S(2)}, u32[]{:S(2)}) collective-permute-start(bf16[8,6144]{1,0:T(8,128)(2,1)S(1)} %stack_line.1.own_ref), channel_id=1, source_target_pairs={{0,2},{2,0},{4,6},{6,4},{8,10},{10,8},{12,14},{14,12},{1,3},{3,1},... | collective-permute-start | bytes 294920 | tf_op jit(solution)/shard_map/ppermute | solution.py:28
  13.3 0.0 collective-permute-start.1
  13.3 4.3 %collective-permute-done.1.got_ref = bf16[256,128]{1,0:T(8,128)(2,1)S(1)} collective-permute-done((bf16[256,128]{1,0:T(8,128)(2,1)S(1)}, bf16[256,128]{1,0:T(8,128)(2,1)S(1)}, u32[]{:S(2)}, u32[]{:S(2)}) %collective-permute-start.1) | collective-permute-done | bytes 65568 | tf_op jit(solution)/shard_map/ppermute | solution.py:28
  17.6 0.0 collective-permute-done.5.got_ref
  17.6 0.1 collective-permute-start.6
  17.7 0.3 collective-permute-start.2
  18.0 1.1 %collective-permute-done.6.other_ref = bf16[16,6144]{1,0:T(8,128)(2,1)S(1)} collective-permute-done((bf16[16,6144]{1,0:T(8,128)(2,1)S(1)}, bf16[16,6144]{1,0:T(8,128)(2,1)S(1)}, u32[]{:S(2)}, u32[]{:S(2)}) %collective-permute-start.6) | collective-permute-done | bytes 196640 | tf_op jit(solution)/shard_map/ppermute | solution.py:28
  19.1 0.0 copy-done
  19.1 0.0 copy-done.1
  19.2 5.0 %gate_all.1 = (bf16[32,1024]{1,0:T(8,128)(2,1)S(1)}, bf16[1024,6144]{1,0:T(8,128)(2,1)S(1)}) custom-call(bf16[16,6144]{1,0:T(8,128)(2,1)S(1)} %stack_after.1.own_ref, bf16[16,6144]{1,0:T(8,128)(2,1)S(1)} %collective-permute-done.6.other_ref, bf16[1,6144,1024]{2,1,0:T(8,128)(2,1)S(1)} %copy-done, bf16[1,6144,1024]{2,1,0:T(8,128)(2,1)S(1)} %copy-done.1, ...), custom_call_target="tpu_custom_call" | custom-call | flops 805306368 | bytes 37748736 | tf_op jit(solution)/shard_map/gate_all/pallas_call | solution.py:54
  24.2 0.0 copy-start.2
  24.2 0.0 copy-start.3
  24.2 0.0 copy-start.5
  24.2 0.0 copy-start.6
  24.2 2.7 %down_most.1 = (f32[16,5376]{1,0:T(8,128)S(1)}, bf16[16,5376]{1,0:T(8,128)(2,1)S(1)}) custom-call(bf16[32,1024]{1,0:T(8,128)(2,1)S(1)} %get-tuple-element.17.hidden_ref.after, bf16[1024,6144]{1,0:T(8,128)(2,1)S(1)} %get-tuple-element.18.down_ref), custom_call_target="tpu_custom_call" | custom-call | tf_op jit(solution)/shard_map/down_most/pallas_call | solution.py:54
  26.9 0.0 copy-start.4
  26.9 0.0 collective-permute-done.2.after.far_ref.refs_1_
  26.9 0.4 down_rest.1
  27.3 0.1 collective-permute-start.7
  27.5 1.3 %collective-permute-done.7.taken_ref = bf16[16,6144]{1,0:T(8,128)(2,1)S(1)} collective-permute-done((bf16[16,6144]{1,0:T(8,128)(2,1)S(1)}, bf16[16,6144]{1,0:T(8,128)(2,1)S(1)}, u32[]{:S(2)}, u32[]{:S(2)}) %collective-permute-start.7) | collective-permute-done | bytes 196640 | tf_op jit(solution)/shard_map/ppermute | solution.py:28
  28.8 0.6 %collective-permute-start.8 = (bf16[8,6144]{1,0:T(8,128)(2,1)S(1)}, bf16[8,6144]{1,0:T(8,128)(2,1)S(1)}, u32[]{:S(2)}, u32[]{:S(2)}) collective-permute-start(bf16[8,6144]{1,0:T(8,128)(2,1)S(1)} %get-tuple-element.24.after), channel_id=1, source_target_pairs={{0,2},{2,0},{4,6},{6,4},{8,10},{10,8},{12,14},{14,12},{1,3},{3,1},... | collective-permute-start | bytes 294920 | tf_op jit(solution)/shard_map/ppermute | solution.py:28
  29.4 0.0 copy-done.2
  29.4 0.0 copy-done.3
  29.4 0.0 copy-done.5
  29.4 0.0 copy-done.6
  29.4 2.2 %attend.1.after.refs_7_ = f32[72,128]{1,0:T(8,128)S(1)} custom-call(bf16[512,128]{1,0:T(8,128)(2,1)S(1)} %stack.3.after.near_ref.refs_0_, bf16[512,128]{1,0:T(8,128)(2,1)S(1)} %collective-permute-done.2.after.far_ref.refs_1_, bf16[4,512,512]{2,1,0:T(8,128)(2,1)S(1)} %copy-done.2, bf16[4,512,512]{2,1,0:T(8,128)(2,1)S(1)} %copy-done.3, s32[4]{0:T(128)S(1)} %copy-done.5, ...), custom_call_target="tpu_custom_call" | custom-call | flops 12582912 | bytes 2097152 | tf_op jit(solution)/shard_map/attend/pallas_call | solution.py:54
  31.6 2.1 %collective-permute-done.8.taken_ref = bf16[8,6144]{1,0:T(8,128)(2,1)S(1)} collective-permute-done((bf16[8,6144]{1,0:T(8,128)(2,1)S(1)}, bf16[8,6144]{1,0:T(8,128)(2,1)S(1)}, u32[]{:S(2)}, u32[]{:S(2)}) %collective-permute-start.8) | collective-permute-done | bytes 98336 | tf_op jit(solution)/shard_map/ppermute | solution.py:28
  33.7 0.1 part_line.1
  33.8 1.5 %collective-permute-start.10 = (bf16[4,6144]{1,0:T(4,128)(2,1)S(1)}, bf16[4,6144]{1,0:T(4,128)(2,1)S(1)}, u32[]{:S(2)}, u32[]{:S(2)}) collective-permute-start(bf16[4,6144]{1,0:T(4,128)(2,1)S(1)} %get-tuple-element.27), channel_id=1, source_target_pairs={{0,12},{2,14},{4,8},{6,10},{8,4},{10,6},{12,0},{14,2},{1,5},{3,7},... | collective-permute-start | bytes 147464 | tf_op jit(solution)/shard_map/ppermute | solution.py:33
  35.3 0.7 %collective-permute-start.9 = (bf16[4,6144]{1,0:T(4,128)(2,1)S(1)}, bf16[4,6144]{1,0:T(4,128)(2,1)S(1)}, u32[]{:S(2)}, u32[]{:S(2)}) collective-permute-start(bf16[4,6144]{1,0:T(4,128)(2,1)S(1)} %get-tuple-element.25.refs_6_), channel_id=1, source_target_pairs={{1,9},{3,11},{5,13},{7,15},{9,1},{11,3},{13,5},{15,7},{17,25},{19,... | collective-permute-start | bytes 147464 | tf_op jit(solution)/shard_map/ppermute | solution.py:33
  35.9 1.8 %attend_last.1.after = bf16[4,3072]{1,0:T(4,128)(2,1)} custom-call(bf16[512,128]{1,0:T(8,128)(2,1)S(1)} %stack.3.after.near_ref.refs_0_, bf16[512,128]{1,0:T(8,128)(2,1)S(1)} %collective-permute-done.2.after.far_ref.refs_1_, bf16[4,512,512]{2,1,0:T(8,128)(2,1)S(1)} %copy-done.2, bf16[4,512,512]{2,1,0:T(8,128)(2,1)S(1)} %copy-done.3, s32[4]{0:T(128)S(1)} %copy-done.5, ...), custom_call_target="tpu_custom_call" | custom-call | flops 12582912 | bytes 2097152 | tf_op jit(solution)/shard_map/attend_last/pallas_call | solution.py:54
  37.7 2.1 %collective-permute-done.10.first_ref = bf16[4,6144]{1,0:T(4,128)(2,1)S(1)} collective-permute-done((bf16[4,6144]{1,0:T(4,128)(2,1)S(1)}, bf16[4,6144]{1,0:T(4,128)(2,1)S(1)}, u32[]{:S(2)}, u32[]{:S(2)}) %collective-permute-start.10) | collective-permute-done | bytes 49184 | tf_op jit(solution)/shard_map/ppermute | solution.py:33
  39.8 0.0 collective-permute-done.9.second_ref
  39.8 0.1 collective-permute-start.11
  39.9 1.2 %collective-permute-done.11.other_ref = bf16[4,6144]{1,0:T(4,128)(2,1)S(1)} collective-permute-done((bf16[4,6144]{1,0:T(4,128)(2,1)S(1)}, bf16[4,6144]{1,0:T(4,128)(2,1)S(1)}, u32[]{:S(2)}, u32[]{:S(2)}) %collective-permute-start.11) | collective-permute-done | bytes 49184 | tf_op jit(solution)/shard_map/ppermute | solution.py:28
  41.1 0.0 copy-done.4
  41.1 0.7 %finish.1 = bf16[4,6144]{1,0:T(4,128)(2,1)} custom-call(bf16[4,6144]{1,0:T(4,128)(2,1)S(1)} %merge.1.own_ref, bf16[4,6144]{1,0:T(4,128)(2,1)S(1)} %collective-permute-done.11.other_ref, bf16[4,6144]{1,0:T(4,128)(2,1)S(1)} %copy-done.4), custom_call_target="tpu_custom_call" | custom-call | bytes 196608 | tf_op jit(solution)/shard_map/finish/pallas_call | solution.py:54
  (6 shorter events, 0.2 us)
Async XLA Ops:
  1.6 10.0 %collective-permute-start.4 = (bf16[4,6144]{1,0:T(4,128)(2,1)S(1)}, bf16[4,6144]{1,0:T(4,128)(2,1)S(1)}, u32[]{:S(2)}, u32[]{:S(2)}) collective-permute-start(bf16[4,6144]{1,0:T(4,128)(2,1)S(1)} %get-tuple-element.16.refs_0_.own_ref), channel_id=1, source_target_pairs={{0,12},{2,14},{4,8},{6,10},{8,4},{10,6},{12,0},{14,2},{1,5},{3,7},... | collective-permute-start | bytes 147464 | tf_op jit(solution)/shard_map/ppermute | solution.py:33
  6.8 4.9 %collective-permute-start.3 = (bf16[4,6144]{1,0:T(4,128)(2,1)S(1)}, bf16[4,6144]{1,0:T(4,128)(2,1)S(1)}, u32[]{:S(2)}, u32[]{:S(2)}) collective-permute-start(bf16[4,6144]{1,0:T(4,128)(2,1)S(1)} %get-tuple-element.16.refs_0_.own_ref), channel_id=1, source_target_pairs={{1,9},{3,11},{5,13},{7,15},{9,1},{11,3},{13,5},{15,7},{17,25},{19,... | collective-permute-start | bytes 147464 | tf_op jit(solution)/shard_map/ppermute | solution.py:33
  7.4 4.2 %collective-permute-start = (bf16[128,128]{1,0:T(8,128)(2,1)S(1)}, bf16[128,128]{1,0:T(8,128)(2,1)S(1)}, u32[]{:S(2)}, u32[]{:S(2)}) collective-permute-start(bf16[128,128]{1,0:T(8,128)(2,1)S(1)} %get-tuple-element.15.own_ref), channel_id=1, source_target_pairs={{0,2},{2,0},{4,6},{6,4},{8,10},{10,8},{12,14},{14,12},{1,3},{3,1},... | collective-permute-start | bytes 98312 | tf_op jit(solution)/shard_map/ppermute | solution.py:28
  9.0 10.1 %copy-start = (bf16[1,6144,1024]{2,1,0:T(8,128)(2,1)S(1)}, bf16[1,6144,1024]{2,1,0:T(8,128)(2,1)}, u32[]{:S(2)}) copy-start(bf16[1,6144,1024]{2,1,0:T(8,128)(2,1)} %gate_ref.1) | copy-start | bytes 37748740
  9.0 10.1 %copy-start.1 = (bf16[1,6144,1024]{2,1,0:T(8,128)(2,1)S(1)}, bf16[1,6144,1024]{2,1,0:T(8,128)(2,1)}, u32[]{:S(2)}) copy-start(bf16[1,6144,1024]{2,1,0:T(8,128)(2,1)} %up_ref.1) | copy-start | bytes 37748740
  11.7 5.9 %collective-permute-start.5 = (bf16[8,6144]{1,0:T(8,128)(2,1)S(1)}, bf16[8,6144]{1,0:T(8,128)(2,1)S(1)}, u32[]{:S(2)}, u32[]{:S(2)}) collective-permute-start(bf16[8,6144]{1,0:T(8,128)(2,1)S(1)} %stack_line.1.own_ref), channel_id=1, source_target_pairs={{0,2},{2,0},{4,6},{6,4},{8,10},{10,8},{12,14},{14,12},{1,3},{3,1},... | collective-permute-start | bytes 294920 | tf_op jit(solution)/shard_map/ppermute | solution.py:28
  13.3 4.3 %collective-permute-start.1 = (bf16[256,128]{1,0:T(8,128)(2,1)S(1)}, bf16[256,128]{1,0:T(8,128)(2,1)S(1)}, u32[]{:S(2)}, u32[]{:S(2)}) collective-permute-start(bf16[256,128]{1,0:T(8,128)(2,1)S(1)} %stack.2.own_ref.heads), channel_id=1, source_target_pairs={{0,4},{2,6},{4,0},{6,2},{8,12},{10,14},{12,8},{14,10},{1,5},{3,7},... | collective-permute-start | bytes 196616 | tf_op jit(solution)/shard_map/ppermute | solution.py:28
  17.6 1.5 %collective-permute-start.6 = (bf16[16,6144]{1,0:T(8,128)(2,1)S(1)}, bf16[16,6144]{1,0:T(8,128)(2,1)S(1)}, u32[]{:S(2)}, u32[]{:S(2)}) collective-permute-start(bf16[16,6144]{1,0:T(8,128)(2,1)S(1)} %stack_after.1.own_ref), channel_id=1, source_target_pairs={{0,1},{1,0},{2,3},{3,2},{4,5},{5,4},{6,7},{7,6},{8,9},{9,8},{10,11... | collective-permute-start | bytes 589832 | tf_op jit(solution)/shard_map/ppermute | solution.py:28
  17.7 9.2 %collective-permute-start.2 = (bf16[512,128]{1,0:T(8,128)(2,1)S(1)}, bf16[512,128]{1,0:T(8,128)(2,1)S(1)}, u32[]{:S(2)}, u32[]{:S(2)}) collective-permute-start(bf16[512,128]{1,0:T(8,128)(2,1)S(1)} %stack.3.after.near_ref.refs_0_), channel_id=1, source_target_pairs={{0,8},{2,10},{4,12},{6,14},{8,0},{10,2},{12,4},{14,6},{1,9},{3,11}... | collective-permute-start | bytes 393224 | tf_op jit(solution)/shard_map/ppermute | solution.py:28
  24.2 5.2 %copy-start.2 = (bf16[4,512,512]{2,1,0:T(8,128)(2,1)S(1)}, bf16[4,512,512]{2,1,0:T(8,128)(2,1)}, u32[]{:S(2)}) copy-start(bf16[4,512,512]{2,1,0:T(8,128)(2,1)} %refs_2_.3) | copy-start | bytes 6291460
  24.2 5.2 %copy-start.3 = (bf16[4,512,512]{2,1,0:T(8,128)(2,1)S(1)}, bf16[4,512,512]{2,1,0:T(8,128)(2,1)}, u32[]{:S(2)}) copy-start(bf16[4,512,512]{2,1,0:T(8,128)(2,1)} %refs_3_.1) | copy-start | bytes 6291460
  24.2 5.2 %copy-start.5 = (s32[4]{0:T(128)S(1)}, s32[4]{0:T(128)}, u32[]{:S(2)}) copy-start(s32[4]{0:T(128)} %refs_4_.1) | copy-start | bytes 52
  24.2 5.2 %copy-start.6 = (s32[4]{0:T(128)S(1)}, s32[4]{0:T(128)}, u32[]{:S(2)}) copy-start(s32[4]{0:T(128)} %refs_5_.1) | copy-start | bytes 52
  26.9 14.3 %copy-start.4 = (bf16[4,6144]{1,0:T(4,128)(2,1)S(1)}, bf16[4,6144]{1,0:T(4,128)(2,1)}, u32[]{:S(2)}) copy-start(bf16[4,6144]{1,0:T(4,128)(2,1)} %tokens_ref.1) | copy-start | bytes 147460
  27.3 1.4 %collective-permute-start.7 = (bf16[16,6144]{1,0:T(8,128)(2,1)S(1)}, bf16[16,6144]{1,0:T(8,128)(2,1)S(1)}, u32[]{:S(2)}, u32[]{:S(2)}) collective-permute-start(bf16[16,6144]{1,0:T(8,128)(2,1)S(1)} %get-tuple-element.22), channel_id=1, source_target_pairs={{0,1},{1,0},{2,3},{3,2},{4,5},{5,4},{6,7},{7,6},{8,9},{9,8},{10,11... | collective-permute-start | bytes 589832 | tf_op jit(solution)/shard_map/ppermute | solution.py:28
  28.8 4.9 %collective-permute-start.8 = (bf16[8,6144]{1,0:T(8,128)(2,1)S(1)}, bf16[8,6144]{1,0:T(8,128)(2,1)S(1)}, u32[]{:S(2)}, u32[]{:S(2)}) collective-permute-start(bf16[8,6144]{1,0:T(8,128)(2,1)S(1)} %get-tuple-element.24.after), channel_id=1, source_target_pairs={{0,2},{2,0},{4,6},{6,4},{8,10},{10,8},{12,14},{14,12},{1,3},{3,1},... | collective-permute-start | bytes 294920 | tf_op jit(solution)/shard_map/ppermute | solution.py:28
  33.8 6.0 %collective-permute-start.10 = (bf16[4,6144]{1,0:T(4,128)(2,1)S(1)}, bf16[4,6144]{1,0:T(4,128)(2,1)S(1)}, u32[]{:S(2)}, u32[]{:S(2)}) collective-permute-start(bf16[4,6144]{1,0:T(4,128)(2,1)S(1)} %get-tuple-element.27), channel_id=1, source_target_pairs={{0,12},{2,14},{4,8},{6,10},{8,4},{10,6},{12,0},{14,2},{1,5},{3,7},... | collective-permute-start | bytes 147464 | tf_op jit(solution)/shard_map/ppermute | solution.py:33
  35.3 4.5 %collective-permute-start.9 = (bf16[4,6144]{1,0:T(4,128)(2,1)S(1)}, bf16[4,6144]{1,0:T(4,128)(2,1)S(1)}, u32[]{:S(2)}, u32[]{:S(2)}) collective-permute-start(bf16[4,6144]{1,0:T(4,128)(2,1)S(1)} %get-tuple-element.25.refs_6_), channel_id=1, source_target_pairs={{1,9},{3,11},{5,13},{7,15},{9,1},{11,3},{13,5},{15,7},{17,25},{19,... | collective-permute-start | bytes 147464 | tf_op jit(solution)/shard_map/ppermute | solution.py:33
  39.8 1.3 %collective-permute-start.11 = (bf16[4,6144]{1,0:T(4,128)(2,1)S(1)}, bf16[4,6144]{1,0:T(4,128)(2,1)S(1)}, u32[]{:S(2)}, u32[]{:S(2)}) collective-permute-start(bf16[4,6144]{1,0:T(4,128)(2,1)S(1)} %merge.1.own_ref), channel_id=1, source_target_pairs={{0,1},{1,0},{2,3},{3,2},{4,5},{5,4},{6,7},{7,6},{8,9},{9,8},{10,11... | collective-permute-start | bytes 147464 | tf_op jit(solution)/shard_map/ppermute | solution.py:28

commit v9 on v8

--- a/solution.py
+++ b/solution.py
@@ -29,7 +29,7 @@
 
 
 def swap_by_core(block, wide, steps):
-    pairs = [(2 * i + c, 2 * (i ^ step) + c) for c, step in enumerate(steps) if step for i in range(wide)]
+    pairs = [(2 * i + c, 2 * (i ^ step) + c) for c, step in enumerate(steps) for i in range(wide)]
     return lax.ppermute(block, ("wide", "narrow"), pairs)
 
 

time: 42 us -> 42 us (level)
  no operation moved by 1% of the time
where the time goes in v9:
time: 42 us; the launch traced here: 41.8 us
  Pallas kernels  14.9 us (35%)
  waiting for transfers between devices  13.8 us (33%)
  starting transfers between devices  12.2 us (29%)
  between operations  0.82 us (2%)
    pallas_call x15, Pallas kernels, call(): pl.pallas_call(kernel, name=getattr(kernel, 'func', kernel).__name__, out...  14.9 us
    ppermute x8, waiting for transfers between devices, swap(): return lax.ppermute(block, axis, [(i, i ^ step) for i in range(count)])  11.7 us
    ppermute x4, starting transfers between devices, swap_by_core(): return lax.ppermute(block, ('wide', 'narrow'), pairs)  7.93 us
    ppermute x8, starting transfers between devices, swap(): return lax.ppermute(block, axis, [(i, i ^ step) for i in range(count)])  4.31 us
    ppermute x4, waiting for transfers between devices, swap_by_core(): return lax.ppermute(block, ('wide', 'narrow'), pairs)  2.09 us
  transfers between devices with their start and end apart: 12, of which 7 were waited for; matrix products, arithmetic and copies ran while one was open for 0% of the time, Pallas kernels for 30%

profile of v9, /device:TPU:0, one launch (start us, length us, event | category | flops | bytes accessed | tf_op | source)
XLA Modules:
  0.0 41.8 jit_solution(497067647678147227)
XLA Ops:
  0.6 1.0 %prepare.1 = (bf16[4,6144]{1,0:T(4,128)(2,1)S(1)}, bf16[128,128]{1,0:T(8,128)(2,1)S(1)}) custom-call(bf16[4,6144]{1,0:T(4,128)(2,1)} %tokens_ref.1, f32[1,6144]{1,0:T(1,128)} %bitcast.3, bf16[4,3072]{1,0:T(4,128)(2,1)} %far_query.1, bf16[4,512]{1,0:T(4,128)(2,1)} %far_key.1, bf16[4,512]{1,0:T(4,128)(2,1)} %far_value.1), custom_call_target="tpu_custom_call" | custom-call | bytes 100000 | tf_op jit(solution)/shard_map/prepare/pallas_call | solution.py:54
  1.6 5.1 %collective-permute-start.4 = (bf16[4,6144]{1,0:T(4,128)(2,1)S(1)}, bf16[4,6144]{1,0:T(4,128)(2,1)S(1)}, u32[]{:S(2)}, u32[]{:S(2)}) collective-permute-start(bf16[4,6144]{1,0:T(4,128)(2,1)S(1)} %get-tuple-element.16.refs_0_.own_ref), channel_id=1, source_target_pairs={{0,12},{2,14},{4,8},{6,10},{8,4},{10,6},{12,0},{14,2},{1,5},{3,7},... | collective-permute-start | bytes 147464 | tf_op jit(solution)/shard_map/ppermute | solution.py:33
  6.8 0.7 %collective-permute-start.3 = (bf16[4,6144]{1,0:T(4,128)(2,1)S(1)}, bf16[4,6144]{1,0:T(4,128)(2,1)S(1)}, u32[]{:S(2)}, u32[]{:S(2)}) collective-permute-start(bf16[4,6144]{1,0:T(4,128)(2,1)S(1)} %get-tuple-element.16.refs_0_.own_ref), channel_id=1, source_target_pairs={{0,0},{2,2},{4,4},{6,6},{8,8},{10,10},{12,12},{14,14},{1,9},{3,11}... | collective-permute-start | bytes 147464 | tf_op jit(solution)/shard_map/ppermute | solution.py:33
  7.4 1.6 %collective-permute-start = (bf16[128,128]{1,0:T(8,128)(2,1)S(1)}, bf16[128,128]{1,0:T(8,128)(2,1)S(1)}, u32[]{:S(2)}, u32[]{:S(2)}) collective-permute-start(bf16[128,128]{1,0:T(8,128)(2,1)S(1)} %get-tuple-element.15.own_ref), channel_id=1, source_target_pairs={{0,2},{2,0},{4,6},{6,4},{8,10},{10,8},{12,14},{14,12},{1,3},{3,1},... | collective-permute-start | bytes 98312 | tf_op jit(solution)/shard_map/ppermute | solution.py:28
  9.0 0.0 copy-start
  9.0 0.0 copy-start.1
  9.0 1.0 %shares.1.share.share_ref = f32[32,128]{1,0:T(8,128)S(1)} custom-call(s32[2,32]{1,0:T(2,128)} %bitcast.4, f32[2,32]{1,0:T(2,128)} %bitcast.5, bf16[4,6144]{1,0:T(4,128)(2,1)S(1)} %get-tuple-element.16.refs_0_.own_ref, bf16[1,6144,1024]{2,1,0:T(8,128)(2,1)} %gate_ref.1, bf16[1,6144,1024]{2,1,0:T(8,128)(2,1)} %up_ref.1), custom_call_target="tpu_custom_call" | custom-call | bytes 100000 | tf_op jit(solution)/shard_map/shares/pallas_call | solution.py:54
  10.0 1.7 %collective-permute-done.got_ref = bf16[128,128]{1,0:T(8,128)(2,1)S(1)} collective-permute-done((bf16[128,128]{1,0:T(8,128)(2,1)S(1)}, bf16[128,128]{1,0:T(8,128)(2,1)S(1)}, u32[]{:S(2)}, u32[]{:S(2)}) %collective-permute-start) | collective-permute-done | bytes 32800 | tf_op jit(solution)/shard_map/ppermute | solution.py:28
  11.7 0.0 collective-permute-done.4.first_ref
  11.7 0.0 collective-permute-done.3.second_ref
  11.7 1.6 %collective-permute-start.5 = (bf16[8,6144]{1,0:T(8,128)(2,1)S(1)}, bf16[8,6144]{1,0:T(8,128)(2,1)S(1)}, u32[]{:S(2)}, u32[]{:S(2)}) collective-permute-start(bf16[8,6144]{1,0:T(8,128)(2,1)S(1)} %stack_line.1.own_ref), channel_id=1, source_target_pairs={{0,2},{2,0},{4,6},{6,4},{8,10},{10,8},{12,14},{14,12},{1,3},{3,1},... | collective-permute-start | bytes 294920 | tf_op jit(solution)/shard_map/ppermute | solution.py:28
  13.3 0.0 collective-permute-start.1
  13.3 4.3 %collective-permute-done.1.got_ref = bf16[256,128]{1,0:T(8,128)(2,1)S(1)} collective-permute-done((bf16[256,128]{1,0:T(8,128)(2,1)S(1)}, bf16[256,128]{1,0:T(8,128)(2,1)S(1)}, u32[]{:S(2)}, u32[]{:S(2)}) %collective-permute-start.1) | collective-permute-done | bytes 65568 | tf_op jit(solution)/shard_map/ppermute | solution.py:28
  17.6 0.0 collective-permute-done.5.got_ref
  17.6 0.1 collective-permute-start.6
  17.7 0.3 collective-permute-start.2
  18.0 1.1 %collective-permute-done.6.other_ref = bf16[16,6144]{1,0:T(8,128)(2,1)S(1)} collective-permute-done((bf16[16,6144]{1,0:T(8,128)(2,1)S(1)}, bf16[16,6144]{1,0:T(8,128)(2,1)S(1)}, u32[]{:S(2)}, u32[]{:S(2)}) %collective-permute-start.6) | collective-permute-done | bytes 196640 | tf_op jit(solution)/shard_map/ppermute | solution.py:28
  19.1 0.0 copy-done
  19.1 0.0 copy-done.1
  19.2 5.0 %gate_all.1 = (bf16[32,1024]{1,0:T(8,128)(2,1)S(1)}, bf16[1024,6144]{1,0:T(8,128)(2,1)S(1)}) custom-call(bf16[16,6144]{1,0:T(8,128)(2,1)S(1)} %stack_after.1.own_ref, bf16[16,6144]{1,0:T(8,128)(2,1)S(1)} %collective-permute-done.6.other_ref, bf16[1,6144,1024]{2,1,0:T(8,128)(2,1)S(1)} %copy-done, bf16[1,6144,1024]{2,1,0:T(8,128)(2,1)S(1)} %copy-done.1, ...), custom_call_target="tpu_custom_call" | custom-call | flops 805306368 | bytes 37748736 | tf_op jit(solution)/shard_map/gate_all/pallas_call | solution.py:54
  24.2 0.0 copy-start.2
  24.2 0.0 copy-start.3
  24.2 0.0 copy-start.5
  24.2 0.0 copy-start.6
  24.2 2.7 %down_most.1 = (f32[16,5376]{1,0:T(8,128)S(1)}, bf16[16,5376]{1,0:T(8,128)(2,1)S(1)}) custom-call(bf16[32,1024]{1,0:T(8,128)(2,1)S(1)} %get-tuple-element.17.hidden_ref.after, bf16[1024,6144]{1,0:T(8,128)(2,1)S(1)} %get-tuple-element.18.down_ref), custom_call_target="tpu_custom_call" | custom-call | tf_op jit(solution)/shard_map/down_most/pallas_call | solution.py:54
  26.9 0.0 copy-start.4
  26.9 0.0 collective-permute-done.2.after.far_ref.refs_1_
  26.9 0.4 down_rest.1
  27.3 0.1 collective-permute-start.7
  27.5 1.3 %collective-permute-done.7.taken_ref = bf16[16,6144]{1,0:T(8,128)(2,1)S(1)} collective-permute-done((bf16[16,6144]{1,0:T(8,128)(2,1)S(1)}, bf16[16,6144]{1,0:T(8,128)(2,1)S(1)}, u32[]{:S(2)}, u32[]{:S(2)}) %collective-permute-start.7) | collective-permute-done | bytes 196640 | tf_op jit(solution)/shard_map/ppermute | solution.py:28
  28.8 0.6 %collective-permute-start.8 = (bf16[8,6144]{1,0:T(8,128)(2,1)S(1)}, bf16[8,6144]{1,0:T(8,128)(2,1)S(1)}, u32[]{:S(2)}, u32[]{:S(2)}) collective-permute-start(bf16[8,6144]{1,0:T(8,128)(2,1)S(1)} %get-tuple-element.24.after), channel_id=1, source_target_pairs={{0,2},{2,0},{4,6},{6,4},{8,10},{10,8},{12,14},{14,12},{1,3},{3,1},... | collective-permute-start | bytes 294920 | tf_op jit(solution)/shard_map/ppermute | solution.py:28
  29.4 0.0 copy-done.2
  29.4 0.0 copy-done.3
  29.4 0.0 copy-done.5
  29.4 0.0 copy-done.6
  29.4 2.2 %attend.1.after.refs_7_ = f32[72,128]{1,0:T(8,128)S(1)} custom-call(bf16[512,128]{1,0:T(8,128)(2,1)S(1)} %stack.3.after.near_ref.refs_0_, bf16[512,128]{1,0:T(8,128)(2,1)S(1)} %collective-permute-done.2.after.far_ref.refs_1_, bf16[4,512,512]{2,1,0:T(8,128)(2,1)S(1)} %copy-done.2, bf16[4,512,512]{2,1,0:T(8,128)(2,1)S(1)} %copy-done.3, s32[4]{0:T(128)S(1)} %copy-done.5, ...), custom_call_target="tpu_custom_call" | custom-call | flops 12582912 | bytes 2097152 | tf_op jit(solution)/shard_map/attend/pallas_call | solution.py:54
  31.6 2.1 %collective-permute-done.8.taken_ref = bf16[8,6144]{1,0:T(8,128)(2,1)S(1)} collective-permute-done((bf16[8,6144]{1,0:T(8,128)(2,1)S(1)}, bf16[8,6144]{1,0:T(8,128)(2,1)S(1)}, u32[]{:S(2)}, u32[]{:S(2)}) %collective-permute-start.8) | collective-permute-done | bytes 98336 | tf_op jit(solution)/shard_map/ppermute | solution.py:28
  33.7 0.1 part_line.1
  33.8 1.5 %collective-permute-start.10 = (bf16[4,6144]{1,0:T(4,128)(2,1)S(1)}, bf16[4,6144]{1,0:T(4,128)(2,1)S(1)}, u32[]{:S(2)}, u32[]{:S(2)}) collective-permute-start(bf16[4,6144]{1,0:T(4,128)(2,1)S(1)} %get-tuple-element.27), channel_id=1, source_target_pairs={{0,12},{2,14},{4,8},{6,10},{8,4},{10,6},{12,0},{14,2},{1,5},{3,7},... | collective-permute-start | bytes 147464 | tf_op jit(solution)/shard_map/ppermute | solution.py:33
  35.3 0.7 %collective-permute-start.9 = (bf16[4,6144]{1,0:T(4,128)(2,1)S(1)}, bf16[4,6144]{1,0:T(4,128)(2,1)S(1)}, u32[]{:S(2)}, u32[]{:S(2)}) collective-permute-start(bf16[4,6144]{1,0:T(4,128)(2,1)S(1)} %get-tuple-element.25.refs_6_), channel_id=1, source_target_pairs={{0,0},{2,2},{4,4},{6,6},{8,8},{10,10},{12,12},{14,14},{1,9},{3,11}... | collective-permute-start | bytes 147464 | tf_op jit(solution)/shard_map/ppermute | solution.py:33
  35.9 1.8 %attend_last.1.after = bf16[4,3072]{1,0:T(4,128)(2,1)} custom-call(bf16[512,128]{1,0:T(8,128)(2,1)S(1)} %stack.3.after.near_ref.refs_0_, bf16[512,128]{1,0:T(8,128)(2,1)S(1)} %collective-permute-done.2.after.far_ref.refs_1_, bf16[4,512,512]{2,1,0:T(8,128)(2,1)S(1)} %copy-done.2, bf16[4,512,512]{2,1,0:T(8,128)(2,1)S(1)} %copy-done.3, s32[4]{0:T(128)S(1)} %copy-done.5, ...), custom_call_target="tpu_custom_call" | custom-call | flops 12582912 | bytes 2097152 | tf_op jit(solution)/shard_map/attend_last/pallas_call | solution.py:54
  37.7 2.1 %collective-permute-done.10.first_ref = bf16[4,6144]{1,0:T(4,128)(2,1)S(1)} collective-permute-done((bf16[4,6144]{1,0:T(4,128)(2,1)S(1)}, bf16[4,6144]{1,0:T(4,128)(2,1)S(1)}, u32[]{:S(2)}, u32[]{:S(2)}) %collective-permute-start.10) | collective-permute-done | bytes 49184 | tf_op jit(solution)/shard_map/ppermute | solution.py:33
  39.8 0.0 collective-permute-done.9.second_ref
  39.8 0.1 collective-permute-start.11
  39.9 1.2 %collective-permute-done.11.other_ref = bf16[4,6144]{1,0:T(4,128)(2,1)S(1)} collective-permute-done((bf16[4,6144]{1,0:T(4,128)(2,1)S(1)}, bf16[4,6144]{1,0:T(4,128)(2,1)S(1)}, u32[]{:S(2)}, u32[]{:S(2)}) %collective-permute-start.11) | collective-permute-done | bytes 49184 | tf_op jit(solution)/shard_map/ppermute | solution.py:28
  41.1 0.0 copy-done.4
  41.1 0.7 %finish.1 = bf16[4,6144]{1,0:T(4,128)(2,1)} custom-call(bf16[4,6144]{1,0:T(4,128)(2,1)S(1)} %merge.1.own_ref, bf16[4,6144]{1,0:T(4,128)(2,1)S(1)} %collective-permute-done.11.other_ref, bf16[4,6144]{1,0:T(4,128)(2,1)S(1)} %copy-done.4), custom_call_target="tpu_custom_call" | custom-call | bytes 196608 | tf_op jit(solution)/shard_map/finish/pallas_call | solution.py:54
  (6 shorter events, 0.2 us)
Async XLA Ops:
  1.6 10.0 %collective-permute-start.4 = (bf16[4,6144]{1,0:T(4,128)(2,1)S(1)}, bf16[4,6144]{1,0:T(4,128)(2,1)S(1)}, u32[]{:S(2)}, u32[]{:S(2)}) collective-permute-start(bf16[4,6144]{1,0:T(4,128)(2,1)S(1)} %get-tuple-element.16.refs_0_.own_ref), channel_id=1, source_target_pairs={{0,12},{2,14},{4,8},{6,10},{8,4},{10,6},{12,0},{14,2},{1,5},{3,7},... | collective-permute-start | bytes 147464 | tf_op jit(solution)/shard_map/ppermute | solution.py:33
  6.8 4.9 %collective-permute-start.3 = (bf16[4,6144]{1,0:T(4,128)(2,1)S(1)}, bf16[4,6144]{1,0:T(4,128)(2,1)S(1)}, u32[]{:S(2)}, u32[]{:S(2)}) collective-permute-start(bf16[4,6144]{1,0:T(4,128)(2,1)S(1)} %get-tuple-element.16.refs_0_.own_ref), channel_id=1, source_target_pairs={{0,0},{2,2},{4,4},{6,6},{8,8},{10,10},{12,12},{14,14},{1,9},{3,11}... | collective-permute-start | bytes 147464 | tf_op jit(solution)/shard_map/ppermute | solution.py:33
  7.4 4.2 %collective-permute-start = (bf16[128,128]{1,0:T(8,128)(2,1)S(1)}, bf16[128,128]{1,0:T(8,128)(2,1)S(1)}, u32[]{:S(2)}, u32[]{:S(2)}) collective-permute-start(bf16[128,128]{1,0:T(8,128)(2,1)S(1)} %get-tuple-element.15.own_ref), channel_id=1, source_target_pairs={{0,2},{2,0},{4,6},{6,4},{8,10},{10,8},{12,14},{14,12},{1,3},{3,1},... | collective-permute-start | bytes 98312 | tf_op jit(solution)/shard_map/ppermute | solution.py:28
  9.0 10.1 %copy-start = (bf16[1,6144,1024]{2,1,0:T(8,128)(2,1)S(1)}, bf16[1,6144,1024]{2,1,0:T(8,128)(2,1)}, u32[]{:S(2)}) copy-start(bf16[1,6144,1024]{2,1,0:T(8,128)(2,1)} %gate_ref.1) | copy-start | bytes 37748740
  9.0 10.1 %copy-start.1 = (bf16[1,6144,1024]{2,1,0:T(8,128)(2,1)S(1)}, bf16[1,6144,1024]{2,1,0:T(8,128)(2,1)}, u32[]{:S(2)}) copy-start(bf16[1,6144,1024]{2,1,0:T(8,128)(2,1)} %up_ref.1) | copy-start | bytes 37748740
  11.7 5.9 %collective-permute-start.5 = (bf16[8,6144]{1,0:T(8,128)(2,1)S(1)}, bf16[8,6144]{1,0:T(8,128)(2,1)S(1)}, u32[]{:S(2)}, u32[]{:S(2)}) collective-permute-start(bf16[8,6144]{1,0:T(8,128)(2,1)S(1)} %stack_line.1.own_ref), channel_id=1, source_target_pairs={{0,2},{2,0},{4,6},{6,4},{8,10},{10,8},{12,14},{14,12},{1,3},{3,1},... | collective-permute-start | bytes 294920 | tf_op jit(solution)/shard_map/ppermute | solution.py:28
  13.3 4.3 %collective-permute-start.1 = (bf16[256,128]{1,0:T(8,128)(2,1)S(1)}, bf16[256,128]{1,0:T(8,128)(2,1)S(1)}, u32[]{:S(2)}, u32[]{:S(2)}) collective-permute-start(bf16[256,128]{1,0:T(8,128)(2,1)S(1)} %stack.2.own_ref.heads), channel_id=1, source_target_pairs={{0,4},{2,6},{4,0},{6,2},{8,12},{10,14},{12,8},{14,10},{1,5},{3,7},... | collective-permute-start | bytes 196616 | tf_op jit(solution)/shard_map/ppermute | solution.py:28
  17.6 1.5 %collective-permute-start.6 = (bf16[16,6144]{1,0:T(8,128)(2,1)S(1)}, bf16[16,6144]{1,0:T(8,128)(2,1)S(1)}, u32[]{:S(2)}, u32[]{:S(2)}) collective-permute-start(bf16[16,6144]{1,0:T(8,128)(2,1)S(1)} %stack_after.1.own_ref), channel_id=1, source_target_pairs={{0,1},{1,0},{2,3},{3,2},{4,5},{5,4},{6,7},{7,6},{8,9},{9,8},{10,11... | collective-permute-start | bytes 589832 | tf_op jit(solution)/shard_map/ppermute | solution.py:28
  17.7 9.2 %collective-permute-start.2 = (bf16[512,128]{1,0:T(8,128)(2,1)S(1)}, bf16[512,128]{1,0:T(8,128)(2,1)S(1)}, u32[]{:S(2)}, u32[]{:S(2)}) collective-permute-start(bf16[512,128]{1,0:T(8,128)(2,1)S(1)} %stack.3.after.near_ref.refs_0_), channel_id=1, source_target_pairs={{0,8},{2,10},{4,12},{6,14},{8,0},{10,2},{12,4},{14,6},{1,9},{3,11}... | collective-permute-start | bytes 393224 | tf_op jit(solution)/shard_map/ppermute | solution.py:28
  24.2 5.2 %copy-start.2 = (bf16[4,512,512]{2,1,0:T(8,128)(2,1)S(1)}, bf16[4,512,512]{2,1,0:T(8,128)(2,1)}, u32[]{:S(2)}) copy-start(bf16[4,512,512]{2,1,0:T(8,128)(2,1)} %refs_2_.3) | copy-start | bytes 6291460
  24.2 5.2 %copy-start.3 = (bf16[4,512,512]{2,1,0:T(8,128)(2,1)S(1)}, bf16[4,512,512]{2,1,0:T(8,128)(2,1)}, u32[]{:S(2)}) copy-start(bf16[4,512,512]{2,1,0:T(8,128)(2,1)} %refs_3_.1) | copy-start | bytes 6291460
  24.2 5.2 %copy-start.5 = (s32[4]{0:T(128)S(1)}, s32[4]{0:T(128)}, u32[]{:S(2)}) copy-start(s32[4]{0:T(128)} %refs_4_.1) | copy-start | bytes 52
  24.2 5.2 %copy-start.6 = (s32[4]{0:T(128)S(1)}, s32[4]{0:T(128)}, u32[]{:S(2)}) copy-start(s32[4]{0:T(128)} %refs_5_.1) | copy-start | bytes 52
  26.9 14.3 %copy-start.4 = (bf16[4,6144]{1,0:T(4,128)(2,1)S(1)}, bf16[4,6144]{1,0:T(4,128)(2,1)}, u32[]{:S(2)}) copy-start(bf16[4,6144]{1,0:T(4,128)(2,1)} %tokens_ref.1) | copy-start | bytes 147460
  27.3 1.4 %collective-permute-start.7 = (bf16[16,6144]{1,0:T(8,128)(2,1)S(1)}, bf16[16,6144]{1,0:T(8,128)(2,1)S(1)}, u32[]{:S(2)}, u32[]{:S(2)}) collective-permute-start(bf16[16,6144]{1,0:T(8,128)(2,1)S(1)} %get-tuple-element.22), channel_id=1, source_target_pairs={{0,1},{1,0},{2,3},{3,2},{4,5},{5,4},{6,7},{7,6},{8,9},{9,8},{10,11... | collective-permute-start | bytes 589832 | tf_op jit(solution)/shard_map/ppermute | solution.py:28
  28.8 4.9 %collective-permute-start.8 = (bf16[8,6144]{1,0:T(8,128)(2,1)S(1)}, bf16[8,6144]{1,0:T(8,128)(2,1)S(1)}, u32[]{:S(2)}, u32[]{:S(2)}) collective-permute-start(bf16[8,6144]{1,0:T(8,128)(2,1)S(1)} %get-tuple-element.24.after), channel_id=1, source_target_pairs={{0,2},{2,0},{4,6},{6,4},{8,10},{10,8},{12,14},{14,12},{1,3},{3,1},... | collective-permute-start | bytes 294920 | tf_op jit(solution)/shard_map/ppermute | solution.py:28
  33.8 6.0 %collective-permute-start.10 = (bf16[4,6144]{1,0:T(4,128)(2,1)S(1)}, bf16[4,6144]{1,0:T(4,128)(2,1)S(1)}, u32[]{:S(2)}, u32[]{:S(2)}) collective-permute-start(bf16[4,6144]{1,0:T(4,128)(2,1)S(1)} %get-tuple-element.27), channel_id=1, source_target_pairs={{0,12},{2,14},{4,8},{6,10},{8,4},{10,6},{12,0},{14,2},{1,5},{3,7},... | collective-permute-start | bytes 147464 | tf_op jit(solution)/shard_map/ppermute | solution.py:33
  35.3 4.5 %collective-permute-start.9 = (bf16[4,6144]{1,0:T(4,128)(2,1)S(1)}, bf16[4,6144]{1,0:T(4,128)(2,1)S(1)}, u32[]{:S(2)}, u32[]{:S(2)}) collective-permute-start(bf16[4,6144]{1,0:T(4,128)(2,1)S(1)} %get-tuple-element.25.refs_6_), channel_id=1, source_target_pairs={{0,0},{2,2},{4,4},{6,6},{8,8},{10,10},{12,12},{14,14},{1,9},{3,11}... | collective-permute-start | bytes 147464 | tf_op jit(solution)/shard_map/ppermute | solution.py:33
  39.8 1.3 %collective-permute-start.11 = (bf16[4,6144]{1,0:T(4,128)(2,1)S(1)}, bf16[4,6144]{1,0:T(4,128)(2,1)S(1)}, u32[]{:S(2)}, u32[]{:S(2)}) collective-permute-start(bf16[4,6144]{1,0:T(4,128)(2,1)S(1)} %merge.1.own_ref), channel_id=1, source_target_pairs={{0,1},{1,0},{2,3},{3,2},{4,5},{5,4},{6,7},{7,6},{8,9},{9,8},{10,11... | collective-permute-start | bytes 147464 | tf_op jit(solution)/shard_map/ppermute | solution.py:28

commit v10 on v6

--- a/solution.py
+++ b/solution.py
@@ -13,8 +13,8 @@
 HD = 128
 GROUP = HQ // KVH
 SCALE = HD ** (-0.5)
-TILE = 256
-WIDE_TILE = 768
+TILE = 512
+WIDE_TILE = 1536
 CUTS = 4
 MIB = 1024 * 1024
 
@@ -82,61 +82,46 @@
     return pltpu.with_memory_space_constraint(array, pltpu.HBM)
 
 
-def prepare(far_tokens, far_gain, far_query, far_key, far_value, out_ref, both_ref, *held):
-    *near_refs, packed, sems = held
-    far_refs = (far_tokens, far_gain, far_query, far_key, far_value)
+def pack(far_query, far_key, far_value, far_tokens, far_gain, heads_ref, *held):
+    tokens_ref, gain_ref, *near_refs, packed, sems = held
+    far_refs = (far_query, far_key, far_value, far_tokens, far_gain)
     copies = [
         pltpu.make_async_copy(far, ref, sems.at[i])
-        for i, (far, ref) in enumerate(zip(far_refs, near_refs))
+        for i, (far, ref) in enumerate(zip(far_refs, (*near_refs, tokens_ref, gain_ref)))
     ]
     for copy in copies:
         copy.start()
     for copy in copies:
         copy.wait()
-    tokens_ref, gain_ref, *head_refs = near_refs
-    rows, half = out_ref.shape
-    core = lax.axis_index("narrow")
-    values = tokens_ref[...].astype(jnp.float32)
-    scale = lax.rsqrt(jnp.mean(values * values, axis=-1, keepdims=True) + 1e-05)
-    normed = values * scale * gain_ref[...]
-    normed = jnp.where(core == 0, normed[:, :half], normed[:, half:])
-    out_ref[...] = normed.astype(jnp.bfloat16)
-    pieces = half // HD
-    for piece in range(pieces):
-        packed[pl.ds(piece, rows, stride=pieces), :] = normed[:, piece * HD : (piece + 1) * HD]
-    at = rows * pieces
-    each = (both_ref.shape[0] - at) // rows
-    for ref in head_refs:
+    rows = near_refs[0].shape[0]
+    at = 0
+    each = heads_ref.shape[0] // rows
+    for ref in near_refs:
         block = ref[...].astype(jnp.float32)
         for head in range(ref.shape[1] // HD):
             packed[pl.ds(at, rows, stride=each), :] = block[:, head * HD : (head + 1) * HD]
             at += 1
-    both_ref[...] = packed[...].astype(jnp.bfloat16)
+    heads_ref[...] = packed[...].astype(jnp.bfloat16)
+
+
+def norm_both(own_ref, got_ref, gain_ref, share, heads, out_ref):
+    half = out_ref.shape[1]
+    core = lax.axis_index("narrow")
+    values = stacked([own_ref, got_ref])
+    scale = lax.rsqrt(jnp.mean(values * values, axis=-1, keepdims=True) + 1e-05)
+    normed = values * scale * gain_ref[...]
+    out_ref[...] = jnp.where(core == 0, normed[:, :half], normed[:, half:]).astype(jnp.bfloat16)
 
 
 def stacked(refs):
     return jnp.concatenate([ref[...].astype(jnp.float32) for ref in refs], axis=0)
 
 
-def grow_first(own_ref, far_both, own_both, after, out_ref, heads_ref, packed):
-    rows, half = own_ref.shape
-    pieces = half // HD
-    tokens = rows * pieces
-    packed[...] = far_both[:tokens, :].astype(jnp.float32)
-    far = [packed[pl.ds(piece, rows, stride=pieces), :] for piece in range(pieces)]
-    far = jnp.concatenate(far, axis=1)
-    own = own_ref[...].astype(jnp.float32)
-    out_ref[...] = jnp.concatenate([own, far], axis=0).astype(jnp.bfloat16)
-    count = heads_ref.shape[0] // 2
-    heads_ref[:count, :] = own_both[tokens:, :]
-    heads_ref[count:, :] = far_both[tokens:, :]
-
-
 def stack(*refs):
     refs[-1][...] = stacked(refs[:-1]).astype(refs[-1].dtype)
 
 
-def stack_line(own_ref, last_ref, far_ref, next_ref, out_ref):
+def stack_line(own_ref, last_ref, far_ref, next_ref, heads, out_ref):
     stack(own_ref, far_ref, next_ref, last_ref, out_ref)
 
 
@@ -366,23 +351,22 @@
         dma = pltpu.SemaphoreType.DMA
         piece_bytes = 2 * half * units
 
-        firsts = [tokens, norm_gain[None], queries, new_keys, new_values]
-        both_rows = rows * (half // HD + each)
-        weights = [distant(w_gate), distant(w_up)]
-        x, both = call(
-            prepare,
-            [shape((rows, half), bf16), shape((both_rows, HD), bf16)],
-            [distant(a) for a in firsts],
-            [pltpu.VMEM(a.shape, a.dtype) for a in firsts]
-            + [pltpu.VMEM((both_rows, HD), f32), dma((len(firsts),))],
+        got = swap(tokens, "wide", wide, steps[0])
+        heads_in = [queries, new_keys, new_values]
+        row_in = [tokens, norm_gain[None]]
+        heads, *row_near = call(
+            pack,
+            [shape((rows * each, HD), bf16)] + [pltpu.VMEM(a.shape, a.dtype) for a in row_in],
+            [distant(a) for a in heads_in + row_in],
+            [pltpu.VMEM(a.shape, a.dtype) for a in heads_in]
+            + [pltpu.VMEM((rows * each, HD), f32), dma((5,))],
             size=100000,
-            far=range(len(firsts)),
-        )
-        far_both = swap(both, "wide", wide, steps[0])
+            far=range(5),
+        )
         share = call(
             functools.partial(shares, steps, rows),
             shape((count, HD), f32),
-            [distant(routes.T), distant(route_logits.T), x, *weights],
+            [distant(routes.T), distant(route_logits.T), heads, distant(w_gate), distant(w_up)],
             [
                 pltpu.VMEM(routes.T.shape, jnp.int32),
                 pltpu.VMEM(route_logits.T.shape, f32),
@@ -391,24 +375,40 @@
             size=100000,
             far=range(5),
         )
-        x, heads = call(
-            grow_first,
-            [shape((2 * rows, half), bf16), shape((2 * rows * each, HD), bf16)],
-            [x, far_both, both, share],
-            [pltpu.VMEM((rows * half // HD, HD), f32)],
+        x = call(
+            norm_both,
+            shape((2 * rows, half), bf16),
+            [near(row_near[0]), got, near(row_near[1]), share, heads],
             size=100000,
-            far=(3,),
-        )
+            far=(3, 4),
+        )
+
+        def grown(heads, step):
+            got = swap(heads, "wide", wide, step)
+            return call(
+                stack, shape((2 * heads.shape[0], HD), bf16), [heads, got], size=4 * heads.size
+            )
+
         for step in steps[1:-2]:
-            ins = [x, swap(x, "wide", wide, step), heads, swap(heads, "wide", wide, step)]
-            outs = [shape((2 * x.shape[0], half), bf16), shape((2 * heads.shape[0], HD), bf16)]
-            x, heads = call(grow_both, outs, ins, size=8 * (x.size + heads.size))
+            heads = grown(heads, step)
+            x = call(
+                stack_after,
+                shape((2 * x.shape[0], half), bf16),
+                [x, swap(x, "wide", wide, step), heads],
+                size=8 * x.size,
+                far=(2,),
+            )
+        heads = grown(heads, steps[0])
         line_steps = [steps[-2], steps[-1], steps[-2] ^ steps[-1]]
         last = swap(x, "wide", wide, line_steps[2])
         line = [swap(x, "wide", wide, step) for step in line_steps[:2]]
         got_heads = swap(heads, "wide", wide, steps[-2])
         x = call(
-            stack_line, shape((count, half), bf16), [x, last, *line], size=8 * count * half
+            stack_line,
+            shape((count, half), bf16),
+            [x, last, *line, heads],
+            size=8 * count * half,
+            far=(4,),
         )
 
         product = 2 * count * half * units

time: 41.4 us -> 41.7 us (level)
  starting transfers between devices: 16.3 us -> 19 us
  waiting for transfers between devices: 9.24 us -> 7.41 us
  Pallas kernels: 14.8 us -> 14.2 us
    ppermute x13 -> x14, starting transfers between devices: 16.3 us -> 19 us  [swap(): return lax.ppermute(block, axis, [(i, i ^ step) for i in range(count)])]
    ppermute x13 -> x14, waiting for transfers between devices: 9.24 us -> 7.41 us  [swap(): return lax.ppermute(block, axis, [(i, i ^ step) for i in range(count)])]
    pallas_call x14 -> x15, Pallas kernels: 14.8 us -> 14.2 us  [call(): pl.pallas_call(kernel, name=getattr(kernel, 'func', kernel).__name__, out...]
  transfers between devices with their start and end apart: 13 -> 14, of which waited for: 6 -> 7; matrix products, arithmetic and copies ran while one was open for 0% -> 0% of each run, Pallas kernels for 28% -> 29%
where the time goes in v10:
time: 41.7 us; the launch traced here: 41.5 us
  starting transfers between devices  19 us (46%)
  Pallas kernels  14.2 us (34%)
  waiting for transfers between devices  7.41 us (18%)
  between operations  0.87 us (2%)
    ppermute x14, starting transfers between devices, swap(): return lax.ppermute(block, axis, [(i, i ^ step) for i in range(count)])  19 us
    pallas_call x15, Pallas kernels, call(): pl.pallas_call(kernel, name=getattr(kernel, 'func', kernel).__name__, out...  14.2 us
    ppermute x14, waiting for transfers between devices, swap(): return lax.ppermute(block, axis, [(i, i ^ step) for i in range(count)])  7.41 us
  transfers between devices with their start and end apart: 14, of which 7 were waited for; matrix products, arithmetic and copies ran while one was open for 0% of the time, Pallas kernels for 29%

profile of v10, /device:TPU:0, one launch (start us, length us, event | category | flops | bytes accessed | tf_op | source)
XLA Modules:
  0.0 41.5 jit_solution(14485923295214229995)
XLA Ops:
  0.6 3.0 %collective-permute-start.2 = (bf16[4,6144]{1,0:T(4,128)(2,1)}, bf16[4,6144]{1,0:T(4,128)(2,1)S(1)}, u32[]{:S(2)}, u32[]{:S(2)}) collective-permute-start(bf16[4,6144]{1,0:T(4,128)(2,1)} %tokens_ref.1), channel_id=1, source_target_pairs={{0,2},{2,0},{4,6},{6,4},{8,10},{10,8},{12,14},{14,12},{1,3},{3,1},... | collective-permute-start | bytes 147464 | tf_op jit(solution)/shard_map/ppermute | solution.py:28
  3.7 1.0 %pack.1 = (bf16[128,128]{1,0:T(8,128)(2,1)S(1)}, bf16[4,6144]{1,0:T(4,128)(2,1)S(1)}, f32[1,6144]{1,0:T(1,128)S(1)}) custom-call(bf16[4,3072]{1,0:T(4,128)(2,1)} %far_query.1, bf16[4,512]{1,0:T(4,128)(2,1)} %far_key.1, bf16[4,512]{1,0:T(4,128)(2,1)} %far_value.1, bf16[4,6144]{1,0:T(4,128)(2,1)} %tokens_ref.1, f32[1,6144]{1,0:T(1,128)} %bitcast.5), custom_call_target="tpu_custom_call" | custom-call | bytes 100000 | tf_op jit(solution)/shard_map/pack/pallas_call | solution.py:49
  4.6 0.0 slice-start
  4.6 0.0 slice-start.1
  4.7 0.0 slice-start.2
  4.7 0.0 copy-start
  4.7 1.0 %shares.1.share.share_ref = f32[32,128]{1,0:T(8,128)S(1)} custom-call(s32[2,32]{1,0:T(2,128)} %bitcast.6, f32[2,32]{1,0:T(2,128)} %bitcast.7, bf16[128,128]{1,0:T(8,128)(2,1)S(1)} %get-tuple-element.14.refs_0_.heads, bf16[1,6144,1024]{2,1,0:T(8,128)(2,1)} %gate_ref.1, bf16[1,6144,1024]{2,1,0:T(8,128)(2,1)} %up_ref.1), custom_call_target="tpu_custom_call" | custom-call | bytes 100000 | tf_op jit(solution)/shard_map/shares/pallas_call | solution.py:49
  5.7 0.3 collective-permute-done.2.got_ref
  5.9 0.2 norm_both.1.own_ref
  6.1 4.2 %collective-permute-start.3 = (bf16[8,3072]{1,0:T(8,128)(2,1)S(1)}, bf16[8,3072]{1,0:T(8,128)(2,1)S(1)}, u32[]{:S(2)}, u32[]{:S(2)}) collective-permute-start(bf16[8,3072]{1,0:T(8,128)(2,1)S(1)} %norm_both.1.own_ref), channel_id=1, source_target_pairs={{0,12},{2,14},{4,8},{6,10},{8,4},{10,6},{12,0},{14,2},{1,13},{3,15... | collective-permute-start | bytes 147464 | tf_op jit(solution)/shard_map/ppermute | solution.py:28
  10.3 0.0 collective-permute-start.4
  10.3 0.6 %collective-permute-start.5 = (bf16[8,3072]{1,0:T(8,128)(2,1)S(1)}, bf16[8,3072]{1,0:T(8,128)(2,1)S(1)}, u32[]{:S(2)}, u32[]{:S(2)}) collective-permute-start(bf16[8,3072]{1,0:T(8,128)(2,1)S(1)} %norm_both.1.own_ref), channel_id=1, source_target_pairs={{0,4},{2,6},{4,0},{6,2},{8,12},{10,14},{12,8},{14,10},{1,5},{3,7},... | collective-permute-start | bytes 147464 | tf_op jit(solution)/shard_map/ppermute | solution.py:28
  10.9 1.7 %collective-permute-start = (bf16[128,128]{1,0:T(8,128)(2,1)S(1)}, bf16[128,128]{1,0:T(8,128)(2,1)S(1)}, u32[]{:S(2)}, u32[]{:S(2)}) collective-permute-start(bf16[128,128]{1,0:T(8,128)(2,1)S(1)} %get-tuple-element.14.refs_0_.heads), channel_id=1, source_target_pairs={{0,2},{2,0},{4,6},{6,4},{8,10},{10,8},{12,14},{14,12},{1,3},{3,1},... | collective-permute-start | bytes 98312 | tf_op jit(solution)/shard_map/ppermute | solution.py:28
  12.6 2.3 %collective-permute-done.refs_1_ = bf16[128,128]{1,0:T(8,128)(2,1)S(1)} collective-permute-done((bf16[128,128]{1,0:T(8,128)(2,1)S(1)}, bf16[128,128]{1,0:T(8,128)(2,1)S(1)}, u32[]{:S(2)}, u32[]{:S(2)}) %collective-permute-start) | collective-permute-done | bytes 32800 | tf_op jit(solution)/shard_map/ppermute | solution.py:28
  14.9 0.0 collective-permute-done.3.last_ref
  14.9 0.4 collective-permute-done.4.far_ref
  15.3 0.0 collective-permute-done.5.next_ref
  15.3 0.1 collective-permute-start.6
  15.4 2.1 %collective-permute-start.1 = (bf16[256,128]{1,0:T(8,128)(2,1)S(1)}, bf16[256,128]{1,0:T(8,128)(2,1)S(1)}, u32[]{:S(2)}, u32[]{:S(2)}) collective-permute-start(bf16[256,128]{1,0:T(8,128)(2,1)S(1)} %stack.1.heads.own_ref), channel_id=1, source_target_pairs={{0,8},{2,10},{4,12},{6,14},{8,0},{10,2},{12,4},{14,6},{1,9},{3,11}... | collective-permute-start | bytes 196616 | tf_op jit(solution)/shard_map/ppermute | solution.py:28
  17.5 0.0 collective-permute-done.6.other_ref
  17.5 0.0 slice-done
  17.5 0.0 slice-done.1
  17.5 0.0 slice-done.2
  17.5 4.8 %gate_all.1 = (bf16[32,1024]{1,0:T(8,128)(2,1)S(1)}, bf16[1024,3072]{1,0:T(8,128)(2,1)S(1)}, bf16[1024,3072]{1,0:T(8,128)(2,1)S(1)}) custom-call(bf16[32,3072]{1,0:T(8,128)(2,1)S(1)} %stack_line.1.x_ref, bf16[32,3072]{1,0:T(8,128)(2,1)S(1)} %collective-permute-done.6.other_ref, bf16[1,6144,1024]{2,1,0:T(8,128)(2,1)S(1)} %bitcast.4, ...), custom_call_target="tpu_custom_call" | custom-call | flops 805306368 | bytes 37748736 | tf_op jit(solution)/shard_map/gate_all/pallas_call | solution.py:49
  22.3 0.0 collective-permute-done.1.got_ref
  22.3 0.0 copy-start.1
  22.3 0.0 copy-start.2
  22.3 0.0 copy-start.4
  22.4 0.0 copy-start.5
  22.4 1.3 %down.2.after = bf16[32,3072]{1,0:T(8,128)(2,1)S(1)} custom-call(bf16[32,1024]{1,0:T(8,128)(2,1)S(1)} %get-tuple-element.17.after.hidden_ref, bf16[1024,3072]{1,0:T(8,128)(2,1)S(1)} %get-tuple-element.19.down_ref, bf16[512,128]{1,0:T(8,128)(2,1)S(1)} %stack_after.1.after.near_ref.refs_0_), custom_call_target="tpu_custom_call" | custom-call | flops 201326592 | bytes 6291456 | tf_op jit(solution)/shard_map/down/pallas_call | solution.py:49
  23.7 0.2 collective-permute-start.8
  23.8 1.9 %collective-permute-start.7 = (bf16[512,128]{1,0:T(8,128)(2,1)S(1)}, bf16[512,128]{1,0:T(8,128)(2,1)S(1)}, u32[]{:S(2)}, u32[]{:S(2)}) collective-permute-start(bf16[512,128]{1,0:T(8,128)(2,1)S(1)} %stack_after.1.after.near_ref.refs_0_), channel_id=1, source_target_pairs={{0,4},{2,6},{4,0},{6,2},{8,12},{10,14},{12,8},{14,10},{1,5},{3,7},... | collective-permute-start | bytes 393224 | tf_op jit(solution)/shard_map/ppermute | solution.py:28
  25.8 1.3 %down.3.terms_ref = f32[32,3072]{1,0:T(8,128)S(1)} custom-call(bf16[32,1024]{1,0:T(8,128)(2,1)S(1)} %get-tuple-element.17.after.hidden_ref, bf16[1024,3072]{1,0:T(8,128)(2,1)S(1)} %get-tuple-element.18.down_ref, bf16[32,3072]{1,0:T(8,128)(2,1)S(1)} %down.2.after), custom_call_target="tpu_custom_call" | custom-call | flops 201326592 | bytes 6291456 | tf_op jit(solution)/shard_map/down/pallas_call | solution.py:49
  27.0 0.0 collective-permute-done.8.taken_ref
  27.1 0.2 collective-permute-start.10
  27.3 2.7 %collective-permute-start.11 = (bf16[8,3072]{1,0:T(8,128)(2,1)S(1)}, bf16[8,3072]{1,0:T(8,128)(2,1)S(1)}, u32[]{:S(2)}, u32[]{:S(2)}) collective-permute-start(bf16[8,3072]{1,0:T(8,128)(2,1)S(1)} %get-tuple-element.23), channel_id=1, source_target_pairs={{0,12},{2,14},{4,8},{6,10},{8,4},{10,6},{12,0},{14,2},{1,13},{3,15... | collective-permute-start | bytes 147464 | tf_op jit(solution)/shard_map/ppermute | solution.py:28
  30.0 0.7 %collective-permute-start.9 = (bf16[8,3072]{1,0:T(8,128)(2,1)S(1)}, bf16[8,3072]{1,0:T(8,128)(2,1)S(1)}, u32[]{:S(2)}, u32[]{:S(2)}) collective-permute-start(bf16[8,3072]{1,0:T(8,128)(2,1)S(1)} %get-tuple-element.21.after), channel_id=1, source_target_pairs={{0,8},{2,10},{4,12},{6,14},{8,0},{10,2},{12,4},{14,6},{1,9},{3,11}... | collective-permute-start | bytes 147464 | tf_op jit(solution)/shard_map/ppermute | solution.py:28
  30.7 0.0 collective-permute-done.7.far_ref.refs_1_
  30.7 2.2 %attend.1.refs_4_.refs_7_ = f32[72,128]{1,0:T(8,128)S(1)} custom-call(bf16[512,128]{1,0:T(8,128)(2,1)S(1)} %stack_after.1.after.near_ref.refs_0_, bf16[512,128]{1,0:T(8,128)(2,1)S(1)} %collective-permute-done.7.far_ref.refs_1_, bf16[4,512,512]{2,1,0:T(8,128)(2,1)S(1)} %copy-done.1, bf16[4,512,512]{2,1,0:T(8,128)(2,1)S(1)} %copy-done.2, s32[4]{0:T(128)S(1)} %copy-done.4, ...), custom_call_target="tpu_custom_call" | custom-call | flops 12582912 | bytes 2097152 | tf_op jit(solution)/shard_map/attend/pallas_call | solution.py:49
  32.9 0.0 collective-permute-done.10.refs_2_
  32.9 0.8 %collective-permute-done.11.refs_3_ = bf16[8,3072]{1,0:T(8,128)(2,1)S(1)} collective-permute-done((bf16[8,3072]{1,0:T(8,128)(2,1)S(1)}, bf16[8,3072]{1,0:T(8,128)(2,1)S(1)}, u32[]{:S(2)}, u32[]{:S(2)}) %collective-permute-start.11) | collective-permute-done | bytes 49184 | tf_op jit(solution)/shard_map/ppermute | solution.py:28
  33.8 1.9 %collective-permute-done.9.refs_1_ = bf16[8,3072]{1,0:T(8,128)(2,1)S(1)} collective-permute-done((bf16[8,3072]{1,0:T(8,128)(2,1)S(1)}, bf16[8,3072]{1,0:T(8,128)(2,1)S(1)}, u32[]{:S(2)}, u32[]{:S(2)}) %collective-permute-start.9) | collective-permute-done | bytes 49184 | tf_op jit(solution)/shard_map/ppermute | solution.py:28
  35.7 1.6 %collective-permute-start.12 = (bf16[4,3072]{1,0:T(4,128)(2,1)S(1)}, bf16[4,3072]{1,0:T(4,128)(2,1)S(1)}, u32[]{:S(2)}, u32[]{:S(2)}) collective-permute-start(bf16[4,3072]{1,0:T(4,128)(2,1)S(1)} %get-tuple-element.24.refs_6_), channel_id=1, source_target_pairs={{0,2},{2,0},{4,6},{6,4},{8,10},{10,8},{12,14},{14,12},{1,3},{3,1},... | collective-permute-start | bytes 73736 | tf_op jit(solution)/shard_map/ppermute | solution.py:28
  37.3 1.8 %attend_last.1.after = bf16[4,3072]{1,0:T(4,128)(2,1)} custom-call(bf16[512,128]{1,0:T(8,128)(2,1)S(1)} %stack_after.1.after.near_ref.refs_0_, bf16[512,128]{1,0:T(8,128)(2,1)S(1)} %collective-permute-done.7.far_ref.refs_1_, bf16[4,512,512]{2,1,0:T(8,128)(2,1)S(1)} %copy-done.1, bf16[4,512,512]{2,1,0:T(8,128)(2,1)S(1)} %copy-done.2, s32[4]{0:T(128)S(1)} %copy-done.4, ...), custom_call_target="tpu_custom_call" | custom-call | flops 12582912 | bytes 2097152 | tf_op jit(solution)/shard_map/attend_last/pallas_call | solution.py:49
  39.1 0.5 %collective-permute-done.12.taken_ref = bf16[4,3072]{1,0:T(4,128)(2,1)S(1)} collective-permute-done((bf16[4,3072]{1,0:T(4,128)(2,1)S(1)}, bf16[4,3072]{1,0:T(4,128)(2,1)S(1)}, u32[]{:S(2)}, u32[]{:S(2)}) %collective-permute-start.12) | collective-permute-done | bytes 24608 | tf_op jit(solution)/shard_map/ppermute | solution.py:28
  39.6 0.1 collective-permute-start.13
  39.7 1.2 %collective-permute-done.13.other_ref = bf16[4,3072]{1,0:T(4,128)(2,1)S(1)} collective-permute-done((bf16[4,3072]{1,0:T(4,128)(2,1)S(1)}, bf16[4,3072]{1,0:T(4,128)(2,1)S(1)}, u32[]{:S(2)}, u32[]{:S(2)}) %collective-permute-start.13) | collective-permute-done | bytes 24608 | tf_op jit(solution)/shard_map/ppermute | solution.py:28
  40.9 0.6 %join.1 = bf16[4,6144]{1,0:T(4,128)(2,1)} custom-call(bf16[4,3072]{1,0:T(4,128)(2,1)S(1)} %finish.1.own_ref, bf16[4,3072]{1,0:T(4,128)(2,1)S(1)} %collective-permute-done.13.other_ref), custom_call_target="tpu_custom_call" | custom-call | bytes 49152 | tf_op jit(solution)/shard_map/join/pallas_call | solution.py:49
  (14 shorter events, 0.2 us)
Async XLA Ops:
  0.6 5.3 %collective-permute-start.2 = (bf16[4,6144]{1,0:T(4,128)(2,1)}, bf16[4,6144]{1,0:T(4,128)(2,1)S(1)}, u32[]{:S(2)}, u32[]{:S(2)}) collective-permute-start(bf16[4,6144]{1,0:T(4,128)(2,1)} %tokens_ref.1), channel_id=1, source_target_pairs={{0,2},{2,0},{4,6},{6,4},{8,10},{10,8},{12,14},{14,12},{1,3},{3,1},... | collective-permute-start | bytes 147464 | tf_op jit(solution)/shard_map/ppermute | solution.py:28
  4.6 12.8 %slice-start = ((s8[12582912]{0:T(1024)(128)(4,1)}), s8[4194304]{0:T(1024)(128)(4,1)S(1)}, s32[]{:S(2)}) async-start(s8[12582912]{0:T(1024)(128)(4,1)} %bitcast.3), calls=%async_computation | async-start | bytes 8388608
  4.6 12.8 %slice-start.1 = ((s8[12582912]{0:T(1024)(128)(4,1)}), s8[4194304]{0:T(1024)(128)(4,1)S(1)}, s32[]{:S(2)}) async-start(s8[12582912]{0:T(1024)(128)(4,1)} %bitcast.3), calls=%async_computation.1 | async-start | bytes 8388608
  4.7 12.8 %slice-start.2 = ((s8[12582912]{0:T(1024)(128)(4,1)}), s8[4194304]{0:T(1024)(128)(4,1)S(1)}, s32[]{:S(2)}) async-start(s8[12582912]{0:T(1024)(128)(4,1)} %bitcast.3), calls=%async_computation.2 | async-start | bytes 8388608
  4.7 12.8 %copy-start = (bf16[1,6144,1024]{2,1,0:T(8,128)(2,1)S(1)}, bf16[1,6144,1024]{2,1,0:T(8,128)(2,1)}, u32[]{:S(2)}) copy-start(bf16[1,6144,1024]{2,1,0:T(8,128)(2,1)} %up_ref.1) | copy-start | bytes 37748740
  6.1 8.7 %collective-permute-start.3 = (bf16[8,3072]{1,0:T(8,128)(2,1)S(1)}, bf16[8,3072]{1,0:T(8,128)(2,1)S(1)}, u32[]{:S(2)}, u32[]{:S(2)}) collective-permute-start(bf16[8,3072]{1,0:T(8,128)(2,1)S(1)} %norm_both.1.own_ref), channel_id=1, source_target_pairs={{0,12},{2,14},{4,8},{6,10},{8,4},{10,6},{12,0},{14,2},{1,13},{3,15... | collective-permute-start | bytes 147464 | tf_op jit(solution)/shard_map/ppermute | solution.py:28
  10.3 5.0 %collective-permute-start.4 = (bf16[8,3072]{1,0:T(8,128)(2,1)S(1)}, bf16[8,3072]{1,0:T(8,128)(2,1)S(1)}, u32[]{:S(2)}, u32[]{:S(2)}) collective-permute-start(bf16[8,3072]{1,0:T(8,128)(2,1)S(1)} %norm_both.1.own_ref), channel_id=1, source_target_pairs={{0,8},{2,10},{4,12},{6,14},{8,0},{10,2},{12,4},{14,6},{1,9},{3,11}... | collective-permute-start | bytes 147464 | tf_op jit(solution)/shard_map/ppermute | solution.py:28
  10.3 5.0 %collective-permute-start.5 = (bf16[8,3072]{1,0:T(8,128)(2,1)S(1)}, bf16[8,3072]{1,0:T(8,128)(2,1)S(1)}, u32[]{:S(2)}, u32[]{:S(2)}) collective-permute-start(bf16[8,3072]{1,0:T(8,128)(2,1)S(1)} %norm_both.1.own_ref), channel_id=1, source_target_pairs={{0,4},{2,6},{4,0},{6,2},{8,12},{10,14},{12,8},{14,10},{1,5},{3,7},... | collective-permute-start | bytes 147464 | tf_op jit(solution)/shard_map/ppermute | solution.py:28
  10.9 3.9 %collective-permute-start = (bf16[128,128]{1,0:T(8,128)(2,1)S(1)}, bf16[128,128]{1,0:T(8,128)(2,1)S(1)}, u32[]{:S(2)}, u32[]{:S(2)}) collective-permute-start(bf16[128,128]{1,0:T(8,128)(2,1)S(1)} %get-tuple-element.14.refs_0_.heads), channel_id=1, source_target_pairs={{0,2},{2,0},{4,6},{6,4},{8,10},{10,8},{12,14},{14,12},{1,3},{3,1},... | collective-permute-start | bytes 98312 | tf_op jit(solution)/shard_map/ppermute | solution.py:28
  15.3 2.2 %collective-permute-start.6 = (bf16[32,3072]{1,0:T(8,128)(2,1)S(1)}, bf16[32,3072]{1,0:T(8,128)(2,1)S(1)}, u32[]{:S(2)}, u32[]{:S(2)}) collective-permute-start(bf16[32,3072]{1,0:T(8,128)(2,1)S(1)} %stack_line.1.x_ref), channel_id=1, source_target_pairs={{0,1},{1,0},{2,3},{3,2},{4,5},{5,4},{6,7},{7,6},{8,9},{9,8},{10,11... | collective-permute-start | bytes 589832 | tf_op jit(solution)/shard_map/ppermute | solution.py:28
  15.4 6.9 %collective-permute-start.1 = (bf16[256,128]{1,0:T(8,128)(2,1)S(1)}, bf16[256,128]{1,0:T(8,128)(2,1)S(1)}, u32[]{:S(2)}, u32[]{:S(2)}) collective-permute-start(bf16[256,128]{1,0:T(8,128)(2,1)S(1)} %stack.1.heads.own_ref), channel_id=1, source_target_pairs={{0,8},{2,10},{4,12},{6,14},{8,0},{10,2},{12,4},{14,6},{1,9},{3,11}... | collective-permute-start | bytes 196616 | tf_op jit(solution)/shard_map/ppermute | solution.py:28
  22.3 8.3 %copy-start.1 = (bf16[4,512,512]{2,1,0:T(8,128)(2,1)S(1)}, bf16[4,512,512]{2,1,0:T(8,128)(2,1)}, u32[]{:S(2)}) copy-start(bf16[4,512,512]{2,1,0:T(8,128)(2,1)} %refs_2_.3) | copy-start | bytes 6291460
  22.3 8.3 %copy-start.2 = (bf16[4,512,512]{2,1,0:T(8,128)(2,1)S(1)}, bf16[4,512,512]{2,1,0:T(8,128)(2,1)}, u32[]{:S(2)}) copy-start(bf16[4,512,512]{2,1,0:T(8,128)(2,1)} %refs_3_.1) | copy-start | bytes 6291460
  22.3 8.3 %copy-start.4 = (s32[4]{0:T(128)S(1)}, s32[4]{0:T(128)}, u32[]{:S(2)}) copy-start(s32[4]{0:T(128)} %refs_4_.1) | copy-start | bytes 52
  22.4 8.3 %copy-start.5 = (s32[4]{0:T(128)S(1)}, s32[4]{0:T(128)}, u32[]{:S(2)}) copy-start(s32[4]{0:T(128)} %refs_5_.1) | copy-start | bytes 52
  23.7 3.4 %collective-permute-start.8 = (bf16[32,3072]{1,0:T(8,128)(2,1)S(1)}, bf16[32,3072]{1,0:T(8,128)(2,1)S(1)}, u32[]{:S(2)}, u32[]{:S(2)}) collective-permute-start(bf16[32,3072]{1,0:T(8,128)(2,1)S(1)} %down.2.after), channel_id=1, source_target_pairs={{0,1},{1,0},{2,3},{3,2},{4,5},{5,4},{6,7},{7,6},{8,9},{9,8},{10,11... | collective-permute-start | bytes 589832 | tf_op jit(solution)/shard_map/ppermute | solution.py:28
  23.8 6.8 %collective-permute-start.7 = (bf16[512,128]{1,0:T(8,128)(2,1)S(1)}, bf16[512,128]{1,0:T(8,128)(2,1)S(1)}, u32[]{:S(2)}, u32[]{:S(2)}) collective-permute-start(bf16[512,128]{1,0:T(8,128)(2,1)S(1)} %stack_after.1.after.near_ref.refs_0_), channel_id=1, source_target_pairs={{0,4},{2,6},{4,0},{6,2},{8,12},{10,14},{12,8},{14,10},{1,5},{3,7},... | collective-permute-start | bytes 393224 | tf_op jit(solution)/shard_map/ppermute | solution.py:28
  27.0 12.5 %copy-start.3 = (bf16[4,6144]{1,0:T(4,128)(2,1)S(1)}, bf16[4,6144]{1,0:T(4,128)(2,1)}, u32[]{:S(2)}) copy-start(bf16[4,6144]{1,0:T(4,128)(2,1)} %tokens_ref.1) | copy-start | bytes 147460
  27.1 5.8 %collective-permute-start.10 = (bf16[8,3072]{1,0:T(8,128)(2,1)S(1)}, bf16[8,3072]{1,0:T(8,128)(2,1)S(1)}, u32[]{:S(2)}, u32[]{:S(2)}) collective-permute-start(bf16[8,3072]{1,0:T(8,128)(2,1)S(1)} %get-tuple-element.22), channel_id=1, source_target_pairs={{0,4},{2,6},{4,0},{6,2},{8,12},{10,14},{12,8},{14,10},{1,5},{3,7},... | collective-permute-start | bytes 147464 | tf_op jit(solution)/shard_map/ppermute | solution.py:28
  27.3 6.5 %collective-permute-start.11 = (bf16[8,3072]{1,0:T(8,128)(2,1)S(1)}, bf16[8,3072]{1,0:T(8,128)(2,1)S(1)}, u32[]{:S(2)}, u32[]{:S(2)}) collective-permute-start(bf16[8,3072]{1,0:T(8,128)(2,1)S(1)} %get-tuple-element.23), channel_id=1, source_target_pairs={{0,12},{2,14},{4,8},{6,10},{8,4},{10,6},{12,0},{14,2},{1,13},{3,15... | collective-permute-start | bytes 147464 | tf_op jit(solution)/shard_map/ppermute | solution.py:28
  30.0 5.6 %collective-permute-start.9 = (bf16[8,3072]{1,0:T(8,128)(2,1)S(1)}, bf16[8,3072]{1,0:T(8,128)(2,1)S(1)}, u32[]{:S(2)}, u32[]{:S(2)}) collective-permute-start(bf16[8,3072]{1,0:T(8,128)(2,1)S(1)} %get-tuple-element.21.after), channel_id=1, source_target_pairs={{0,8},{2,10},{4,12},{6,14},{8,0},{10,2},{12,4},{14,6},{1,9},{3,11}... | collective-permute-start | bytes 147464 | tf_op jit(solution)/shard_map/ppermute | solution.py:28
  35.7 3.9 %collective-permute-start.12 = (bf16[4,3072]{1,0:T(4,128)(2,1)S(1)}, bf16[4,3072]{1,0:T(4,128)(2,1)S(1)}, u32[]{:S(2)}, u32[]{:S(2)}) collective-permute-start(bf16[4,3072]{1,0:T(4,128)(2,1)S(1)} %get-tuple-element.24.refs_6_), channel_id=1, source_target_pairs={{0,2},{2,0},{4,6},{6,4},{8,10},{10,8},{12,14},{14,12},{1,3},{3,1},... | collective-permute-start | bytes 73736 | tf_op jit(solution)/shard_map/ppermute | solution.py:28
  39.6 1.3 %collective-permute-start.13 = (bf16[4,3072]{1,0:T(4,128)(2,1)S(1)}, bf16[4,3072]{1,0:T(4,128)(2,1)S(1)}, u32[]{:S(2)}, u32[]{:S(2)}) collective-permute-start(bf16[4,3072]{1,0:T(4,128)(2,1)S(1)} %finish.1.own_ref), channel_id=1, source_target_pairs={{0,1},{1,0},{2,3},{3,2},{4,5},{5,4},{6,7},{7,6},{8,9},{9,8},{10,11... | collective-permute-start | bytes 73736 | tf_op jit(solution)/shard_map/ppermute | solution.py:28

commit v11 on v10

--- a/solution.py
+++ b/solution.py
@@ -121,8 +121,18 @@
     refs[-1][...] = stacked(refs[:-1]).astype(refs[-1].dtype)
 
 
-def stack_line(own_ref, last_ref, far_ref, next_ref, heads, out_ref):
-    stack(own_ref, far_ref, next_ref, last_ref, out_ref)
+def stack_line(own_ref, last_ref, far_ref, got_heads, next_ref, own_heads, out_ref, heads_ref):
+    count = own_heads.shape[0]
+    heads_ref[:count, :] = own_heads[...]
+    heads_ref[count:, :] = got_heads[:count, :]
+    rows = [own_ref, far_ref, next_ref, last_ref]
+    out_ref[...] = stacked(rows).astype(jnp.bfloat16)
+
+
+def widen(own_ref, out_ref):
+    count = own_ref.shape[0]
+    out_ref[:count, :] = own_ref[...]
+    out_ref[count:, :] = jnp.zeros((out_ref.shape[0] - count, HD), out_ref.dtype)
 
 
 def stack_after(own_ref, got_ref, after, out_ref):
@@ -323,6 +333,7 @@
 
 def make_local(wide):
     steps = steps_of(wide)
+    head_steps = [*steps[1:-2], *steps[:1], *steps[-2:]]
 
     def local(
         queries,
@@ -398,18 +409,19 @@
                 size=8 * x.size,
                 far=(2,),
             )
-        heads = grown(heads, steps[0])
         line_steps = [steps[-2], steps[-1], steps[-2] ^ steps[-1]]
         last = swap(x, "wide", wide, line_steps[2])
         line = [swap(x, "wide", wide, step) for step in line_steps[:2]]
+        wider = max(x.shape[0] * half // HD, heads.shape[0])
+        sent_heads = call(widen, shape((wider, HD), bf16), [heads], size=4 * wider * HD)
+        far_rows = swap(sent_heads, "wide", wide, steps[0])
+        x, heads = call(
+            stack_line,
+            [shape((count, half), bf16), shape((2 * heads.shape[0], HD), bf16)],
+            [x, last, line[0], far_rows, line[1], heads],
+            size=8 * count * half,
+        )
         got_heads = swap(heads, "wide", wide, steps[-2])
-        x = call(
-            stack_line,
-            shape((count, half), bf16),
-            [x, last, *line, heads],
-            size=8 * count * half,
-            far=(4,),
-        )
 
         product = 2 * count * half * units
         other_x = swap(x, "narrow", 2, 1)
@@ -469,8 +481,9 @@
             size=terms.size * 8,
         )
         taken = [swap(part, "wide", wide, step) for part, step in zip(sent, line_steps)]
+        taken = [taken[i] for i in (1, 2, 0)]
         early = call(
-            functools.partial(attend, steps, early_slots),
+            functools.partial(attend, head_steps, early_slots),
             shape((len(early_slots) * heads_local, HD), f32),
             [heads, far_heads, *caches, sent[0]],
             flops=2 * key_cache.size * GROUP,
@@ -489,7 +502,7 @@
             )
             taken = [swap(sent, "wide", wide, step)]
         context = call(
-            functools.partial(attend_last, steps, late_slots, heads_local),
+            functools.partial(attend_last, head_steps, late_slots, heads_local),
             shape(queries.shape, bf16),
             [heads, far_heads, *caches, sent, early],
             [

time: 41.7 us -> 39.9 us (0.957)
  starting transfers between devices: 19 us -> 16.9 us
    ppermute x14, starting transfers between devices: 19 us -> 16.9 us  [swap(): return lax.ppermute(block, axis, [(i, i ^ step) for i in range(count)])]
  transfers between devices with their start and end apart: 14 -> 14, of which waited for: 7 -> 6; matrix products, arithmetic and copies ran while one was open for 0% -> 0% of each run, Pallas kernels for 29% -> 31%
where the time goes in v11:
time: 39.9 us; the launch traced here: 39.8 us
  starting transfers between devices  16.9 us (42%)
  Pallas kernels  14.2 us (36%)
  waiting for transfers between devices  7.7 us (19%)
  between operations  0.87 us (2%)
    ppermute x14, starting transfers between devices, swap(): return lax.ppermute(block, axis, [(i, i ^ step) for i in range(count)])  16.9 us
    pallas_call x15, Pallas kernels, call(): pl.pallas_call(kernel, name=getattr(kernel, 'func', kernel).__name__, out...  14.2 us
    ppermute x14, waiting for transfers between devices, swap(): return lax.ppermute(block, axis, [(i, i ^ step) for i in range(count)])  7.7 us
  transfers between devices with their start and end apart: 14, of which 6 were waited for; matrix products, arithmetic and copies ran while one was open for 0% of the time, Pallas kernels for 31%

profile of v11, /device:TPU:0, one launch (start us, length us, event | category | flops | bytes accessed | tf_op | source)
XLA Modules:
  0.0 39.8 jit_solution(1360394045029654179)
XLA Ops:
  0.6 3.0 %collective-permute-start = (bf16[4,6144]{1,0:T(4,128)(2,1)}, bf16[4,6144]{1,0:T(4,128)(2,1)S(1)}, u32[]{:S(2)}, u32[]{:S(2)}) collective-permute-start(bf16[4,6144]{1,0:T(4,128)(2,1)} %tokens_ref.1), channel_id=1, source_target_pairs={{0,2},{2,0},{4,6},{6,4},{8,10},{10,8},{12,14},{14,12},{1,3},{3,1},... | collective-permute-start | bytes 147464 | tf_op jit(solution)/shard_map/ppermute | solution.py:28
  3.7 1.0 %pack.1 = (bf16[128,128]{1,0:T(8,128)(2,1)S(1)}, bf16[4,6144]{1,0:T(4,128)(2,1)S(1)}, f32[1,6144]{1,0:T(1,128)S(1)}) custom-call(bf16[4,3072]{1,0:T(4,128)(2,1)} %far_query.1, bf16[4,512]{1,0:T(4,128)(2,1)} %far_key.1, bf16[4,512]{1,0:T(4,128)(2,1)} %far_value.1, bf16[4,6144]{1,0:T(4,128)(2,1)} %tokens_ref.1, f32[1,6144]{1,0:T(1,128)} %bitcast.5), custom_call_target="tpu_custom_call" | custom-call | bytes 100000 | tf_op jit(solution)/shard_map/pack/pallas_call | solution.py:49
  4.6 0.1 collective-permute-start.3
  4.7 0.0 slice-start
  4.7 0.0 slice-start.1
  4.7 0.0 slice-start.2
  4.8 0.0 copy-start
  4.8 1.0 %shares.1.share.share_ref = f32[32,128]{1,0:T(8,128)S(1)} custom-call(s32[2,32]{1,0:T(2,128)} %bitcast.6, f32[2,32]{1,0:T(2,128)} %bitcast.7, bf16[128,128]{1,0:T(8,128)(2,1)S(1)} %get-tuple-element.18.refs_0_.heads.own_ref.own_heads, bf16[1,6144,1024]{2,1,0:T(8,128)(2,1)} %gate_ref.1, bf16[1,6144,1024]{2,1,0:T(8,128)(2,1)} %up_ref.1), custom_call_target="tpu_custom_call" | custom-call | bytes 100000 | tf_op jit(solution)/shard_map/shares/pallas_call | solution.py:49
  5.7 0.2 collective-permute-done.got_ref
  5.9 0.2 norm_both.1.own_ref
  6.1 4.2 %collective-permute-start.1 = (bf16[8,3072]{1,0:T(8,128)(2,1)S(1)}, bf16[8,3072]{1,0:T(8,128)(2,1)S(1)}, u32[]{:S(2)}, u32[]{:S(2)}) collective-permute-start(bf16[8,3072]{1,0:T(8,128)(2,1)S(1)} %norm_both.1.own_ref), channel_id=1, source_target_pairs={{0,12},{2,14},{4,8},{6,10},{8,4},{10,6},{12,0},{14,2},{1,13},{3,15... | collective-permute-start | bytes 147464 | tf_op jit(solution)/shard_map/ppermute | solution.py:28
  10.3 0.0 collective-permute-start.2
  10.3 0.6 %collective-permute-start.4 = (bf16[8,3072]{1,0:T(8,128)(2,1)S(1)}, bf16[8,3072]{1,0:T(8,128)(2,1)S(1)}, u32[]{:S(2)}, u32[]{:S(2)}) collective-permute-start(bf16[8,3072]{1,0:T(8,128)(2,1)S(1)} %norm_both.1.own_ref), channel_id=1, source_target_pairs={{0,4},{2,6},{4,0},{6,2},{8,12},{10,14},{12,8},{14,10},{1,5},{3,7},... | collective-permute-start | bytes 147464 | tf_op jit(solution)/shard_map/ppermute | solution.py:28
  10.9 0.0 collective-permute-done.3.got_heads
  10.9 1.8 %collective-permute-done.1.last_ref = bf16[8,3072]{1,0:T(8,128)(2,1)S(1)} collective-permute-done((bf16[8,3072]{1,0:T(8,128)(2,1)S(1)}, bf16[8,3072]{1,0:T(8,128)(2,1)S(1)}, u32[]{:S(2)}, u32[]{:S(2)}) %collective-permute-start.1) | collective-permute-done | bytes 49184 | tf_op jit(solution)/shard_map/ppermute | solution.py:28
  12.7 2.6 %collective-permute-done.2.far_ref = bf16[8,3072]{1,0:T(8,128)(2,1)S(1)} collective-permute-done((bf16[8,3072]{1,0:T(8,128)(2,1)S(1)}, bf16[8,3072]{1,0:T(8,128)(2,1)S(1)}, u32[]{:S(2)}, u32[]{:S(2)}) %collective-permute-start.2) | collective-permute-done | bytes 49184 | tf_op jit(solution)/shard_map/ppermute | solution.py:28
  15.3 0.0 collective-permute-done.4.next_ref
  15.3 0.1 collective-permute-start.6
  15.4 2.1 %collective-permute-start.5 = (bf16[256,128]{1,0:T(8,128)(2,1)S(1)}, bf16[256,128]{1,0:T(8,128)(2,1)S(1)}, u32[]{:S(2)}, u32[]{:S(2)}) collective-permute-start(bf16[256,128]{1,0:T(8,128)(2,1)S(1)} %get-tuple-element.19.own_ref), channel_id=1, source_target_pairs={{0,8},{2,10},{4,12},{6,14},{8,0},{10,2},{12,4},{14,6},{1,9},{3,11}... | collective-permute-start | bytes 196616 | tf_op jit(solution)/shard_map/ppermute | solution.py:28
  17.5 0.0 collective-permute-done.6.other_ref
  17.5 0.0 slice-done
  17.5 0.0 slice-done.1
  17.5 0.0 slice-done.2
  17.5 4.8 %gate_all.1 = (bf16[32,1024]{1,0:T(8,128)(2,1)S(1)}, bf16[1024,3072]{1,0:T(8,128)(2,1)S(1)}, bf16[1024,3072]{1,0:T(8,128)(2,1)S(1)}) custom-call(bf16[32,3072]{1,0:T(8,128)(2,1)S(1)} %get-tuple-element.20.x_ref, bf16[32,3072]{1,0:T(8,128)(2,1)S(1)} %collective-permute-done.6.other_ref, bf16[1,6144,1024]{2,1,0:T(8,128)(2,1)S(1)} %bitcast.4, ...), custom_call_target="tpu_custom_call" | custom-call | flops 805306368 | bytes 37748736 | tf_op jit(solution)/shard_map/gate_all/pallas_call | solution.py:49
  22.3 0.0 collective-permute-done.5.got_ref
  22.3 0.0 copy-start.1
  22.3 0.0 copy-start.2
  22.3 0.0 copy-start.4
  22.4 0.0 copy-start.5
  22.4 1.3 %down.2.after = bf16[32,3072]{1,0:T(8,128)(2,1)S(1)} custom-call(bf16[32,1024]{1,0:T(8,128)(2,1)S(1)} %get-tuple-element.21.after.hidden_ref, bf16[1024,3072]{1,0:T(8,128)(2,1)S(1)} %get-tuple-element.23.down_ref, bf16[512,128]{1,0:T(8,128)(2,1)S(1)} %stack_after.1.after.near_ref.refs_0_), custom_call_target="tpu_custom_call" | custom-call | flops 201326592 | bytes 6291456 | tf_op jit(solution)/shard_map/down/pallas_call | solution.py:49
  23.7 0.2 collective-permute-start.8
  23.9 0.1 collective-permute-start.7
  24.0 1.3 %down.3.terms_ref = f32[32,3072]{1,0:T(8,128)S(1)} custom-call(bf16[32,1024]{1,0:T(8,128)(2,1)S(1)} %get-tuple-element.21.after.hidden_ref, bf16[1024,3072]{1,0:T(8,128)(2,1)S(1)} %get-tuple-element.22.down_ref, bf16[32,3072]{1,0:T(8,128)(2,1)S(1)} %down.2.after), custom_call_target="tpu_custom_call" | custom-call | flops 201326592 | bytes 6291456 | tf_op jit(solution)/shard_map/down/pallas_call | solution.py:49
  25.3 0.0 collective-permute-done.8.taken_ref
  25.4 2.7 %collective-permute-start.10 = (bf16[8,3072]{1,0:T(8,128)(2,1)S(1)}, bf16[8,3072]{1,0:T(8,128)(2,1)S(1)}, u32[]{:S(2)}, u32[]{:S(2)}) collective-permute-start(bf16[8,3072]{1,0:T(8,128)(2,1)S(1)} %get-tuple-element.26), channel_id=1, source_target_pairs={{0,12},{2,14},{4,8},{6,10},{8,4},{10,6},{12,0},{14,2},{1,13},{3,15... | collective-permute-start | bytes 147464 | tf_op jit(solution)/shard_map/ppermute | solution.py:28
  28.1 0.7 %collective-permute-start.11 = (bf16[8,3072]{1,0:T(8,128)(2,1)S(1)}, bf16[8,3072]{1,0:T(8,128)(2,1)S(1)}, u32[]{:S(2)}, u32[]{:S(2)}) collective-permute-start(bf16[8,3072]{1,0:T(8,128)(2,1)S(1)} %get-tuple-element.27.after), channel_id=1, source_target_pairs={{0,8},{2,10},{4,12},{6,14},{8,0},{10,2},{12,4},{14,6},{1,9},{3,11}... | collective-permute-start | bytes 147464 | tf_op jit(solution)/shard_map/ppermute | solution.py:28
  28.8 1.0 %collective-permute-start.9 = (bf16[8,3072]{1,0:T(8,128)(2,1)S(1)}, bf16[8,3072]{1,0:T(8,128)(2,1)S(1)}, u32[]{:S(2)}, u32[]{:S(2)}) collective-permute-start(bf16[8,3072]{1,0:T(8,128)(2,1)S(1)} %get-tuple-element.25), channel_id=1, source_target_pairs={{0,4},{2,6},{4,0},{6,2},{8,12},{10,14},{12,8},{14,10},{1,5},{3,7},... | collective-permute-start | bytes 147464 | tf_op jit(solution)/shard_map/ppermute | solution.py:28
  29.8 0.0 collective-permute-done.7.far_ref.refs_1_
  29.8 2.2 %attend.1.refs_4_.refs_7_ = f32[72,128]{1,0:T(8,128)S(1)} custom-call(bf16[512,128]{1,0:T(8,128)(2,1)S(1)} %stack_after.1.after.near_ref.refs_0_, bf16[512,128]{1,0:T(8,128)(2,1)S(1)} %collective-permute-done.7.far_ref.refs_1_, bf16[4,512,512]{2,1,0:T(8,128)(2,1)S(1)} %copy-done.1, bf16[4,512,512]{2,1,0:T(8,128)(2,1)S(1)} %copy-done.2, s32[4]{0:T(128)S(1)} %copy-done.4, ...), custom_call_target="tpu_custom_call" | custom-call | flops 12582912 | bytes 2097152 | tf_op jit(solution)/shard_map/attend/pallas_call | solution.py:49
  32.0 0.0 collective-permute-done.10.refs_2_
  32.1 1.9 %collective-permute-done.11.refs_3_ = bf16[8,3072]{1,0:T(8,128)(2,1)S(1)} collective-permute-done((bf16[8,3072]{1,0:T(8,128)(2,1)S(1)}, bf16[8,3072]{1,0:T(8,128)(2,1)S(1)}, u32[]{:S(2)}, u32[]{:S(2)}) %collective-permute-start.11) | collective-permute-done | bytes 49184 | tf_op jit(solution)/shard_map/ppermute | solution.py:28
  33.9 0.0 collective-permute-done.9.refs_1_
  33.9 2.0 %collective-permute-start.12 = (bf16[4,3072]{1,0:T(4,128)(2,1)S(1)}, bf16[4,3072]{1,0:T(4,128)(2,1)S(1)}, u32[]{:S(2)}, u32[]{:S(2)}) collective-permute-start(bf16[4,3072]{1,0:T(4,128)(2,1)S(1)} %get-tuple-element.28.refs_6_), channel_id=1, source_target_pairs={{0,2},{2,0},{4,6},{6,4},{8,10},{10,8},{12,14},{14,12},{1,3},{3,1},... | collective-permute-start | bytes 73736 | tf_op jit(solution)/shard_map/ppermute | solution.py:28
  36.0 1.8 %attend_last.1.after = bf16[4,3072]{1,0:T(4,128)(2,1)} custom-call(bf16[512,128]{1,0:T(8,128)(2,1)S(1)} %stack_after.1.after.near_ref.refs_0_, bf16[512,128]{1,0:T(8,128)(2,1)S(1)} %collective-permute-done.7.far_ref.refs_1_, bf16[4,512,512]{2,1,0:T(8,128)(2,1)S(1)} %copy-done.1, bf16[4,512,512]{2,1,0:T(8,128)(2,1)S(1)} %copy-done.2, s32[4]{0:T(128)S(1)} %copy-done.4, ...), custom_call_target="tpu_custom_call" | custom-call | flops 12582912 | bytes 2097152 | tf_op jit(solution)/shard_map/attend_last/pallas_call | solution.py:49
  37.8 0.1 collective-permute-done.12.taken_ref
  37.9 0.1 collective-permute-start.13
  37.9 1.2 %collective-permute-done.13.other_ref = bf16[4,3072]{1,0:T(4,128)(2,1)S(1)} collective-permute-done((bf16[4,3072]{1,0:T(4,128)(2,1)S(1)}, bf16[4,3072]{1,0:T(4,128)(2,1)S(1)}, u32[]{:S(2)}, u32[]{:S(2)}) %collective-permute-start.13) | collective-permute-done | bytes 24608 | tf_op jit(solution)/shard_map/ppermute | solution.py:28
  39.1 0.6 %join.1 = bf16[4,6144]{1,0:T(4,128)(2,1)} custom-call(bf16[4,3072]{1,0:T(4,128)(2,1)S(1)} %finish.1.own_ref, bf16[4,3072]{1,0:T(4,128)(2,1)S(1)} %collective-permute-done.13.other_ref), custom_call_target="tpu_custom_call" | custom-call | bytes 49152 | tf_op jit(solution)/shard_map/join/pallas_call | solution.py:49
  (14 shorter events, 0.2 us)
Async XLA Ops:
  0.6 5.3 %collective-permute-start = (bf16[4,6144]{1,0:T(4,128)(2,1)}, bf16[4,6144]{1,0:T(4,128)(2,1)S(1)}, u32[]{:S(2)}, u32[]{:S(2)}) collective-permute-start(bf16[4,6144]{1,0:T(4,128)(2,1)} %tokens_ref.1), channel_id=1, source_target_pairs={{0,2},{2,0},{4,6},{6,4},{8,10},{10,8},{12,14},{14,12},{1,3},{3,1},... | collective-permute-start | bytes 147464 | tf_op jit(solution)/shard_map/ppermute | solution.py:28
  4.6 6.3 %collective-permute-start.3 = (bf16[192,128]{1,0:T(8,128)(2,1)S(1)}, bf16[192,128]{1,0:T(8,128)(2,1)S(1)}, u32[]{:S(2)}, u32[]{:S(2)}) collective-permute-start(bf16[192,128]{1,0:T(8,128)(2,1)S(1)} %widen.1), channel_id=1, source_target_pairs={{0,2},{2,0},{4,6},{6,4},{8,10},{10,8},{12,14},{14,12},{1,3},{3,1},... | collective-permute-start | bytes 147464 | tf_op jit(solution)/shard_map/ppermute | solution.py:28
  4.7 12.7 %slice-start = ((s8[12582912]{0:T(1024)(128)(4,1)}), s8[4194304]{0:T(1024)(128)(4,1)S(1)}, s32[]{:S(2)}) async-start(s8[12582912]{0:T(1024)(128)(4,1)} %bitcast.3), calls=%async_computation | async-start | bytes 8388608
  4.7 12.7 %slice-start.1 = ((s8[12582912]{0:T(1024)(128)(4,1)}), s8[4194304]{0:T(1024)(128)(4,1)S(1)}, s32[]{:S(2)}) async-start(s8[12582912]{0:T(1024)(128)(4,1)} %bitcast.3), calls=%async_computation.1 | async-start | bytes 8388608
  4.7 12.7 %slice-start.2 = ((s8[12582912]{0:T(1024)(128)(4,1)}), s8[4194304]{0:T(1024)(128)(4,1)S(1)}, s32[]{:S(2)}) async-start(s8[12582912]{0:T(1024)(128)(4,1)} %bitcast.3), calls=%async_computation.2 | async-start | bytes 8388608
  4.8 12.7 %copy-start = (bf16[1,6144,1024]{2,1,0:T(8,128)(2,1)S(1)}, bf16[1,6144,1024]{2,1,0:T(8,128)(2,1)}, u32[]{:S(2)}) copy-start(bf16[1,6144,1024]{2,1,0:T(8,128)(2,1)} %up_ref.1) | copy-start | bytes 37748740
  6.1 6.6 %collective-permute-start.1 = (bf16[8,3072]{1,0:T(8,128)(2,1)S(1)}, bf16[8,3072]{1,0:T(8,128)(2,1)S(1)}, u32[]{:S(2)}, u32[]{:S(2)}) collective-permute-start(bf16[8,3072]{1,0:T(8,128)(2,1)S(1)} %norm_both.1.own_ref), channel_id=1, source_target_pairs={{0,12},{2,14},{4,8},{6,10},{8,4},{10,6},{12,0},{14,2},{1,13},{3,15... | collective-permute-start | bytes 147464 | tf_op jit(solution)/shard_map/ppermute | solution.py:28
  10.3 5.0 %collective-permute-start.2 = (bf16[8,3072]{1,0:T(8,128)(2,1)S(1)}, bf16[8,3072]{1,0:T(8,128)(2,1)S(1)}, u32[]{:S(2)}, u32[]{:S(2)}) collective-permute-start(bf16[8,3072]{1,0:T(8,128)(2,1)S(1)} %norm_both.1.own_ref), channel_id=1, source_target_pairs={{0,8},{2,10},{4,12},{6,14},{8,0},{10,2},{12,4},{14,6},{1,9},{3,11}... | collective-permute-start | bytes 147464 | tf_op jit(solution)/shard_map/ppermute | solution.py:28
  10.3 5.0 %collective-permute-start.4 = (bf16[8,3072]{1,0:T(8,128)(2,1)S(1)}, bf16[8,3072]{1,0:T(8,128)(2,1)S(1)}, u32[]{:S(2)}, u32[]{:S(2)}) collective-permute-start(bf16[8,3072]{1,0:T(8,128)(2,1)S(1)} %norm_both.1.own_ref), channel_id=1, source_target_pairs={{0,4},{2,6},{4,0},{6,2},{8,12},{10,14},{12,8},{14,10},{1,5},{3,7},... | collective-permute-start | bytes 147464 | tf_op jit(solution)/shard_map/ppermute | solution.py:28
  15.3 2.1 %collective-permute-start.6 = (bf16[32,3072]{1,0:T(8,128)(2,1)S(1)}, bf16[32,3072]{1,0:T(8,128)(2,1)S(1)}, u32[]{:S(2)}, u32[]{:S(2)}) collective-permute-start(bf16[32,3072]{1,0:T(8,128)(2,1)S(1)} %get-tuple-element.20.x_ref), channel_id=1, source_target_pairs={{0,1},{1,0},{2,3},{3,2},{4,5},{5,4},{6,7},{7,6},{8,9},{9,8},{10,11... | collective-permute-start | bytes 589832 | tf_op jit(solution)/shard_map/ppermute | solution.py:28
  15.4 6.9 %collective-permute-start.5 = (bf16[256,128]{1,0:T(8,128)(2,1)S(1)}, bf16[256,128]{1,0:T(8,128)(2,1)S(1)}, u32[]{:S(2)}, u32[]{:S(2)}) collective-permute-start(bf16[256,128]{1,0:T(8,128)(2,1)S(1)} %get-tuple-element.19.own_ref), channel_id=1, source_target_pairs={{0,8},{2,10},{4,12},{6,14},{8,0},{10,2},{12,4},{14,6},{1,9},{3,11}... | collective-permute-start | bytes 196616 | tf_op jit(solution)/shard_map/ppermute | solution.py:28
  22.3 7.5 %copy-start.1 = (bf16[4,512,512]{2,1,0:T(8,128)(2,1)S(1)}, bf16[4,512,512]{2,1,0:T(8,128)(2,1)}, u32[]{:S(2)}) copy-start(bf16[4,512,512]{2,1,0:T(8,128)(2,1)} %refs_2_.3) | copy-start | bytes 6291460
  22.3 7.5 %copy-start.2 = (bf16[4,512,512]{2,1,0:T(8,128)(2,1)S(1)}, bf16[4,512,512]{2,1,0:T(8,128)(2,1)}, u32[]{:S(2)}) copy-start(bf16[4,512,512]{2,1,0:T(8,128)(2,1)} %refs_3_.1) | copy-start | bytes 6291460
  22.3 7.5 %copy-start.4 = (s32[4]{0:T(128)S(1)}, s32[4]{0:T(128)}, u32[]{:S(2)}) copy-start(s32[4]{0:T(128)} %refs_4_.1) | copy-start | bytes 52
  22.4 7.5 %copy-start.5 = (s32[4]{0:T(128)S(1)}, s32[4]{0:T(128)}, u32[]{:S(2)}) copy-start(s32[4]{0:T(128)} %refs_5_.1) | copy-start | bytes 52
  23.7 1.6 %collective-permute-start.8 = (bf16[32,3072]{1,0:T(8,128)(2,1)S(1)}, bf16[32,3072]{1,0:T(8,128)(2,1)S(1)}, u32[]{:S(2)}, u32[]{:S(2)}) collective-permute-start(bf16[32,3072]{1,0:T(8,128)(2,1)S(1)} %down.2.after), channel_id=1, source_target_pairs={{0,1},{1,0},{2,3},{3,2},{4,5},{5,4},{6,7},{7,6},{8,9},{9,8},{10,11... | collective-permute-start | bytes 589832 | tf_op jit(solution)/shard_map/ppermute | solution.py:28
  23.9 6.0 %collective-permute-start.7 = (bf16[512,128]{1,0:T(8,128)(2,1)S(1)}, bf16[512,128]{1,0:T(8,128)(2,1)S(1)}, u32[]{:S(2)}, u32[]{:S(2)}) collective-permute-start(bf16[512,128]{1,0:T(8,128)(2,1)S(1)} %stack_after.1.after.near_ref.refs_0_), channel_id=1, source_target_pairs={{0,4},{2,6},{4,0},{6,2},{8,12},{10,14},{12,8},{14,10},{1,5},{3,7},... | collective-permute-start | bytes 393224 | tf_op jit(solution)/shard_map/ppermute | solution.py:28
  25.3 12.6 %copy-start.3 = (bf16[4,6144]{1,0:T(4,128)(2,1)S(1)}, bf16[4,6144]{1,0:T(4,128)(2,1)}, u32[]{:S(2)}) copy-start(bf16[4,6144]{1,0:T(4,128)(2,1)} %tokens_ref.1) | copy-start | bytes 147460
  25.4 6.7 %collective-permute-start.10 = (bf16[8,3072]{1,0:T(8,128)(2,1)S(1)}, bf16[8,3072]{1,0:T(8,128)(2,1)S(1)}, u32[]{:S(2)}, u32[]{:S(2)}) collective-permute-start(bf16[8,3072]{1,0:T(8,128)(2,1)S(1)} %get-tuple-element.26), channel_id=1, source_target_pairs={{0,12},{2,14},{4,8},{6,10},{8,4},{10,6},{12,0},{14,2},{1,13},{3,15... | collective-permute-start | bytes 147464 | tf_op jit(solution)/shard_map/ppermute | solution.py:28
  28.1 5.8 %collective-permute-start.11 = (bf16[8,3072]{1,0:T(8,128)(2,1)S(1)}, bf16[8,3072]{1,0:T(8,128)(2,1)S(1)}, u32[]{:S(2)}, u32[]{:S(2)}) collective-permute-start(bf16[8,3072]{1,0:T(8,128)(2,1)S(1)} %get-tuple-element.27.after), channel_id=1, source_target_pairs={{0,8},{2,10},{4,12},{6,14},{8,0},{10,2},{12,4},{14,6},{1,9},{3,11}... | collective-permute-start | bytes 147464 | tf_op jit(solution)/shard_map/ppermute | solution.py:28
  28.8 5.1 %collective-permute-start.9 = (bf16[8,3072]{1,0:T(8,128)(2,1)S(1)}, bf16[8,3072]{1,0:T(8,128)(2,1)S(1)}, u32[]{:S(2)}, u32[]{:S(2)}) collective-permute-start(bf16[8,3072]{1,0:T(8,128)(2,1)S(1)} %get-tuple-element.25), channel_id=1, source_target_pairs={{0,4},{2,6},{4,0},{6,2},{8,12},{10,14},{12,8},{14,10},{1,5},{3,7},... | collective-permute-start | bytes 147464 | tf_op jit(solution)/shard_map/ppermute | solution.py:28
  33.9 3.9 %collective-permute-start.12 = (bf16[4,3072]{1,0:T(4,128)(2,1)S(1)}, bf16[4,3072]{1,0:T(4,128)(2,1)S(1)}, u32[]{:S(2)}, u32[]{:S(2)}) collective-permute-start(bf16[4,3072]{1,0:T(4,128)(2,1)S(1)} %get-tuple-element.28.refs_6_), channel_id=1, source_target_pairs={{0,2},{2,0},{4,6},{6,4},{8,10},{10,8},{12,14},{14,12},{1,3},{3,1},... | collective-permute-start | bytes 73736 | tf_op jit(solution)/shard_map/ppermute | solution.py:28
  37.9 1.3 %collective-permute-start.13 = (bf16[4,3072]{1,0:T(4,128)(2,1)S(1)}, bf16[4,3072]{1,0:T(4,128)(2,1)S(1)}, u32[]{:S(2)}, u32[]{:S(2)}) collective-permute-start(bf16[4,3072]{1,0:T(4,128)(2,1)S(1)} %finish.1.own_ref), channel_id=1, source_target_pairs={{0,1},{1,0},{2,3},{3,2},{4,5},{5,4},{6,7},{7,6},{8,9},{9,8},{10,11... | collective-permute-start | bytes 73736 | tf_op jit(solution)/shard_map/ppermute | solution.py:28

commit v12 on v11

--- a/solution.py
+++ b/solution.py
@@ -231,25 +231,20 @@
     for ref in taken:
         total = total + ref[...].astype(jnp.float32)
     kept = kept_ref.shape[0]
-    kept_ref[...] = total[:kept]
+    kept_ref[...] = total[:kept].astype(kept_ref.dtype)
     sent_ref[...] = total[kept:].astype(jnp.bfloat16)
 
 
-def finish(kept_ref, taken_ref, tokens_ref, after, out_ref):
+def finish(kept_ref, other_kept, other_taken, taken_ref, tokens_ref, after, out_ref):
     half = kept_ref.shape[1]
-    core = lax.axis_index("narrow")
-    own = tokens_ref[...].astype(jnp.float32)
-    own = jnp.where(core == 0, own[:, :half], own[:, half:])
-    total = kept_ref[...] + taken_ref[...].astype(jnp.float32)
-    out_ref[...] = (own + total).astype(jnp.bfloat16)
-
-
-def join(own_ref, other_ref, out_ref):
-    half = own_ref.shape[1]
-    core = lax.axis_index("narrow")
-    own, other = own_ref[...], other_ref[...]
-    out_ref[:, :half] = jnp.where(core == 0, own, other)
-    out_ref[:, half:] = jnp.where(core == 0, other, own)
+    first = lax.axis_index("narrow") == 0
+    own = kept_ref[...].astype(jnp.float32) + taken_ref[...].astype(jnp.float32)
+    other = other_kept[...].astype(jnp.float32) + other_taken[...].astype(jnp.float32)
+    tokens = tokens_ref[...].astype(jnp.float32)
+    left = tokens[:, :half] + jnp.where(first, own, other)
+    right = tokens[:, half:] + jnp.where(first, other, own)
+    out_ref[:, :half] = left.astype(jnp.bfloat16)
+    out_ref[:, half:] = right.astype(jnp.bfloat16)
 
 
 def attend(
@@ -495,7 +490,7 @@
             kept = terms.shape[0] // 2
             terms, sent = call(
                 combine,
-                [shape((kept, half), f32), shape((kept, half), bf16)],
+                [shape((kept, half), bf16 if kept == rows else f32), shape((kept, half), bf16)],
                 [terms, *taken, early],
                 size=terms.size * 8,
                 far=(1 + len(taken),),
@@ -514,15 +509,16 @@
             smem=(4, 5),
             far=(6,),
         )
-        piece = call(
+        other_kept = swap(terms, "narrow", 2, 1)
+        crossed = [(i, (((i >> 1) ^ steps[0]) << 1) | (1 - (i & 1))) for i in range(2 * wide)]
+        other_taken = lax.ppermute(sent, ("wide", "narrow"), crossed)
+        mixed_out = call(
             finish,
-            shape((rows, half), bf16),
-            [terms, *taken, tokens, distant(context)],
+            shape((rows, width), bf16),
+            [terms, other_kept, other_taken, *taken, tokens, distant(context)],
             size=terms.size * 8,
-            far=(3,),
-        )
-        other = swap(piece, "narrow", 2, 1)
-        mixed_out = call(join, shape((rows, width), bf16), [piece, other], size=terms.size * 4)
+            far=(5,),
+        )
         return (context, mixed_out)
 
     return local

time: 39.9 us -> 40.8 us (1.023)
  waiting for transfers between devices: 7.7 us -> 8.44 us
    ppermute x0 -> x1, starting transfers between devices: none -> 2.09 us  [local(): other_taken = lax.ppermute(sent, ('wide', 'narrow'), crossed)]
    ppermute x14, starting transfers between devices: 16.9 us -> 15 us  [swap(): return lax.ppermute(block, axis, [(i, i ^ step) for i in range(count)])]
    ppermute x14, waiting for transfers between devices: 7.7 us -> 8.44 us  [swap(): return lax.ppermute(block, axis, [(i, i ^ step) for i in range(count)])]
    pallas_call x15 -> x14, Pallas kernels: 14.2 us -> 14.2 us  [call(): pl.pallas_call(kernel, name=getattr(kernel, 'func', kernel).__name__, out...]
  transfers between devices with their start and end apart: 14 -> 15, of which waited for: 6 -> 5; matrix products, arithmetic and copies ran while one was open for 0% -> 0% of each run, Pallas kernels for 31% -> 30%
where the time goes in v12:
time: 40.8 us; the launch traced here: 40.6 us
  starting transfers between devices  17 us (42%)
  Pallas kernels  14.2 us (35%)
  waiting for transfers between devices  8.44 us (21%)
  between operations  0.87 us (2%)
    ppermute x14, starting transfers between devices, swap(): return lax.ppermute(block, axis, [(i, i ^ step) for i in range(count)])  15 us
    pallas_call x14, Pallas kernels, call(): pl.pallas_call(kernel, name=getattr(kernel, 'func', kernel).__name__, out...  14.2 us
    ppermute x14, waiting for transfers between devices, swap(): return lax.ppermute(block, axis, [(i, i ^ step) for i in range(count)])  8.44 us
    ppermute x1, starting transfers between devices, local(): other_taken = lax.ppermute(sent, ('wide', 'narrow'), crossed)  2.09 us
  transfers between devices with their start and end apart: 15, of which 5 were waited for; matrix products, arithmetic and copies ran while one was open for 0% of the time, Pallas kernels for 30%

profile of v12, /device:TPU:0, one launch (start us, length us, event | category | flops | bytes accessed | tf_op | source)
XLA Modules:
  0.0 40.6 jit_solution(17036525405110914091)
XLA Ops:
  0.6 3.0 %collective-permute-start = (bf16[4,6144]{1,0:T(4,128)(2,1)}, bf16[4,6144]{1,0:T(4,128)(2,1)S(1)}, u32[]{:S(2)}, u32[]{:S(2)}) collective-permute-start(bf16[4,6144]{1,0:T(4,128)(2,1)} %tokens_ref.1), channel_id=1, source_target_pairs={{0,2},{2,0},{4,6},{6,4},{8,10},{10,8},{12,14},{14,12},{1,3},{3,1},... | collective-permute-start | bytes 147464 | tf_op jit(solution)/shard_map/ppermute | solution.py:28
  3.7 1.0 %pack.1 = (bf16[128,128]{1,0:T(8,128)(2,1)S(1)}, bf16[4,6144]{1,0:T(4,128)(2,1)S(1)}, f32[1,6144]{1,0:T(1,128)S(1)}) custom-call(bf16[4,3072]{1,0:T(4,128)(2,1)} %far_query.1, bf16[4,512]{1,0:T(4,128)(2,1)} %far_key.1, bf16[4,512]{1,0:T(4,128)(2,1)} %far_value.1, bf16[4,6144]{1,0:T(4,128)(2,1)} %tokens_ref.1, f32[1,6144]{1,0:T(1,128)} %bitcast.5), custom_call_target="tpu_custom_call" | custom-call | bytes 100000 | tf_op jit(solution)/shard_map/pack/pallas_call | solution.py:49
  4.6 0.1 collective-permute-start.3
  4.7 0.0 slice-start
  4.7 0.0 slice-start.1
  4.7 0.0 slice-start.2
  4.8 0.0 copy-start
  4.8 1.0 %shares.1.share.share_ref = f32[32,128]{1,0:T(8,128)S(1)} custom-call(s32[2,32]{1,0:T(2,128)} %bitcast.6, f32[2,32]{1,0:T(2,128)} %bitcast.7, bf16[128,128]{1,0:T(8,128)(2,1)S(1)} %get-tuple-element.18.refs_0_.heads.own_ref.own_heads, bf16[1,6144,1024]{2,1,0:T(8,128)(2,1)} %gate_ref.1, bf16[1,6144,1024]{2,1,0:T(8,128)(2,1)} %up_ref.1), custom_call_target="tpu_custom_call" | custom-call | bytes 100000 | tf_op jit(solution)/shard_map/shares/pallas_call | solution.py:49
  5.7 0.2 collective-permute-done.got_ref
  5.9 0.2 norm_both.1.own_ref
  6.1 4.2 %collective-permute-start.1 = (bf16[8,3072]{1,0:T(8,128)(2,1)S(1)}, bf16[8,3072]{1,0:T(8,128)(2,1)S(1)}, u32[]{:S(2)}, u32[]{:S(2)}) collective-permute-start(bf16[8,3072]{1,0:T(8,128)(2,1)S(1)} %norm_both.1.own_ref), channel_id=1, source_target_pairs={{0,12},{2,14},{4,8},{6,10},{8,4},{10,6},{12,0},{14,2},{1,13},{3,15... | collective-permute-start | bytes 147464 | tf_op jit(solution)/shard_map/ppermute | solution.py:28
  10.3 0.0 collective-permute-start.2
  10.3 0.6 %collective-permute-start.4 = (bf16[8,3072]{1,0:T(8,128)(2,1)S(1)}, bf16[8,3072]{1,0:T(8,128)(2,1)S(1)}, u32[]{:S(2)}, u32[]{:S(2)}) collective-permute-start(bf16[8,3072]{1,0:T(8,128)(2,1)S(1)} %norm_both.1.own_ref), channel_id=1, source_target_pairs={{0,4},{2,6},{4,0},{6,2},{8,12},{10,14},{12,8},{14,10},{1,5},{3,7},... | collective-permute-start | bytes 147464 | tf_op jit(solution)/shard_map/ppermute | solution.py:28
  10.9 0.0 collective-permute-done.3.got_heads
  10.9 1.8 %collective-permute-done.1.last_ref = bf16[8,3072]{1,0:T(8,128)(2,1)S(1)} collective-permute-done((bf16[8,3072]{1,0:T(8,128)(2,1)S(1)}, bf16[8,3072]{1,0:T(8,128)(2,1)S(1)}, u32[]{:S(2)}, u32[]{:S(2)}) %collective-permute-start.1) | collective-permute-done | bytes 49184 | tf_op jit(solution)/shard_map/ppermute | solution.py:28
  12.7 2.6 %collective-permute-done.2.far_ref = bf16[8,3072]{1,0:T(8,128)(2,1)S(1)} collective-permute-done((bf16[8,3072]{1,0:T(8,128)(2,1)S(1)}, bf16[8,3072]{1,0:T(8,128)(2,1)S(1)}, u32[]{:S(2)}, u32[]{:S(2)}) %collective-permute-start.2) | collective-permute-done | bytes 49184 | tf_op jit(solution)/shard_map/ppermute | solution.py:28
  15.3 0.0 collective-permute-done.4.next_ref
  15.3 0.1 collective-permute-start.6
  15.4 2.1 %collective-permute-start.5 = (bf16[256,128]{1,0:T(8,128)(2,1)S(1)}, bf16[256,128]{1,0:T(8,128)(2,1)S(1)}, u32[]{:S(2)}, u32[]{:S(2)}) collective-permute-start(bf16[256,128]{1,0:T(8,128)(2,1)S(1)} %get-tuple-element.19.own_ref), channel_id=1, source_target_pairs={{0,8},{2,10},{4,12},{6,14},{8,0},{10,2},{12,4},{14,6},{1,9},{3,11}... | collective-permute-start | bytes 196616 | tf_op jit(solution)/shard_map/ppermute | solution.py:28
  17.5 0.0 collective-permute-done.6.other_ref
  17.5 0.0 slice-done
  17.5 4.8 %gate_all.1 = (bf16[32,1024]{1,0:T(8,128)(2,1)S(1)}, bf16[1024,3072]{1,0:T(8,128)(2,1)S(1)}, bf16[1024,3072]{1,0:T(8,128)(2,1)S(1)}) custom-call(bf16[32,3072]{1,0:T(8,128)(2,1)S(1)} %get-tuple-element.20.x_ref, bf16[32,3072]{1,0:T(8,128)(2,1)S(1)} %collective-permute-done.6.other_ref, bf16[1,6144,1024]{2,1,0:T(8,128)(2,1)S(1)} %bitcast.4, ...), custom_call_target="tpu_custom_call" | custom-call | flops 805306368 | bytes 37748736 | tf_op jit(solution)/shard_map/gate_all/pallas_call | solution.py:49
  22.3 0.0 collective-permute-done.5.got_ref
  22.3 0.0 copy-start.1
  22.3 0.0 copy-start.2
  22.3 0.0 copy-start.4
  22.4 0.0 copy-start.5
  22.4 1.3 %down.2.after = bf16[32,3072]{1,0:T(8,128)(2,1)S(1)} custom-call(bf16[32,1024]{1,0:T(8,128)(2,1)S(1)} %get-tuple-element.21.after.hidden_ref, bf16[1024,3072]{1,0:T(8,128)(2,1)S(1)} %get-tuple-element.23.down_ref, bf16[512,128]{1,0:T(8,128)(2,1)S(1)} %stack_after.1.after.near_ref.refs_0_), custom_call_target="tpu_custom_call" | custom-call | flops 201326592 | bytes 6291456 | tf_op jit(solution)/shard_map/down/pallas_call | solution.py:49
  23.7 0.2 collective-permute-start.8
  23.9 0.1 collective-permute-start.7
  24.0 1.3 %down.3.terms_ref = f32[32,3072]{1,0:T(8,128)S(1)} custom-call(bf16[32,1024]{1,0:T(8,128)(2,1)S(1)} %get-tuple-element.21.after.hidden_ref, bf16[1024,3072]{1,0:T(8,128)(2,1)S(1)} %get-tuple-element.22.down_ref, bf16[32,3072]{1,0:T(8,128)(2,1)S(1)} %down.2.after), custom_call_target="tpu_custom_call" | custom-call | flops 201326592 | bytes 6291456 | tf_op jit(solution)/shard_map/down/pallas_call | solution.py:49
  25.3 0.0 collective-permute-done.8.taken_ref
  25.4 2.7 %collective-permute-start.10 = (bf16[8,3072]{1,0:T(8,128)(2,1)S(1)}, bf16[8,3072]{1,0:T(8,128)(2,1)S(1)}, u32[]{:S(2)}, u32[]{:S(2)}) collective-permute-start(bf16[8,3072]{1,0:T(8,128)(2,1)S(1)} %get-tuple-element.26), channel_id=1, source_target_pairs={{0,12},{2,14},{4,8},{6,10},{8,4},{10,6},{12,0},{14,2},{1,13},{3,15... | collective-permute-start | bytes 147464 | tf_op jit(solution)/shard_map/ppermute | solution.py:28
  28.1 0.7 %collective-permute-start.11 = (bf16[8,3072]{1,0:T(8,128)(2,1)S(1)}, bf16[8,3072]{1,0:T(8,128)(2,1)S(1)}, u32[]{:S(2)}, u32[]{:S(2)}) collective-permute-start(bf16[8,3072]{1,0:T(8,128)(2,1)S(1)} %get-tuple-element.27.after), channel_id=1, source_target_pairs={{0,8},{2,10},{4,12},{6,14},{8,0},{10,2},{12,4},{14,6},{1,9},{3,11}... | collective-permute-start | bytes 147464 | tf_op jit(solution)/shard_map/ppermute | solution.py:28
  28.8 1.0 %collective-permute-start.9 = (bf16[8,3072]{1,0:T(8,128)(2,1)S(1)}, bf16[8,3072]{1,0:T(8,128)(2,1)S(1)}, u32[]{:S(2)}, u32[]{:S(2)}) collective-permute-start(bf16[8,3072]{1,0:T(8,128)(2,1)S(1)} %get-tuple-element.25), channel_id=1, source_target_pairs={{0,4},{2,6},{4,0},{6,2},{8,12},{10,14},{12,8},{14,10},{1,5},{3,7},... | collective-permute-start | bytes 147464 | tf_op jit(solution)/shard_map/ppermute | solution.py:28
  29.8 0.0 collective-permute-done.7.far_ref.refs_1_
  29.8 2.2 %attend.1.refs_4_.refs_7_ = f32[72,128]{1,0:T(8,128)S(1)} custom-call(bf16[512,128]{1,0:T(8,128)(2,1)S(1)} %stack_after.1.after.near_ref.refs_0_, bf16[512,128]{1,0:T(8,128)(2,1)S(1)} %collective-permute-done.7.far_ref.refs_1_, bf16[4,512,512]{2,1,0:T(8,128)(2,1)S(1)} %copy-done.1, bf16[4,512,512]{2,1,0:T(8,128)(2,1)S(1)} %copy-done.2, s32[4]{0:T(128)S(1)} %copy-done.4, ...), custom_call_target="tpu_custom_call" | custom-call | flops 12582912 | bytes 2097152 | tf_op jit(solution)/shard_map/attend/pallas_call | solution.py:49
  32.0 0.0 collective-permute-done.10.refs_2_
  32.1 1.9 %collective-permute-done.11.refs_3_ = bf16[8,3072]{1,0:T(8,128)(2,1)S(1)} collective-permute-done((bf16[8,3072]{1,0:T(8,128)(2,1)S(1)}, bf16[8,3072]{1,0:T(8,128)(2,1)S(1)}, u32[]{:S(2)}, u32[]{:S(2)}) %collective-permute-start.11) | collective-permute-done | bytes 49184 | tf_op jit(solution)/shard_map/ppermute | solution.py:28
  33.9 0.0 collective-permute-done.9.refs_1_
  33.9 0.1 collective-permute-start.12
  34.0 2.1 %collective-permute-start.13 = (bf16[4,3072]{1,0:T(4,128)(2,1)S(1)}, bf16[4,3072]{1,0:T(4,128)(2,1)S(1)}, u32[]{:S(2)}, u32[]{:S(2)}) collective-permute-start(bf16[4,3072]{1,0:T(4,128)(2,1)S(1)} %get-tuple-element.28.refs_6_), channel_id=1, source_target_pairs={{0,3},{1,2},{2,1},{3,0},{4,7},{5,6},{6,5},{7,4},{8,11},{9,10},{10,... | collective-permute-start | bytes 73736 | tf_op jit(solution)/shard_map/ppermute | solution.py:514
  36.1 0.1 collective-permute-start.14
  36.2 1.8 %attend_last.1.after = bf16[4,3072]{1,0:T(4,128)(2,1)} custom-call(bf16[512,128]{1,0:T(8,128)(2,1)S(1)} %stack_after.1.after.near_ref.refs_0_, bf16[512,128]{1,0:T(8,128)(2,1)S(1)} %collective-permute-done.7.far_ref.refs_1_, bf16[4,512,512]{2,1,0:T(8,128)(2,1)S(1)} %copy-done.1, bf16[4,512,512]{2,1,0:T(8,128)(2,1)S(1)} %copy-done.2, s32[4]{0:T(128)S(1)} %copy-done.4, ...), custom_call_target="tpu_custom_call" | custom-call | flops 12582912 | bytes 2097152 | tf_op jit(solution)/shard_map/attend_last/pallas_call | solution.py:49
  38.0 0.0 collective-permute-done.12.other_kept
  38.0 0.0 collective-permute-done.13.other_taken
  38.0 2.0 %collective-permute-done.14.taken_ref = bf16[4,3072]{1,0:T(4,128)(2,1)S(1)} collective-permute-done((bf16[4,3072]{1,0:T(4,128)(2,1)S(1)}, bf16[4,3072]{1,0:T(4,128)(2,1)S(1)}, u32[]{:S(2)}, u32[]{:S(2)}) %collective-permute-start.14) | collective-permute-done | bytes 24608 | tf_op jit(solution)/shard_map/ppermute | solution.py:28
  39.9 0.7 %finish.1 = bf16[4,6144]{1,0:T(4,128)(2,1)} custom-call(bf16[4,3072]{1,0:T(4,128)(2,1)S(1)} %get-tuple-element.29.kept_ref, bf16[4,3072]{1,0:T(4,128)(2,1)S(1)} %collective-permute-done.12.other_kept, bf16[4,3072]{1,0:T(4,128)(2,1)S(1)} %collective-permute-done.13.other_taken, bf16[4,3072]{1,0:T(4,128)(2,1)S(1)} %collective-permute-done.14.taken_ref, ...), custom_call_target="tpu_custom_call" | custom-call | bytes 98304 | tf_op jit(solution)/shard_map/finish/pallas_call | solution.py:49
  (15 shorter events, 0.1 us)
Async XLA Ops:
  0.6 5.3 %collective-permute-start = (bf16[4,6144]{1,0:T(4,128)(2,1)}, bf16[4,6144]{1,0:T(4,128)(2,1)S(1)}, u32[]{:S(2)}, u32[]{:S(2)}) collective-permute-start(bf16[4,6144]{1,0:T(4,128)(2,1)} %tokens_ref.1), channel_id=1, source_target_pairs={{0,2},{2,0},{4,6},{6,4},{8,10},{10,8},{12,14},{14,12},{1,3},{3,1},... | collective-permute-start | bytes 147464 | tf_op jit(solution)/shard_map/ppermute | solution.py:28
  4.6 6.3 %collective-permute-start.3 = (bf16[192,128]{1,0:T(8,128)(2,1)S(1)}, bf16[192,128]{1,0:T(8,128)(2,1)S(1)}, u32[]{:S(2)}, u32[]{:S(2)}) collective-permute-start(bf16[192,128]{1,0:T(8,128)(2,1)S(1)} %widen.1), channel_id=1, source_target_pairs={{0,2},{2,0},{4,6},{6,4},{8,10},{10,8},{12,14},{14,12},{1,3},{3,1},... | collective-permute-start | bytes 147464 | tf_op jit(solution)/shard_map/ppermute | solution.py:28
  4.7 12.7 %slice-start = ((s8[12582912]{0:T(1024)(128)(4,1)}), s8[4194304]{0:T(1024)(128)(4,1)S(1)}, s32[]{:S(2)}) async-start(s8[12582912]{0:T(1024)(128)(4,1)} %bitcast.3), calls=%async_computation | async-start | bytes 8388608
  4.7 12.7 %slice-start.1 = ((s8[12582912]{0:T(1024)(128)(4,1)}), s8[4194304]{0:T(1024)(128)(4,1)S(1)}, s32[]{:S(2)}) async-start(s8[12582912]{0:T(1024)(128)(4,1)} %bitcast.3), calls=%async_computation.1 | async-start | bytes 8388608
  4.7 12.7 %slice-start.2 = ((s8[12582912]{0:T(1024)(128)(4,1)}), s8[4194304]{0:T(1024)(128)(4,1)S(1)}, s32[]{:S(2)}) async-start(s8[12582912]{0:T(1024)(128)(4,1)} %bitcast.3), calls=%async_computation.2 | async-start | bytes 8388608
  4.8 12.7 %copy-start = (bf16[1,6144,1024]{2,1,0:T(8,128)(2,1)S(1)}, bf16[1,6144,1024]{2,1,0:T(8,128)(2,1)}, u32[]{:S(2)}) copy-start(bf16[1,6144,1024]{2,1,0:T(8,128)(2,1)} %up_ref.1) | copy-start | bytes 37748740
  6.1 6.6 %collective-permute-start.1 = (bf16[8,3072]{1,0:T(8,128)(2,1)S(1)}, bf16[8,3072]{1,0:T(8,128)(2,1)S(1)}, u32[]{:S(2)}, u32[]{:S(2)}) collective-permute-start(bf16[8,3072]{1,0:T(8,128)(2,1)S(1)} %norm_both.1.own_ref), channel_id=1, source_target_pairs={{0,12},{2,14},{4,8},{6,10},{8,4},{10,6},{12,0},{14,2},{1,13},{3,15... | collective-permute-start | bytes 147464 | tf_op jit(solution)/shard_map/ppermute | solution.py:28
  10.3 5.0 %collective-permute-start.2 = (bf16[8,3072]{1,0:T(8,128)(2,1)S(1)}, bf16[8,3072]{1,0:T(8,128)(2,1)S(1)}, u32[]{:S(2)}, u32[]{:S(2)}) collective-permute-start(bf16[8,3072]{1,0:T(8,128)(2,1)S(1)} %norm_both.1.own_ref), channel_id=1, source_target_pairs={{0,8},{2,10},{4,12},{6,14},{8,0},{10,2},{12,4},{14,6},{1,9},{3,11}... | collective-permute-start | bytes 147464 | tf_op jit(solution)/shard_map/ppermute | solution.py:28
  10.3 5.0 %collective-permute-start.4 = (bf16[8,3072]{1,0:T(8,128)(2,1)S(1)}, bf16[8,3072]{1,0:T(8,128)(2,1)S(1)}, u32[]{:S(2)}, u32[]{:S(2)}) collective-permute-start(bf16[8,3072]{1,0:T(8,128)(2,1)S(1)} %norm_both.1.own_ref), channel_id=1, source_target_pairs={{0,4},{2,6},{4,0},{6,2},{8,12},{10,14},{12,8},{14,10},{1,5},{3,7},... | collective-permute-start | bytes 147464 | tf_op jit(solution)/shard_map/ppermute | solution.py:28
  15.3 2.1 %collective-permute-start.6 = (bf16[32,3072]{1,0:T(8,128)(2,1)S(1)}, bf16[32,3072]{1,0:T(8,128)(2,1)S(1)}, u32[]{:S(2)}, u32[]{:S(2)}) collective-permute-start(bf16[32,3072]{1,0:T(8,128)(2,1)S(1)} %get-tuple-element.20.x_ref), channel_id=1, source_target_pairs={{0,1},{1,0},{2,3},{3,2},{4,5},{5,4},{6,7},{7,6},{8,9},{9,8},{10,11... | collective-permute-start | bytes 589832 | tf_op jit(solution)/shard_map/ppermute | solution.py:28
  15.4 6.9 %collective-permute-start.5 = (bf16[256,128]{1,0:T(8,128)(2,1)S(1)}, bf16[256,128]{1,0:T(8,128)(2,1)S(1)}, u32[]{:S(2)}, u32[]{:S(2)}) collective-permute-start(bf16[256,128]{1,0:T(8,128)(2,1)S(1)} %get-tuple-element.19.own_ref), channel_id=1, source_target_pairs={{0,8},{2,10},{4,12},{6,14},{8,0},{10,2},{12,4},{14,6},{1,9},{3,11}... | collective-permute-start | bytes 196616 | tf_op jit(solution)/shard_map/ppermute | solution.py:28
  22.3 7.5 %copy-start.1 = (bf16[4,512,512]{2,1,0:T(8,128)(2,1)S(1)}, bf16[4,512,512]{2,1,0:T(8,128)(2,1)}, u32[]{:S(2)}) copy-start(bf16[4,512,512]{2,1,0:T(8,128)(2,1)} %refs_2_.3) | copy-start | bytes 6291460
  22.3 7.5 %copy-start.2 = (bf16[4,512,512]{2,1,0:T(8,128)(2,1)S(1)}, bf16[4,512,512]{2,1,0:T(8,128)(2,1)}, u32[]{:S(2)}) copy-start(bf16[4,512,512]{2,1,0:T(8,128)(2,1)} %refs_3_.1) | copy-start | bytes 6291460
  22.3 7.5 %copy-start.4 = (s32[4]{0:T(128)S(1)}, s32[4]{0:T(128)}, u32[]{:S(2)}) copy-start(s32[4]{0:T(128)} %refs_4_.1) | copy-start | bytes 52
  22.4 7.5 %copy-start.5 = (s32[4]{0:T(128)S(1)}, s32[4]{0:T(128)}, u32[]{:S(2)}) copy-start(s32[4]{0:T(128)} %refs_5_.1) | copy-start | bytes 52
  23.7 1.6 %collective-permute-start.8 = (bf16[32,3072]{1,0:T(8,128)(2,1)S(1)}, bf16[32,3072]{1,0:T(8,128)(2,1)S(1)}, u32[]{:S(2)}, u32[]{:S(2)}) collective-permute-start(bf16[32,3072]{1,0:T(8,128)(2,1)S(1)} %down.2.after), channel_id=1, source_target_pairs={{0,1},{1,0},{2,3},{3,2},{4,5},{5,4},{6,7},{7,6},{8,9},{9,8},{10,11... | collective-permute-start | bytes 589832 | tf_op jit(solution)/shard_map/ppermute | solution.py:28
  23.9 6.0 %collective-permute-start.7 = (bf16[512,128]{1,0:T(8,128)(2,1)S(1)}, bf16[512,128]{1,0:T(8,128)(2,1)S(1)}, u32[]{:S(2)}, u32[]{:S(2)}) collective-permute-start(bf16[512,128]{1,0:T(8,128)(2,1)S(1)} %stack_after.1.after.near_ref.refs_0_), channel_id=1, source_target_pairs={{0,4},{2,6},{4,0},{6,2},{8,12},{10,14},{12,8},{14,10},{1,5},{3,7},... | collective-permute-start | bytes 393224 | tf_op jit(solution)/shard_map/ppermute | solution.py:28
  25.3 14.7 %copy-start.3 = (bf16[4,6144]{1,0:T(4,128)(2,1)S(1)}, bf16[4,6144]{1,0:T(4,128)(2,1)}, u32[]{:S(2)}) copy-start(bf16[4,6144]{1,0:T(4,128)(2,1)} %tokens_ref.1) | copy-start | bytes 147460
  25.4 6.7 %collective-permute-start.10 = (bf16[8,3072]{1,0:T(8,128)(2,1)S(1)}, bf16[8,3072]{1,0:T(8,128)(2,1)S(1)}, u32[]{:S(2)}, u32[]{:S(2)}) collective-permute-start(bf16[8,3072]{1,0:T(8,128)(2,1)S(1)} %get-tuple-element.26), channel_id=1, source_target_pairs={{0,12},{2,14},{4,8},{6,10},{8,4},{10,6},{12,0},{14,2},{1,13},{3,15... | collective-permute-start | bytes 147464 | tf_op jit(solution)/shard_map/ppermute | solution.py:28
  28.1 5.8 %collective-permute-start.11 = (bf16[8,3072]{1,0:T(8,128)(2,1)S(1)}, bf16[8,3072]{1,0:T(8,128)(2,1)S(1)}, u32[]{:S(2)}, u32[]{:S(2)}) collective-permute-start(bf16[8,3072]{1,0:T(8,128)(2,1)S(1)} %get-tuple-element.27.after), channel_id=1, source_target_pairs={{0,8},{2,10},{4,12},{6,14},{8,0},{10,2},{12,4},{14,6},{1,9},{3,11}... | collective-permute-start | bytes 147464 | tf_op jit(solution)/shard_map/ppermute | solution.py:28
  28.8 5.1 %collective-permute-start.9 = (bf16[8,3072]{1,0:T(8,128)(2,1)S(1)}, bf16[8,3072]{1,0:T(8,128)(2,1)S(1)}, u32[]{:S(2)}, u32[]{:S(2)}) collective-permute-start(bf16[8,3072]{1,0:T(8,128)(2,1)S(1)} %get-tuple-element.25), channel_id=1, source_target_pairs={{0,4},{2,6},{4,0},{6,2},{8,12},{10,14},{12,8},{14,10},{1,5},{3,7},... | collective-permute-start | bytes 147464 | tf_op jit(solution)/shard_map/ppermute | solution.py:28
  33.9 4.0 %collective-permute-start.12 = (bf16[4,3072]{1,0:T(4,128)(2,1)S(1)}, bf16[4,3072]{1,0:T(4,128)(2,1)S(1)}, u32[]{:S(2)}, u32[]{:S(2)}) collective-permute-start(bf16[4,3072]{1,0:T(4,128)(2,1)S(1)} %get-tuple-element.29.kept_ref), channel_id=1, source_target_pairs={{0,1},{1,0},{2,3},{3,2},{4,5},{5,4},{6,7},{7,6},{8,9},{9,8},{10,11... | collective-permute-start | bytes 73736 | tf_op jit(solution)/shard_map/ppermute | solution.py:28
  34.0 3.9 %collective-permute-start.13 = (bf16[4,3072]{1,0:T(4,128)(2,1)S(1)}, bf16[4,3072]{1,0:T(4,128)(2,1)S(1)}, u32[]{:S(2)}, u32[]{:S(2)}) collective-permute-start(bf16[4,3072]{1,0:T(4,128)(2,1)S(1)} %get-tuple-element.28.refs_6_), channel_id=1, source_target_pairs={{0,3},{1,2},{2,1},{3,0},{4,7},{5,6},{6,5},{7,4},{8,11},{9,10},{10,... | collective-permute-start | bytes 73736 | tf_op jit(solution)/shard_map/ppermute | solution.py:514
  36.1 3.8 %collective-permute-start.14 = (bf16[4,3072]{1,0:T(4,128)(2,1)S(1)}, bf16[4,3072]{1,0:T(4,128)(2,1)S(1)}, u32[]{:S(2)}, u32[]{:S(2)}) collective-permute-start(bf16[4,3072]{1,0:T(4,128)(2,1)S(1)} %get-tuple-element.28.refs_6_), channel_id=1, source_target_pairs={{0,2},{2,0},{4,6},{6,4},{8,10},{10,8},{12,14},{14,12},{1,3},{3,1},... | collective-permute-start | bytes 73736 | tf_op jit(solution)/shard_map/ppermute | solution.py:28

commit v13 on v12

--- a/solution.py
+++ b/solution.py
@@ -235,7 +235,7 @@
     sent_ref[...] = total[kept:].astype(jnp.bfloat16)
 
 
-def finish(kept_ref, other_kept, other_taken, taken_ref, tokens_ref, after, out_ref):
+def finish(kept_ref, taken_ref, other_kept, other_taken, tokens_ref, after, out_ref):
     half = kept_ref.shape[1]
     first = lax.axis_index("narrow") == 0
     own = kept_ref[...].astype(jnp.float32) + taken_ref[...].astype(jnp.float32)
@@ -515,7 +515,7 @@
         mixed_out = call(
             finish,
             shape((rows, width), bf16),
-            [terms, other_kept, other_taken, *taken, tokens, distant(context)],
+            [terms, *taken, other_kept, other_taken, tokens, distant(context)],
             size=terms.size * 8,
             far=(5,),
         )

time: 40.8 us -> 40.1 us (0.983)
  waiting for transfers between devices: 8.44 us -> 7.71 us
    ppermute x14, waiting for transfers between devices: 8.44 us -> 6.46 us  [swap(): return lax.ppermute(block, axis, [(i, i ^ step) for i in range(count)])]
    ppermute x14, starting transfers between devices: 15 us -> 16.9 us  [swap(): return lax.ppermute(block, axis, [(i, i ^ step) for i in range(count)])]
    ppermute x1, starting transfers between devices: 2.09 us -> 0.2 us  [local(): other_taken = lax.ppermute(sent, ('wide', 'narrow'), crossed)]
    ppermute x1, waiting for transfers between devices: 0.01 us -> 1.25 us  [local(): other_taken = lax.ppermute(sent, ('wide', 'narrow'), crossed)]
where the time goes in v13:
time: 40.1 us; the launch traced here: 39.9 us
  starting transfers between devices  17.1 us (43%)
  Pallas kernels  14.2 us (35%)
  waiting for transfers between devices  7.71 us (19%)
  between operations  0.86 us (2%)
    ppermute x14, starting transfers between devices, swap(): return lax.ppermute(block, axis, [(i, i ^ step) for i in range(count)])  16.9 us
    pallas_call x14, Pallas kernels, call(): pl.pallas_call(kernel, name=getattr(kernel, 'func', kernel).__name__, out...  14.2 us
    ppermute x14, waiting for transfers between devices, swap(): return lax.ppermute(block, axis, [(i, i ^ step) for i in range(count)])  6.46 us
    ppermute x1, waiting for transfers between devices, local(): other_taken = lax.ppermute(sent, ('wide', 'narrow'), crossed)  1.25 us
  transfers between devices with their start and end apart: 15, of which 5 were waited for; matrix products, arithmetic and copies ran while one was open for 0% of the time, Pallas kernels for 30%

profile of v13, /device:TPU:0, one launch (start us, length us, event | category | flops | bytes accessed | tf_op | source)
XLA Modules:
  0.0 39.9 jit_solution(7949435927901298304)
XLA Ops:
  0.6 3.0 %collective-permute-start = (bf16[4,6144]{1,0:T(4,128)(2,1)}, bf16[4,6144]{1,0:T(4,128)(2,1)S(1)}, u32[]{:S(2)}, u32[]{:S(2)}) collective-permute-start(bf16[4,6144]{1,0:T(4,128)(2,1)} %tokens_ref.1), channel_id=1, source_target_pairs={{0,2},{2,0},{4,6},{6,4},{8,10},{10,8},{12,14},{14,12},{1,3},{3,1},... | collective-permute-start | bytes 147464 | tf_op jit(solution)/shard_map/ppermute | solution.py:28
  3.7 1.0 %pack.1 = (bf16[128,128]{1,0:T(8,128)(2,1)S(1)}, bf16[4,6144]{1,0:T(4,128)(2,1)S(1)}, f32[1,6144]{1,0:T(1,128)S(1)}) custom-call(bf16[4,3072]{1,0:T(4,128)(2,1)} %far_query.1, bf16[4,512]{1,0:T(4,128)(2,1)} %far_key.1, bf16[4,512]{1,0:T(4,128)(2,1)} %far_value.1, bf16[4,6144]{1,0:T(4,128)(2,1)} %tokens_ref.1, f32[1,6144]{1,0:T(1,128)} %bitcast.5), custom_call_target="tpu_custom_call" | custom-call | bytes 100000 | tf_op jit(solution)/shard_map/pack/pallas_call | solution.py:49
  4.6 0.1 collective-permute-start.3
  4.7 0.0 slice-start
  4.7 0.0 slice-start.1
  4.7 0.0 slice-start.2
  4.8 0.0 copy-start
  4.8 1.0 %shares.1.share.share_ref = f32[32,128]{1,0:T(8,128)S(1)} custom-call(s32[2,32]{1,0:T(2,128)} %bitcast.6, f32[2,32]{1,0:T(2,128)} %bitcast.7, bf16[128,128]{1,0:T(8,128)(2,1)S(1)} %get-tuple-element.18.refs_0_.heads.own_ref.own_heads, bf16[1,6144,1024]{2,1,0:T(8,128)(2,1)} %gate_ref.1, bf16[1,6144,1024]{2,1,0:T(8,128)(2,1)} %up_ref.1), custom_call_target="tpu_custom_call" | custom-call | bytes 100000 | tf_op jit(solution)/shard_map/shares/pallas_call | solution.py:49
  5.7 0.2 collective-permute-done.got_ref
  5.9 0.2 norm_both.1.own_ref
  6.1 4.2 %collective-permute-start.1 = (bf16[8,3072]{1,0:T(8,128)(2,1)S(1)}, bf16[8,3072]{1,0:T(8,128)(2,1)S(1)}, u32[]{:S(2)}, u32[]{:S(2)}) collective-permute-start(bf16[8,3072]{1,0:T(8,128)(2,1)S(1)} %norm_both.1.own_ref), channel_id=1, source_target_pairs={{0,12},{2,14},{4,8},{6,10},{8,4},{10,6},{12,0},{14,2},{1,13},{3,15... | collective-permute-start | bytes 147464 | tf_op jit(solution)/shard_map/ppermute | solution.py:28
  10.3 0.0 collective-permute-start.2
  10.3 0.6 %collective-permute-start.4 = (bf16[8,3072]{1,0:T(8,128)(2,1)S(1)}, bf16[8,3072]{1,0:T(8,128)(2,1)S(1)}, u32[]{:S(2)}, u32[]{:S(2)}) collective-permute-start(bf16[8,3072]{1,0:T(8,128)(2,1)S(1)} %norm_both.1.own_ref), channel_id=1, source_target_pairs={{0,4},{2,6},{4,0},{6,2},{8,12},{10,14},{12,8},{14,10},{1,5},{3,7},... | collective-permute-start | bytes 147464 | tf_op jit(solution)/shard_map/ppermute | solution.py:28
  10.9 0.0 collective-permute-done.3.got_heads
  10.9 1.8 %collective-permute-done.1.last_ref = bf16[8,3072]{1,0:T(8,128)(2,1)S(1)} collective-permute-done((bf16[8,3072]{1,0:T(8,128)(2,1)S(1)}, bf16[8,3072]{1,0:T(8,128)(2,1)S(1)}, u32[]{:S(2)}, u32[]{:S(2)}) %collective-permute-start.1) | collective-permute-done | bytes 49184 | tf_op jit(solution)/shard_map/ppermute | solution.py:28
  12.7 2.6 %collective-permute-done.2.far_ref = bf16[8,3072]{1,0:T(8,128)(2,1)S(1)} collective-permute-done((bf16[8,3072]{1,0:T(8,128)(2,1)S(1)}, bf16[8,3072]{1,0:T(8,128)(2,1)S(1)}, u32[]{:S(2)}, u32[]{:S(2)}) %collective-permute-start.2) | collective-permute-done | bytes 49184 | tf_op jit(solution)/shard_map/ppermute | solution.py:28
  15.3 0.0 collective-permute-done.4.next_ref
  15.3 0.1 collective-permute-start.6
  15.4 2.1 %collective-permute-start.5 = (bf16[256,128]{1,0:T(8,128)(2,1)S(1)}, bf16[256,128]{1,0:T(8,128)(2,1)S(1)}, u32[]{:S(2)}, u32[]{:S(2)}) collective-permute-start(bf16[256,128]{1,0:T(8,128)(2,1)S(1)} %get-tuple-element.19.own_ref), channel_id=1, source_target_pairs={{0,8},{2,10},{4,12},{6,14},{8,0},{10,2},{12,4},{14,6},{1,9},{3,11}... | collective-permute-start | bytes 196616 | tf_op jit(solution)/shard_map/ppermute | solution.py:28
  17.5 0.0 collective-permute-done.6.other_ref
  17.5 0.0 slice-done
  17.5 4.8 %gate_all.1 = (bf16[32,1024]{1,0:T(8,128)(2,1)S(1)}, bf16[1024,3072]{1,0:T(8,128)(2,1)S(1)}, bf16[1024,3072]{1,0:T(8,128)(2,1)S(1)}) custom-call(bf16[32,3072]{1,0:T(8,128)(2,1)S(1)} %get-tuple-element.20.x_ref, bf16[32,3072]{1,0:T(8,128)(2,1)S(1)} %collective-permute-done.6.other_ref, bf16[1,6144,1024]{2,1,0:T(8,128)(2,1)S(1)} %bitcast.4, ...), custom_call_target="tpu_custom_call" | custom-call | flops 805306368 | bytes 37748736 | tf_op jit(solution)/shard_map/gate_all/pallas_call | solution.py:49
  22.3 0.0 collective-permute-done.5.got_ref
  22.3 0.0 copy-start.1
  22.3 0.0 copy-start.2
  22.3 0.0 copy-start.4
  22.4 0.0 copy-start.5
  22.4 1.3 %down.2.after = bf16[32,3072]{1,0:T(8,128)(2,1)S(1)} custom-call(bf16[32,1024]{1,0:T(8,128)(2,1)S(1)} %get-tuple-element.21.after.hidden_ref, bf16[1024,3072]{1,0:T(8,128)(2,1)S(1)} %get-tuple-element.23.down_ref, bf16[512,128]{1,0:T(8,128)(2,1)S(1)} %stack_after.1.after.near_ref.refs_0_), custom_call_target="tpu_custom_call" | custom-call | flops 201326592 | bytes 6291456 | tf_op jit(solution)/shard_map/down/pallas_call | solution.py:49
  23.7 0.2 collective-permute-start.8
  23.9 0.1 collective-permute-start.7
  24.0 1.3 %down.3.terms_ref = f32[32,3072]{1,0:T(8,128)S(1)} custom-call(bf16[32,1024]{1,0:T(8,128)(2,1)S(1)} %get-tuple-element.21.after.hidden_ref, bf16[1024,3072]{1,0:T(8,128)(2,1)S(1)} %get-tuple-element.22.down_ref, bf16[32,3072]{1,0:T(8,128)(2,1)S(1)} %down.2.after), custom_call_target="tpu_custom_call" | custom-call | flops 201326592 | bytes 6291456 | tf_op jit(solution)/shard_map/down/pallas_call | solution.py:49
  25.3 0.0 collective-permute-done.8.taken_ref
  25.4 2.7 %collective-permute-start.10 = (bf16[8,3072]{1,0:T(8,128)(2,1)S(1)}, bf16[8,3072]{1,0:T(8,128)(2,1)S(1)}, u32[]{:S(2)}, u32[]{:S(2)}) collective-permute-start(bf16[8,3072]{1,0:T(8,128)(2,1)S(1)} %get-tuple-element.26), channel_id=1, source_target_pairs={{0,12},{2,14},{4,8},{6,10},{8,4},{10,6},{12,0},{14,2},{1,13},{3,15... | collective-permute-start | bytes 147464 | tf_op jit(solution)/shard_map/ppermute | solution.py:28
  28.1 0.7 %collective-permute-start.11 = (bf16[8,3072]{1,0:T(8,128)(2,1)S(1)}, bf16[8,3072]{1,0:T(8,128)(2,1)S(1)}, u32[]{:S(2)}, u32[]{:S(2)}) collective-permute-start(bf16[8,3072]{1,0:T(8,128)(2,1)S(1)} %get-tuple-element.27.after), channel_id=1, source_target_pairs={{0,8},{2,10},{4,12},{6,14},{8,0},{10,2},{12,4},{14,6},{1,9},{3,11}... | collective-permute-start | bytes 147464 | tf_op jit(solution)/shard_map/ppermute | solution.py:28
  28.8 1.0 %collective-permute-start.9 = (bf16[8,3072]{1,0:T(8,128)(2,1)S(1)}, bf16[8,3072]{1,0:T(8,128)(2,1)S(1)}, u32[]{:S(2)}, u32[]{:S(2)}) collective-permute-start(bf16[8,3072]{1,0:T(8,128)(2,1)S(1)} %get-tuple-element.25), channel_id=1, source_target_pairs={{0,4},{2,6},{4,0},{6,2},{8,12},{10,14},{12,8},{14,10},{1,5},{3,7},... | collective-permute-start | bytes 147464 | tf_op jit(solution)/shard_map/ppermute | solution.py:28
  29.8 0.0 collective-permute-done.7.far_ref.refs_1_
  29.8 2.2 %attend.1.refs_4_.refs_7_ = f32[72,128]{1,0:T(8,128)S(1)} custom-call(bf16[512,128]{1,0:T(8,128)(2,1)S(1)} %stack_after.1.after.near_ref.refs_0_, bf16[512,128]{1,0:T(8,128)(2,1)S(1)} %collective-permute-done.7.far_ref.refs_1_, bf16[4,512,512]{2,1,0:T(8,128)(2,1)S(1)} %copy-done.1, bf16[4,512,512]{2,1,0:T(8,128)(2,1)S(1)} %copy-done.2, s32[4]{0:T(128)S(1)} %copy-done.4, ...), custom_call_target="tpu_custom_call" | custom-call | flops 12582912 | bytes 2097152 | tf_op jit(solution)/shard_map/attend/pallas_call | solution.py:49
  32.0 0.0 collective-permute-done.10.refs_2_
  32.1 1.9 %collective-permute-done.11.refs_3_ = bf16[8,3072]{1,0:T(8,128)(2,1)S(1)} collective-permute-done((bf16[8,3072]{1,0:T(8,128)(2,1)S(1)}, bf16[8,3072]{1,0:T(8,128)(2,1)S(1)}, u32[]{:S(2)}, u32[]{:S(2)}) %collective-permute-start.11) | collective-permute-done | bytes 49184 | tf_op jit(solution)/shard_map/ppermute | solution.py:28
  33.9 0.0 collective-permute-done.9.refs_1_
  33.9 2.0 %collective-permute-start.12 = (bf16[4,3072]{1,0:T(4,128)(2,1)S(1)}, bf16[4,3072]{1,0:T(4,128)(2,1)S(1)}, u32[]{:S(2)}, u32[]{:S(2)}) collective-permute-start(bf16[4,3072]{1,0:T(4,128)(2,1)S(1)} %get-tuple-element.28.refs_6_), channel_id=1, source_target_pairs={{0,2},{2,0},{4,6},{6,4},{8,10},{10,8},{12,14},{14,12},{1,3},{3,1},... | collective-permute-start | bytes 73736 | tf_op jit(solution)/shard_map/ppermute | solution.py:28
  36.0 0.0 collective-permute-start.13
  36.0 0.2 collective-permute-start.14
  36.2 1.8 %attend_last.1.after = bf16[4,3072]{1,0:T(4,128)(2,1)} custom-call(bf16[512,128]{1,0:T(8,128)(2,1)S(1)} %stack_after.1.after.near_ref.refs_0_, bf16[512,128]{1,0:T(8,128)(2,1)S(1)} %collective-permute-done.7.far_ref.refs_1_, bf16[4,512,512]{2,1,0:T(8,128)(2,1)S(1)} %copy-done.1, bf16[4,512,512]{2,1,0:T(8,128)(2,1)S(1)} %copy-done.2, s32[4]{0:T(128)S(1)} %copy-done.4, ...), custom_call_target="tpu_custom_call" | custom-call | flops 12582912 | bytes 2097152 | tf_op jit(solution)/shard_map/attend_last/pallas_call | solution.py:49
  38.0 0.0 collective-permute-done.12.taken_ref
  38.0 0.0 collective-permute-done.13.other_kept
  38.0 1.2 %collective-permute-done.14.other_taken = bf16[4,3072]{1,0:T(4,128)(2,1)S(1)} collective-permute-done((bf16[4,3072]{1,0:T(4,128)(2,1)S(1)}, bf16[4,3072]{1,0:T(4,128)(2,1)S(1)}, u32[]{:S(2)}, u32[]{:S(2)}) %collective-permute-start.14) | collective-permute-done | bytes 24608 | tf_op jit(solution)/shard_map/ppermute | solution.py:514
  39.2 0.7 %finish.1 = bf16[4,6144]{1,0:T(4,128)(2,1)} custom-call(bf16[4,3072]{1,0:T(4,128)(2,1)S(1)} %get-tuple-element.29.kept_ref, bf16[4,3072]{1,0:T(4,128)(2,1)S(1)} %collective-permute-done.12.taken_ref, bf16[4,3072]{1,0:T(4,128)(2,1)S(1)} %collective-permute-done.13.other_kept, bf16[4,3072]{1,0:T(4,128)(2,1)S(1)} %collective-permute-done.14.other_taken, ...), custom_call_target="tpu_custom_call" | custom-call | bytes 98304 | tf_op jit(solution)/shard_map/finish/pallas_call | solution.py:49
  (15 shorter events, 0.1 us)
Async XLA Ops:
  0.6 5.3 %collective-permute-start = (bf16[4,6144]{1,0:T(4,128)(2,1)}, bf16[4,6144]{1,0:T(4,128)(2,1)S(1)}, u32[]{:S(2)}, u32[]{:S(2)}) collective-permute-start(bf16[4,6144]{1,0:T(4,128)(2,1)} %tokens_ref.1), channel_id=1, source_target_pairs={{0,2},{2,0},{4,6},{6,4},{8,10},{10,8},{12,14},{14,12},{1,3},{3,1},... | collective-permute-start | bytes 147464 | tf_op jit(solution)/shard_map/ppermute | solution.py:28
  4.6 6.3 %collective-permute-start.3 = (bf16[192,128]{1,0:T(8,128)(2,1)S(1)}, bf16[192,128]{1,0:T(8,128)(2,1)S(1)}, u32[]{:S(2)}, u32[]{:S(2)}) collective-permute-start(bf16[192,128]{1,0:T(8,128)(2,1)S(1)} %widen.1), channel_id=1, source_target_pairs={{0,2},{2,0},{4,6},{6,4},{8,10},{10,8},{12,14},{14,12},{1,3},{3,1},... | collective-permute-start | bytes 147464 | tf_op jit(solution)/shard_map/ppermute | solution.py:28
  4.7 12.7 %slice-start = ((s8[12582912]{0:T(1024)(128)(4,1)}), s8[4194304]{0:T(1024)(128)(4,1)S(1)}, s32[]{:S(2)}) async-start(s8[12582912]{0:T(1024)(128)(4,1)} %bitcast.3), calls=%async_computation | async-start | bytes 8388608
  4.7 12.7 %slice-start.1 = ((s8[12582912]{0:T(1024)(128)(4,1)}), s8[4194304]{0:T(1024)(128)(4,1)S(1)}, s32[]{:S(2)}) async-start(s8[12582912]{0:T(1024)(128)(4,1)} %bitcast.3), calls=%async_computation.1 | async-start | bytes 8388608
  4.7 12.7 %slice-start.2 = ((s8[12582912]{0:T(1024)(128)(4,1)}), s8[4194304]{0:T(1024)(128)(4,1)S(1)}, s32[]{:S(2)}) async-start(s8[12582912]{0:T(1024)(128)(4,1)} %bitcast.3), calls=%async_computation.2 | async-start | bytes 8388608
  4.8 12.7 %copy-start = (bf16[1,6144,1024]{2,1,0:T(8,128)(2,1)S(1)}, bf16[1,6144,1024]{2,1,0:T(8,128)(2,1)}, u32[]{:S(2)}) copy-start(bf16[1,6144,1024]{2,1,0:T(8,128)(2,1)} %up_ref.1) | copy-start | bytes 37748740
  6.1 6.6 %collective-permute-start.1 = (bf16[8,3072]{1,0:T(8,128)(2,1)S(1)}, bf16[8,3072]{1,0:T(8,128)(2,1)S(1)}, u32[]{:S(2)}, u32[]{:S(2)}) collective-permute-start(bf16[8,3072]{1,0:T(8,128)(2,1)S(1)} %norm_both.1.own_ref), channel_id=1, source_target_pairs={{0,12},{2,14},{4,8},{6,10},{8,4},{10,6},{12,0},{14,2},{1,13},{3,15... | collective-permute-start | bytes 147464 | tf_op jit(solution)/shard_map/ppermute | solution.py:28
  10.3 5.0 %collective-permute-start.2 = (bf16[8,3072]{1,0:T(8,128)(2,1)S(1)}, bf16[8,3072]{1,0:T(8,128)(2,1)S(1)}, u32[]{:S(2)}, u32[]{:S(2)}) collective-permute-start(bf16[8,3072]{1,0:T(8,128)(2,1)S(1)} %norm_both.1.own_ref), channel_id=1, source_target_pairs={{0,8},{2,10},{4,12},{6,14},{8,0},{10,2},{12,4},{14,6},{1,9},{3,11}... | collective-permute-start | bytes 147464 | tf_op jit(solution)/shard_map/ppermute | solution.py:28
  10.3 5.0 %collective-permute-start.4 = (bf16[8,3072]{1,0:T(8,128)(2,1)S(1)}, bf16[8,3072]{1,0:T(8,128)(2,1)S(1)}, u32[]{:S(2)}, u32[]{:S(2)}) collective-permute-start(bf16[8,3072]{1,0:T(8,128)(2,1)S(1)} %norm_both.1.own_ref), channel_id=1, source_target_pairs={{0,4},{2,6},{4,0},{6,2},{8,12},{10,14},{12,8},{14,10},{1,5},{3,7},... | collective-permute-start | bytes 147464 | tf_op jit(solution)/shard_map/ppermute | solution.py:28
  15.3 2.1 %collective-permute-start.6 = (bf16[32,3072]{1,0:T(8,128)(2,1)S(1)}, bf16[32,3072]{1,0:T(8,128)(2,1)S(1)}, u32[]{:S(2)}, u32[]{:S(2)}) collective-permute-start(bf16[32,3072]{1,0:T(8,128)(2,1)S(1)} %get-tuple-element.20.x_ref), channel_id=1, source_target_pairs={{0,1},{1,0},{2,3},{3,2},{4,5},{5,4},{6,7},{7,6},{8,9},{9,8},{10,11... | collective-permute-start | bytes 589832 | tf_op jit(solution)/shard_map/ppermute | solution.py:28
  15.4 6.9 %collective-permute-start.5 = (bf16[256,128]{1,0:T(8,128)(2,1)S(1)}, bf16[256,128]{1,0:T(8,128)(2,1)S(1)}, u32[]{:S(2)}, u32[]{:S(2)}) collective-permute-start(bf16[256,128]{1,0:T(8,128)(2,1)S(1)} %get-tuple-element.19.own_ref), channel_id=1, source_target_pairs={{0,8},{2,10},{4,12},{6,14},{8,0},{10,2},{12,4},{14,6},{1,9},{3,11}... | collective-permute-start | bytes 196616 | tf_op jit(solution)/shard_map/ppermute | solution.py:28
  22.3 7.5 %copy-start.1 = (bf16[4,512,512]{2,1,0:T(8,128)(2,1)S(1)}, bf16[4,512,512]{2,1,0:T(8,128)(2,1)}, u32[]{:S(2)}) copy-start(bf16[4,512,512]{2,1,0:T(8,128)(2,1)} %refs_2_.3) | copy-start | bytes 6291460
  22.3 7.5 %copy-start.2 = (bf16[4,512,512]{2,1,0:T(8,128)(2,1)S(1)}, bf16[4,512,512]{2,1,0:T(8,128)(2,1)}, u32[]{:S(2)}) copy-start(bf16[4,512,512]{2,1,0:T(8,128)(2,1)} %refs_3_.1) | copy-start | bytes 6291460
  22.3 7.5 %copy-start.4 = (s32[4]{0:T(128)S(1)}, s32[4]{0:T(128)}, u32[]{:S(2)}) copy-start(s32[4]{0:T(128)} %refs_4_.1) | copy-start | bytes 52
  22.4 7.5 %copy-start.5 = (s32[4]{0:T(128)S(1)}, s32[4]{0:T(128)}, u32[]{:S(2)}) copy-start(s32[4]{0:T(128)} %refs_5_.1) | copy-start | bytes 52
  23.7 1.6 %collective-permute-start.8 = (bf16[32,3072]{1,0:T(8,128)(2,1)S(1)}, bf16[32,3072]{1,0:T(8,128)(2,1)S(1)}, u32[]{:S(2)}, u32[]{:S(2)}) collective-permute-start(bf16[32,3072]{1,0:T(8,128)(2,1)S(1)} %down.2.after), channel_id=1, source_target_pairs={{0,1},{1,0},{2,3},{3,2},{4,5},{5,4},{6,7},{7,6},{8,9},{9,8},{10,11... | collective-permute-start | bytes 589832 | tf_op jit(solution)/shard_map/ppermute | solution.py:28
  23.9 6.0 %collective-permute-start.7 = (bf16[512,128]{1,0:T(8,128)(2,1)S(1)}, bf16[512,128]{1,0:T(8,128)(2,1)S(1)}, u32[]{:S(2)}, u32[]{:S(2)}) collective-permute-start(bf16[512,128]{1,0:T(8,128)(2,1)S(1)} %stack_after.1.after.near_ref.refs_0_), channel_id=1, source_target_pairs={{0,4},{2,6},{4,0},{6,2},{8,12},{10,14},{12,8},{14,10},{1,5},{3,7},... | collective-permute-start | bytes 393224 | tf_op jit(solution)/shard_map/ppermute | solution.py:28
  25.3 14.0 %copy-start.3 = (bf16[4,6144]{1,0:T(4,128)(2,1)S(1)}, bf16[4,6144]{1,0:T(4,128)(2,1)}, u32[]{:S(2)}) copy-start(bf16[4,6144]{1,0:T(4,128)(2,1)} %tokens_ref.1) | copy-start | bytes 147460
  25.4 6.7 %collective-permute-start.10 = (bf16[8,3072]{1,0:T(8,128)(2,1)S(1)}, bf16[8,3072]{1,0:T(8,128)(2,1)S(1)}, u32[]{:S(2)}, u32[]{:S(2)}) collective-permute-start(bf16[8,3072]{1,0:T(8,128)(2,1)S(1)} %get-tuple-element.26), channel_id=1, source_target_pairs={{0,12},{2,14},{4,8},{6,10},{8,4},{10,6},{12,0},{14,2},{1,13},{3,15... | collective-permute-start | bytes 147464 | tf_op jit(solution)/shard_map/ppermute | solution.py:28
  28.1 5.8 %collective-permute-start.11 = (bf16[8,3072]{1,0:T(8,128)(2,1)S(1)}, bf16[8,3072]{1,0:T(8,128)(2,1)S(1)}, u32[]{:S(2)}, u32[]{:S(2)}) collective-permute-start(bf16[8,3072]{1,0:T(8,128)(2,1)S(1)} %get-tuple-element.27.after), channel_id=1, source_target_pairs={{0,8},{2,10},{4,12},{6,14},{8,0},{10,2},{12,4},{14,6},{1,9},{3,11}... | collective-permute-start | bytes 147464 | tf_op jit(solution)/shard_map/ppermute | solution.py:28
  28.8 5.1 %collective-permute-start.9 = (bf16[8,3072]{1,0:T(8,128)(2,1)S(1)}, bf16[8,3072]{1,0:T(8,128)(2,1)S(1)}, u32[]{:S(2)}, u32[]{:S(2)}) collective-permute-start(bf16[8,3072]{1,0:T(8,128)(2,1)S(1)} %get-tuple-element.25), channel_id=1, source_target_pairs={{0,4},{2,6},{4,0},{6,2},{8,12},{10,14},{12,8},{14,10},{1,5},{3,7},... | collective-permute-start | bytes 147464 | tf_op jit(solution)/shard_map/ppermute | solution.py:28
  33.9 4.0 %collective-permute-start.12 = (bf16[4,3072]{1,0:T(4,128)(2,1)S(1)}, bf16[4,3072]{1,0:T(4,128)(2,1)S(1)}, u32[]{:S(2)}, u32[]{:S(2)}) collective-permute-start(bf16[4,3072]{1,0:T(4,128)(2,1)S(1)} %get-tuple-element.28.refs_6_), channel_id=1, source_target_pairs={{0,2},{2,0},{4,6},{6,4},{8,10},{10,8},{12,14},{14,12},{1,3},{3,1},... | collective-permute-start | bytes 73736 | tf_op jit(solution)/shard_map/ppermute | solution.py:28
  36.0 2.0 %collective-permute-start.13 = (bf16[4,3072]{1,0:T(4,128)(2,1)S(1)}, bf16[4,3072]{1,0:T(4,128)(2,1)S(1)}, u32[]{:S(2)}, u32[]{:S(2)}) collective-permute-start(bf16[4,3072]{1,0:T(4,128)(2,1)S(1)} %get-tuple-element.29.kept_ref), channel_id=1, source_target_pairs={{0,1},{1,0},{2,3},{3,2},{4,5},{5,4},{6,7},{7,6},{8,9},{9,8},{10,11... | collective-permute-start | bytes 73736 | tf_op jit(solution)/shard_map/ppermute | solution.py:28
  36.0 3.3 %collective-permute-start.14 = (bf16[4,3072]{1,0:T(4,128)(2,1)S(1)}, bf16[4,3072]{1,0:T(4,128)(2,1)S(1)}, u32[]{:S(2)}, u32[]{:S(2)}) collective-permute-start(bf16[4,3072]{1,0:T(4,128)(2,1)S(1)} %get-tuple-element.28.refs_6_), channel_id=1, source_target_pairs={{0,3},{1,2},{2,1},{3,0},{4,7},{5,6},{6,5},{7,4},{8,11},{9,10},{10,... | collective-permute-start | bytes 73736 | tf_op jit(solution)/shard_map/ppermute | solution.py:514

commit v14 on v13

--- a/solution.py
+++ b/solution.py
@@ -26,6 +26,16 @@
 
 def swap(block, axis, count, step):
     return lax.ppermute(block, axis, [(i, i ^ step) for i in range(count)])
+
+
+def cross(block, wide, step):
+    pairs = [(2 * i + c, 2 * (i ^ step) + 1 - c) for i in range(wide) for c in range(2)]
+    return lax.ppermute(block, ("wide", "narrow"), pairs)
+
+
+def side_of(flip):
+    bit = (lax.axis_index("wide") // flip) % 2
+    return lax.axis_index("narrow") ^ bit
 
 
 def owner_of(place, me, steps):
@@ -104,13 +114,12 @@
     heads_ref[...] = packed[...].astype(jnp.bfloat16)
 
 
-def norm_both(own_ref, got_ref, gain_ref, share, heads, out_ref):
+def norm_both(flip, own_ref, got_ref, gain_ref, share, heads, out_ref):
     half = out_ref.shape[1]
-    core = lax.axis_index("narrow")
     values = stacked([own_ref, got_ref])
     scale = lax.rsqrt(jnp.mean(values * values, axis=-1, keepdims=True) + 1e-05)
     normed = values * scale * gain_ref[...]
-    out_ref[...] = jnp.where(core == 0, normed[:, :half], normed[:, half:]).astype(jnp.bfloat16)
+    out_ref[...] = jnp.where(side_of(flip) == 0, normed[:, :half], normed[:, half:]).astype(jnp.bfloat16)
 
 
 def stacked(refs):
@@ -171,6 +180,7 @@
 
 
 def gate_all(
+    flip,
     x_ref,
     other_ref,
     gate_ref,
@@ -183,14 +193,14 @@
     sems,
 ):
     count, depth = x_ref.shape
-    core = lax.axis_index("narrow")
-    other_copies = column_copies(far_down, down_other, sems.at[0], (1 - core) * depth)
-    own_copies = column_copies(far_down, down_own, sems.at[1], core * depth)
+    side = side_of(flip)
+    other_copies = column_copies(far_down, down_other, sems.at[0], (1 - side) * depth)
+    own_copies = column_copies(far_down, down_own, sems.at[1], side * depth)
     for copy in other_copies + own_copies:
         copy.start()
     tile = min(TILE, gate_ref.shape[2])
-    own = pl.ds(pl.multiple_of(core * depth, depth), depth)
-    other = pl.ds(pl.multiple_of((1 - core) * depth, depth), depth)
+    own = pl.ds(pl.multiple_of(side * depth, depth), depth)
+    other = pl.ds(pl.multiple_of((1 - side) * depth, depth), depth)
 
     weight = share_ref[:, 0:1]
 
@@ -235,9 +245,9 @@
     sent_ref[...] = total[kept:].astype(jnp.bfloat16)
 
 
-def finish(kept_ref, taken_ref, other_kept, other_taken, tokens_ref, after, out_ref):
+def finish(flip, kept_ref, taken_ref, other_kept, other_taken, tokens_ref, after, out_ref):
     half = kept_ref.shape[1]
-    first = lax.axis_index("narrow") == 0
+    first = side_of(flip) == 0
     own = kept_ref[...].astype(jnp.float32) + taken_ref[...].astype(jnp.float32)
     other = other_kept[...].astype(jnp.float32) + other_taken[...].astype(jnp.float32)
     tokens = tokens_ref[...].astype(jnp.float32)
@@ -357,7 +367,7 @@
         dma = pltpu.SemaphoreType.DMA
         piece_bytes = 2 * half * units
 
-        got = swap(tokens, "wide", wide, steps[0])
+        got = cross(tokens, wide, steps[0])
         heads_in = [queries, new_keys, new_values]
         row_in = [tokens, norm_gain[None]]
         heads, *row_near = call(
@@ -382,7 +392,7 @@
             far=range(5),
         )
         x = call(
-            norm_both,
+            functools.partial(norm_both, steps[-2]),
             shape((2 * rows, half), bf16),
             [near(row_near[0]), got, near(row_near[1]), share, heads],
             size=100000,
@@ -405,8 +415,8 @@
                 far=(2,),
             )
         line_steps = [steps[-2], steps[-1], steps[-2] ^ steps[-1]]
-        last = swap(x, "wide", wide, line_steps[2])
-        line = [swap(x, "wide", wide, step) for step in line_steps[:2]]
+        last = cross(x, wide, line_steps[2])
+        line = [cross(x, wide, line_steps[0]), swap(x, "wide", wide, line_steps[1])]
         wider = max(x.shape[0] * half // HD, heads.shape[0])
         sent_heads = call(widen, shape((wider, HD), bf16), [heads], size=4 * wider * HD)
         far_rows = swap(sent_heads, "wide", wide, steps[0])
@@ -422,7 +432,7 @@
         other_x = swap(x, "narrow", 2, 1)
         whole = pltpu.VMEM((units, half), bf16)
         hidden, down_own, down_other = call(
-            gate_all,
+            functools.partial(gate_all, steps[-2]),
             [shape((count, units), bf16), whole, whole],
             [
                 x,
@@ -475,8 +485,11 @@
             [terms, taken],
             size=terms.size * 8,
         )
-        taken = [swap(part, "wide", wide, step) for part, step in zip(sent, line_steps)]
-        taken = [taken[i] for i in (1, 2, 0)]
+        taken = [
+            swap(sent[1], "wide", wide, line_steps[1]),
+            cross(sent[2], wide, line_steps[2]),
+            cross(sent[0], wide, line_steps[0]),
+        ]
         early = call(
             functools.partial(attend, head_steps, early_slots),
             shape((len(early_slots) * heads_local, HD), f32),
@@ -510,10 +523,9 @@
             far=(6,),
         )
         other_kept = swap(terms, "narrow", 2, 1)
-        crossed = [(i, (((i >> 1) ^ steps[0]) << 1) | (1 - (i & 1))) for i in range(2 * wide)]
-        other_taken = lax.ppermute(sent, ("wide", "narrow"), crossed)
+        other_taken = cross(sent, wide, steps[0])
         mixed_out = call(
-            finish,
+            functools.partial(finish, steps[-2]),
             shape((rows, width), bf16),
             [terms, *taken, other_kept, other_taken, tokens, distant(context)],
             size=terms.size * 8,

time: 40.1 us -> 39.6 us (0.988)
  waiting for transfers between devices: 7.71 us -> 6.54 us
  starting transfers between devices: 17.1 us -> 17.7 us
    ppermute x1 -> x6, starting transfers between devices: 0.2 us -> 9.38 us  [cross(): return lax.ppermute(block, ('wide', 'narrow'), pairs)]
    ppermute x14 -> x9, starting transfers between devices: 16.9 us -> 8.32 us  [swap(): return lax.ppermute(block, axis, [(i, i ^ step) for i in range(count)])]
    ppermute x14 -> x9, waiting for transfers between devices: 6.46 us -> 0.03 us  [swap(): return lax.ppermute(block, axis, [(i, i ^ step) for i in range(count)])]
    ppermute x1 -> x6, waiting for transfers between devices: 1.25 us -> 6.51 us  [cross(): return lax.ppermute(block, ('wide', 'narrow'), pairs)]
  transfers between devices with their start and end apart: 15 -> 15, of which waited for: 5 -> 4; matrix products, arithmetic and copies ran while one was open for 0% -> 0% of each run, Pallas kernels for 30% -> 31%
where the time goes in v14:
time: 39.6 us; the launch traced here: 39.3 us
  starting transfers between devices  17.7 us (45%)
  Pallas kernels  14.2 us (36%)
  waiting for transfers between devices  6.54 us (17%)
  between operations  0.83 us (2%)
    pallas_call x14, Pallas kernels, call(): pl.pallas_call(kernel, name=getattr(kernel, 'func', kernel).__name__, out...  14.2 us
    ppermute x6, starting transfers between devices, cross(): return lax.ppermute(block, ('wide', 'narrow'), pairs)  9.38 us
    ppermute x9, starting transfers between devices, swap(): return lax.ppermute(block, axis, [(i, i ^ step) for i in range(count)])  8.32 us
    ppermute x6, waiting for transfers between devices, cross(): return lax.ppermute(block, ('wide', 'narrow'), pairs)  6.51 us
  transfers between devices with their start and end apart: 15, of which 4 were waited for; matrix products, arithmetic and copies ran while one was open for 0% of the time, Pallas kernels for 31%

profile of v14, /device:TPU:0, one launch (start us, length us, event | category | flops | bytes accessed | tf_op | source)
XLA Modules:
  0.0 39.3 jit_solution(8127162891315075910)
XLA Ops:
  0.6 2.5 %collective-permute-start = (bf16[4,6144]{1,0:T(4,128)(2,1)}, bf16[4,6144]{1,0:T(4,128)(2,1)S(1)}, u32[]{:S(2)}, u32[]{:S(2)}) collective-permute-start(bf16[4,6144]{1,0:T(4,128)(2,1)} %tokens_ref.1), channel_id=1, source_target_pairs={{0,3},{1,2},{2,1},{3,0},{4,7},{5,6},{6,5},{7,4},{8,11},{9,10},{10,... | collective-permute-start | bytes 147464 | tf_op jit(solution)/shard_map/ppermute | solution.py:33
  3.1 1.0 %pack.1 = (bf16[128,128]{1,0:T(8,128)(2,1)S(1)}, bf16[4,6144]{1,0:T(4,128)(2,1)S(1)}, f32[1,6144]{1,0:T(1,128)S(1)}) custom-call(bf16[4,3072]{1,0:T(4,128)(2,1)} %far_query.1, bf16[4,512]{1,0:T(4,128)(2,1)} %far_key.1, bf16[4,512]{1,0:T(4,128)(2,1)} %far_value.1, bf16[4,6144]{1,0:T(4,128)(2,1)} %tokens_ref.1, f32[1,6144]{1,0:T(1,128)} %bitcast.5), custom_call_target="tpu_custom_call" | custom-call | bytes 100000 | tf_op jit(solution)/shard_map/pack/pallas_call | solution.py:59
  4.1 0.6 %collective-permute-start.3 = (bf16[192,128]{1,0:T(8,128)(2,1)S(1)}, bf16[192,128]{1,0:T(8,128)(2,1)S(1)}, u32[]{:S(2)}, u32[]{:S(2)}) collective-permute-start(bf16[192,128]{1,0:T(8,128)(2,1)S(1)} %widen.1), channel_id=1, source_target_pairs={{0,2},{2,0},{4,6},{6,4},{8,10},{10,8},{12,14},{14,12},{1,3},{3,1},... | collective-permute-start | bytes 147464 | tf_op jit(solution)/shard_map/ppermute | solution.py:28
  4.7 1.0 %shares.1.share.share_ref = f32[32,128]{1,0:T(8,128)S(1)} custom-call(s32[2,32]{1,0:T(2,128)} %bitcast.6, f32[2,32]{1,0:T(2,128)} %bitcast.7, bf16[128,128]{1,0:T(8,128)(2,1)S(1)} %get-tuple-element.18.refs_0_.heads.own_ref.own_heads, bf16[1,6144,1024]{2,1,0:T(8,128)(2,1)} %gate_ref.1, bf16[1,6144,1024]{2,1,0:T(8,128)(2,1)} %up_ref.1), custom_call_target="tpu_custom_call" | custom-call | bytes 100000 | tf_op jit(solution)/shard_map/shares/pallas_call | solution.py:59
  5.7 0.0 collective-permute-done.got_ref
  5.7 0.2 norm_both.1.own_ref
  5.9 4.0 %collective-permute-start.1 = (bf16[8,3072]{1,0:T(8,128)(2,1)S(1)}, bf16[8,3072]{1,0:T(8,128)(2,1)S(1)}, u32[]{:S(2)}, u32[]{:S(2)}) collective-permute-start(bf16[8,3072]{1,0:T(8,128)(2,1)S(1)} %norm_both.1.own_ref), channel_id=1, source_target_pairs={{0,13},{1,12},{2,15},{3,14},{4,9},{5,8},{6,11},{7,10},{8,5},{9,4},... | collective-permute-start | bytes 147464 | tf_op jit(solution)/shard_map/ppermute | solution.py:33
  9.9 0.0 collective-permute-start.2
  9.9 0.6 %collective-permute-start.4 = (bf16[8,3072]{1,0:T(8,128)(2,1)S(1)}, bf16[8,3072]{1,0:T(8,128)(2,1)S(1)}, u32[]{:S(2)}, u32[]{:S(2)}) collective-permute-start(bf16[8,3072]{1,0:T(8,128)(2,1)S(1)} %norm_both.1.own_ref), channel_id=1, source_target_pairs={{0,4},{2,6},{4,0},{6,2},{8,12},{10,14},{12,8},{14,10},{1,5},{3,7},... | collective-permute-start | bytes 147464 | tf_op jit(solution)/shard_map/ppermute | solution.py:28
  10.5 0.0 collective-permute-done.3.got_heads
  10.5 1.5 %collective-permute-done.1.last_ref = bf16[8,3072]{1,0:T(8,128)(2,1)S(1)} collective-permute-done((bf16[8,3072]{1,0:T(8,128)(2,1)S(1)}, bf16[8,3072]{1,0:T(8,128)(2,1)S(1)}, u32[]{:S(2)}, u32[]{:S(2)}) %collective-permute-start.1) | collective-permute-done | bytes 49184 | tf_op jit(solution)/shard_map/ppermute | solution.py:33
  12.1 2.5 %collective-permute-done.2.far_ref = bf16[8,3072]{1,0:T(8,128)(2,1)S(1)} collective-permute-done((bf16[8,3072]{1,0:T(8,128)(2,1)S(1)}, bf16[8,3072]{1,0:T(8,128)(2,1)S(1)}, u32[]{:S(2)}, u32[]{:S(2)}) %collective-permute-start.2) | collective-permute-done | bytes 49184 | tf_op jit(solution)/shard_map/ppermute | solution.py:33
  14.6 0.0 collective-permute-done.4.next_ref
  14.6 0.3 collective-permute-start.6
  14.9 2.2 %collective-permute-start.5 = (bf16[256,128]{1,0:T(8,128)(2,1)S(1)}, bf16[256,128]{1,0:T(8,128)(2,1)S(1)}, u32[]{:S(2)}, u32[]{:S(2)}) collective-permute-start(bf16[256,128]{1,0:T(8,128)(2,1)S(1)} %get-tuple-element.19.own_ref), channel_id=1, source_target_pairs={{0,8},{2,10},{4,12},{6,14},{8,0},{10,2},{12,4},{14,6},{1,9},{3,11}... | collective-permute-start | bytes 196616 | tf_op jit(solution)/shard_map/ppermute | solution.py:28
  17.1 0.0 collective-permute-done.6.other_ref
  17.1 0.0 slice-done.1
  17.1 0.0 slice-done.2
  17.1 0.0 copy-done
  17.1 4.8 %gate_all.1 = (bf16[32,1024]{1,0:T(8,128)(2,1)S(1)}, bf16[1024,3072]{1,0:T(8,128)(2,1)S(1)}, bf16[1024,3072]{1,0:T(8,128)(2,1)S(1)}) custom-call(bf16[32,3072]{1,0:T(8,128)(2,1)S(1)} %get-tuple-element.20.x_ref, bf16[32,3072]{1,0:T(8,128)(2,1)S(1)} %collective-permute-done.6.other_ref, bf16[1,6144,1024]{2,1,0:T(8,128)(2,1)S(1)} %bitcast.4, ...), custom_call_target="tpu_custom_call" | custom-call | flops 805306368 | bytes 37748736 | tf_op jit(solution)/shard_map/gate_all/pallas_call | solution.py:59
  21.9 0.0 collective-permute-done.5.got_ref
  22.0 0.0 copy-start.1
  22.0 0.0 copy-start.2
  22.0 0.0 copy-start.4
  22.0 0.0 copy-start.5
  22.0 1.3 %down.2.after = bf16[32,3072]{1,0:T(8,128)(2,1)S(1)} custom-call(bf16[32,1024]{1,0:T(8,128)(2,1)S(1)} %get-tuple-element.21.after.hidden_ref, bf16[1024,3072]{1,0:T(8,128)(2,1)S(1)} %get-tuple-element.23.down_ref, bf16[512,128]{1,0:T(8,128)(2,1)S(1)} %stack_after.1.after.near_ref.refs_0_), custom_call_target="tpu_custom_call" | custom-call | flops 201326592 | bytes 6291456 | tf_op jit(solution)/shard_map/down/pallas_call | solution.py:59
  23.3 0.2 collective-permute-start.8
  23.5 0.9 %collective-permute-start.7 = (bf16[512,128]{1,0:T(8,128)(2,1)S(1)}, bf16[512,128]{1,0:T(8,128)(2,1)S(1)}, u32[]{:S(2)}, u32[]{:S(2)}) collective-permute-start(bf16[512,128]{1,0:T(8,128)(2,1)S(1)} %stack_after.1.after.near_ref.refs_0_), channel_id=1, source_target_pairs={{0,4},{2,6},{4,0},{6,2},{8,12},{10,14},{12,8},{14,10},{1,5},{3,7},... | collective-permute-start | bytes 393224 | tf_op jit(solution)/shard_map/ppermute | solution.py:28
  24.4 1.3 %down.3.terms_ref = f32[32,3072]{1,0:T(8,128)S(1)} custom-call(bf16[32,1024]{1,0:T(8,128)(2,1)S(1)} %get-tuple-element.21.after.hidden_ref, bf16[1024,3072]{1,0:T(8,128)(2,1)S(1)} %get-tuple-element.22.down_ref, bf16[32,3072]{1,0:T(8,128)(2,1)S(1)} %down.2.after), custom_call_target="tpu_custom_call" | custom-call | flops 201326592 | bytes 6291456 | tf_op jit(solution)/shard_map/down/pallas_call | solution.py:59
  25.7 0.0 collective-permute-done.8.taken_ref
  25.8 1.6 %collective-permute-start.10 = (bf16[8,3072]{1,0:T(8,128)(2,1)S(1)}, bf16[8,3072]{1,0:T(8,128)(2,1)S(1)}, u32[]{:S(2)}, u32[]{:S(2)}) collective-permute-start(bf16[8,3072]{1,0:T(8,128)(2,1)S(1)} %get-tuple-element.26), channel_id=1, source_target_pairs={{0,13},{1,12},{2,15},{3,14},{4,9},{5,8},{6,11},{7,10},{8,5},{9,4},... | collective-permute-start | bytes 147464 | tf_op jit(solution)/shard_map/ppermute | solution.py:33
  27.4 0.7 %collective-permute-start.11 = (bf16[8,3072]{1,0:T(8,128)(2,1)S(1)}, bf16[8,3072]{1,0:T(8,128)(2,1)S(1)}, u32[]{:S(2)}, u32[]{:S(2)}) collective-permute-start(bf16[8,3072]{1,0:T(8,128)(2,1)S(1)} %get-tuple-element.27.after), channel_id=1, source_target_pairs={{0,9},{1,8},{2,11},{3,10},{4,13},{5,12},{6,15},{7,14},{8,1},{9,0},... | collective-permute-start | bytes 147464 | tf_op jit(solution)/shard_map/ppermute | solution.py:33
  28.1 1.8 %collective-permute-start.9 = (bf16[8,3072]{1,0:T(8,128)(2,1)S(1)}, bf16[8,3072]{1,0:T(8,128)(2,1)S(1)}, u32[]{:S(2)}, u32[]{:S(2)}) collective-permute-start(bf16[8,3072]{1,0:T(8,128)(2,1)S(1)} %get-tuple-element.25), channel_id=1, source_target_pairs={{0,4},{2,6},{4,0},{6,2},{8,12},{10,14},{12,8},{14,10},{1,5},{3,7},... | collective-permute-start | bytes 147464 | tf_op jit(solution)/shard_map/ppermute | solution.py:28
  29.9 0.0 collective-permute-done.7.far_ref.refs_1_
  30.0 0.0 copy-done.4
  30.0 0.0 copy-done.5
  30.0 2.2 %attend.1.refs_4_.refs_7_ = f32[72,128]{1,0:T(8,128)S(1)} custom-call(bf16[512,128]{1,0:T(8,128)(2,1)S(1)} %stack_after.1.after.near_ref.refs_0_, bf16[512,128]{1,0:T(8,128)(2,1)S(1)} %collective-permute-done.7.far_ref.refs_1_, bf16[4,512,512]{2,1,0:T(8,128)(2,1)S(1)} %copy-done.1, bf16[4,512,512]{2,1,0:T(8,128)(2,1)S(1)} %copy-done.2, s32[4]{0:T(128)S(1)} %copy-done.4, ...), custom_call_target="tpu_custom_call" | custom-call | flops 12582912 | bytes 2097152 | tf_op jit(solution)/shard_map/attend/pallas_call | solution.py:59
  32.2 0.0 collective-permute-done.10.refs_2_
  32.2 1.5 %collective-permute-done.11.refs_3_ = bf16[8,3072]{1,0:T(8,128)(2,1)S(1)} collective-permute-done((bf16[8,3072]{1,0:T(8,128)(2,1)S(1)}, bf16[8,3072]{1,0:T(8,128)(2,1)S(1)}, u32[]{:S(2)}, u32[]{:S(2)}) %collective-permute-start.11) | collective-permute-done | bytes 49184 | tf_op jit(solution)/shard_map/ppermute | solution.py:33
  33.7 0.0 collective-permute-done.9.refs_1_
  33.8 1.6 %collective-permute-start.12 = (bf16[4,3072]{1,0:T(4,128)(2,1)S(1)}, bf16[4,3072]{1,0:T(4,128)(2,1)S(1)}, u32[]{:S(2)}, u32[]{:S(2)}) collective-permute-start(bf16[4,3072]{1,0:T(4,128)(2,1)S(1)} %get-tuple-element.28.refs_6_), channel_id=1, source_target_pairs={{0,2},{2,0},{4,6},{6,4},{8,10},{10,8},{12,14},{14,12},{1,3},{3,1},... | collective-permute-start | bytes 73736 | tf_op jit(solution)/shard_map/ppermute | solution.py:28
  35.4 0.0 collective-permute-start.13
  35.4 0.6 %collective-permute-start.14 = (bf16[4,3072]{1,0:T(4,128)(2,1)S(1)}, bf16[4,3072]{1,0:T(4,128)(2,1)S(1)}, u32[]{:S(2)}, u32[]{:S(2)}) collective-permute-start(bf16[4,3072]{1,0:T(4,128)(2,1)S(1)} %get-tuple-element.28.refs_6_), channel_id=1, source_target_pairs={{0,3},{1,2},{2,1},{3,0},{4,7},{5,6},{6,5},{7,4},{8,11},{9,10},{10,... | collective-permute-start | bytes 73736 | tf_op jit(solution)/shard_map/ppermute | solution.py:33
  36.0 1.8 %attend_last.1.after = bf16[4,3072]{1,0:T(4,128)(2,1)} custom-call(bf16[512,128]{1,0:T(8,128)(2,1)S(1)} %stack_after.1.after.near_ref.refs_0_, bf16[512,128]{1,0:T(8,128)(2,1)S(1)} %collective-permute-done.7.far_ref.refs_1_, bf16[4,512,512]{2,1,0:T(8,128)(2,1)S(1)} %copy-done.1, bf16[4,512,512]{2,1,0:T(8,128)(2,1)S(1)} %copy-done.2, s32[4]{0:T(128)S(1)} %copy-done.4, ...), custom_call_target="tpu_custom_call" | custom-call | flops 12582912 | bytes 2097152 | tf_op jit(solution)/shard_map/attend_last/pallas_call | solution.py:59
  37.8 0.0 collective-permute-done.12.taken_ref
  37.8 0.0 collective-permute-done.13.other_kept
  37.8 0.9 %collective-permute-done.14.other_taken = bf16[4,3072]{1,0:T(4,128)(2,1)S(1)} collective-permute-done((bf16[4,3072]{1,0:T(4,128)(2,1)S(1)}, bf16[4,3072]{1,0:T(4,128)(2,1)S(1)}, u32[]{:S(2)}, u32[]{:S(2)}) %collective-permute-start.14) | collective-permute-done | bytes 24608 | tf_op jit(solution)/shard_map/ppermute | solution.py:33
  38.7 0.7 %finish.1 = bf16[4,6144]{1,0:T(4,128)(2,1)} custom-call(bf16[4,3072]{1,0:T(4,128)(2,1)S(1)} %get-tuple-element.29.kept_ref, bf16[4,3072]{1,0:T(4,128)(2,1)S(1)} %collective-permute-done.12.taken_ref, bf16[4,3072]{1,0:T(4,128)(2,1)S(1)} %collective-permute-done.13.other_kept, bf16[4,3072]{1,0:T(4,128)(2,1)S(1)} %collective-permute-done.14.other_taken, ...), custom_call_target="tpu_custom_call" | custom-call | bytes 98304 | tf_op jit(solution)/shard_map/finish/pallas_call | solution.py:59
  (15 shorter events, 0.1 us)
Async XLA Ops:
  0.6 5.1 %collective-permute-start = (bf16[4,6144]{1,0:T(4,128)(2,1)}, bf16[4,6144]{1,0:T(4,128)(2,1)S(1)}, u32[]{:S(2)}, u32[]{:S(2)}) collective-permute-start(bf16[4,6144]{1,0:T(4,128)(2,1)} %tokens_ref.1), channel_id=1, source_target_pairs={{0,3},{1,2},{2,1},{3,0},{4,7},{5,6},{6,5},{7,4},{8,11},{9,10},{10,... | collective-permute-start | bytes 147464 | tf_op jit(solution)/shard_map/ppermute | solution.py:33
  4.1 6.4 %collective-permute-start.3 = (bf16[192,128]{1,0:T(8,128)(2,1)S(1)}, bf16[192,128]{1,0:T(8,128)(2,1)S(1)}, u32[]{:S(2)}, u32[]{:S(2)}) collective-permute-start(bf16[192,128]{1,0:T(8,128)(2,1)S(1)} %widen.1), channel_id=1, source_target_pairs={{0,2},{2,0},{4,6},{6,4},{8,10},{10,8},{12,14},{14,12},{1,3},{3,1},... | collective-permute-start | bytes 147464 | tf_op jit(solution)/shard_map/ppermute | solution.py:28
  4.7 12.4 %slice-start = ((s8[12582912]{0:T(1024)(128)(4,1)}), s8[4194304]{0:T(1024)(128)(4,1)S(1)}, s32[]{:S(2)}) async-start(s8[12582912]{0:T(1024)(128)(4,1)} %bitcast.3), calls=%async_computation | async-start | bytes 8388608
  4.7 12.4 %slice-start.1 = ((s8[12582912]{0:T(1024)(128)(4,1)}), s8[4194304]{0:T(1024)(128)(4,1)S(1)}, s32[]{:S(2)}) async-start(s8[12582912]{0:T(1024)(128)(4,1)} %bitcast.3), calls=%async_computation.1 | async-start | bytes 8388608
  4.7 12.4 %slice-start.2 = ((s8[12582912]{0:T(1024)(128)(4,1)}), s8[4194304]{0:T(1024)(128)(4,1)S(1)}, s32[]{:S(2)}) async-start(s8[12582912]{0:T(1024)(128)(4,1)} %bitcast.3), calls=%async_computation.2 | async-start | bytes 8388608
  4.7 12.4 %copy-start = (bf16[1,6144,1024]{2,1,0:T(8,128)(2,1)S(1)}, bf16[1,6144,1024]{2,1,0:T(8,128)(2,1)}, u32[]{:S(2)}) copy-start(bf16[1,6144,1024]{2,1,0:T(8,128)(2,1)} %up_ref.1) | copy-start | bytes 37748740
  5.9 6.2 %collective-permute-start.1 = (bf16[8,3072]{1,0:T(8,128)(2,1)S(1)}, bf16[8,3072]{1,0:T(8,128)(2,1)S(1)}, u32[]{:S(2)}, u32[]{:S(2)}) collective-permute-start(bf16[8,3072]{1,0:T(8,128)(2,1)S(1)} %norm_both.1.own_ref), channel_id=1, source_target_pairs={{0,13},{1,12},{2,15},{3,14},{4,9},{5,8},{6,11},{7,10},{8,5},{9,4},... | collective-permute-start | bytes 147464 | tf_op jit(solution)/shard_map/ppermute | solution.py:33
  9.9 4.7 %collective-permute-start.2 = (bf16[8,3072]{1,0:T(8,128)(2,1)S(1)}, bf16[8,3072]{1,0:T(8,128)(2,1)S(1)}, u32[]{:S(2)}, u32[]{:S(2)}) collective-permute-start(bf16[8,3072]{1,0:T(8,128)(2,1)S(1)} %norm_both.1.own_ref), channel_id=1, source_target_pairs={{0,9},{1,8},{2,11},{3,10},{4,13},{5,12},{6,15},{7,14},{8,1},{9,0},... | collective-permute-start | bytes 147464 | tf_op jit(solution)/shard_map/ppermute | solution.py:33
  9.9 4.7 %collective-permute-start.4 = (bf16[8,3072]{1,0:T(8,128)(2,1)S(1)}, bf16[8,3072]{1,0:T(8,128)(2,1)S(1)}, u32[]{:S(2)}, u32[]{:S(2)}) collective-permute-start(bf16[8,3072]{1,0:T(8,128)(2,1)S(1)} %norm_both.1.own_ref), channel_id=1, source_target_pairs={{0,4},{2,6},{4,0},{6,2},{8,12},{10,14},{12,8},{14,10},{1,5},{3,7},... | collective-permute-start | bytes 147464 | tf_op jit(solution)/shard_map/ppermute | solution.py:28
  14.6 2.5 %collective-permute-start.6 = (bf16[32,3072]{1,0:T(8,128)(2,1)S(1)}, bf16[32,3072]{1,0:T(8,128)(2,1)S(1)}, u32[]{:S(2)}, u32[]{:S(2)}) collective-permute-start(bf16[32,3072]{1,0:T(8,128)(2,1)S(1)} %get-tuple-element.20.x_ref), channel_id=1, source_target_pairs={{0,1},{1,0},{2,3},{3,2},{4,5},{5,4},{6,7},{7,6},{8,9},{9,8},{10,11... | collective-permute-start | bytes 589832 | tf_op jit(solution)/shard_map/ppermute | solution.py:28
  14.9 7.0 %collective-permute-start.5 = (bf16[256,128]{1,0:T(8,128)(2,1)S(1)}, bf16[256,128]{1,0:T(8,128)(2,1)S(1)}, u32[]{:S(2)}, u32[]{:S(2)}) collective-permute-start(bf16[256,128]{1,0:T(8,128)(2,1)S(1)} %get-tuple-element.19.own_ref), channel_id=1, source_target_pairs={{0,8},{2,10},{4,12},{6,14},{8,0},{10,2},{12,4},{14,6},{1,9},{3,11}... | collective-permute-start | bytes 196616 | tf_op jit(solution)/shard_map/ppermute | solution.py:28
  22.0 8.0 %copy-start.1 = (bf16[4,512,512]{2,1,0:T(8,128)(2,1)S(1)}, bf16[4,512,512]{2,1,0:T(8,128)(2,1)}, u32[]{:S(2)}) copy-start(bf16[4,512,512]{2,1,0:T(8,128)(2,1)} %refs_2_.3) | copy-start | bytes 6291460
  22.0 8.0 %copy-start.2 = (bf16[4,512,512]{2,1,0:T(8,128)(2,1)S(1)}, bf16[4,512,512]{2,1,0:T(8,128)(2,1)}, u32[]{:S(2)}) copy-start(bf16[4,512,512]{2,1,0:T(8,128)(2,1)} %refs_3_.1) | copy-start | bytes 6291460
  22.0 8.0 %copy-start.4 = (s32[4]{0:T(128)S(1)}, s32[4]{0:T(128)}, u32[]{:S(2)}) copy-start(s32[4]{0:T(128)} %refs_4_.1) | copy-start | bytes 52
  22.0 8.0 %copy-start.5 = (s32[4]{0:T(128)S(1)}, s32[4]{0:T(128)}, u32[]{:S(2)}) copy-start(s32[4]{0:T(128)} %refs_5_.1) | copy-start | bytes 52
  23.3 2.4 %collective-permute-start.8 = (bf16[32,3072]{1,0:T(8,128)(2,1)S(1)}, bf16[32,3072]{1,0:T(8,128)(2,1)S(1)}, u32[]{:S(2)}, u32[]{:S(2)}) collective-permute-start(bf16[32,3072]{1,0:T(8,128)(2,1)S(1)} %down.2.after), channel_id=1, source_target_pairs={{0,1},{1,0},{2,3},{3,2},{4,5},{5,4},{6,7},{7,6},{8,9},{9,8},{10,11... | collective-permute-start | bytes 589832 | tf_op jit(solution)/shard_map/ppermute | solution.py:28
  23.5 6.5 %collective-permute-start.7 = (bf16[512,128]{1,0:T(8,128)(2,1)S(1)}, bf16[512,128]{1,0:T(8,128)(2,1)S(1)}, u32[]{:S(2)}, u32[]{:S(2)}) collective-permute-start(bf16[512,128]{1,0:T(8,128)(2,1)S(1)} %stack_after.1.after.near_ref.refs_0_), channel_id=1, source_target_pairs={{0,4},{2,6},{4,0},{6,2},{8,12},{10,14},{12,8},{14,10},{1,5},{3,7},... | collective-permute-start | bytes 393224 | tf_op jit(solution)/shard_map/ppermute | solution.py:28
  25.7 13.0 %copy-start.3 = (bf16[4,6144]{1,0:T(4,128)(2,1)S(1)}, bf16[4,6144]{1,0:T(4,128)(2,1)}, u32[]{:S(2)}) copy-start(bf16[4,6144]{1,0:T(4,128)(2,1)} %tokens_ref.1) | copy-start | bytes 147460
  25.8 6.4 %collective-permute-start.10 = (bf16[8,3072]{1,0:T(8,128)(2,1)S(1)}, bf16[8,3072]{1,0:T(8,128)(2,1)S(1)}, u32[]{:S(2)}, u32[]{:S(2)}) collective-permute-start(bf16[8,3072]{1,0:T(8,128)(2,1)S(1)} %get-tuple-element.26), channel_id=1, source_target_pairs={{0,13},{1,12},{2,15},{3,14},{4,9},{5,8},{6,11},{7,10},{8,5},{9,4},... | collective-permute-start | bytes 147464 | tf_op jit(solution)/shard_map/ppermute | solution.py:33
  27.4 6.3 %collective-permute-start.11 = (bf16[8,3072]{1,0:T(8,128)(2,1)S(1)}, bf16[8,3072]{1,0:T(8,128)(2,1)S(1)}, u32[]{:S(2)}, u32[]{:S(2)}) collective-permute-start(bf16[8,3072]{1,0:T(8,128)(2,1)S(1)} %get-tuple-element.27.after), channel_id=1, source_target_pairs={{0,9},{1,8},{2,11},{3,10},{4,13},{5,12},{6,15},{7,14},{8,1},{9,0},... | collective-permute-start | bytes 147464 | tf_op jit(solution)/shard_map/ppermute | solution.py:33
  28.1 5.6 %collective-permute-start.9 = (bf16[8,3072]{1,0:T(8,128)(2,1)S(1)}, bf16[8,3072]{1,0:T(8,128)(2,1)S(1)}, u32[]{:S(2)}, u32[]{:S(2)}) collective-permute-start(bf16[8,3072]{1,0:T(8,128)(2,1)S(1)} %get-tuple-element.25), channel_id=1, source_target_pairs={{0,4},{2,6},{4,0},{6,2},{8,12},{10,14},{12,8},{14,10},{1,5},{3,7},... | collective-permute-start | bytes 147464 | tf_op jit(solution)/shard_map/ppermute | solution.py:28
  33.8 4.0 %collective-permute-start.12 = (bf16[4,3072]{1,0:T(4,128)(2,1)S(1)}, bf16[4,3072]{1,0:T(4,128)(2,1)S(1)}, u32[]{:S(2)}, u32[]{:S(2)}) collective-permute-start(bf16[4,3072]{1,0:T(4,128)(2,1)S(1)} %get-tuple-element.28.refs_6_), channel_id=1, source_target_pairs={{0,2},{2,0},{4,6},{6,4},{8,10},{10,8},{12,14},{14,12},{1,3},{3,1},... | collective-permute-start | bytes 73736 | tf_op jit(solution)/shard_map/ppermute | solution.py:28
  35.4 2.4 %collective-permute-start.13 = (bf16[4,3072]{1,0:T(4,128)(2,1)S(1)}, bf16[4,3072]{1,0:T(4,128)(2,1)S(1)}, u32[]{:S(2)}, u32[]{:S(2)}) collective-permute-start(bf16[4,3072]{1,0:T(4,128)(2,1)S(1)} %get-tuple-element.29.kept_ref), channel_id=1, source_target_pairs={{0,1},{1,0},{2,3},{3,2},{4,5},{5,4},{6,7},{7,6},{8,9},{9,8},{10,11... | collective-permute-start | bytes 73736 | tf_op jit(solution)/shard_map/ppermute | solution.py:28
  35.4 3.3 %collective-permute-start.14 = (bf16[4,3072]{1,0:T(4,128)(2,1)S(1)}, bf16[4,3072]{1,0:T(4,128)(2,1)S(1)}, u32[]{:S(2)}, u32[]{:S(2)}) collective-permute-start(bf16[4,3072]{1,0:T(4,128)(2,1)S(1)} %get-tuple-element.28.refs_6_), channel_id=1, source_target_pairs={{0,3},{1,2},{2,1},{3,0},{4,7},{5,6},{6,5},{7,4},{8,11},{9,10},{10,... | collective-permute-start | bytes 73736 | tf_op jit(solution)/shard_map/ppermute | solution.py:33

commit v15 on v14

--- a/solution.py
+++ b/solution.py
@@ -33,9 +33,11 @@
     return lax.ppermute(block, ("wide", "narrow"), pairs)
 
 
-def side_of(flip):
-    bit = (lax.axis_index("wide") // flip) % 2
-    return lax.axis_index("narrow") ^ bit
+def side_of(flips):
+    side = lax.axis_index("narrow")
+    for flip in flips:
+        side = side ^ ((lax.axis_index("wide") // flip) % 2)
+    return side
 
 
 def owner_of(place, me, steps):
@@ -114,12 +116,12 @@
     heads_ref[...] = packed[...].astype(jnp.bfloat16)
 
 
-def norm_both(flip, own_ref, got_ref, gain_ref, share, heads, out_ref):
+def norm_both(flips, own_ref, got_ref, gain_ref, share, heads, out_ref):
     half = out_ref.shape[1]
     values = stacked([own_ref, got_ref])
     scale = lax.rsqrt(jnp.mean(values * values, axis=-1, keepdims=True) + 1e-05)
     normed = values * scale * gain_ref[...]
-    out_ref[...] = jnp.where(side_of(flip) == 0, normed[:, :half], normed[:, half:]).astype(jnp.bfloat16)
+    out_ref[...] = jnp.where(side_of(flips) == 0, normed[:, :half], normed[:, half:]).astype(jnp.bfloat16)
 
 
 def stacked(refs):
@@ -130,12 +132,14 @@
     refs[-1][...] = stacked(refs[:-1]).astype(refs[-1].dtype)
 
 
-def stack_line(own_ref, last_ref, far_ref, got_heads, next_ref, own_heads, out_ref, heads_ref):
+def stack_line(rows, own_ref, last_ref, far_ref, got_heads, next_ref, own_heads, out_ref, heads_ref):
     count = own_heads.shape[0]
     heads_ref[:count, :] = own_heads[...]
     heads_ref[count:, :] = got_heads[:count, :]
-    rows = [own_ref, far_ref, next_ref, last_ref]
-    out_ref[...] = stacked(rows).astype(jnp.bfloat16)
+    line = [ref[...].astype(jnp.float32) for ref in (own_ref, far_ref, next_ref, last_ref)]
+    blocks = range(0, own_ref.shape[0], rows)
+    parts = [values[at : at + rows] for at in blocks for values in line]
+    out_ref[...] = jnp.concatenate(parts, axis=0).astype(jnp.bfloat16)
 
 
 def widen(own_ref, out_ref):
@@ -180,7 +184,7 @@
 
 
 def gate_all(
-    flip,
+    flips,
     x_ref,
     other_ref,
     gate_ref,
@@ -193,7 +197,7 @@
     sems,
 ):
     count, depth = x_ref.shape
-    side = side_of(flip)
+    side = side_of(flips)
     other_copies = column_copies(far_down, down_other, sems.at[0], (1 - side) * depth)
     own_copies = column_copies(far_down, down_own, sems.at[1], side * depth)
     for copy in other_copies + own_copies:
@@ -227,7 +231,14 @@
         ).astype(out_ref.dtype)
 
 
-def part_line(terms_ref, taken_ref, kept_ref, far_ref, next_ref, last_ref):
+def combine(terms_ref, taken_ref, after, kept_ref, sent_ref):
+    total = terms_ref[...] + taken_ref[...].astype(jnp.float32)
+    kept = kept_ref.shape[0]
+    kept_ref[...] = total[:kept]
+    sent_ref[...] = total[kept:].astype(jnp.bfloat16)
+
+
+def part_line(terms_ref, taken_ref, after, kept_ref, far_ref, next_ref, last_ref):
     total = terms_ref[...] + taken_ref[...].astype(jnp.float32)
     rows = kept_ref.shape[0]
     kept_ref[...] = total[:rows]
@@ -235,26 +246,23 @@
         ref[...] = total[(i + 1) * rows : (i + 2) * rows].astype(jnp.bfloat16)
 
 
-def combine(*refs):
-    terms_ref, *taken, after, kept_ref, sent_ref = refs
-    total = terms_ref[...]
+def finish(flips, kept_ref, *refs):
+    *taken, tokens_ref, after, out_ref = refs
+    half = kept_ref.shape[1]
+    total = kept_ref[...]
     for ref in taken:
         total = total + ref[...].astype(jnp.float32)
-    kept = kept_ref.shape[0]
-    kept_ref[...] = total[:kept].astype(kept_ref.dtype)
-    sent_ref[...] = total[kept:].astype(jnp.bfloat16)
-
-
-def finish(flip, kept_ref, taken_ref, other_kept, other_taken, tokens_ref, after, out_ref):
-    half = kept_ref.shape[1]
-    first = side_of(flip) == 0
-    own = kept_ref[...].astype(jnp.float32) + taken_ref[...].astype(jnp.float32)
-    other = other_kept[...].astype(jnp.float32) + other_taken[...].astype(jnp.float32)
     tokens = tokens_ref[...].astype(jnp.float32)
-    left = tokens[:, :half] + jnp.where(first, own, other)
-    right = tokens[:, half:] + jnp.where(first, other, own)
-    out_ref[:, :half] = left.astype(jnp.bfloat16)
-    out_ref[:, half:] = right.astype(jnp.bfloat16)
+    tokens = jnp.where(side_of(flips) == 0, tokens[:, :half], tokens[:, half:])
+    out_ref[...] = (tokens + total).astype(jnp.bfloat16)
+
+
+def join(flips, own_ref, other_ref, out_ref):
+    half = own_ref.shape[1]
+    first = side_of(flips) == 0
+    own, other = own_ref[...], other_ref[...]
+    out_ref[:, :half] = jnp.where(first, own, other)
+    out_ref[:, half:] = jnp.where(first, other, own)
 
 
 def attend(
@@ -339,6 +347,8 @@
 def make_local(wide):
     steps = steps_of(wide)
     head_steps = [*steps[1:-2], *steps[:1], *steps[-2:]]
+    row_steps = [*steps[-2:], *steps[:-2]]
+    flips = [steps[-2], steps[0]]
 
     def local(
         queries,
@@ -380,7 +390,7 @@
             far=range(5),
         )
         share = call(
-            functools.partial(shares, steps, rows),
+            functools.partial(shares, row_steps, rows),
             shape((count, HD), f32),
             [distant(routes.T), distant(route_logits.T), heads, distant(w_gate), distant(w_up)],
             [
@@ -392,7 +402,7 @@
             far=range(5),
         )
         x = call(
-            functools.partial(norm_both, steps[-2]),
+            functools.partial(norm_both, flips),
             shape((2 * rows, half), bf16),
             [near(row_near[0]), got, near(row_near[1]), share, heads],
             size=100000,
@@ -421,7 +431,7 @@
         sent_heads = call(widen, shape((wider, HD), bf16), [heads], size=4 * wider * HD)
         far_rows = swap(sent_heads, "wide", wide, steps[0])
         x, heads = call(
-            stack_line,
+            functools.partial(stack_line, rows),
             [shape((count, half), bf16), shape((2 * heads.shape[0], HD), bf16)],
             [x, last, line[0], far_rows, line[1], heads],
             size=8 * count * half,
@@ -432,7 +442,7 @@
         other_x = swap(x, "narrow", 2, 1)
         whole = pltpu.VMEM((units, half), bf16)
         hidden, down_own, down_other = call(
-            functools.partial(gate_all, steps[-2]),
+            functools.partial(gate_all, flips),
             [shape((count, units), bf16), whole, whole],
             [
                 x,
@@ -475,44 +485,46 @@
 
         caches = [near(key_cache), near(value_cache), lengths, assignment]
         slots = queries.shape[0]
-        early_slots = list(range(slots - 1))
-        late_slots = list(range(slots - 1, slots))
-        quarter = count // 4
-        block = shape((quarter, half), bf16)
-        terms, *sent = call(
-            part_line,
-            [shape((quarter, half), f32), block, block, block],
-            [terms, taken],
-            size=terms.size * 8,
-        )
-        taken = [
-            swap(sent[1], "wide", wide, line_steps[1]),
-            cross(sent[2], wide, line_steps[2]),
-            cross(sent[0], wide, line_steps[0]),
-        ]
-        early = call(
-            functools.partial(attend, head_steps, early_slots),
-            shape((len(early_slots) * heads_local, HD), f32),
-            [heads, far_heads, *caches, sent[0]],
-            flops=2 * key_cache.size * GROUP,
-            size=2 * key_cache.size,
-            smem=(4, 5),
-            far=(6,),
-        )
+        early_slots = list(range(slots // 2))
+        late_slots = list(range(slots // 2, slots))
+        early = hidden
         for step in reversed(steps[:-2]):
             kept = terms.shape[0] // 2
             terms, sent = call(
                 combine,
-                [shape((kept, half), bf16 if kept == rows else f32), shape((kept, half), bf16)],
-                [terms, *taken, early],
+                [shape((kept, half), f32), shape((kept, half), bf16)],
+                [terms, taken, early],
                 size=terms.size * 8,
-                far=(1 + len(taken),),
+                far=(2,),
             )
-            taken = [swap(sent, "wide", wide, step)]
+            taken = cross(sent, wide, step) if step in flips else swap(sent, "wide", wide, step)
+            if early is hidden:
+                early = call(
+                    functools.partial(attend, head_steps, early_slots),
+                    shape((len(early_slots) * heads_local, HD), f32),
+                    [heads, far_heads, *caches, sent],
+                    flops=2 * key_cache.size * GROUP,
+                    size=2 * key_cache.size,
+                    smem=(4, 5),
+                    far=(6,),
+                )
+        block = shape((rows, half), bf16)
+        terms, *sent = call(
+            part_line,
+            [shape((rows, half), f32), block, block, block],
+            [terms, taken, early],
+            size=terms.size * 8,
+            far=(2,),
+        )
+        taken = [
+            cross(sent[2], wide, line_steps[2]),
+            cross(sent[0], wide, line_steps[0]),
+            swap(sent[1], "wide", wide, line_steps[1]),
+        ]
         context = call(
             functools.partial(attend_last, head_steps, late_slots, heads_local),
             shape(queries.shape, bf16),
-            [heads, far_heads, *caches, sent, early],
+            [heads, far_heads, *caches, sent[0], early],
             [
                 pltpu.VMEM((len(late_slots) * heads_local, HD), f32),
                 pltpu.VMEM((slots * heads_local, HD), f32),
@@ -522,14 +534,19 @@
             smem=(4, 5),
             far=(6,),
         )
-        other_kept = swap(terms, "narrow", 2, 1)
-        other_taken = cross(sent, wide, steps[0])
-        mixed_out = call(
-            functools.partial(finish, steps[-2]),
-            shape((rows, width), bf16),
-            [terms, *taken, other_kept, other_taken, tokens, distant(context)],
+        piece = call(
+            functools.partial(finish, flips),
+            block,
+            [terms, *taken, tokens, distant(context)],
             size=terms.size * 8,
             far=(5,),
+        )
+        other = swap(piece, "narrow", 2, 1)
+        mixed_out = call(
+            functools.partial(join, flips),
+            shape((rows, width), bf16),
+            [piece, other],
+            size=terms.size * 4,
         )
         return (context, mixed_out)
 

time: 39.6 us -> 39.7 us (level)
  waiting for transfers between devices: 6.54 us -> 7.38 us
  starting transfers between devices: 17.7 us -> 17 us
    ppermute x9 -> x8, waiting for transfers between devices: 0.03 us -> 3.29 us  [swap(): return lax.ppermute(block, axis, [(i, i ^ step) for i in range(count)])]
    ppermute x6, waiting for transfers between devices: 6.51 us -> 4.09 us  [cross(): return lax.ppermute(block, ('wide', 'narrow'), pairs)]
    ppermute x9 -> x8, starting transfers between devices: 8.32 us -> 7 us  [swap(): return lax.ppermute(block, axis, [(i, i ^ step) for i in range(count)])]
    ppermute x6, starting transfers between devices: 9.38 us -> 9.95 us  [cross(): return lax.ppermute(block, ('wide', 'narrow'), pairs)]
    pallas_call x14 -> x15, Pallas kernels: 14.2 us -> 14.3 us  [call(): pl.pallas_call(kernel, name=getattr(kernel, 'func', kernel).__name__, out...]
  transfers between devices with their start and end apart: 15 -> 14, of which waited for: 4 -> 4; matrix products, arithmetic and copies ran while one was open for 0% -> 0% of each run, Pallas kernels for 31% -> 31%
where the time goes in v15:
time: 39.7 us; the launch traced here: 39.5 us
  starting transfers between devices  17 us (43%)
  Pallas kernels  14.3 us (36%)
  waiting for transfers between devices  7.38 us (19%)
  between operations  0.84 us (2%)
    pallas_call x15, Pallas kernels, call(): pl.pallas_call(kernel, name=getattr(kernel, 'func', kernel).__name__, out...  14.3 us
    ppermute x6, starting transfers between devices, cross(): return lax.ppermute(block, ('wide', 'narrow'), pairs)  9.95 us
    ppermute x8, starting transfers between devices, swap(): return lax.ppermute(block, axis, [(i, i ^ step) for i in range(count)])  7 us
    ppermute x6, waiting for transfers between devices, cross(): return lax.ppermute(block, ('wide', 'narrow'), pairs)  4.09 us
    ppermute x8, waiting for transfers between devices, swap(): return lax.ppermute(block, axis, [(i, i ^ step) for i in range(count)])  3.29 us
  transfers between devices with their start and end apart: 14, of which 4 were waited for; matrix products, arithmetic and copies ran while one was open for 0% of the time, Pallas kernels for 31%

profile of v15, /device:TPU:0, one launch (start us, length us, event | category | flops | bytes accessed | tf_op | source)
XLA Modules:
  0.0 39.5 jit_solution(8532810007189980012)
XLA Ops:
  0.6 2.5 %collective-permute-start = (bf16[4,6144]{1,0:T(4,128)(2,1)}, bf16[4,6144]{1,0:T(4,128)(2,1)S(1)}, u32[]{:S(2)}, u32[]{:S(2)}) collective-permute-start(bf16[4,6144]{1,0:T(4,128)(2,1)} %refs_3_.3), channel_id=1, source_target_pairs={{0,3},{1,2},{2,1},{3,0},{4,7},{5,6},{6,5},{7,4},{8,11},{9,10},{10,... | collective-permute-start | bytes 147464 | tf_op jit(solution)/shard_map/ppermute | solution.py:33
  3.1 1.0 %pack.1 = (bf16[128,128]{1,0:T(8,128)(2,1)S(1)}, bf16[4,6144]{1,0:T(4,128)(2,1)S(1)}, f32[1,6144]{1,0:T(1,128)S(1)}) custom-call(bf16[4,3072]{1,0:T(4,128)(2,1)} %far_query.1, bf16[4,512]{1,0:T(4,128)(2,1)} %far_key.1, bf16[4,512]{1,0:T(4,128)(2,1)} %far_value.1, bf16[4,6144]{1,0:T(4,128)(2,1)} %refs_3_.3, f32[1,6144]{1,0:T(1,128)} %bitcast.5), custom_call_target="tpu_custom_call" | custom-call | bytes 100000 | tf_op jit(solution)/shard_map/pack/pallas_call | solution.py:61
  4.1 0.6 %collective-permute-start.3 = (bf16[192,128]{1,0:T(8,128)(2,1)S(1)}, bf16[192,128]{1,0:T(8,128)(2,1)S(1)}, u32[]{:S(2)}, u32[]{:S(2)}) collective-permute-start(bf16[192,128]{1,0:T(8,128)(2,1)S(1)} %widen.1), channel_id=1, source_target_pairs={{0,2},{2,0},{4,6},{6,4},{8,10},{10,8},{12,14},{14,12},{1,3},{3,1},... | collective-permute-start | bytes 147464 | tf_op jit(solution)/shard_map/ppermute | solution.py:28
  4.7 1.0 %shares.1.share.share_ref = f32[32,128]{1,0:T(8,128)S(1)} custom-call(s32[2,32]{1,0:T(2,128)} %bitcast.6, f32[2,32]{1,0:T(2,128)} %bitcast.7, bf16[128,128]{1,0:T(8,128)(2,1)S(1)} %get-tuple-element.18.refs_0_.heads.own_ref.own_heads, bf16[1,6144,1024]{2,1,0:T(8,128)(2,1)} %gate_ref.1, bf16[1,6144,1024]{2,1,0:T(8,128)(2,1)} %up_ref.1), custom_call_target="tpu_custom_call" | custom-call | bytes 100000 | tf_op jit(solution)/shard_map/shares/pallas_call | solution.py:61
  5.7 0.0 collective-permute-done.got_ref
  5.7 0.2 norm_both.1.own_ref
  5.9 4.0 %collective-permute-start.1 = (bf16[8,3072]{1,0:T(8,128)(2,1)S(1)}, bf16[8,3072]{1,0:T(8,128)(2,1)S(1)}, u32[]{:S(2)}, u32[]{:S(2)}) collective-permute-start(bf16[8,3072]{1,0:T(8,128)(2,1)S(1)} %norm_both.1.own_ref), channel_id=1, source_target_pairs={{0,13},{1,12},{2,15},{3,14},{4,9},{5,8},{6,11},{7,10},{8,5},{9,4},... | collective-permute-start | bytes 147464 | tf_op jit(solution)/shard_map/ppermute | solution.py:33
  9.9 0.0 collective-permute-start.2
  9.9 0.6 %collective-permute-start.4 = (bf16[8,3072]{1,0:T(8,128)(2,1)S(1)}, bf16[8,3072]{1,0:T(8,128)(2,1)S(1)}, u32[]{:S(2)}, u32[]{:S(2)}) collective-permute-start(bf16[8,3072]{1,0:T(8,128)(2,1)S(1)} %norm_both.1.own_ref), channel_id=1, source_target_pairs={{0,4},{2,6},{4,0},{6,2},{8,12},{10,14},{12,8},{14,10},{1,5},{3,7},... | collective-permute-start | bytes 147464 | tf_op jit(solution)/shard_map/ppermute | solution.py:28
  10.5 0.0 collective-permute-done.3.got_heads
  10.5 1.5 %collective-permute-done.1.last_ref = bf16[8,3072]{1,0:T(8,128)(2,1)S(1)} collective-permute-done((bf16[8,3072]{1,0:T(8,128)(2,1)S(1)}, bf16[8,3072]{1,0:T(8,128)(2,1)S(1)}, u32[]{:S(2)}, u32[]{:S(2)}) %collective-permute-start.1) | collective-permute-done | bytes 49184 | tf_op jit(solution)/shard_map/ppermute | solution.py:33
  12.1 2.5 %collective-permute-done.2.far_ref = bf16[8,3072]{1,0:T(8,128)(2,1)S(1)} collective-permute-done((bf16[8,3072]{1,0:T(8,128)(2,1)S(1)}, bf16[8,3072]{1,0:T(8,128)(2,1)S(1)}, u32[]{:S(2)}, u32[]{:S(2)}) %collective-permute-start.2) | collective-permute-done | bytes 49184 | tf_op jit(solution)/shard_map/ppermute | solution.py:33
  14.6 0.0 collective-permute-done.4.next_ref
  14.6 0.1 stack_line.1
  14.7 0.3 collective-permute-start.6
  15.0 2.2 %collective-permute-start.5 = (bf16[256,128]{1,0:T(8,128)(2,1)S(1)}, bf16[256,128]{1,0:T(8,128)(2,1)S(1)}, u32[]{:S(2)}, u32[]{:S(2)}) collective-permute-start(bf16[256,128]{1,0:T(8,128)(2,1)S(1)} %get-tuple-element.19.own_ref), channel_id=1, source_target_pairs={{0,8},{2,10},{4,12},{6,14},{8,0},{10,2},{12,4},{14,6},{1,9},{3,11}... | collective-permute-start | bytes 196616 | tf_op jit(solution)/shard_map/ppermute | solution.py:28
  17.1 0.0 collective-permute-done.6.other_ref
  17.1 0.0 slice-done
  17.1 0.0 slice-done.1
  17.1 0.0 slice-done.2
  17.2 0.0 copy-done
  17.2 4.8 %gate_all.1 = (bf16[32,1024]{1,0:T(8,128)(2,1)S(1)}, bf16[1024,3072]{1,0:T(8,128)(2,1)S(1)}, bf16[1024,3072]{1,0:T(8,128)(2,1)S(1)}) custom-call(bf16[32,3072]{1,0:T(8,128)(2,1)S(1)} %get-tuple-element.20.x_ref, bf16[32,3072]{1,0:T(8,128)(2,1)S(1)} %collective-permute-done.6.other_ref, bf16[1,6144,1024]{2,1,0:T(8,128)(2,1)S(1)} %bitcast.4, ...), custom_call_target="tpu_custom_call" | custom-call | flops 805306368 | bytes 37748736 | tf_op jit(solution)/shard_map/gate_all/pallas_call | solution.py:61
  22.0 0.0 collective-permute-done.5.got_ref
  22.0 0.0 copy-start.1
  22.0 0.0 copy-start.2
  22.0 0.0 copy-start.4
  22.0 0.0 copy-start.5
  22.1 1.3 %down.2.after = bf16[32,3072]{1,0:T(8,128)(2,1)S(1)} custom-call(bf16[32,1024]{1,0:T(8,128)(2,1)S(1)} %get-tuple-element.21.after.hidden_ref, bf16[1024,3072]{1,0:T(8,128)(2,1)S(1)} %get-tuple-element.23.down_ref, bf16[512,128]{1,0:T(8,128)(2,1)S(1)} %stack_after.1.after.near_ref.refs_0_), custom_call_target="tpu_custom_call" | custom-call | flops 201326592 | bytes 6291456 | tf_op jit(solution)/shard_map/down/pallas_call | solution.py:61
  23.4 0.2 collective-permute-start.8
  23.5 0.9 %collective-permute-start.7 = (bf16[512,128]{1,0:T(8,128)(2,1)S(1)}, bf16[512,128]{1,0:T(8,128)(2,1)S(1)}, u32[]{:S(2)}, u32[]{:S(2)}) collective-permute-start(bf16[512,128]{1,0:T(8,128)(2,1)S(1)} %stack_after.1.after.near_ref.refs_0_), channel_id=1, source_target_pairs={{0,4},{2,6},{4,0},{6,2},{8,12},{10,14},{12,8},{14,10},{1,5},{3,7},... | collective-permute-start | bytes 393224 | tf_op jit(solution)/shard_map/ppermute | solution.py:28
  24.5 1.3 %down.3.terms_ref = f32[32,3072]{1,0:T(8,128)S(1)} custom-call(bf16[32,1024]{1,0:T(8,128)(2,1)S(1)} %get-tuple-element.21.after.hidden_ref, bf16[1024,3072]{1,0:T(8,128)(2,1)S(1)} %get-tuple-element.22.down_ref, bf16[32,3072]{1,0:T(8,128)(2,1)S(1)} %down.2.after), custom_call_target="tpu_custom_call" | custom-call | flops 201326592 | bytes 6291456 | tf_op jit(solution)/shard_map/down/pallas_call | solution.py:61
  25.8 0.0 collective-permute-done.8.taken_ref
  25.8 1.3 %collective-permute-start.9 = (bf16[16,3072]{1,0:T(8,128)(2,1)S(1)}, bf16[16,3072]{1,0:T(8,128)(2,1)S(1)}, u32[]{:S(2)}, u32[]{:S(2)}) collective-permute-start(bf16[16,3072]{1,0:T(8,128)(2,1)S(1)} %get-tuple-element.25.after), channel_id=1, source_target_pairs={{0,3},{1,2},{2,1},{3,0},{4,7},{5,6},{6,5},{7,4},{8,11},{9,10},{10,... | collective-permute-start | bytes 294920 | tf_op jit(solution)/shard_map/ppermute | solution.py:33
  27.1 2.1 %collective-permute-done.7.far_ref.refs_1_ = bf16[512,128]{1,0:T(8,128)(2,1)S(1)} collective-permute-done((bf16[512,128]{1,0:T(8,128)(2,1)S(1)}, bf16[512,128]{1,0:T(8,128)(2,1)S(1)}, u32[]{:S(2)}, u32[]{:S(2)}) %collective-permute-start.7) | collective-permute-done | bytes 131104 | tf_op jit(solution)/shard_map/ppermute | solution.py:28
  29.3 0.0 copy-done.1
  29.3 0.0 copy-done.2
  29.3 1.7 %attend.1.after.refs_7_ = f32[48,128]{1,0:T(8,128)S(1)} custom-call(bf16[512,128]{1,0:T(8,128)(2,1)S(1)} %stack_after.1.after.near_ref.refs_0_, bf16[512,128]{1,0:T(8,128)(2,1)S(1)} %collective-permute-done.7.far_ref.refs_1_, bf16[4,512,512]{2,1,0:T(8,128)(2,1)S(1)} %copy-done.1, bf16[4,512,512]{2,1,0:T(8,128)(2,1)S(1)} %copy-done.2, s32[4]{0:T(128)S(1)} %copy-done.4, ...), custom_call_target="tpu_custom_call" | custom-call | flops 12582912 | bytes 2097152 | tf_op jit(solution)/shard_map/attend/pallas_call | solution.py:61
  31.0 0.0 collective-permute-done.9.taken_ref
  31.0 1.6 %collective-permute-start.10 = (bf16[4,3072]{1,0:T(4,128)(2,1)S(1)}, bf16[4,3072]{1,0:T(4,128)(2,1)S(1)}, u32[]{:S(2)}, u32[]{:S(2)}) collective-permute-start(bf16[4,3072]{1,0:T(4,128)(2,1)S(1)} %get-tuple-element.28), channel_id=1, source_target_pairs={{0,13},{1,12},{2,15},{3,14},{4,9},{5,8},{6,11},{7,10},{8,5},{9,4},... | collective-permute-start | bytes 73736 | tf_op jit(solution)/shard_map/ppermute | solution.py:33
  32.6 0.6 %collective-permute-start.11 = (bf16[4,3072]{1,0:T(4,128)(2,1)S(1)}, bf16[4,3072]{1,0:T(4,128)(2,1)S(1)}, u32[]{:S(2)}, u32[]{:S(2)}) collective-permute-start(bf16[4,3072]{1,0:T(4,128)(2,1)S(1)} %get-tuple-element.26.refs_6_), channel_id=1, source_target_pairs={{0,9},{1,8},{2,11},{3,10},{4,13},{5,12},{6,15},{7,14},{8,1},{9,0},... | collective-permute-start | bytes 73736 | tf_op jit(solution)/shard_map/ppermute | solution.py:33
  33.2 2.0 %collective-permute-start.12 = (bf16[4,3072]{1,0:T(4,128)(2,1)S(1)}, bf16[4,3072]{1,0:T(4,128)(2,1)S(1)}, u32[]{:S(2)}, u32[]{:S(2)}) collective-permute-start(bf16[4,3072]{1,0:T(4,128)(2,1)S(1)} %get-tuple-element.29), channel_id=1, source_target_pairs={{0,4},{2,6},{4,0},{6,2},{8,12},{10,14},{12,8},{14,10},{1,5},{3,7},... | collective-permute-start | bytes 73736 | tf_op jit(solution)/shard_map/ppermute | solution.py:28
  35.2 2.3 %attend_last.1.refs_4_ = bf16[4,3072]{1,0:T(4,128)(2,1)} custom-call(bf16[512,128]{1,0:T(8,128)(2,1)S(1)} %stack_after.1.after.near_ref.refs_0_, bf16[512,128]{1,0:T(8,128)(2,1)S(1)} %collective-permute-done.7.far_ref.refs_1_, bf16[4,512,512]{2,1,0:T(8,128)(2,1)S(1)} %copy-done.1, bf16[4,512,512]{2,1,0:T(8,128)(2,1)S(1)} %copy-done.2, s32[4]{0:T(128)S(1)} %copy-done.4, ...), custom_call_target="tpu_custom_call" | custom-call | flops 12582912 | bytes 2097152 | tf_op jit(solution)/shard_map/attend_last/pallas_call | solution.py:61
  37.5 0.0 collective-permute-done.10.refs_0_
  37.5 0.0 collective-permute-done.11.refs_1_
  37.5 0.0 collective-permute-done.12.refs_2_
  37.6 0.1 collective-permute-start.13
  37.7 1.1 %collective-permute-done.13.other_ref = bf16[4,3072]{1,0:T(4,128)(2,1)S(1)} collective-permute-done((bf16[4,3072]{1,0:T(4,128)(2,1)S(1)}, bf16[4,3072]{1,0:T(4,128)(2,1)S(1)}, u32[]{:S(2)}, u32[]{:S(2)}) %collective-permute-start.13) | collective-permute-done | bytes 24608 | tf_op jit(solution)/shard_map/ppermute | solution.py:28
  38.9 0.6 %join.1 = bf16[4,6144]{1,0:T(4,128)(2,1)} custom-call(bf16[4,3072]{1,0:T(4,128)(2,1)S(1)} %finish.1.own_ref, bf16[4,3072]{1,0:T(4,128)(2,1)S(1)} %collective-permute-done.13.other_ref), custom_call_target="tpu_custom_call" | custom-call | bytes 49152 | tf_op jit(solution)/shard_map/join/pallas_call | solution.py:61
  (14 shorter events, 0.2 us)
Async XLA Ops:
  0.6 5.1 %collective-permute-start = (bf16[4,6144]{1,0:T(4,128)(2,1)}, bf16[4,6144]{1,0:T(4,128)(2,1)S(1)}, u32[]{:S(2)}, u32[]{:S(2)}) collective-permute-start(bf16[4,6144]{1,0:T(4,128)(2,1)} %refs_3_.3), channel_id=1, source_target_pairs={{0,3},{1,2},{2,1},{3,0},{4,7},{5,6},{6,5},{7,4},{8,11},{9,10},{10,... | collective-permute-start | bytes 147464 | tf_op jit(solution)/shard_map/ppermute | solution.py:33
  4.1 6.4 %collective-permute-start.3 = (bf16[192,128]{1,0:T(8,128)(2,1)S(1)}, bf16[192,128]{1,0:T(8,128)(2,1)S(1)}, u32[]{:S(2)}, u32[]{:S(2)}) collective-permute-start(bf16[192,128]{1,0:T(8,128)(2,1)S(1)} %widen.1), channel_id=1, source_target_pairs={{0,2},{2,0},{4,6},{6,4},{8,10},{10,8},{12,14},{14,12},{1,3},{3,1},... | collective-permute-start | bytes 147464 | tf_op jit(solution)/shard_map/ppermute | solution.py:28
  4.7 12.4 %slice-start = ((s8[12582912]{0:T(1024)(128)(4,1)}), s8[4194304]{0:T(1024)(128)(4,1)S(1)}, s32[]{:S(2)}) async-start(s8[12582912]{0:T(1024)(128)(4,1)} %bitcast.3), calls=%async_computation | async-start | bytes 8388608
  4.7 12.4 %slice-start.1 = ((s8[12582912]{0:T(1024)(128)(4,1)}), s8[4194304]{0:T(1024)(128)(4,1)S(1)}, s32[]{:S(2)}) async-start(s8[12582912]{0:T(1024)(128)(4,1)} %bitcast.3), calls=%async_computation.1 | async-start | bytes 8388608
  4.7 12.4 %slice-start.2 = ((s8[12582912]{0:T(1024)(128)(4,1)}), s8[4194304]{0:T(1024)(128)(4,1)S(1)}, s32[]{:S(2)}) async-start(s8[12582912]{0:T(1024)(128)(4,1)} %bitcast.3), calls=%async_computation.2 | async-start | bytes 8388608
  4.7 12.4 %copy-start = (bf16[1,6144,1024]{2,1,0:T(8,128)(2,1)S(1)}, bf16[1,6144,1024]{2,1,0:T(8,128)(2,1)}, u32[]{:S(2)}) copy-start(bf16[1,6144,1024]{2,1,0:T(8,128)(2,1)} %up_ref.1) | copy-start | bytes 37748740
  5.9 6.2 %collective-permute-start.1 = (bf16[8,3072]{1,0:T(8,128)(2,1)S(1)}, bf16[8,3072]{1,0:T(8,128)(2,1)S(1)}, u32[]{:S(2)}, u32[]{:S(2)}) collective-permute-start(bf16[8,3072]{1,0:T(8,128)(2,1)S(1)} %norm_both.1.own_ref), channel_id=1, source_target_pairs={{0,13},{1,12},{2,15},{3,14},{4,9},{5,8},{6,11},{7,10},{8,5},{9,4},... | collective-permute-start | bytes 147464 | tf_op jit(solution)/shard_map/ppermute | solution.py:33
  9.9 4.7 %collective-permute-start.2 = (bf16[8,3072]{1,0:T(8,128)(2,1)S(1)}, bf16[8,3072]{1,0:T(8,128)(2,1)S(1)}, u32[]{:S(2)}, u32[]{:S(2)}) collective-permute-start(bf16[8,3072]{1,0:T(8,128)(2,1)S(1)} %norm_both.1.own_ref), channel_id=1, source_target_pairs={{0,9},{1,8},{2,11},{3,10},{4,13},{5,12},{6,15},{7,14},{8,1},{9,0},... | collective-permute-start | bytes 147464 | tf_op jit(solution)/shard_map/ppermute | solution.py:33
  9.9 4.7 %collective-permute-start.4 = (bf16[8,3072]{1,0:T(8,128)(2,1)S(1)}, bf16[8,3072]{1,0:T(8,128)(2,1)S(1)}, u32[]{:S(2)}, u32[]{:S(2)}) collective-permute-start(bf16[8,3072]{1,0:T(8,128)(2,1)S(1)} %norm_both.1.own_ref), channel_id=1, source_target_pairs={{0,4},{2,6},{4,0},{6,2},{8,12},{10,14},{12,8},{14,10},{1,5},{3,7},... | collective-permute-start | bytes 147464 | tf_op jit(solution)/shard_map/ppermute | solution.py:28
  14.7 2.5 %collective-permute-start.6 = (bf16[32,3072]{1,0:T(8,128)(2,1)S(1)}, bf16[32,3072]{1,0:T(8,128)(2,1)S(1)}, u32[]{:S(2)}, u32[]{:S(2)}) collective-permute-start(bf16[32,3072]{1,0:T(8,128)(2,1)S(1)} %get-tuple-element.20.x_ref), channel_id=1, source_target_pairs={{0,1},{1,0},{2,3},{3,2},{4,5},{5,4},{6,7},{7,6},{8,9},{9,8},{10,11... | collective-permute-start | bytes 589832 | tf_op jit(solution)/shard_map/ppermute | solution.py:28
  15.0 7.0 %collective-permute-start.5 = (bf16[256,128]{1,0:T(8,128)(2,1)S(1)}, bf16[256,128]{1,0:T(8,128)(2,1)S(1)}, u32[]{:S(2)}, u32[]{:S(2)}) collective-permute-start(bf16[256,128]{1,0:T(8,128)(2,1)S(1)} %get-tuple-element.19.own_ref), channel_id=1, source_target_pairs={{0,8},{2,10},{4,12},{6,14},{8,0},{10,2},{12,4},{14,6},{1,9},{3,11}... | collective-permute-start | bytes 196616 | tf_op jit(solution)/shard_map/ppermute | solution.py:28
  22.0 7.3 %copy-start.1 = (bf16[4,512,512]{2,1,0:T(8,128)(2,1)S(1)}, bf16[4,512,512]{2,1,0:T(8,128)(2,1)}, u32[]{:S(2)}) copy-start(bf16[4,512,512]{2,1,0:T(8,128)(2,1)} %refs_2_.3) | copy-start | bytes 6291460
  22.0 7.3 %copy-start.2 = (bf16[4,512,512]{2,1,0:T(8,128)(2,1)S(1)}, bf16[4,512,512]{2,1,0:T(8,128)(2,1)}, u32[]{:S(2)}) copy-start(bf16[4,512,512]{2,1,0:T(8,128)(2,1)} %refs_3_.2) | copy-start | bytes 6291460
  22.0 7.3 %copy-start.4 = (s32[4]{0:T(128)S(1)}, s32[4]{0:T(128)}, u32[]{:S(2)}) copy-start(s32[4]{0:T(128)} %refs_4_.1) | copy-start | bytes 52
  22.0 7.2 %copy-start.5 = (s32[4]{0:T(128)S(1)}, s32[4]{0:T(128)}, u32[]{:S(2)}) copy-start(s32[4]{0:T(128)} %refs_5_.1) | copy-start | bytes 52
  23.4 2.4 %collective-permute-start.8 = (bf16[32,3072]{1,0:T(8,128)(2,1)S(1)}, bf16[32,3072]{1,0:T(8,128)(2,1)S(1)}, u32[]{:S(2)}, u32[]{:S(2)}) collective-permute-start(bf16[32,3072]{1,0:T(8,128)(2,1)S(1)} %down.2.after), channel_id=1, source_target_pairs={{0,1},{1,0},{2,3},{3,2},{4,5},{5,4},{6,7},{7,6},{8,9},{9,8},{10,11... | collective-permute-start | bytes 589832 | tf_op jit(solution)/shard_map/ppermute | solution.py:28
  23.5 5.7 %collective-permute-start.7 = (bf16[512,128]{1,0:T(8,128)(2,1)S(1)}, bf16[512,128]{1,0:T(8,128)(2,1)S(1)}, u32[]{:S(2)}, u32[]{:S(2)}) collective-permute-start(bf16[512,128]{1,0:T(8,128)(2,1)S(1)} %stack_after.1.after.near_ref.refs_0_), channel_id=1, source_target_pairs={{0,4},{2,6},{4,0},{6,2},{8,12},{10,14},{12,8},{14,10},{1,5},{3,7},... | collective-permute-start | bytes 393224 | tf_op jit(solution)/shard_map/ppermute | solution.py:28
  25.8 11.8 %copy-start.3 = (bf16[4,6144]{1,0:T(4,128)(2,1)S(1)}, bf16[4,6144]{1,0:T(4,128)(2,1)}, u32[]{:S(2)}) copy-start(bf16[4,6144]{1,0:T(4,128)(2,1)} %refs_3_.3) | copy-start | bytes 147460
  25.8 5.2 %collective-permute-start.9 = (bf16[16,3072]{1,0:T(8,128)(2,1)S(1)}, bf16[16,3072]{1,0:T(8,128)(2,1)S(1)}, u32[]{:S(2)}, u32[]{:S(2)}) collective-permute-start(bf16[16,3072]{1,0:T(8,128)(2,1)S(1)} %get-tuple-element.25.after), channel_id=1, source_target_pairs={{0,3},{1,2},{2,1},{3,0},{4,7},{5,6},{6,5},{7,4},{8,11},{9,10},{10,... | collective-permute-start | bytes 294920 | tf_op jit(solution)/shard_map/ppermute | solution.py:33
  31.0 6.5 %collective-permute-start.10 = (bf16[4,3072]{1,0:T(4,128)(2,1)S(1)}, bf16[4,3072]{1,0:T(4,128)(2,1)S(1)}, u32[]{:S(2)}, u32[]{:S(2)}) collective-permute-start(bf16[4,3072]{1,0:T(4,128)(2,1)S(1)} %get-tuple-element.28), channel_id=1, source_target_pairs={{0,13},{1,12},{2,15},{3,14},{4,9},{5,8},{6,11},{7,10},{8,5},{9,4},... | collective-permute-start | bytes 73736 | tf_op jit(solution)/shard_map/ppermute | solution.py:33
  32.6 4.9 %collective-permute-start.11 = (bf16[4,3072]{1,0:T(4,128)(2,1)S(1)}, bf16[4,3072]{1,0:T(4,128)(2,1)S(1)}, u32[]{:S(2)}, u32[]{:S(2)}) collective-permute-start(bf16[4,3072]{1,0:T(4,128)(2,1)S(1)} %get-tuple-element.26.refs_6_), channel_id=1, source_target_pairs={{0,9},{1,8},{2,11},{3,10},{4,13},{5,12},{6,15},{7,14},{8,1},{9,0},... | collective-permute-start | bytes 73736 | tf_op jit(solution)/shard_map/ppermute | solution.py:33
  33.2 4.3 %collective-permute-start.12 = (bf16[4,3072]{1,0:T(4,128)(2,1)S(1)}, bf16[4,3072]{1,0:T(4,128)(2,1)S(1)}, u32[]{:S(2)}, u32[]{:S(2)}) collective-permute-start(bf16[4,3072]{1,0:T(4,128)(2,1)S(1)} %get-tuple-element.29), channel_id=1, source_target_pairs={{0,4},{2,6},{4,0},{6,2},{8,12},{10,14},{12,8},{14,10},{1,5},{3,7},... | collective-permute-start | bytes 73736 | tf_op jit(solution)/shard_map/ppermute | solution.py:28
  37.6 1.3 %collective-permute-start.13 = (bf16[4,3072]{1,0:T(4,128)(2,1)S(1)}, bf16[4,3072]{1,0:T(4,128)(2,1)S(1)}, u32[]{:S(2)}, u32[]{:S(2)}) collective-permute-start(bf16[4,3072]{1,0:T(4,128)(2,1)S(1)} %finish.1.own_ref), channel_id=1, source_target_pairs={{0,1},{1,0},{2,3},{3,2},{4,5},{5,4},{6,7},{7,6},{8,9},{9,8},{10,11... | collective-permute-start | bytes 73736 | tf_op jit(solution)/shard_map/ppermute | solution.py:28

commit v16 on v14

--- a/solution.py
+++ b/solution.py
@@ -92,12 +92,13 @@
     return pltpu.with_memory_space_constraint(array, pltpu.HBM)
 
 
-def pack(far_query, far_key, far_value, far_tokens, far_gain, heads_ref, *held):
-    tokens_ref, gain_ref, *near_refs, packed, sems = held
-    far_refs = (far_query, far_key, far_value, far_tokens, far_gain)
+def pack(far_query, far_key, far_value, far_tokens, far_gain, far_place, heads_ref, *held):
+    *row_refs, query_ref, key_ref, value_ref, packed, sems = held
+    near_refs = (query_ref, key_ref, value_ref)
+    far_refs = (far_query, far_key, far_value, far_tokens, far_gain, far_place)
     copies = [
         pltpu.make_async_copy(far, ref, sems.at[i])
-        for i, (far, ref) in enumerate(zip(far_refs, (*near_refs, tokens_ref, gain_ref)))
+        for i, (far, ref) in enumerate(zip(far_refs, (*near_refs, *row_refs)))
     ]
     for copy in copies:
         copy.start()
@@ -130,12 +131,58 @@
     refs[-1][...] = stacked(refs[:-1]).astype(refs[-1].dtype)
 
 
-def stack_line(own_ref, last_ref, far_ref, got_heads, next_ref, own_heads, out_ref, heads_ref):
-    count = own_heads.shape[0]
-    heads_ref[:count, :] = own_heads[...]
-    heads_ref[count:, :] = got_heads[:count, :]
-    rows = [own_ref, far_ref, next_ref, last_ref]
+def tag(rows_ref, place_ref, out_ref):
+    count, half = rows_ref.shape
+    slots = place_ref.shape[1]
+    out_ref[:, :half] = rows_ref[...]
+    out_ref[:, half:] = jnp.zeros((count, HD), jnp.bfloat16)
+    names = jnp.broadcast_to(place_ref[...].astype(jnp.float32), (count, slots))
+    out_ref[:, half : half + slots] = names.astype(jnp.bfloat16)
+
+
+def halve(own_ref, got_ref, out_ref, first_ref, second_ref):
+    count = own_ref.shape[0]
+    out_ref[:count, :] = own_ref[...]
+    out_ref[count:, :] = got_ref[:count, :]
+    first_ref[...] = own_ref[...]
+    second_ref[...] = got_ref[:count, :]
+
+
+def stack_line(
+    steps,
+    each,
+    own_ref,
+    next_ref,
+    far_ref,
+    last_ref,
+    first_ref,
+    second_ref,
+    own_heads,
+    out_ref,
+    heads_ref,
+    asked_ref,
+):
+    half = out_ref.shape[1]
+    rows = [own_ref, far_ref.at[:, :half], next_ref, last_ref]
     out_ref[...] = stacked(rows).astype(jnp.bfloat16)
+    count = first_ref.shape[0]
+    heads_ref[: 2 * count, :] = own_heads[...]
+    heads_ref[2 * count : 3 * count, :] = first_ref[...]
+    heads_ref[3 * count :, :] = second_ref[...]
+    me = lax.axis_index("wide")
+    slots = asked_ref.shape[0] // each
+    shift = int(math.log2(slots))
+    names = far_ref[:, half : half + HD].astype(jnp.float32)
+    found = [jnp.zeros((each, HD), jnp.float32)] * slots
+    for at in range(heads_ref.shape[0] // each):
+        name = (owner_of(at >> shift, me, steps) << shift) | (at & (slots - 1))
+        name = name.astype(jnp.float32)
+        block = heads_ref[at * each : (at + 1) * each, :].astype(jnp.float32)
+        for slot in range(slots):
+            asked = names[0:1, slot : slot + 1] == name
+            found[slot] = jnp.where(asked, block, found[slot])
+    for slot in range(slots):
+        asked_ref[slot * each : (slot + 1) * each, :] = found[slot].astype(jnp.bfloat16)
 
 
 def widen(own_ref, out_ref):
@@ -245,7 +292,7 @@
     sent_ref[...] = total[kept:].astype(jnp.bfloat16)
 
 
-def finish(flip, kept_ref, taken_ref, other_kept, other_taken, tokens_ref, after, out_ref):
+def finish(flip, kept_ref, other_kept, other_taken, taken_ref, tokens_ref, after, out_ref):
     half = kept_ref.shape[1]
     first = side_of(flip) == 0
     own = kept_ref[...].astype(jnp.float32) + taken_ref[...].astype(jnp.float32)
@@ -281,8 +328,9 @@
         request = place_ref[slot]
         at = (place_of(request >> shift, me, steps) << shift) | (request & (rows - 1))
         at = at * each
-        inside = pl.ds(pl.multiple_of(jnp.where(at < half, at, at - half), each), each)
-        block = jnp.where(at < half, near_ref[inside, :], far_ref[inside, :])
+        inside = pl.ds(pl.multiple_of(jnp.where(at < half, at, 0), each), each)
+        far = far_ref[slot * each : (slot + 1) * each, :]
+        block = jnp.where(at < half, near_ref[inside, :], far)
         query = block[:heads]
         own = block[heads:].astype(jnp.float32)
         own_key = by_group([own[g : g + 1] for g in range(kv_local)])
@@ -338,7 +386,7 @@
 
 def make_local(wide):
     steps = steps_of(wide)
-    head_steps = [*steps[1:-2], *steps[:1], *steps[-2:]]
+    head_steps = [*steps[1:-2], steps[0], steps[-1], steps[-2]]
 
     def local(
         queries,
@@ -369,15 +417,15 @@
 
         got = cross(tokens, wide, steps[0])
         heads_in = [queries, new_keys, new_values]
-        row_in = [tokens, norm_gain[None]]
+        row_in = [tokens, norm_gain[None], assignment[None]]
         heads, *row_near = call(
             pack,
             [shape((rows * each, HD), bf16)] + [pltpu.VMEM(a.shape, a.dtype) for a in row_in],
             [distant(a) for a in heads_in + row_in],
             [pltpu.VMEM(a.shape, a.dtype) for a in heads_in]
-            + [pltpu.VMEM((rows * each, HD), f32), dma((5,))],
+            + [pltpu.VMEM((rows * each, HD), f32), dma((6,))],
             size=100000,
-            far=range(5),
+            far=range(6),
         )
         share = call(
             functools.partial(shares, steps, rows),
@@ -416,17 +464,32 @@
             )
         line_steps = [steps[-2], steps[-1], steps[-2] ^ steps[-1]]
         last = cross(x, wide, line_steps[2])
-        line = [cross(x, wide, line_steps[0]), swap(x, "wide", wide, line_steps[1])]
+        tagged = call(
+            tag, shape((x.shape[0], half + HD), bf16), [x, near(row_near[2])], size=4 * x.size
+        )
+        line = [cross(tagged, wide, line_steps[0]), swap(x, "wide", wide, line_steps[1])]
         wider = max(x.shape[0] * half // HD, heads.shape[0])
         sent_heads = call(widen, shape((wider, HD), bf16), [heads], size=4 * wider * HD)
         far_rows = swap(sent_heads, "wide", wide, steps[0])
-        x, heads = call(
-            stack_line,
-            [shape((count, half), bf16), shape((2 * heads.shape[0], HD), bf16)],
-            [x, last, line[0], far_rows, line[1], heads],
+        part = shape(heads.shape, bf16)
+        heads, *parts = call(
+            halve,
+            [shape((2 * heads.shape[0], HD), bf16), part, part],
+            [heads, far_rows],
+            size=8 * heads.size,
+        )
+        parts = [swap(part, "wide", wide, line_steps[1]) for part in parts]
+        x, heads, asked = call(
+            functools.partial(stack_line, head_steps[:-1], each),
+            [
+                shape((count, half), bf16),
+                shape((2 * heads.shape[0], HD), bf16),
+                shape((rows * each, HD), bf16),
+            ],
+            [x, line[1], line[0], last, *parts, heads],
             size=8 * count * half,
         )
-        got_heads = swap(heads, "wide", wide, steps[-2])
+        far_heads = swap(asked, "wide", wide, steps[-2])
 
         product = 2 * count * half * units
         other_x = swap(x, "narrow", 2, 1)
@@ -447,23 +510,15 @@
             size=6 * piece_bytes,
             far=(5,),
         )
-        heads = call(
-            stack_after,
-            shape((2 * heads.shape[0], HD), bf16),
-            [heads, got_heads, hidden],
-            size=8 * heads.size,
-            far=(2,),
-        )
         given = call(
             down,
             shape((count, half), bf16),
-            [hidden, near(down_other), heads],
+            [hidden, near(down_other), far_heads],
             flops=product,
             size=piece_bytes,
             far=(2,),
         )
         taken = swap(given, "narrow", 2, 1)
-        far_heads = swap(heads, "wide", wide, steps[-1])
         terms = call(
             down,
             shape((count, half), f32),
@@ -486,14 +541,14 @@
             size=terms.size * 8,
         )
         taken = [
+            cross(sent[0], wide, line_steps[0]),
             swap(sent[1], "wide", wide, line_steps[1]),
             cross(sent[2], wide, line_steps[2]),
-            cross(sent[0], wide, line_steps[0]),
         ]
         early = call(
             functools.partial(attend, head_steps, early_slots),
             shape((len(early_slots) * heads_local, HD), f32),
-            [heads, far_heads, *caches, sent[0]],
+            [heads, far_heads, *caches, sent[1]],
             flops=2 * key_cache.size * GROUP,
             size=2 * key_cache.size,
             smem=(4, 5),
@@ -512,7 +567,7 @@
         context = call(
             functools.partial(attend_last, head_steps, late_slots, heads_local),
             shape(queries.shape, bf16),
-            [heads, far_heads, *caches, sent, early],
+            [heads, far_heads, *caches, terms, early],
             [
                 pltpu.VMEM((len(late_slots) * heads_local, HD), f32),
                 pltpu.VMEM((slots * heads_local, HD), f32),
@@ -527,7 +582,7 @@
         mixed_out = call(
             functools.partial(finish, steps[-2]),
             shape((rows, width), bf16),
-            [terms, *taken, other_kept, other_taken, tokens, distant(context)],
+            [terms, other_kept, other_taken, *taken, tokens, distant(context)],
             size=terms.size * 8,
             far=(5,),
         )

time: 39.6 us -> 40.8 us (1.030)
  waiting for transfers between devices: 6.54 us -> 7.15 us
    ppermute x9 -> x10, waiting for transfers between devices: 0.03 us -> 5.44 us  [swap(): return lax.ppermute(block, axis, [(i, i ^ step) for i in range(count)])]
    ppermute x6, waiting for transfers between devices: 6.51 us -> 1.72 us  [cross(): return lax.ppermute(block, ('wide', 'narrow'), pairs)]
    ppermute x6, starting transfers between devices: 9.38 us -> 11.2 us  [cross(): return lax.ppermute(block, ('wide', 'narrow'), pairs)]
    ppermute x9 -> x10, starting transfers between devices: 8.32 us -> 6.98 us  [swap(): return lax.ppermute(block, axis, [(i, i ^ step) for i in range(count)])]
    pallas_call x14 -> x15, Pallas kernels: 14.2 us -> 14.4 us  [call(): pl.pallas_call(kernel, name=getattr(kernel, 'func', kernel).__name__, out...]
  transfers between devices with their start and end apart: 15 -> 16, of which waited for: 4 -> 5; matrix products, arithmetic and copies ran while one was open for 0% -> 0% of each run, Pallas kernels for 31% -> 30%
where the time goes in v16:
time: 40.8 us; the launch traced here: 40.6 us
  starting transfers between devices  18.1 us (44%)
  Pallas kernels  14.4 us (35%)
  waiting for transfers between devices  7.15 us (18%)
  between operations  0.84 us (2%)
    pallas_call x15, Pallas kernels, call(): pl.pallas_call(kernel, name=getattr(kernel, 'func', kernel).__name__, out...  14.4 us
    ppermute x6, starting transfers between devices, cross(): return lax.ppermute(block, ('wide', 'narrow'), pairs)  11.2 us
    ppermute x10, starting transfers between devices, swap(): return lax.ppermute(block, axis, [(i, i ^ step) for i in range(count)])  6.98 us
    ppermute x10, waiting for transfers between devices, swap(): return lax.ppermute(block, axis, [(i, i ^ step) for i in range(count)])  5.44 us
    ppermute x6, waiting for transfers between devices, cross(): return lax.ppermute(block, ('wide', 'narrow'), pairs)  1.72 us
  transfers between devices with their start and end apart: 16, of which 5 were waited for; matrix products, arithmetic and copies ran while one was open for 0% of the time, Pallas kernels for 30%

profile of v16, /device:TPU:0, one launch (start us, length us, event | category | flops | bytes accessed | tf_op | source)
XLA Modules:
  0.0 40.6 jit_solution(5798458512581361293)
XLA Ops:
  0.6 2.5 %collective-permute-start = (bf16[4,6144]{1,0:T(4,128)(2,1)}, bf16[4,6144]{1,0:T(4,128)(2,1)S(1)}, u32[]{:S(2)}, u32[]{:S(2)}) collective-permute-start(bf16[4,6144]{1,0:T(4,128)(2,1)} %tokens_ref.1), channel_id=1, source_target_pairs={{0,3},{1,2},{2,1},{3,0},{4,7},{5,6},{6,5},{7,4},{8,11},{9,10},{10,... | collective-permute-start | bytes 147464 | tf_op jit(solution)/shard_map/ppermute | solution.py:33
  3.1 1.0 %pack.1 = (bf16[128,128]{1,0:T(8,128)(2,1)S(1)}, bf16[4,6144]{1,0:T(4,128)(2,1)S(1)}, f32[1,6144]{1,0:T(1,128)S(1)}, s32[1,4]{1,0:T(1,128)S(1)}) custom-call(bf16[4,3072]{1,0:T(4,128)(2,1)} %far_query.1, bf16[4,512]{1,0:T(4,128)(2,1)} %far_key.1, bf16[4,512]{1,0:T(4,128)(2,1)} %far_value.1, bf16[4,6144]{1,0:T(4,128)(2,1)} %tokens_ref.1, f32[1,6144]{1,0:T(1,128)} %bitcast.7, ...), custom_call_target="tpu_custom_call" | custom-call | bytes 100000 | tf_op jit(solution)/shard_map/pack/pallas_call | solution.py:59
  4.1 0.6 %collective-permute-start.4 = (bf16[192,128]{1,0:T(8,128)(2,1)S(1)}, bf16[192,128]{1,0:T(8,128)(2,1)S(1)}, u32[]{:S(2)}, u32[]{:S(2)}) collective-permute-start(bf16[192,128]{1,0:T(8,128)(2,1)S(1)} %widen.1), channel_id=1, source_target_pairs={{0,2},{2,0},{4,6},{6,4},{8,10},{10,8},{12,14},{14,12},{1,3},{3,1},... | collective-permute-start | bytes 147464 | tf_op jit(solution)/shard_map/ppermute | solution.py:28
  4.7 1.0 %shares.1.share.share_ref = f32[32,128]{1,0:T(8,128)S(1)} custom-call(s32[2,32]{1,0:T(2,128)} %bitcast.8, f32[2,32]{1,0:T(2,128)} %bitcast.9, bf16[128,128]{1,0:T(8,128)(2,1)S(1)} %get-tuple-element.23.refs_0_.heads.own_ref, bf16[1,6144,1024]{2,1,0:T(8,128)(2,1)} %gate_ref.1, bf16[1,6144,1024]{2,1,0:T(8,128)(2,1)} %up_ref.1), custom_call_target="tpu_custom_call" | custom-call | bytes 100000 | tf_op jit(solution)/shard_map/shares/pallas_call | solution.py:59
  5.7 0.0 collective-permute-done.got_ref
  5.7 0.2 norm_both.1.rows_ref.own_ref
  5.9 3.0 %collective-permute-start.2 = (bf16[8,3200]{1,0:T(8,128)(2,1)S(1)}, bf16[8,3200]{1,0:T(8,128)(2,1)S(1)}, u32[]{:S(2)}, u32[]{:S(2)}) collective-permute-start(bf16[8,3200]{1,0:T(8,128)(2,1)S(1)} %tag.1), channel_id=1, source_target_pairs={{0,9},{1,8},{2,11},{3,10},{4,13},{5,12},{6,15},{7,14},{8,1},{9,0},... | collective-permute-start | bytes 153608 | tf_op jit(solution)/shard_map/ppermute | solution.py:33
  8.9 1.3 %collective-permute-start.3 = (bf16[8,3072]{1,0:T(8,128)(2,1)S(1)}, bf16[8,3072]{1,0:T(8,128)(2,1)S(1)}, u32[]{:S(2)}, u32[]{:S(2)}) collective-permute-start(bf16[8,3072]{1,0:T(8,128)(2,1)S(1)} %norm_both.1.rows_ref.own_ref), channel_id=1, source_target_pairs={{0,13},{1,12},{2,15},{3,14},{4,9},{5,8},{6,11},{7,10},{8,5},{9,4},... | collective-permute-start | bytes 147464 | tf_op jit(solution)/shard_map/ppermute | solution.py:33
  10.2 0.2 collective-permute-start.1
  10.5 0.0 collective-permute-done.4.got_ref
  10.5 1.9 %collective-permute-start.5 = (bf16[128,128]{1,0:T(8,128)(2,1)S(1)}, bf16[128,128]{1,0:T(8,128)(2,1)S(1)}, u32[]{:S(2)}, u32[]{:S(2)}) collective-permute-start(bf16[128,128]{1,0:T(8,128)(2,1)S(1)} %get-tuple-element.25), channel_id=1, source_target_pairs={{0,4},{2,6},{4,0},{6,2},{8,12},{10,14},{12,8},{14,10},{1,5},{3,7},... | collective-permute-start | bytes 98312 | tf_op jit(solution)/shard_map/ppermute | solution.py:28
  12.3 0.2 collective-permute-start.6
  12.6 3.6 %collective-permute-done.5.first_ref = bf16[128,128]{1,0:T(8,128)(2,1)S(1)} collective-permute-done((bf16[128,128]{1,0:T(8,128)(2,1)S(1)}, bf16[128,128]{1,0:T(8,128)(2,1)S(1)}, u32[]{:S(2)}, u32[]{:S(2)}) %collective-permute-start.5) | collective-permute-done | bytes 32800 | tf_op jit(solution)/shard_map/ppermute | solution.py:28
  16.1 0.4 collective-permute-done.6.second_ref
  16.5 0.0 collective-permute-done.3.last_ref
  16.5 0.0 collective-permute-done.1.next_ref
  16.5 0.0 collective-permute-done.2.far_ref
  16.5 0.2 stack_line.1
  16.7 0.1 collective-permute-start.8
  16.8 1.6 %collective-permute-start.7 = (bf16[128,128]{1,0:T(8,128)(2,1)S(1)}, bf16[128,128]{1,0:T(8,128)(2,1)S(1)}, u32[]{:S(2)}, u32[]{:S(2)}) collective-permute-start(bf16[128,128]{1,0:T(8,128)(2,1)S(1)} %get-tuple-element.29), channel_id=1, source_target_pairs={{0,8},{2,10},{4,12},{6,14},{8,0},{10,2},{12,4},{14,6},{1,9},{3,11}... | collective-permute-start | bytes 98312 | tf_op jit(solution)/shard_map/ppermute | solution.py:28
  18.3 0.0 collective-permute-done.8.other_ref
  18.3 0.0 slice-done
  18.4 4.8 %gate_all.1 = (bf16[32,1024]{1,0:T(8,128)(2,1)S(1)}, bf16[1024,3072]{1,0:T(8,128)(2,1)S(1)}, bf16[1024,3072]{1,0:T(8,128)(2,1)S(1)}) custom-call(bf16[32,3072]{1,0:T(8,128)(2,1)S(1)} %get-tuple-element.30.x_ref, bf16[32,3072]{1,0:T(8,128)(2,1)S(1)} %collective-permute-done.8.other_ref, bf16[1,6144,1024]{2,1,0:T(8,128)(2,1)S(1)} %bitcast.5, ...), custom_call_target="tpu_custom_call" | custom-call | flops 805306368 | bytes 37748736 | tf_op jit(solution)/shard_map/gate_all/pallas_call | solution.py:59
  23.2 0.0 collective-permute-done.7.after.far_ref.refs_1_
  23.2 0.0 copy-start.1
  23.2 0.0 copy-start.2
  23.2 0.0 copy-start.4
  23.2 0.0 copy-start.5
  23.2 1.3 %down.2.after = bf16[32,3072]{1,0:T(8,128)(2,1)S(1)} custom-call(bf16[32,1024]{1,0:T(8,128)(2,1)S(1)} %get-tuple-element.31.hidden_ref, bf16[1024,3072]{1,0:T(8,128)(2,1)S(1)} %get-tuple-element.33.down_ref, bf16[128,128]{1,0:T(8,128)(2,1)S(1)} %collective-permute-done.7.after.far_ref.refs_1_), custom_call_target="tpu_custom_call" | custom-call | flops 201326592 | bytes 6291456 | tf_op jit(solution)/shard_map/down/pallas_call | solution.py:59
  24.5 0.2 collective-permute-start.9
  24.7 1.3 %down.3.terms_ref = f32[32,3072]{1,0:T(8,128)S(1)} custom-call(bf16[32,1024]{1,0:T(8,128)(2,1)S(1)} %get-tuple-element.31.hidden_ref, bf16[1024,3072]{1,0:T(8,128)(2,1)S(1)} %get-tuple-element.32.down_ref, bf16[32,3072]{1,0:T(8,128)(2,1)S(1)} %down.2.after), custom_call_target="tpu_custom_call" | custom-call | flops 201326592 | bytes 6291456 | tf_op jit(solution)/shard_map/down/pallas_call | solution.py:59
  26.0 0.0 collective-permute-done.9.taken_ref
  26.1 1.4 %collective-permute-start.10 = (bf16[8,3072]{1,0:T(8,128)(2,1)S(1)}, bf16[8,3072]{1,0:T(8,128)(2,1)S(1)}, u32[]{:S(2)}, u32[]{:S(2)}) collective-permute-start(bf16[8,3072]{1,0:T(8,128)(2,1)S(1)} %get-tuple-element.35), channel_id=1, source_target_pairs={{0,9},{1,8},{2,11},{3,10},{4,13},{5,12},{6,15},{7,14},{8,1},{9,0},... | collective-permute-start | bytes 147464 | tf_op jit(solution)/shard_map/ppermute | solution.py:33
  27.5 2.9 %collective-permute-start.12 = (bf16[8,3072]{1,0:T(8,128)(2,1)S(1)}, bf16[8,3072]{1,0:T(8,128)(2,1)S(1)}, u32[]{:S(2)}, u32[]{:S(2)}) collective-permute-start(bf16[8,3072]{1,0:T(8,128)(2,1)S(1)} %get-tuple-element.37), channel_id=1, source_target_pairs={{0,13},{1,12},{2,15},{3,14},{4,9},{5,8},{6,11},{7,10},{8,5},{9,4},... | collective-permute-start | bytes 147464 | tf_op jit(solution)/shard_map/ppermute | solution.py:33
  30.4 0.0 collective-permute-start.11
  30.4 0.0 copy-done.1
  30.5 2.2 %attend.1.refs_4_.refs_7_ = f32[72,128]{1,0:T(8,128)S(1)} custom-call(bf16[512,128]{1,0:T(8,128)(2,1)S(1)} %get-tuple-element.28.near_ref.refs_0_, bf16[128,128]{1,0:T(8,128)(2,1)S(1)} %collective-permute-done.7.after.far_ref.refs_1_, bf16[4,512,512]{2,1,0:T(8,128)(2,1)S(1)} %copy-done.1, bf16[4,512,512]{2,1,0:T(8,128)(2,1)S(1)} %copy-done.2, ...), custom_call_target="tpu_custom_call" | custom-call | flops 12582912 | bytes 2097152 | tf_op jit(solution)/shard_map/attend/pallas_call | solution.py:59
  32.7 0.0 collective-permute-done.10.refs_1_
  32.7 0.8 %collective-permute-done.12.refs_3_ = bf16[8,3072]{1,0:T(8,128)(2,1)S(1)} collective-permute-done((bf16[8,3072]{1,0:T(8,128)(2,1)S(1)}, bf16[8,3072]{1,0:T(8,128)(2,1)S(1)}, u32[]{:S(2)}, u32[]{:S(2)}) %collective-permute-start.12) | collective-permute-done | bytes 49184 | tf_op jit(solution)/shard_map/ppermute | solution.py:33
  33.4 1.5 %collective-permute-done.11.refs_2_ = bf16[8,3072]{1,0:T(8,128)(2,1)S(1)} collective-permute-done((bf16[8,3072]{1,0:T(8,128)(2,1)S(1)}, bf16[8,3072]{1,0:T(8,128)(2,1)S(1)}, u32[]{:S(2)}, u32[]{:S(2)}) %collective-permute-start.11) | collective-permute-done | bytes 49184 | tf_op jit(solution)/shard_map/ppermute | solution.py:28
  35.0 1.6 %collective-permute-start.15 = (bf16[4,3072]{1,0:T(4,128)(2,1)S(1)}, bf16[4,3072]{1,0:T(4,128)(2,1)S(1)}, u32[]{:S(2)}, u32[]{:S(2)}) collective-permute-start(bf16[4,3072]{1,0:T(4,128)(2,1)S(1)} %get-tuple-element.39), channel_id=1, source_target_pairs={{0,2},{2,0},{4,6},{6,4},{8,10},{10,8},{12,14},{14,12},{1,3},{3,1},... | collective-permute-start | bytes 73736 | tf_op jit(solution)/shard_map/ppermute | solution.py:28
  36.6 0.0 collective-permute-start.14
  36.6 0.6 %collective-permute-start.13 = (bf16[4,3072]{1,0:T(4,128)(2,1)S(1)}, bf16[4,3072]{1,0:T(4,128)(2,1)S(1)}, u32[]{:S(2)}, u32[]{:S(2)}) collective-permute-start(bf16[4,3072]{1,0:T(4,128)(2,1)S(1)} %get-tuple-element.38.refs_6_.kept_ref), channel_id=1, source_target_pairs={{0,1},{1,0},{2,3},{3,2},{4,5},{5,4},{6,7},{7,6},{8,9},{9,8},{10,11... | collective-permute-start | bytes 73736 | tf_op jit(solution)/shard_map/ppermute | solution.py:28
  37.2 1.8 %attend_last.1.after = bf16[4,3072]{1,0:T(4,128)(2,1)} custom-call(bf16[512,128]{1,0:T(8,128)(2,1)S(1)} %get-tuple-element.28.near_ref.refs_0_, bf16[128,128]{1,0:T(8,128)(2,1)S(1)} %collective-permute-done.7.after.far_ref.refs_1_, bf16[4,512,512]{2,1,0:T(8,128)(2,1)S(1)} %copy-done.1, bf16[4,512,512]{2,1,0:T(8,128)(2,1)S(1)} %copy-done.2, s32[4]{0:T(128)S(1)} %copy-done.5, ...), custom_call_target="tpu_custom_call" | custom-call | flops 12582912 | bytes 2097152 | tf_op jit(solution)/shard_map/attend_last/pallas_call | solution.py:59
  39.0 0.0 collective-permute-done.15.taken_ref
  39.0 0.9 %collective-permute-done.14.other_taken = bf16[4,3072]{1,0:T(4,128)(2,1)S(1)} collective-permute-done((bf16[4,3072]{1,0:T(4,128)(2,1)S(1)}, bf16[4,3072]{1,0:T(4,128)(2,1)S(1)}, u32[]{:S(2)}, u32[]{:S(2)}) %collective-permute-start.14) | collective-permute-done | bytes 24608 | tf_op jit(solution)/shard_map/ppermute | solution.py:33
  39.9 0.0 collective-permute-done.13.other_kept
  39.9 0.7 %finish.1 = bf16[4,6144]{1,0:T(4,128)(2,1)} custom-call(bf16[4,3072]{1,0:T(4,128)(2,1)S(1)} %get-tuple-element.38.refs_6_.kept_ref, bf16[4,3072]{1,0:T(4,128)(2,1)S(1)} %collective-permute-done.13.other_kept, bf16[4,3072]{1,0:T(4,128)(2,1)S(1)} %collective-permute-done.14.other_taken, bf16[4,3072]{1,0:T(4,128)(2,1)S(1)} %collective-permute-done.15.taken_ref, ...), custom_call_target="tpu_custom_call" | custom-call | bytes 98304 | tf_op jit(solution)/shard_map/finish/pallas_call | solution.py:59
  (18 shorter events, 0.1 us)
Async XLA Ops:
  0.6 5.1 %collective-permute-start = (bf16[4,6144]{1,0:T(4,128)(2,1)}, bf16[4,6144]{1,0:T(4,128)(2,1)S(1)}, u32[]{:S(2)}, u32[]{:S(2)}) collective-permute-start(bf16[4,6144]{1,0:T(4,128)(2,1)} %tokens_ref.1), channel_id=1, source_target_pairs={{0,3},{1,2},{2,1},{3,0},{4,7},{5,6},{6,5},{7,4},{8,11},{9,10},{10,... | collective-permute-start | bytes 147464 | tf_op jit(solution)/shard_map/ppermute | solution.py:33
  4.1 6.4 %collective-permute-start.4 = (bf16[192,128]{1,0:T(8,128)(2,1)S(1)}, bf16[192,128]{1,0:T(8,128)(2,1)S(1)}, u32[]{:S(2)}, u32[]{:S(2)}) collective-permute-start(bf16[192,128]{1,0:T(8,128)(2,1)S(1)} %widen.1), channel_id=1, source_target_pairs={{0,2},{2,0},{4,6},{6,4},{8,10},{10,8},{12,14},{14,12},{1,3},{3,1},... | collective-permute-start | bytes 147464 | tf_op jit(solution)/shard_map/ppermute | solution.py:28
  4.7 13.6 %slice-start = ((s8[12582912]{0:T(1024)(128)(4,1)}), s8[4194304]{0:T(1024)(128)(4,1)S(1)}, s32[]{:S(2)}) async-start(s8[12582912]{0:T(1024)(128)(4,1)} %bitcast.4), calls=%async_computation | async-start | bytes 8388608
  4.7 13.6 %slice-start.1 = ((s8[12582912]{0:T(1024)(128)(4,1)}), s8[4194304]{0:T(1024)(128)(4,1)S(1)}, s32[]{:S(2)}) async-start(s8[12582912]{0:T(1024)(128)(4,1)} %bitcast.4), calls=%async_computation.1 | async-start | bytes 8388608
  4.7 13.6 %slice-start.2 = ((s8[12582912]{0:T(1024)(128)(4,1)}), s8[4194304]{0:T(1024)(128)(4,1)S(1)}, s32[]{:S(2)}) async-start(s8[12582912]{0:T(1024)(128)(4,1)} %bitcast.4), calls=%async_computation.2 | async-start | bytes 8388608
  4.7 13.6 %copy-start = (bf16[1,6144,1024]{2,1,0:T(8,128)(2,1)S(1)}, bf16[1,6144,1024]{2,1,0:T(8,128)(2,1)}, u32[]{:S(2)}) copy-start(bf16[1,6144,1024]{2,1,0:T(8,128)(2,1)} %up_ref.1) | copy-start | bytes 37748740
  5.9 10.6 %collective-permute-start.2 = (bf16[8,3200]{1,0:T(8,128)(2,1)S(1)}, bf16[8,3200]{1,0:T(8,128)(2,1)S(1)}, u32[]{:S(2)}, u32[]{:S(2)}) collective-permute-start(bf16[8,3200]{1,0:T(8,128)(2,1)S(1)} %tag.1), channel_id=1, source_target_pairs={{0,9},{1,8},{2,11},{3,10},{4,13},{5,12},{6,15},{7,14},{8,1},{9,0},... | collective-permute-start | bytes 153608 | tf_op jit(solution)/shard_map/ppermute | solution.py:33
  8.9 7.6 %collective-permute-start.3 = (bf16[8,3072]{1,0:T(8,128)(2,1)S(1)}, bf16[8,3072]{1,0:T(8,128)(2,1)S(1)}, u32[]{:S(2)}, u32[]{:S(2)}) collective-permute-start(bf16[8,3072]{1,0:T(8,128)(2,1)S(1)} %norm_both.1.rows_ref.own_ref), channel_id=1, source_target_pairs={{0,13},{1,12},{2,15},{3,14},{4,9},{5,8},{6,11},{7,10},{8,5},{9,4},... | collective-permute-start | bytes 147464 | tf_op jit(solution)/shard_map/ppermute | solution.py:33
  10.2 6.3 %collective-permute-start.1 = (bf16[8,3072]{1,0:T(8,128)(2,1)S(1)}, bf16[8,3072]{1,0:T(8,128)(2,1)S(1)}, u32[]{:S(2)}, u32[]{:S(2)}) collective-permute-start(bf16[8,3072]{1,0:T(8,128)(2,1)S(1)} %norm_both.1.rows_ref.own_ref), channel_id=1, source_target_pairs={{0,4},{2,6},{4,0},{6,2},{8,12},{10,14},{12,8},{14,10},{1,5},{3,7},... | collective-permute-start | bytes 147464 | tf_op jit(solution)/shard_map/ppermute | solution.py:28
  10.5 5.6 %collective-permute-start.5 = (bf16[128,128]{1,0:T(8,128)(2,1)S(1)}, bf16[128,128]{1,0:T(8,128)(2,1)S(1)}, u32[]{:S(2)}, u32[]{:S(2)}) collective-permute-start(bf16[128,128]{1,0:T(8,128)(2,1)S(1)} %get-tuple-element.25), channel_id=1, source_target_pairs={{0,4},{2,6},{4,0},{6,2},{8,12},{10,14},{12,8},{14,10},{1,5},{3,7},... | collective-permute-start | bytes 98312 | tf_op jit(solution)/shard_map/ppermute | solution.py:28
  12.3 4.1 %collective-permute-start.6 = (bf16[128,128]{1,0:T(8,128)(2,1)S(1)}, bf16[128,128]{1,0:T(8,128)(2,1)S(1)}, u32[]{:S(2)}, u32[]{:S(2)}) collective-permute-start(bf16[128,128]{1,0:T(8,128)(2,1)S(1)} %get-tuple-element.26), channel_id=1, source_target_pairs={{0,4},{2,6},{4,0},{6,2},{8,12},{10,14},{12,8},{14,10},{1,5},{3,7},... | collective-permute-start | bytes 98312 | tf_op jit(solution)/shard_map/ppermute | solution.py:28
  16.7 1.6 %collective-permute-start.8 = (bf16[32,3072]{1,0:T(8,128)(2,1)S(1)}, bf16[32,3072]{1,0:T(8,128)(2,1)S(1)}, u32[]{:S(2)}, u32[]{:S(2)}) collective-permute-start(bf16[32,3072]{1,0:T(8,128)(2,1)S(1)} %get-tuple-element.30.x_ref), channel_id=1, source_target_pairs={{0,1},{1,0},{2,3},{3,2},{4,5},{5,4},{6,7},{7,6},{8,9},{9,8},{10,11... | collective-permute-start | bytes 589832 | tf_op jit(solution)/shard_map/ppermute | solution.py:28
  16.8 6.4 %collective-permute-start.7 = (bf16[128,128]{1,0:T(8,128)(2,1)S(1)}, bf16[128,128]{1,0:T(8,128)(2,1)S(1)}, u32[]{:S(2)}, u32[]{:S(2)}) collective-permute-start(bf16[128,128]{1,0:T(8,128)(2,1)S(1)} %get-tuple-element.29), channel_id=1, source_target_pairs={{0,8},{2,10},{4,12},{6,14},{8,0},{10,2},{12,4},{14,6},{1,9},{3,11}... | collective-permute-start | bytes 98312 | tf_op jit(solution)/shard_map/ppermute | solution.py:28
  23.2 7.3 %copy-start.1 = (bf16[4,512,512]{2,1,0:T(8,128)(2,1)S(1)}, bf16[4,512,512]{2,1,0:T(8,128)(2,1)}, u32[]{:S(2)}) copy-start(bf16[4,512,512]{2,1,0:T(8,128)(2,1)} %refs_2_.3) | copy-start | bytes 6291460
  23.2 7.3 %copy-start.2 = (bf16[4,512,512]{2,1,0:T(8,128)(2,1)S(1)}, bf16[4,512,512]{2,1,0:T(8,128)(2,1)}, u32[]{:S(2)}) copy-start(bf16[4,512,512]{2,1,0:T(8,128)(2,1)} %refs_3_.1) | copy-start | bytes 6291460
  23.2 7.3 %copy-start.4 = (s32[4]{0:T(128)S(1)}, s32[4]{0:T(128)}, u32[]{:S(2)}) copy-start(s32[4]{0:T(128)} %refs_5_.1) | copy-start | bytes 52
  23.2 7.3 %copy-start.5 = (s32[4]{0:T(128)S(1)}, s32[4]{0:T(128)}, u32[]{:S(2)}) copy-start(s32[4]{0:T(128)} %refs_4_.1) | copy-start | bytes 52
  24.5 1.5 %collective-permute-start.9 = (bf16[32,3072]{1,0:T(8,128)(2,1)S(1)}, bf16[32,3072]{1,0:T(8,128)(2,1)S(1)}, u32[]{:S(2)}, u32[]{:S(2)}) collective-permute-start(bf16[32,3072]{1,0:T(8,128)(2,1)S(1)} %down.2.after), channel_id=1, source_target_pairs={{0,1},{1,0},{2,3},{3,2},{4,5},{5,4},{6,7},{7,6},{8,9},{9,8},{10,11... | collective-permute-start | bytes 589832 | tf_op jit(solution)/shard_map/ppermute | solution.py:28
  26.0 13.9 %copy-start.3 = (bf16[4,6144]{1,0:T(4,128)(2,1)S(1)}, bf16[4,6144]{1,0:T(4,128)(2,1)}, u32[]{:S(2)}) copy-start(bf16[4,6144]{1,0:T(4,128)(2,1)} %tokens_ref.1) | copy-start | bytes 147460
  26.1 6.6 %collective-permute-start.10 = (bf16[8,3072]{1,0:T(8,128)(2,1)S(1)}, bf16[8,3072]{1,0:T(8,128)(2,1)S(1)}, u32[]{:S(2)}, u32[]{:S(2)}) collective-permute-start(bf16[8,3072]{1,0:T(8,128)(2,1)S(1)} %get-tuple-element.35), channel_id=1, source_target_pairs={{0,9},{1,8},{2,11},{3,10},{4,13},{5,12},{6,15},{7,14},{8,1},{9,0},... | collective-permute-start | bytes 147464 | tf_op jit(solution)/shard_map/ppermute | solution.py:33
  27.5 5.9 %collective-permute-start.12 = (bf16[8,3072]{1,0:T(8,128)(2,1)S(1)}, bf16[8,3072]{1,0:T(8,128)(2,1)S(1)}, u32[]{:S(2)}, u32[]{:S(2)}) collective-permute-start(bf16[8,3072]{1,0:T(8,128)(2,1)S(1)} %get-tuple-element.37), channel_id=1, source_target_pairs={{0,13},{1,12},{2,15},{3,14},{4,9},{5,8},{6,11},{7,10},{8,5},{9,4},... | collective-permute-start | bytes 147464 | tf_op jit(solution)/shard_map/ppermute | solution.py:33
  30.4 4.5 %collective-permute-start.11 = (bf16[8,3072]{1,0:T(8,128)(2,1)S(1)}, bf16[8,3072]{1,0:T(8,128)(2,1)S(1)}, u32[]{:S(2)}, u32[]{:S(2)}) collective-permute-start(bf16[8,3072]{1,0:T(8,128)(2,1)S(1)} %get-tuple-element.36.after), channel_id=1, source_target_pairs={{0,4},{2,6},{4,0},{6,2},{8,12},{10,14},{12,8},{14,10},{1,5},{3,7},... | collective-permute-start | bytes 147464 | tf_op jit(solution)/shard_map/ppermute | solution.py:28
  35.0 4.0 %collective-permute-start.15 = (bf16[4,3072]{1,0:T(4,128)(2,1)S(1)}, bf16[4,3072]{1,0:T(4,128)(2,1)S(1)}, u32[]{:S(2)}, u32[]{:S(2)}) collective-permute-start(bf16[4,3072]{1,0:T(4,128)(2,1)S(1)} %get-tuple-element.39), channel_id=1, source_target_pairs={{0,2},{2,0},{4,6},{6,4},{8,10},{10,8},{12,14},{14,12},{1,3},{3,1},... | collective-permute-start | bytes 73736 | tf_op jit(solution)/shard_map/ppermute | solution.py:28
  36.6 3.3 %collective-permute-start.14 = (bf16[4,3072]{1,0:T(4,128)(2,1)S(1)}, bf16[4,3072]{1,0:T(4,128)(2,1)S(1)}, u32[]{:S(2)}, u32[]{:S(2)}) collective-permute-start(bf16[4,3072]{1,0:T(4,128)(2,1)S(1)} %get-tuple-element.39), channel_id=1, source_target_pairs={{0,3},{1,2},{2,1},{3,0},{4,7},{5,6},{6,5},{7,4},{8,11},{9,10},{10,... | collective-permute-start | bytes 73736 | tf_op jit(solution)/shard_map/ppermute | solution.py:33
  36.6 3.3 %collective-permute-start.13 = (bf16[4,3072]{1,0:T(4,128)(2,1)S(1)}, bf16[4,3072]{1,0:T(4,128)(2,1)S(1)}, u32[]{:S(2)}, u32[]{:S(2)}) collective-permute-start(bf16[4,3072]{1,0:T(4,128)(2,1)S(1)} %get-tuple-element.38.refs_6_.kept_ref), channel_id=1, source_target_pairs={{0,1},{1,0},{2,3},{3,2},{4,5},{5,4},{6,7},{7,6},{8,9},{9,8},{10,11... | collective-permute-start | bytes 73736 | tf_op jit(solution)/shard_map/ppermute | solution.py:28

commit v17 on v14

--- a/solution.py
+++ b/solution.py
@@ -138,7 +138,7 @@
     out_ref[...] = stacked(rows).astype(jnp.bfloat16)
 
 
-def widen(own_ref, out_ref):
+def widen(own_ref, share, out_ref):
     count = own_ref.shape[0]
     out_ref[:count, :] = own_ref[...]
     out_ref[count:, :] = jnp.zeros((out_ref.shape[0] - count, HD), out_ref.dtype)
@@ -245,7 +245,7 @@
     sent_ref[...] = total[kept:].astype(jnp.bfloat16)
 
 
-def finish(flip, kept_ref, taken_ref, other_kept, other_taken, tokens_ref, after, out_ref):
+def finish(flip, kept_ref, taken_ref, other_taken, other_kept, tokens_ref, after, out_ref):
     half = kept_ref.shape[1]
     first = side_of(flip) == 0
     own = kept_ref[...].astype(jnp.float32) + taken_ref[...].astype(jnp.float32)
@@ -418,7 +418,9 @@
         last = cross(x, wide, line_steps[2])
         line = [cross(x, wide, line_steps[0]), swap(x, "wide", wide, line_steps[1])]
         wider = max(x.shape[0] * half // HD, heads.shape[0])
-        sent_heads = call(widen, shape((wider, HD), bf16), [heads], size=4 * wider * HD)
+        sent_heads = call(
+            widen, shape((wider, HD), bf16), [heads, share], size=4 * wider * HD, far=(1,)
+        )
         far_rows = swap(sent_heads, "wide", wide, steps[0])
         x, heads = call(
             stack_line,
@@ -512,7 +514,7 @@
         context = call(
             functools.partial(attend_last, head_steps, late_slots, heads_local),
             shape(queries.shape, bf16),
-            [heads, far_heads, *caches, sent, early],
+            [heads, far_heads, *caches, terms, early],
             [
                 pltpu.VMEM((len(late_slots) * heads_local, HD), f32),
                 pltpu.VMEM((slots * heads_local, HD), f32),
@@ -527,7 +529,7 @@
         mixed_out = call(
             functools.partial(finish, steps[-2]),
             shape((rows, width), bf16),
-            [terms, *taken, other_kept, other_taken, tokens, distant(context)],
+            [terms, *taken, other_taken, other_kept, tokens, distant(context)],
             size=terms.size * 8,
             far=(5,),
         )

time: 39.6 us -> 39.8 us (level)
    ppermute x6, starting transfers between devices: 9.38 us -> 8.79 us  [cross(): return lax.ppermute(block, ('wide', 'narrow'), pairs)]
    ppermute x9, starting transfers between devices: 8.32 us -> 8.88 us  [swap(): return lax.ppermute(block, axis, [(i, i ^ step) for i in range(count)])]
where the time goes in v17:
time: 39.8 us; the launch traced here: 39.6 us
  starting transfers between devices  17.7 us (44%)
  Pallas kernels  14.2 us (36%)
  waiting for transfers between devices  6.78 us (17%)
  between operations  0.85 us (2%)
    pallas_call x14, Pallas kernels, call(): pl.pallas_call(kernel, name=getattr(kernel, 'func', kernel).__name__, out...  14.2 us
    ppermute x9, starting transfers between devices, swap(): return lax.ppermute(block, axis, [(i, i ^ step) for i in range(count)])  8.88 us
    ppermute x6, starting transfers between devices, cross(): return lax.ppermute(block, ('wide', 'narrow'), pairs)  8.79 us
    ppermute x6, waiting for transfers between devices, cross(): return lax.ppermute(block, ('wide', 'narrow'), pairs)  6.75 us
  transfers between devices with their start and end apart: 15, of which 4 were waited for; matrix products, arithmetic and copies ran while one was open for 0% of the time, Pallas kernels for 31%

profile of v17, /device:TPU:0, one launch (start us, length us, event | category | flops | bytes accessed | tf_op | source)
XLA Modules:
  0.0 39.6 jit_solution(15476138503520614728)
XLA Ops:
  0.6 2.5 %collective-permute-start = (bf16[4,6144]{1,0:T(4,128)(2,1)}, bf16[4,6144]{1,0:T(4,128)(2,1)S(1)}, u32[]{:S(2)}, u32[]{:S(2)}) collective-permute-start(bf16[4,6144]{1,0:T(4,128)(2,1)} %tokens_ref.1), channel_id=1, source_target_pairs={{0,3},{1,2},{2,1},{3,0},{4,7},{5,6},{6,5},{7,4},{8,11},{9,10},{10,... | collective-permute-start | bytes 147464 | tf_op jit(solution)/shard_map/ppermute | solution.py:33
  3.1 1.0 %pack.1 = (bf16[128,128]{1,0:T(8,128)(2,1)S(1)}, bf16[4,6144]{1,0:T(4,128)(2,1)S(1)}, f32[1,6144]{1,0:T(1,128)S(1)}) custom-call(bf16[4,3072]{1,0:T(4,128)(2,1)} %far_query.1, bf16[4,512]{1,0:T(4,128)(2,1)} %far_key.1, bf16[4,512]{1,0:T(4,128)(2,1)} %far_value.1, bf16[4,6144]{1,0:T(4,128)(2,1)} %tokens_ref.1, f32[1,6144]{1,0:T(1,128)} %bitcast.5), custom_call_target="tpu_custom_call" | custom-call | bytes 100000 | tf_op jit(solution)/shard_map/pack/pallas_call | solution.py:59
  4.1 0.0 slice-start
  4.1 0.0 slice-start.1
  4.1 0.0 slice-start.2
  4.1 0.0 copy-start
  4.1 1.0 %shares.1.share.share_ref = f32[32,128]{1,0:T(8,128)S(1)} custom-call(s32[2,32]{1,0:T(2,128)} %bitcast.6, f32[2,32]{1,0:T(2,128)} %bitcast.7, bf16[128,128]{1,0:T(8,128)(2,1)S(1)} %get-tuple-element.18.refs_0_.heads.own_ref.own_heads, bf16[1,6144,1024]{2,1,0:T(8,128)(2,1)} %gate_ref.1, bf16[1,6144,1024]{2,1,0:T(8,128)(2,1)} %up_ref.1), custom_call_target="tpu_custom_call" | custom-call | bytes 100000 | tf_op jit(solution)/shard_map/shares/pallas_call | solution.py:59
  5.1 0.6 %collective-permute-start.3 = (bf16[192,128]{1,0:T(8,128)(2,1)S(1)}, bf16[192,128]{1,0:T(8,128)(2,1)S(1)}, u32[]{:S(2)}, u32[]{:S(2)}) collective-permute-start(bf16[192,128]{1,0:T(8,128)(2,1)S(1)} %widen.1), channel_id=1, source_target_pairs={{0,2},{2,0},{4,6},{6,4},{8,10},{10,8},{12,14},{14,12},{1,3},{3,1},... | collective-permute-start | bytes 147464 | tf_op jit(solution)/shard_map/ppermute | solution.py:28
  5.7 0.0 collective-permute-done.got_ref
  5.7 0.2 norm_both.1.own_ref
  5.9 4.0 %collective-permute-start.1 = (bf16[8,3072]{1,0:T(8,128)(2,1)S(1)}, bf16[8,3072]{1,0:T(8,128)(2,1)S(1)}, u32[]{:S(2)}, u32[]{:S(2)}) collective-permute-start(bf16[8,3072]{1,0:T(8,128)(2,1)S(1)} %norm_both.1.own_ref), channel_id=1, source_target_pairs={{0,13},{1,12},{2,15},{3,14},{4,9},{5,8},{6,11},{7,10},{8,5},{9,4},... | collective-permute-start | bytes 147464 | tf_op jit(solution)/shard_map/ppermute | solution.py:33
  9.9 0.0 collective-permute-start.2
  9.9 0.6 %collective-permute-start.4 = (bf16[8,3072]{1,0:T(8,128)(2,1)S(1)}, bf16[8,3072]{1,0:T(8,128)(2,1)S(1)}, u32[]{:S(2)}, u32[]{:S(2)}) collective-permute-start(bf16[8,3072]{1,0:T(8,128)(2,1)S(1)} %norm_both.1.own_ref), channel_id=1, source_target_pairs={{0,4},{2,6},{4,0},{6,2},{8,12},{10,14},{12,8},{14,10},{1,5},{3,7},... | collective-permute-start | bytes 147464 | tf_op jit(solution)/shard_map/ppermute | solution.py:28
  10.5 0.0 collective-permute-done.3.got_heads
  10.5 1.5 %collective-permute-done.1.last_ref = bf16[8,3072]{1,0:T(8,128)(2,1)S(1)} collective-permute-done((bf16[8,3072]{1,0:T(8,128)(2,1)S(1)}, bf16[8,3072]{1,0:T(8,128)(2,1)S(1)}, u32[]{:S(2)}, u32[]{:S(2)}) %collective-permute-start.1) | collective-permute-done | bytes 49184 | tf_op jit(solution)/shard_map/ppermute | solution.py:33
  12.1 2.5 %collective-permute-done.2.far_ref = bf16[8,3072]{1,0:T(8,128)(2,1)S(1)} collective-permute-done((bf16[8,3072]{1,0:T(8,128)(2,1)S(1)}, bf16[8,3072]{1,0:T(8,128)(2,1)S(1)}, u32[]{:S(2)}, u32[]{:S(2)}) %collective-permute-start.2) | collective-permute-done | bytes 49184 | tf_op jit(solution)/shard_map/ppermute | solution.py:33
  14.6 0.0 collective-permute-done.4.next_ref
  14.6 0.3 collective-permute-start.6
  14.9 2.2 %collective-permute-start.5 = (bf16[256,128]{1,0:T(8,128)(2,1)S(1)}, bf16[256,128]{1,0:T(8,128)(2,1)S(1)}, u32[]{:S(2)}, u32[]{:S(2)}) collective-permute-start(bf16[256,128]{1,0:T(8,128)(2,1)S(1)} %get-tuple-element.19.own_ref), channel_id=1, source_target_pairs={{0,8},{2,10},{4,12},{6,14},{8,0},{10,2},{12,4},{14,6},{1,9},{3,11}... | collective-permute-start | bytes 196616 | tf_op jit(solution)/shard_map/ppermute | solution.py:28
  17.1 0.0 collective-permute-done.6.other_ref
  17.1 0.0 slice-done
  17.1 4.8 %gate_all.1 = (bf16[32,1024]{1,0:T(8,128)(2,1)S(1)}, bf16[1024,3072]{1,0:T(8,128)(2,1)S(1)}, bf16[1024,3072]{1,0:T(8,128)(2,1)S(1)}) custom-call(bf16[32,3072]{1,0:T(8,128)(2,1)S(1)} %get-tuple-element.20.x_ref, bf16[32,3072]{1,0:T(8,128)(2,1)S(1)} %collective-permute-done.6.other_ref, bf16[1,6144,1024]{2,1,0:T(8,128)(2,1)S(1)} %bitcast.4, ...), custom_call_target="tpu_custom_call" | custom-call | flops 805306368 | bytes 37748736 | tf_op jit(solution)/shard_map/gate_all/pallas_call | solution.py:59
  21.9 0.0 collective-permute-done.5.got_ref
  22.0 0.0 copy-start.1
  22.0 0.0 copy-start.2
  22.0 0.0 copy-start.4
  22.0 0.0 copy-start.5
  22.0 1.3 %down.2.after = bf16[32,3072]{1,0:T(8,128)(2,1)S(1)} custom-call(bf16[32,1024]{1,0:T(8,128)(2,1)S(1)} %get-tuple-element.21.after.hidden_ref, bf16[1024,3072]{1,0:T(8,128)(2,1)S(1)} %get-tuple-element.23.down_ref, bf16[512,128]{1,0:T(8,128)(2,1)S(1)} %stack_after.1.after.near_ref.refs_0_), custom_call_target="tpu_custom_call" | custom-call | flops 201326592 | bytes 6291456 | tf_op jit(solution)/shard_map/down/pallas_call | solution.py:59
  23.3 0.2 collective-permute-start.8
  23.5 0.9 %collective-permute-start.7 = (bf16[512,128]{1,0:T(8,128)(2,1)S(1)}, bf16[512,128]{1,0:T(8,128)(2,1)S(1)}, u32[]{:S(2)}, u32[]{:S(2)}) collective-permute-start(bf16[512,128]{1,0:T(8,128)(2,1)S(1)} %stack_after.1.after.near_ref.refs_0_), channel_id=1, source_target_pairs={{0,4},{2,6},{4,0},{6,2},{8,12},{10,14},{12,8},{14,10},{1,5},{3,7},... | collective-permute-start | bytes 393224 | tf_op jit(solution)/shard_map/ppermute | solution.py:28
  24.4 1.3 %down.3.terms_ref = f32[32,3072]{1,0:T(8,128)S(1)} custom-call(bf16[32,1024]{1,0:T(8,128)(2,1)S(1)} %get-tuple-element.21.after.hidden_ref, bf16[1024,3072]{1,0:T(8,128)(2,1)S(1)} %get-tuple-element.22.down_ref, bf16[32,3072]{1,0:T(8,128)(2,1)S(1)} %down.2.after), custom_call_target="tpu_custom_call" | custom-call | flops 201326592 | bytes 6291456 | tf_op jit(solution)/shard_map/down/pallas_call | solution.py:59
  25.7 0.0 collective-permute-done.8.taken_ref
  25.8 1.6 %collective-permute-start.10 = (bf16[8,3072]{1,0:T(8,128)(2,1)S(1)}, bf16[8,3072]{1,0:T(8,128)(2,1)S(1)}, u32[]{:S(2)}, u32[]{:S(2)}) collective-permute-start(bf16[8,3072]{1,0:T(8,128)(2,1)S(1)} %get-tuple-element.26), channel_id=1, source_target_pairs={{0,13},{1,12},{2,15},{3,14},{4,9},{5,8},{6,11},{7,10},{8,5},{9,4},... | collective-permute-start | bytes 147464 | tf_op jit(solution)/shard_map/ppermute | solution.py:33
  27.4 0.7 %collective-permute-start.11 = (bf16[8,3072]{1,0:T(8,128)(2,1)S(1)}, bf16[8,3072]{1,0:T(8,128)(2,1)S(1)}, u32[]{:S(2)}, u32[]{:S(2)}) collective-permute-start(bf16[8,3072]{1,0:T(8,128)(2,1)S(1)} %get-tuple-element.27.after), channel_id=1, source_target_pairs={{0,9},{1,8},{2,11},{3,10},{4,13},{5,12},{6,15},{7,14},{8,1},{9,0},... | collective-permute-start | bytes 147464 | tf_op jit(solution)/shard_map/ppermute | solution.py:33
  28.1 1.8 %collective-permute-start.9 = (bf16[8,3072]{1,0:T(8,128)(2,1)S(1)}, bf16[8,3072]{1,0:T(8,128)(2,1)S(1)}, u32[]{:S(2)}, u32[]{:S(2)}) collective-permute-start(bf16[8,3072]{1,0:T(8,128)(2,1)S(1)} %get-tuple-element.25), channel_id=1, source_target_pairs={{0,4},{2,6},{4,0},{6,2},{8,12},{10,14},{12,8},{14,10},{1,5},{3,7},... | collective-permute-start | bytes 147464 | tf_op jit(solution)/shard_map/ppermute | solution.py:28
  29.9 0.0 collective-permute-done.7.far_ref.refs_1_
  30.0 2.2 %attend.1.refs_4_.refs_7_ = f32[72,128]{1,0:T(8,128)S(1)} custom-call(bf16[512,128]{1,0:T(8,128)(2,1)S(1)} %stack_after.1.after.near_ref.refs_0_, bf16[512,128]{1,0:T(8,128)(2,1)S(1)} %collective-permute-done.7.far_ref.refs_1_, bf16[4,512,512]{2,1,0:T(8,128)(2,1)S(1)} %copy-done.1, bf16[4,512,512]{2,1,0:T(8,128)(2,1)S(1)} %copy-done.2, s32[4]{0:T(128)S(1)} %copy-done.4, ...), custom_call_target="tpu_custom_call" | custom-call | flops 12582912 | bytes 2097152 | tf_op jit(solution)/shard_map/attend/pallas_call | solution.py:59
  32.2 0.0 collective-permute-done.10.refs_2_
  32.2 1.5 %collective-permute-done.11.refs_3_ = bf16[8,3072]{1,0:T(8,128)(2,1)S(1)} collective-permute-done((bf16[8,3072]{1,0:T(8,128)(2,1)S(1)}, bf16[8,3072]{1,0:T(8,128)(2,1)S(1)}, u32[]{:S(2)}, u32[]{:S(2)}) %collective-permute-start.11) | collective-permute-done | bytes 49184 | tf_op jit(solution)/shard_map/ppermute | solution.py:33
  33.7 0.0 collective-permute-done.9.refs_1_
  33.8 1.6 %collective-permute-start.12 = (bf16[4,3072]{1,0:T(4,128)(2,1)S(1)}, bf16[4,3072]{1,0:T(4,128)(2,1)S(1)}, u32[]{:S(2)}, u32[]{:S(2)}) collective-permute-start(bf16[4,3072]{1,0:T(4,128)(2,1)S(1)} %get-tuple-element.29), channel_id=1, source_target_pairs={{0,2},{2,0},{4,6},{6,4},{8,10},{10,8},{12,14},{14,12},{1,3},{3,1},... | collective-permute-start | bytes 73736 | tf_op jit(solution)/shard_map/ppermute | solution.py:28
  35.4 0.0 collective-permute-start.13
  35.4 0.6 %collective-permute-start.14 = (bf16[4,3072]{1,0:T(4,128)(2,1)S(1)}, bf16[4,3072]{1,0:T(4,128)(2,1)S(1)}, u32[]{:S(2)}, u32[]{:S(2)}) collective-permute-start(bf16[4,3072]{1,0:T(4,128)(2,1)S(1)} %get-tuple-element.28.refs_6_.kept_ref), channel_id=1, source_target_pairs={{0,1},{1,0},{2,3},{3,2},{4,5},{5,4},{6,7},{7,6},{8,9},{9,8},{10,11... | collective-permute-start | bytes 73736 | tf_op jit(solution)/shard_map/ppermute | solution.py:28
  36.0 1.8 %attend_last.1.after = bf16[4,3072]{1,0:T(4,128)(2,1)} custom-call(bf16[512,128]{1,0:T(8,128)(2,1)S(1)} %stack_after.1.after.near_ref.refs_0_, bf16[512,128]{1,0:T(8,128)(2,1)S(1)} %collective-permute-done.7.far_ref.refs_1_, bf16[4,512,512]{2,1,0:T(8,128)(2,1)S(1)} %copy-done.1, bf16[4,512,512]{2,1,0:T(8,128)(2,1)S(1)} %copy-done.2, s32[4]{0:T(128)S(1)} %copy-done.4, ...), custom_call_target="tpu_custom_call" | custom-call | flops 12582912 | bytes 2097152 | tf_op jit(solution)/shard_map/attend_last/pallas_call | solution.py:59
  37.8 0.0 collective-permute-done.12.taken_ref
  37.8 1.1 %collective-permute-done.13.other_taken = bf16[4,3072]{1,0:T(4,128)(2,1)S(1)} collective-permute-done((bf16[4,3072]{1,0:T(4,128)(2,1)S(1)}, bf16[4,3072]{1,0:T(4,128)(2,1)S(1)}, u32[]{:S(2)}, u32[]{:S(2)}) %collective-permute-start.13) | collective-permute-done | bytes 24608 | tf_op jit(solution)/shard_map/ppermute | solution.py:33
  38.9 0.0 collective-permute-done.14.other_kept
  38.9 0.7 %finish.1 = bf16[4,6144]{1,0:T(4,128)(2,1)} custom-call(bf16[4,3072]{1,0:T(4,128)(2,1)S(1)} %get-tuple-element.28.refs_6_.kept_ref, bf16[4,3072]{1,0:T(4,128)(2,1)S(1)} %collective-permute-done.12.taken_ref, bf16[4,3072]{1,0:T(4,128)(2,1)S(1)} %collective-permute-done.13.other_taken, bf16[4,3072]{1,0:T(4,128)(2,1)S(1)} %collective-permute-done.14.other_kept, ...), custom_call_target="tpu_custom_call" | custom-call | bytes 98304 | tf_op jit(solution)/shard_map/finish/pallas_call | solution.py:59
  (15 shorter events, 0.1 us)
Async XLA Ops:
  0.6 5.1 %collective-permute-start = (bf16[4,6144]{1,0:T(4,128)(2,1)}, bf16[4,6144]{1,0:T(4,128)(2,1)S(1)}, u32[]{:S(2)}, u32[]{:S(2)}) collective-permute-start(bf16[4,6144]{1,0:T(4,128)(2,1)} %tokens_ref.1), channel_id=1, source_target_pairs={{0,3},{1,2},{2,1},{3,0},{4,7},{5,6},{6,5},{7,4},{8,11},{9,10},{10,... | collective-permute-start | bytes 147464 | tf_op jit(solution)/shard_map/ppermute | solution.py:33
  4.1 13.0 %slice-start = ((s8[12582912]{0:T(1024)(128)(4,1)}), s8[4194304]{0:T(1024)(128)(4,1)S(1)}, s32[]{:S(2)}) async-start(s8[12582912]{0:T(1024)(128)(4,1)} %bitcast.3), calls=%async_computation | async-start | bytes 8388608
  4.1 13.0 %slice-start.1 = ((s8[12582912]{0:T(1024)(128)(4,1)}), s8[4194304]{0:T(1024)(128)(4,1)S(1)}, s32[]{:S(2)}) async-start(s8[12582912]{0:T(1024)(128)(4,1)} %bitcast.3), calls=%async_computation.1 | async-start | bytes 8388608
  4.1 13.0 %slice-start.2 = ((s8[12582912]{0:T(1024)(128)(4,1)}), s8[4194304]{0:T(1024)(128)(4,1)S(1)}, s32[]{:S(2)}) async-start(s8[12582912]{0:T(1024)(128)(4,1)} %bitcast.3), calls=%async_computation.2 | async-start | bytes 8388608
  4.1 13.0 %copy-start = (bf16[1,6144,1024]{2,1,0:T(8,128)(2,1)S(1)}, bf16[1,6144,1024]{2,1,0:T(8,128)(2,1)}, u32[]{:S(2)}) copy-start(bf16[1,6144,1024]{2,1,0:T(8,128)(2,1)} %up_ref.1) | copy-start | bytes 37748740
  5.1 5.4 %collective-permute-start.3 = (bf16[192,128]{1,0:T(8,128)(2,1)S(1)}, bf16[192,128]{1,0:T(8,128)(2,1)S(1)}, u32[]{:S(2)}, u32[]{:S(2)}) collective-permute-start(bf16[192,128]{1,0:T(8,128)(2,1)S(1)} %widen.1), channel_id=1, source_target_pairs={{0,2},{2,0},{4,6},{6,4},{8,10},{10,8},{12,14},{14,12},{1,3},{3,1},... | collective-permute-start | bytes 147464 | tf_op jit(solution)/shard_map/ppermute | solution.py:28
  5.9 6.1 %collective-permute-start.1 = (bf16[8,3072]{1,0:T(8,128)(2,1)S(1)}, bf16[8,3072]{1,0:T(8,128)(2,1)S(1)}, u32[]{:S(2)}, u32[]{:S(2)}) collective-permute-start(bf16[8,3072]{1,0:T(8,128)(2,1)S(1)} %norm_both.1.own_ref), channel_id=1, source_target_pairs={{0,13},{1,12},{2,15},{3,14},{4,9},{5,8},{6,11},{7,10},{8,5},{9,4},... | collective-permute-start | bytes 147464 | tf_op jit(solution)/shard_map/ppermute | solution.py:33
  9.9 4.7 %collective-permute-start.2 = (bf16[8,3072]{1,0:T(8,128)(2,1)S(1)}, bf16[8,3072]{1,0:T(8,128)(2,1)S(1)}, u32[]{:S(2)}, u32[]{:S(2)}) collective-permute-start(bf16[8,3072]{1,0:T(8,128)(2,1)S(1)} %norm_both.1.own_ref), channel_id=1, source_target_pairs={{0,9},{1,8},{2,11},{3,10},{4,13},{5,12},{6,15},{7,14},{8,1},{9,0},... | collective-permute-start | bytes 147464 | tf_op jit(solution)/shard_map/ppermute | solution.py:33
  9.9 4.7 %collective-permute-start.4 = (bf16[8,3072]{1,0:T(8,128)(2,1)S(1)}, bf16[8,3072]{1,0:T(8,128)(2,1)S(1)}, u32[]{:S(2)}, u32[]{:S(2)}) collective-permute-start(bf16[8,3072]{1,0:T(8,128)(2,1)S(1)} %norm_both.1.own_ref), channel_id=1, source_target_pairs={{0,4},{2,6},{4,0},{6,2},{8,12},{10,14},{12,8},{14,10},{1,5},{3,7},... | collective-permute-start | bytes 147464 | tf_op jit(solution)/shard_map/ppermute | solution.py:28
  14.6 2.5 %collective-permute-start.6 = (bf16[32,3072]{1,0:T(8,128)(2,1)S(1)}, bf16[32,3072]{1,0:T(8,128)(2,1)S(1)}, u32[]{:S(2)}, u32[]{:S(2)}) collective-permute-start(bf16[32,3072]{1,0:T(8,128)(2,1)S(1)} %get-tuple-element.20.x_ref), channel_id=1, source_target_pairs={{0,1},{1,0},{2,3},{3,2},{4,5},{5,4},{6,7},{7,6},{8,9},{9,8},{10,11... | collective-permute-start | bytes 589832 | tf_op jit(solution)/shard_map/ppermute | solution.py:28
  14.9 7.0 %collective-permute-start.5 = (bf16[256,128]{1,0:T(8,128)(2,1)S(1)}, bf16[256,128]{1,0:T(8,128)(2,1)S(1)}, u32[]{:S(2)}, u32[]{:S(2)}) collective-permute-start(bf16[256,128]{1,0:T(8,128)(2,1)S(1)} %get-tuple-element.19.own_ref), channel_id=1, source_target_pairs={{0,8},{2,10},{4,12},{6,14},{8,0},{10,2},{12,4},{14,6},{1,9},{3,11}... | collective-permute-start | bytes 196616 | tf_op jit(solution)/shard_map/ppermute | solution.py:28
  22.0 8.0 %copy-start.1 = (bf16[4,512,512]{2,1,0:T(8,128)(2,1)S(1)}, bf16[4,512,512]{2,1,0:T(8,128)(2,1)}, u32[]{:S(2)}) copy-start(bf16[4,512,512]{2,1,0:T(8,128)(2,1)} %refs_2_.3) | copy-start | bytes 6291460
  22.0 8.0 %copy-start.2 = (bf16[4,512,512]{2,1,0:T(8,128)(2,1)S(1)}, bf16[4,512,512]{2,1,0:T(8,128)(2,1)}, u32[]{:S(2)}) copy-start(bf16[4,512,512]{2,1,0:T(8,128)(2,1)} %refs_3_.1) | copy-start | bytes 6291460
  22.0 8.0 %copy-start.4 = (s32[4]{0:T(128)S(1)}, s32[4]{0:T(128)}, u32[]{:S(2)}) copy-start(s32[4]{0:T(128)} %refs_4_.1) | copy-start | bytes 52
  22.0 8.0 %copy-start.5 = (s32[4]{0:T(128)S(1)}, s32[4]{0:T(128)}, u32[]{:S(2)}) copy-start(s32[4]{0:T(128)} %refs_5_.1) | copy-start | bytes 52
  23.3 2.4 %collective-permute-start.8 = (bf16[32,3072]{1,0:T(8,128)(2,1)S(1)}, bf16[32,3072]{1,0:T(8,128)(2,1)S(1)}, u32[]{:S(2)}, u32[]{:S(2)}) collective-permute-start(bf16[32,3072]{1,0:T(8,128)(2,1)S(1)} %down.2.after), channel_id=1, source_target_pairs={{0,1},{1,0},{2,3},{3,2},{4,5},{5,4},{6,7},{7,6},{8,9},{9,8},{10,11... | collective-permute-start | bytes 589832 | tf_op jit(solution)/shard_map/ppermute | solution.py:28
  23.5 6.5 %collective-permute-start.7 = (bf16[512,128]{1,0:T(8,128)(2,1)S(1)}, bf16[512,128]{1,0:T(8,128)(2,1)S(1)}, u32[]{:S(2)}, u32[]{:S(2)}) collective-permute-start(bf16[512,128]{1,0:T(8,128)(2,1)S(1)} %stack_after.1.after.near_ref.refs_0_), channel_id=1, source_target_pairs={{0,4},{2,6},{4,0},{6,2},{8,12},{10,14},{12,8},{14,10},{1,5},{3,7},... | collective-permute-start | bytes 393224 | tf_op jit(solution)/shard_map/ppermute | solution.py:28
  25.7 13.2 %copy-start.3 = (bf16[4,6144]{1,0:T(4,128)(2,1)S(1)}, bf16[4,6144]{1,0:T(4,128)(2,1)}, u32[]{:S(2)}) copy-start(bf16[4,6144]{1,0:T(4,128)(2,1)} %tokens_ref.1) | copy-start | bytes 147460
  25.8 6.4 %collective-permute-start.10 = (bf16[8,3072]{1,0:T(8,128)(2,1)S(1)}, bf16[8,3072]{1,0:T(8,128)(2,1)S(1)}, u32[]{:S(2)}, u32[]{:S(2)}) collective-permute-start(bf16[8,3072]{1,0:T(8,128)(2,1)S(1)} %get-tuple-element.26), channel_id=1, source_target_pairs={{0,13},{1,12},{2,15},{3,14},{4,9},{5,8},{6,11},{7,10},{8,5},{9,4},... | collective-permute-start | bytes 147464 | tf_op jit(solution)/shard_map/ppermute | solution.py:33
  27.4 6.3 %collective-permute-start.11 = (bf16[8,3072]{1,0:T(8,128)(2,1)S(1)}, bf16[8,3072]{1,0:T(8,128)(2,1)S(1)}, u32[]{:S(2)}, u32[]{:S(2)}) collective-permute-start(bf16[8,3072]{1,0:T(8,128)(2,1)S(1)} %get-tuple-element.27.after), channel_id=1, source_target_pairs={{0,9},{1,8},{2,11},{3,10},{4,13},{5,12},{6,15},{7,14},{8,1},{9,0},... | collective-permute-start | bytes 147464 | tf_op jit(solution)/shard_map/ppermute | solution.py:33
  28.1 5.6 %collective-permute-start.9 = (bf16[8,3072]{1,0:T(8,128)(2,1)S(1)}, bf16[8,3072]{1,0:T(8,128)(2,1)S(1)}, u32[]{:S(2)}, u32[]{:S(2)}) collective-permute-start(bf16[8,3072]{1,0:T(8,128)(2,1)S(1)} %get-tuple-element.25), channel_id=1, source_target_pairs={{0,4},{2,6},{4,0},{6,2},{8,12},{10,14},{12,8},{14,10},{1,5},{3,7},... | collective-permute-start | bytes 147464 | tf_op jit(solution)/shard_map/ppermute | solution.py:28
  33.8 4.0 %collective-permute-start.12 = (bf16[4,3072]{1,0:T(4,128)(2,1)S(1)}, bf16[4,3072]{1,0:T(4,128)(2,1)S(1)}, u32[]{:S(2)}, u32[]{:S(2)}) collective-permute-start(bf16[4,3072]{1,0:T(4,128)(2,1)S(1)} %get-tuple-element.29), channel_id=1, source_target_pairs={{0,2},{2,0},{4,6},{6,4},{8,10},{10,8},{12,14},{14,12},{1,3},{3,1},... | collective-permute-start | bytes 73736 | tf_op jit(solution)/shard_map/ppermute | solution.py:28
  35.4 3.5 %collective-permute-start.13 = (bf16[4,3072]{1,0:T(4,128)(2,1)S(1)}, bf16[4,3072]{1,0:T(4,128)(2,1)S(1)}, u32[]{:S(2)}, u32[]{:S(2)}) collective-permute-start(bf16[4,3072]{1,0:T(4,128)(2,1)S(1)} %get-tuple-element.29), channel_id=1, source_target_pairs={{0,3},{1,2},{2,1},{3,0},{4,7},{5,6},{6,5},{7,4},{8,11},{9,10},{10,... | collective-permute-start | bytes 73736 | tf_op jit(solution)/shard_map/ppermute | solution.py:33
  35.4 3.5 %collective-permute-start.14 = (bf16[4,3072]{1,0:T(4,128)(2,1)S(1)}, bf16[4,3072]{1,0:T(4,128)(2,1)S(1)}, u32[]{:S(2)}, u32[]{:S(2)}) collective-permute-start(bf16[4,3072]{1,0:T(4,128)(2,1)S(1)} %get-tuple-element.28.refs_6_.kept_ref), channel_id=1, source_target_pairs={{0,1},{1,0},{2,3},{3,2},{4,5},{5,4},{6,7},{7,6},{8,9},{9,8},{10,11... | collective-permute-start | bytes 73736 | tf_op jit(solution)/shard_map/ppermute | solution.py:28

commit v18 on v14

--- a/solution.py
+++ b/solution.py
@@ -392,7 +392,7 @@
             far=range(5),
         )
         x = call(
-            functools.partial(norm_both, steps[-2]),
+            functools.partial(norm_both, steps[-1]),
             shape((2 * rows, half), bf16),
             [near(row_near[0]), got, near(row_near[1]), share, heads],
             size=100000,
@@ -416,7 +416,7 @@
             )
         line_steps = [steps[-2], steps[-1], steps[-2] ^ steps[-1]]
         last = cross(x, wide, line_steps[2])
-        line = [cross(x, wide, line_steps[0]), swap(x, "wide", wide, line_steps[1])]
+        line = [swap(x, "wide", wide, line_steps[0]), cross(x, wide, line_steps[1])]
         wider = max(x.shape[0] * half // HD, heads.shape[0])
         sent_heads = call(widen, shape((wider, HD), bf16), [heads], size=4 * wider * HD)
         far_rows = swap(sent_heads, "wide", wide, steps[0])
@@ -432,7 +432,7 @@
         other_x = swap(x, "narrow", 2, 1)
         whole = pltpu.VMEM((units, half), bf16)
         hidden, down_own, down_other = call(
-            functools.partial(gate_all, steps[-2]),
+            functools.partial(gate_all, steps[-1]),
             [shape((count, units), bf16), whole, whole],
             [
                 x,
@@ -486,9 +486,9 @@
             size=terms.size * 8,
         )
         taken = [
-            swap(sent[1], "wide", wide, line_steps[1]),
+            cross(sent[1], wide, line_steps[1]),
             cross(sent[2], wide, line_steps[2]),
-            cross(sent[0], wide, line_steps[0]),
+            swap(sent[0], "wide", wide, line_steps[0]),
         ]
         early = call(
             functools.partial(attend, head_steps, early_slots),
@@ -525,7 +525,7 @@
         other_kept = swap(terms, "narrow", 2, 1)
         other_taken = cross(sent, wide, steps[0])
         mixed_out = call(
-            functools.partial(finish, steps[-2]),
+            functools.partial(finish, steps[-1]),
             shape((rows, width), bf16),
             [terms, *taken, other_kept, other_taken, tokens, distant(context)],
             size=terms.size * 8,

time: 39.6 us -> 39.6 us (level)
  waiting for transfers between devices: 6.54 us -> 7.92 us
  starting transfers between devices: 17.7 us -> 16.4 us
    ppermute x9, waiting for transfers between devices: 0.03 us -> 5.19 us  [swap(): return lax.ppermute(block, axis, [(i, i ^ step) for i in range(count)])]
    ppermute x6, waiting for transfers between devices: 6.51 us -> 2.72 us  [cross(): return lax.ppermute(block, ('wide', 'narrow'), pairs)]
    ppermute x9, starting transfers between devices: 8.32 us -> 6.05 us  [swap(): return lax.ppermute(block, axis, [(i, i ^ step) for i in range(count)])]
    ppermute x6, starting transfers between devices: 9.38 us -> 10.3 us  [cross(): return lax.ppermute(block, ('wide', 'narrow'), pairs)]
  transfers between devices with their start and end apart: 15 -> 15, of which waited for: 4 -> 5; matrix products, arithmetic and copies ran while one was open for 0% -> 0% of each run, Pallas kernels for 31% -> 31%
where the time goes in v18:
time: 39.6 us; the launch traced here: 39.4 us
  starting transfers between devices  16.4 us (41%)
  Pallas kernels  14.2 us (36%)
  waiting for transfers between devices  7.92 us (20%)
  between operations  0.83 us (2%)
    pallas_call x14, Pallas kernels, call(): pl.pallas_call(kernel, name=getattr(kernel, 'func', kernel).__name__, out...  14.2 us
    ppermute x6, starting transfers between devices, cross(): return lax.ppermute(block, ('wide', 'narrow'), pairs)  10.3 us
    ppermute x9, starting transfers between devices, swap(): return lax.ppermute(block, axis, [(i, i ^ step) for i in range(count)])  6.05 us
    ppermute x9, waiting for transfers between devices, swap(): return lax.ppermute(block, axis, [(i, i ^ step) for i in range(count)])  5.19 us
    ppermute x6, waiting for transfers between devices, cross(): return lax.ppermute(block, ('wide', 'narrow'), pairs)  2.72 us
  transfers between devices with their start and end apart: 15, of which 5 were waited for; matrix products, arithmetic and copies ran while one was open for 0% of the time, Pallas kernels for 31%

profile of v18, /device:TPU:0, one launch (start us, length us, event | category | flops | bytes accessed | tf_op | source)
XLA Modules:
  0.0 39.4 jit_solution(6806483228468320364)
XLA Ops:
  0.6 2.5 %collective-permute-start = (bf16[4,6144]{1,0:T(4,128)(2,1)}, bf16[4,6144]{1,0:T(4,128)(2,1)S(1)}, u32[]{:S(2)}, u32[]{:S(2)}) collective-permute-start(bf16[4,6144]{1,0:T(4,128)(2,1)} %tokens_ref.1), channel_id=1, source_target_pairs={{0,3},{1,2},{2,1},{3,0},{4,7},{5,6},{6,5},{7,4},{8,11},{9,10},{10,... | collective-permute-start | bytes 147464 | tf_op jit(solution)/shard_map/ppermute | solution.py:33
  3.1 1.0 %pack.1 = (bf16[128,128]{1,0:T(8,128)(2,1)S(1)}, bf16[4,6144]{1,0:T(4,128)(2,1)S(1)}, f32[1,6144]{1,0:T(1,128)S(1)}) custom-call(bf16[4,3072]{1,0:T(4,128)(2,1)} %far_query.1, bf16[4,512]{1,0:T(4,128)(2,1)} %far_key.1, bf16[4,512]{1,0:T(4,128)(2,1)} %far_value.1, bf16[4,6144]{1,0:T(4,128)(2,1)} %tokens_ref.1, f32[1,6144]{1,0:T(1,128)} %bitcast.5), custom_call_target="tpu_custom_call" | custom-call | bytes 100000 | tf_op jit(solution)/shard_map/pack/pallas_call | solution.py:59
  4.1 0.6 %collective-permute-start.3 = (bf16[192,128]{1,0:T(8,128)(2,1)S(1)}, bf16[192,128]{1,0:T(8,128)(2,1)S(1)}, u32[]{:S(2)}, u32[]{:S(2)}) collective-permute-start(bf16[192,128]{1,0:T(8,128)(2,1)S(1)} %widen.1), channel_id=1, source_target_pairs={{0,2},{2,0},{4,6},{6,4},{8,10},{10,8},{12,14},{14,12},{1,3},{3,1},... | collective-permute-start | bytes 147464 | tf_op jit(solution)/shard_map/ppermute | solution.py:28
  4.7 1.0 %shares.1.share.share_ref = f32[32,128]{1,0:T(8,128)S(1)} custom-call(s32[2,32]{1,0:T(2,128)} %bitcast.6, f32[2,32]{1,0:T(2,128)} %bitcast.7, bf16[128,128]{1,0:T(8,128)(2,1)S(1)} %get-tuple-element.18.refs_0_.heads.own_ref.own_heads, bf16[1,6144,1024]{2,1,0:T(8,128)(2,1)} %gate_ref.1, bf16[1,6144,1024]{2,1,0:T(8,128)(2,1)} %up_ref.1), custom_call_target="tpu_custom_call" | custom-call | bytes 100000 | tf_op jit(solution)/shard_map/shares/pallas_call | solution.py:59
  5.7 0.0 collective-permute-done.got_ref
  5.7 0.2 norm_both.1.own_ref
  5.9 4.0 %collective-permute-start.1 = (bf16[8,3072]{1,0:T(8,128)(2,1)S(1)}, bf16[8,3072]{1,0:T(8,128)(2,1)S(1)}, u32[]{:S(2)}, u32[]{:S(2)}) collective-permute-start(bf16[8,3072]{1,0:T(8,128)(2,1)S(1)} %norm_both.1.own_ref), channel_id=1, source_target_pairs={{0,13},{1,12},{2,15},{3,14},{4,9},{5,8},{6,11},{7,10},{8,5},{9,4},... | collective-permute-start | bytes 147464 | tf_op jit(solution)/shard_map/ppermute | solution.py:33
  9.9 0.0 collective-permute-start.2
  9.9 0.4 collective-permute-start.4
  10.2 0.0 collective-permute-done.3.got_heads
  10.2 1.8 %collective-permute-done.1.last_ref = bf16[8,3072]{1,0:T(8,128)(2,1)S(1)} collective-permute-done((bf16[8,3072]{1,0:T(8,128)(2,1)S(1)}, bf16[8,3072]{1,0:T(8,128)(2,1)S(1)}, u32[]{:S(2)}, u32[]{:S(2)}) %collective-permute-start.1) | collective-permute-done | bytes 49184 | tf_op jit(solution)/shard_map/ppermute | solution.py:33
  12.1 3.0 %collective-permute-done.2.far_ref = bf16[8,3072]{1,0:T(8,128)(2,1)S(1)} collective-permute-done((bf16[8,3072]{1,0:T(8,128)(2,1)S(1)}, bf16[8,3072]{1,0:T(8,128)(2,1)S(1)}, u32[]{:S(2)}, u32[]{:S(2)}) %collective-permute-start.2) | collective-permute-done | bytes 49184 | tf_op jit(solution)/shard_map/ppermute | solution.py:28
  15.0 0.0 collective-permute-done.4.next_ref
  15.0 0.1 collective-permute-start.6
  15.2 1.6 %collective-permute-start.5 = (bf16[256,128]{1,0:T(8,128)(2,1)S(1)}, bf16[256,128]{1,0:T(8,128)(2,1)S(1)}, u32[]{:S(2)}, u32[]{:S(2)}) collective-permute-start(bf16[256,128]{1,0:T(8,128)(2,1)S(1)} %get-tuple-element.19.own_ref), channel_id=1, source_target_pairs={{0,8},{2,10},{4,12},{6,14},{8,0},{10,2},{12,4},{14,6},{1,9},{3,11}... | collective-permute-start | bytes 196616 | tf_op jit(solution)/shard_map/ppermute | solution.py:28
  16.8 0.0 collective-permute-done.6.other_ref
  16.8 0.0 slice-done
  16.8 0.0 slice-done.1
  16.8 0.0 slice-done.2
  16.8 4.8 %gate_all.1 = (bf16[32,1024]{1,0:T(8,128)(2,1)S(1)}, bf16[1024,3072]{1,0:T(8,128)(2,1)S(1)}, bf16[1024,3072]{1,0:T(8,128)(2,1)S(1)}) custom-call(bf16[32,3072]{1,0:T(8,128)(2,1)S(1)} %get-tuple-element.20.x_ref, bf16[32,3072]{1,0:T(8,128)(2,1)S(1)} %collective-permute-done.6.other_ref, bf16[1,6144,1024]{2,1,0:T(8,128)(2,1)S(1)} %bitcast.4, ...), custom_call_target="tpu_custom_call" | custom-call | flops 805306368 | bytes 37748736 | tf_op jit(solution)/shard_map/gate_all/pallas_call | solution.py:59
  21.6 0.3 collective-permute-done.5.got_ref
  22.0 0.0 copy-start.1
  22.0 0.0 copy-start.2
  22.0 0.0 copy-start.4
  22.0 0.0 copy-start.5
  22.0 1.3 %down.2.after = bf16[32,3072]{1,0:T(8,128)(2,1)S(1)} custom-call(bf16[32,1024]{1,0:T(8,128)(2,1)S(1)} %get-tuple-element.21.after.hidden_ref, bf16[1024,3072]{1,0:T(8,128)(2,1)S(1)} %get-tuple-element.23.down_ref, bf16[512,128]{1,0:T(8,128)(2,1)S(1)} %stack_after.1.after.near_ref.refs_0_), custom_call_target="tpu_custom_call" | custom-call | flops 201326592 | bytes 6291456 | tf_op jit(solution)/shard_map/down/pallas_call | solution.py:59
  23.3 0.0 collective-permute-start.8
  23.3 1.1 %collective-permute-start.7 = (bf16[512,128]{1,0:T(8,128)(2,1)S(1)}, bf16[512,128]{1,0:T(8,128)(2,1)S(1)}, u32[]{:S(2)}, u32[]{:S(2)}) collective-permute-start(bf16[512,128]{1,0:T(8,128)(2,1)S(1)} %stack_after.1.after.near_ref.refs_0_), channel_id=1, source_target_pairs={{0,4},{2,6},{4,0},{6,2},{8,12},{10,14},{12,8},{14,10},{1,5},{3,7},... | collective-permute-start | bytes 393224 | tf_op jit(solution)/shard_map/ppermute | solution.py:28
  24.4 1.3 %down.3.terms_ref = f32[32,3072]{1,0:T(8,128)S(1)} custom-call(bf16[32,1024]{1,0:T(8,128)(2,1)S(1)} %get-tuple-element.21.after.hidden_ref, bf16[1024,3072]{1,0:T(8,128)(2,1)S(1)} %get-tuple-element.22.down_ref, bf16[32,3072]{1,0:T(8,128)(2,1)S(1)} %down.2.after), custom_call_target="tpu_custom_call" | custom-call | flops 201326592 | bytes 6291456 | tf_op jit(solution)/shard_map/down/pallas_call | solution.py:59
  25.7 0.0 collective-permute-done.8.taken_ref
  25.8 1.4 %collective-permute-start.10 = (bf16[8,3072]{1,0:T(8,128)(2,1)S(1)}, bf16[8,3072]{1,0:T(8,128)(2,1)S(1)}, u32[]{:S(2)}, u32[]{:S(2)}) collective-permute-start(bf16[8,3072]{1,0:T(8,128)(2,1)S(1)} %get-tuple-element.26), channel_id=1, source_target_pairs={{0,13},{1,12},{2,15},{3,14},{4,9},{5,8},{6,11},{7,10},{8,5},{9,4},... | collective-permute-start | bytes 147464 | tf_op jit(solution)/shard_map/ppermute | solution.py:33
  27.1 1.0 %collective-permute-start.11 = (bf16[8,3072]{1,0:T(8,128)(2,1)S(1)}, bf16[8,3072]{1,0:T(8,128)(2,1)S(1)}, u32[]{:S(2)}, u32[]{:S(2)}) collective-permute-start(bf16[8,3072]{1,0:T(8,128)(2,1)S(1)} %get-tuple-element.27.after), channel_id=1, source_target_pairs={{0,8},{2,10},{4,12},{6,14},{8,0},{10,2},{12,4},{14,6},{1,9},{3,11}... | collective-permute-start | bytes 147464 | tf_op jit(solution)/shard_map/ppermute | solution.py:28
  28.1 1.6 %collective-permute-start.9 = (bf16[8,3072]{1,0:T(8,128)(2,1)S(1)}, bf16[8,3072]{1,0:T(8,128)(2,1)S(1)}, u32[]{:S(2)}, u32[]{:S(2)}) collective-permute-start(bf16[8,3072]{1,0:T(8,128)(2,1)S(1)} %get-tuple-element.25), channel_id=1, source_target_pairs={{0,5},{1,4},{2,7},{3,6},{4,1},{5,0},{6,3},{7,2},{8,13},{9,12},{10,... | collective-permute-start | bytes 147464 | tf_op jit(solution)/shard_map/ppermute | solution.py:33
  29.7 0.0 collective-permute-done.7.far_ref.refs_1_
  29.7 0.0 copy-done.2
  29.7 2.2 %attend.1.refs_4_.refs_7_ = f32[72,128]{1,0:T(8,128)S(1)} custom-call(bf16[512,128]{1,0:T(8,128)(2,1)S(1)} %stack_after.1.after.near_ref.refs_0_, bf16[512,128]{1,0:T(8,128)(2,1)S(1)} %collective-permute-done.7.far_ref.refs_1_, bf16[4,512,512]{2,1,0:T(8,128)(2,1)S(1)} %copy-done.1, bf16[4,512,512]{2,1,0:T(8,128)(2,1)S(1)} %copy-done.2, s32[4]{0:T(128)S(1)} %copy-done.4, ...), custom_call_target="tpu_custom_call" | custom-call | flops 12582912 | bytes 2097152 | tf_op jit(solution)/shard_map/attend/pallas_call | solution.py:59
  31.9 0.0 collective-permute-done.10.refs_2_
  31.9 1.9 %collective-permute-done.11.refs_3_ = bf16[8,3072]{1,0:T(8,128)(2,1)S(1)} collective-permute-done((bf16[8,3072]{1,0:T(8,128)(2,1)S(1)}, bf16[8,3072]{1,0:T(8,128)(2,1)S(1)}, u32[]{:S(2)}, u32[]{:S(2)}) %collective-permute-start.11) | collective-permute-done | bytes 49184 | tf_op jit(solution)/shard_map/ppermute | solution.py:28
  33.8 0.0 collective-permute-done.9.refs_1_
  33.8 1.6 %collective-permute-start.12 = (bf16[4,3072]{1,0:T(4,128)(2,1)S(1)}, bf16[4,3072]{1,0:T(4,128)(2,1)S(1)}, u32[]{:S(2)}, u32[]{:S(2)}) collective-permute-start(bf16[4,3072]{1,0:T(4,128)(2,1)S(1)} %get-tuple-element.28.refs_6_), channel_id=1, source_target_pairs={{0,2},{2,0},{4,6},{6,4},{8,10},{10,8},{12,14},{14,12},{1,3},{3,1},... | collective-permute-start | bytes 73736 | tf_op jit(solution)/shard_map/ppermute | solution.py:28
  35.5 0.0 collective-permute-start.13
  35.5 0.6 %collective-permute-start.14 = (bf16[4,3072]{1,0:T(4,128)(2,1)S(1)}, bf16[4,3072]{1,0:T(4,128)(2,1)S(1)}, u32[]{:S(2)}, u32[]{:S(2)}) collective-permute-start(bf16[4,3072]{1,0:T(4,128)(2,1)S(1)} %get-tuple-element.28.refs_6_), channel_id=1, source_target_pairs={{0,3},{1,2},{2,1},{3,0},{4,7},{5,6},{6,5},{7,4},{8,11},{9,10},{10,... | collective-permute-start | bytes 73736 | tf_op jit(solution)/shard_map/ppermute | solution.py:33
  36.0 1.8 %attend_last.1.after = bf16[4,3072]{1,0:T(4,128)(2,1)} custom-call(bf16[512,128]{1,0:T(8,128)(2,1)S(1)} %stack_after.1.after.near_ref.refs_0_, bf16[512,128]{1,0:T(8,128)(2,1)S(1)} %collective-permute-done.7.far_ref.refs_1_, bf16[4,512,512]{2,1,0:T(8,128)(2,1)S(1)} %copy-done.1, bf16[4,512,512]{2,1,0:T(8,128)(2,1)S(1)} %copy-done.2, s32[4]{0:T(128)S(1)} %copy-done.4, ...), custom_call_target="tpu_custom_call" | custom-call | flops 12582912 | bytes 2097152 | tf_op jit(solution)/shard_map/attend_last/pallas_call | solution.py:59
  37.8 0.0 collective-permute-done.12.taken_ref
  37.8 0.0 collective-permute-done.13.other_kept
  37.8 0.9 %collective-permute-done.14.other_taken = bf16[4,3072]{1,0:T(4,128)(2,1)S(1)} collective-permute-done((bf16[4,3072]{1,0:T(4,128)(2,1)S(1)}, bf16[4,3072]{1,0:T(4,128)(2,1)S(1)}, u32[]{:S(2)}, u32[]{:S(2)}) %collective-permute-start.14) | collective-permute-done | bytes 24608 | tf_op jit(solution)/shard_map/ppermute | solution.py:33
  38.7 0.0 copy-done.3
  38.7 0.7 %finish.1 = bf16[4,6144]{1,0:T(4,128)(2,1)} custom-call(bf16[4,3072]{1,0:T(4,128)(2,1)S(1)} %get-tuple-element.29.kept_ref, bf16[4,3072]{1,0:T(4,128)(2,1)S(1)} %collective-permute-done.12.taken_ref, bf16[4,3072]{1,0:T(4,128)(2,1)S(1)} %collective-permute-done.13.other_kept, bf16[4,3072]{1,0:T(4,128)(2,1)S(1)} %collective-permute-done.14.other_taken, ...), custom_call_target="tpu_custom_call" | custom-call | bytes 98304 | tf_op jit(solution)/shard_map/finish/pallas_call | solution.py:59
  (15 shorter events, 0.1 us)
Async XLA Ops:
  0.6 5.1 %collective-permute-start = (bf16[4,6144]{1,0:T(4,128)(2,1)}, bf16[4,6144]{1,0:T(4,128)(2,1)S(1)}, u32[]{:S(2)}, u32[]{:S(2)}) collective-permute-start(bf16[4,6144]{1,0:T(4,128)(2,1)} %tokens_ref.1), channel_id=1, source_target_pairs={{0,3},{1,2},{2,1},{3,0},{4,7},{5,6},{6,5},{7,4},{8,11},{9,10},{10,... | collective-permute-start | bytes 147464 | tf_op jit(solution)/shard_map/ppermute | solution.py:33
  4.1 6.2 %collective-permute-start.3 = (bf16[192,128]{1,0:T(8,128)(2,1)S(1)}, bf16[192,128]{1,0:T(8,128)(2,1)S(1)}, u32[]{:S(2)}, u32[]{:S(2)}) collective-permute-start(bf16[192,128]{1,0:T(8,128)(2,1)S(1)} %widen.1), channel_id=1, source_target_pairs={{0,2},{2,0},{4,6},{6,4},{8,10},{10,8},{12,14},{14,12},{1,3},{3,1},... | collective-permute-start | bytes 147464 | tf_op jit(solution)/shard_map/ppermute | solution.py:28
  4.7 12.1 %slice-start = ((s8[12582912]{0:T(1024)(128)(4,1)}), s8[4194304]{0:T(1024)(128)(4,1)S(1)}, s32[]{:S(2)}) async-start(s8[12582912]{0:T(1024)(128)(4,1)} %bitcast.3), calls=%async_computation | async-start | bytes 8388608
  4.7 12.1 %slice-start.1 = ((s8[12582912]{0:T(1024)(128)(4,1)}), s8[4194304]{0:T(1024)(128)(4,1)S(1)}, s32[]{:S(2)}) async-start(s8[12582912]{0:T(1024)(128)(4,1)} %bitcast.3), calls=%async_computation.1 | async-start | bytes 8388608
  4.7 12.1 %slice-start.2 = ((s8[12582912]{0:T(1024)(128)(4,1)}), s8[4194304]{0:T(1024)(128)(4,1)S(1)}, s32[]{:S(2)}) async-start(s8[12582912]{0:T(1024)(128)(4,1)} %bitcast.3), calls=%async_computation.2 | async-start | bytes 8388608
  4.7 12.1 %copy-start = (bf16[1,6144,1024]{2,1,0:T(8,128)(2,1)S(1)}, bf16[1,6144,1024]{2,1,0:T(8,128)(2,1)}, u32[]{:S(2)}) copy-start(bf16[1,6144,1024]{2,1,0:T(8,128)(2,1)} %up_ref.1) | copy-start | bytes 37748740
  5.9 6.2 %collective-permute-start.1 = (bf16[8,3072]{1,0:T(8,128)(2,1)S(1)}, bf16[8,3072]{1,0:T(8,128)(2,1)S(1)}, u32[]{:S(2)}, u32[]{:S(2)}) collective-permute-start(bf16[8,3072]{1,0:T(8,128)(2,1)S(1)} %norm_both.1.own_ref), channel_id=1, source_target_pairs={{0,13},{1,12},{2,15},{3,14},{4,9},{5,8},{6,11},{7,10},{8,5},{9,4},... | collective-permute-start | bytes 147464 | tf_op jit(solution)/shard_map/ppermute | solution.py:33
  9.9 5.1 %collective-permute-start.2 = (bf16[8,3072]{1,0:T(8,128)(2,1)S(1)}, bf16[8,3072]{1,0:T(8,128)(2,1)S(1)}, u32[]{:S(2)}, u32[]{:S(2)}) collective-permute-start(bf16[8,3072]{1,0:T(8,128)(2,1)S(1)} %norm_both.1.own_ref), channel_id=1, source_target_pairs={{0,8},{2,10},{4,12},{6,14},{8,0},{10,2},{12,4},{14,6},{1,9},{3,11}... | collective-permute-start | bytes 147464 | tf_op jit(solution)/shard_map/ppermute | solution.py:28
  9.9 5.1 %collective-permute-start.4 = (bf16[8,3072]{1,0:T(8,128)(2,1)S(1)}, bf16[8,3072]{1,0:T(8,128)(2,1)S(1)}, u32[]{:S(2)}, u32[]{:S(2)}) collective-permute-start(bf16[8,3072]{1,0:T(8,128)(2,1)S(1)} %norm_both.1.own_ref), channel_id=1, source_target_pairs={{0,5},{1,4},{2,7},{3,6},{4,1},{5,0},{6,3},{7,2},{8,13},{9,12},{10,... | collective-permute-start | bytes 147464 | tf_op jit(solution)/shard_map/ppermute | solution.py:33
  15.0 1.7 %collective-permute-start.6 = (bf16[32,3072]{1,0:T(8,128)(2,1)S(1)}, bf16[32,3072]{1,0:T(8,128)(2,1)S(1)}, u32[]{:S(2)}, u32[]{:S(2)}) collective-permute-start(bf16[32,3072]{1,0:T(8,128)(2,1)S(1)} %get-tuple-element.20.x_ref), channel_id=1, source_target_pairs={{0,1},{1,0},{2,3},{3,2},{4,5},{5,4},{6,7},{7,6},{8,9},{9,8},{10,11... | collective-permute-start | bytes 589832 | tf_op jit(solution)/shard_map/ppermute | solution.py:28
  15.2 6.8 %collective-permute-start.5 = (bf16[256,128]{1,0:T(8,128)(2,1)S(1)}, bf16[256,128]{1,0:T(8,128)(2,1)S(1)}, u32[]{:S(2)}, u32[]{:S(2)}) collective-permute-start(bf16[256,128]{1,0:T(8,128)(2,1)S(1)} %get-tuple-element.19.own_ref), channel_id=1, source_target_pairs={{0,8},{2,10},{4,12},{6,14},{8,0},{10,2},{12,4},{14,6},{1,9},{3,11}... | collective-permute-start | bytes 196616 | tf_op jit(solution)/shard_map/ppermute | solution.py:28
  22.0 7.7 %copy-start.1 = (bf16[4,512,512]{2,1,0:T(8,128)(2,1)S(1)}, bf16[4,512,512]{2,1,0:T(8,128)(2,1)}, u32[]{:S(2)}) copy-start(bf16[4,512,512]{2,1,0:T(8,128)(2,1)} %refs_2_.3) | copy-start | bytes 6291460
  22.0 7.7 %copy-start.2 = (bf16[4,512,512]{2,1,0:T(8,128)(2,1)S(1)}, bf16[4,512,512]{2,1,0:T(8,128)(2,1)}, u32[]{:S(2)}) copy-start(bf16[4,512,512]{2,1,0:T(8,128)(2,1)} %refs_3_.1) | copy-start | bytes 6291460
  22.0 7.7 %copy-start.4 = (s32[4]{0:T(128)S(1)}, s32[4]{0:T(128)}, u32[]{:S(2)}) copy-start(s32[4]{0:T(128)} %refs_4_.1) | copy-start | bytes 52
  22.0 7.7 %copy-start.5 = (s32[4]{0:T(128)S(1)}, s32[4]{0:T(128)}, u32[]{:S(2)}) copy-start(s32[4]{0:T(128)} %refs_5_.1) | copy-start | bytes 52
  23.3 2.4 %collective-permute-start.8 = (bf16[32,3072]{1,0:T(8,128)(2,1)S(1)}, bf16[32,3072]{1,0:T(8,128)(2,1)S(1)}, u32[]{:S(2)}, u32[]{:S(2)}) collective-permute-start(bf16[32,3072]{1,0:T(8,128)(2,1)S(1)} %down.2.after), channel_id=1, source_target_pairs={{0,1},{1,0},{2,3},{3,2},{4,5},{5,4},{6,7},{7,6},{8,9},{9,8},{10,11... | collective-permute-start | bytes 589832 | tf_op jit(solution)/shard_map/ppermute | solution.py:28
  23.3 6.3 %collective-permute-start.7 = (bf16[512,128]{1,0:T(8,128)(2,1)S(1)}, bf16[512,128]{1,0:T(8,128)(2,1)S(1)}, u32[]{:S(2)}, u32[]{:S(2)}) collective-permute-start(bf16[512,128]{1,0:T(8,128)(2,1)S(1)} %stack_after.1.after.near_ref.refs_0_), channel_id=1, source_target_pairs={{0,4},{2,6},{4,0},{6,2},{8,12},{10,14},{12,8},{14,10},{1,5},{3,7},... | collective-permute-start | bytes 393224 | tf_op jit(solution)/shard_map/ppermute | solution.py:28
  25.7 13.0 %copy-start.3 = (bf16[4,6144]{1,0:T(4,128)(2,1)S(1)}, bf16[4,6144]{1,0:T(4,128)(2,1)}, u32[]{:S(2)}) copy-start(bf16[4,6144]{1,0:T(4,128)(2,1)} %tokens_ref.1) | copy-start | bytes 147460
  25.8 6.1 %collective-permute-start.10 = (bf16[8,3072]{1,0:T(8,128)(2,1)S(1)}, bf16[8,3072]{1,0:T(8,128)(2,1)S(1)}, u32[]{:S(2)}, u32[]{:S(2)}) collective-permute-start(bf16[8,3072]{1,0:T(8,128)(2,1)S(1)} %get-tuple-element.26), channel_id=1, source_target_pairs={{0,13},{1,12},{2,15},{3,14},{4,9},{5,8},{6,11},{7,10},{8,5},{9,4},... | collective-permute-start | bytes 147464 | tf_op jit(solution)/shard_map/ppermute | solution.py:33
  27.1 6.7 %collective-permute-start.11 = (bf16[8,3072]{1,0:T(8,128)(2,1)S(1)}, bf16[8,3072]{1,0:T(8,128)(2,1)S(1)}, u32[]{:S(2)}, u32[]{:S(2)}) collective-permute-start(bf16[8,3072]{1,0:T(8,128)(2,1)S(1)} %get-tuple-element.27.after), channel_id=1, source_target_pairs={{0,8},{2,10},{4,12},{6,14},{8,0},{10,2},{12,4},{14,6},{1,9},{3,11}... | collective-permute-start | bytes 147464 | tf_op jit(solution)/shard_map/ppermute | solution.py:28
  28.1 5.7 %collective-permute-start.9 = (bf16[8,3072]{1,0:T(8,128)(2,1)S(1)}, bf16[8,3072]{1,0:T(8,128)(2,1)S(1)}, u32[]{:S(2)}, u32[]{:S(2)}) collective-permute-start(bf16[8,3072]{1,0:T(8,128)(2,1)S(1)} %get-tuple-element.25), channel_id=1, source_target_pairs={{0,5},{1,4},{2,7},{3,6},{4,1},{5,0},{6,3},{7,2},{8,13},{9,12},{10,... | collective-permute-start | bytes 147464 | tf_op jit(solution)/shard_map/ppermute | solution.py:33
  33.8 4.0 %collective-permute-start.12 = (bf16[4,3072]{1,0:T(4,128)(2,1)S(1)}, bf16[4,3072]{1,0:T(4,128)(2,1)S(1)}, u32[]{:S(2)}, u32[]{:S(2)}) collective-permute-start(bf16[4,3072]{1,0:T(4,128)(2,1)S(1)} %get-tuple-element.28.refs_6_), channel_id=1, source_target_pairs={{0,2},{2,0},{4,6},{6,4},{8,10},{10,8},{12,14},{14,12},{1,3},{3,1},... | collective-permute-start | bytes 73736 | tf_op jit(solution)/shard_map/ppermute | solution.py:28
  35.5 2.4 %collective-permute-start.13 = (bf16[4,3072]{1,0:T(4,128)(2,1)S(1)}, bf16[4,3072]{1,0:T(4,128)(2,1)S(1)}, u32[]{:S(2)}, u32[]{:S(2)}) collective-permute-start(bf16[4,3072]{1,0:T(4,128)(2,1)S(1)} %get-tuple-element.29.kept_ref), channel_id=1, source_target_pairs={{0,1},{1,0},{2,3},{3,2},{4,5},{5,4},{6,7},{7,6},{8,9},{9,8},{10,11... | collective-permute-start | bytes 73736 | tf_op jit(solution)/shard_map/ppermute | solution.py:28
  35.5 3.3 %collective-permute-start.14 = (bf16[4,3072]{1,0:T(4,128)(2,1)S(1)}, bf16[4,3072]{1,0:T(4,128)(2,1)S(1)}, u32[]{:S(2)}, u32[]{:S(2)}) collective-permute-start(bf16[4,3072]{1,0:T(4,128)(2,1)S(1)} %get-tuple-element.28.refs_6_), channel_id=1, source_target_pairs={{0,3},{1,2},{2,1},{3,0},{4,7},{5,6},{6,5},{7,4},{8,11},{9,10},{10,... | collective-permute-start | bytes 73736 | tf_op jit(solution)/shard_map/ppermute | solution.py:33

commit v19 on v14

--- a/solution.py
+++ b/solution.py
@@ -338,7 +338,7 @@
 
 def make_local(wide):
     steps = steps_of(wide)
-    head_steps = [*steps[1:-2], *steps[:1], *steps[-2:]]
+    head_steps = [*steps[1:-2], steps[-1], steps[-2], steps[0]]
 
     def local(
         queries,
@@ -419,7 +419,7 @@
         line = [cross(x, wide, line_steps[0]), swap(x, "wide", wide, line_steps[1])]
         wider = max(x.shape[0] * half // HD, heads.shape[0])
         sent_heads = call(widen, shape((wider, HD), bf16), [heads], size=4 * wider * HD)
-        far_rows = swap(sent_heads, "wide", wide, steps[0])
+        far_rows = swap(sent_heads, "wide", wide, steps[-1])
         x, heads = call(
             stack_line,
             [shape((count, half), bf16), shape((2 * heads.shape[0], HD), bf16)],
@@ -463,7 +463,7 @@
             far=(2,),
         )
         taken = swap(given, "narrow", 2, 1)
-        far_heads = swap(heads, "wide", wide, steps[-1])
+        far_heads = swap(heads, "wide", wide, steps[0])
         terms = call(
             down,
             shape((count, half), f32),

time: 39.6 us -> 39.5 us (level)
    ppermute x9, waiting for transfers between devices: 0.03 us -> 0.53 us  [swap(): return lax.ppermute(block, axis, [(i, i ^ step) for i in range(count)])]
    ppermute x6, starting transfers between devices: 9.38 us -> 8.94 us  [cross(): return lax.ppermute(block, ('wide', 'narrow'), pairs)]
  transfers between devices with their start and end apart: 15 -> 15, of which waited for: 4 -> 5; matrix products, arithmetic and copies ran while one was open for 0% -> 0% of each run, Pallas kernels for 31% -> 31%
where the time goes in v19:
time: 39.5 us; the launch traced here: 39.3 us
  starting transfers between devices  17.5 us (44%)
  Pallas kernels  14.2 us (36%)
  waiting for transfers between devices  6.68 us (17%)
  between operations  0.83 us (2%)
    pallas_call x14, Pallas kernels, call(): pl.pallas_call(kernel, name=getattr(kernel, 'func', kernel).__name__, out...  14.2 us
    ppermute x6, starting transfers between devices, cross(): return lax.ppermute(block, ('wide', 'narrow'), pairs)  8.94 us
    ppermute x9, starting transfers between devices, swap(): return lax.ppermute(block, axis, [(i, i ^ step) for i in range(count)])  8.54 us
    ppermute x6, waiting for transfers between devices, cross(): return lax.ppermute(block, ('wide', 'narrow'), pairs)  6.15 us
  transfers between devices with their start and end apart: 15, of which 5 were waited for; matrix products, arithmetic and copies ran while one was open for 0% of the time, Pallas kernels for 31%

profile of v19, /device:TPU:0, one launch (start us, length us, event | category | flops | bytes accessed | tf_op | source)
XLA Modules:
  0.0 39.3 jit_solution(17870472744101022466)
XLA Ops:
  0.6 2.5 %collective-permute-start = (bf16[4,6144]{1,0:T(4,128)(2,1)}, bf16[4,6144]{1,0:T(4,128)(2,1)S(1)}, u32[]{:S(2)}, u32[]{:S(2)}) collective-permute-start(bf16[4,6144]{1,0:T(4,128)(2,1)} %tokens_ref.1), channel_id=1, source_target_pairs={{0,3},{1,2},{2,1},{3,0},{4,7},{5,6},{6,5},{7,4},{8,11},{9,10},{10,... | collective-permute-start | bytes 147464 | tf_op jit(solution)/shard_map/ppermute | solution.py:33
  3.1 1.0 %pack.1 = (bf16[128,128]{1,0:T(8,128)(2,1)S(1)}, bf16[4,6144]{1,0:T(4,128)(2,1)S(1)}, f32[1,6144]{1,0:T(1,128)S(1)}) custom-call(bf16[4,3072]{1,0:T(4,128)(2,1)} %far_query.1, bf16[4,512]{1,0:T(4,128)(2,1)} %far_key.1, bf16[4,512]{1,0:T(4,128)(2,1)} %far_value.1, bf16[4,6144]{1,0:T(4,128)(2,1)} %tokens_ref.1, f32[1,6144]{1,0:T(1,128)} %bitcast.5), custom_call_target="tpu_custom_call" | custom-call | bytes 100000 | tf_op jit(solution)/shard_map/pack/pallas_call | solution.py:59
  4.1 1.6 %collective-permute-start.3 = (bf16[192,128]{1,0:T(8,128)(2,1)S(1)}, bf16[192,128]{1,0:T(8,128)(2,1)S(1)}, u32[]{:S(2)}, u32[]{:S(2)}) collective-permute-start(bf16[192,128]{1,0:T(8,128)(2,1)S(1)} %widen.1), channel_id=1, source_target_pairs={{0,4},{2,6},{4,0},{6,2},{8,12},{10,14},{12,8},{14,10},{1,5},{3,7},... | collective-permute-start | bytes 147464 | tf_op jit(solution)/shard_map/ppermute | solution.py:28
  5.7 1.0 %shares.1.share.share_ref = f32[32,128]{1,0:T(8,128)S(1)} custom-call(s32[2,32]{1,0:T(2,128)} %bitcast.6, f32[2,32]{1,0:T(2,128)} %bitcast.7, bf16[128,128]{1,0:T(8,128)(2,1)S(1)} %get-tuple-element.18.refs_0_.heads.own_ref.own_heads, bf16[1,6144,1024]{2,1,0:T(8,128)(2,1)} %gate_ref.1, bf16[1,6144,1024]{2,1,0:T(8,128)(2,1)} %up_ref.1), custom_call_target="tpu_custom_call" | custom-call | bytes 100000 | tf_op jit(solution)/shard_map/shares/pallas_call | solution.py:59
  6.7 0.0 collective-permute-done.got_ref
  6.7 0.2 norm_both.1.own_ref
  6.9 3.0 %collective-permute-start.1 = (bf16[8,3072]{1,0:T(8,128)(2,1)S(1)}, bf16[8,3072]{1,0:T(8,128)(2,1)S(1)}, u32[]{:S(2)}, u32[]{:S(2)}) collective-permute-start(bf16[8,3072]{1,0:T(8,128)(2,1)S(1)} %norm_both.1.own_ref), channel_id=1, source_target_pairs={{0,13},{1,12},{2,15},{3,14},{4,9},{5,8},{6,11},{7,10},{8,5},{9,4},... | collective-permute-start | bytes 147464 | tf_op jit(solution)/shard_map/ppermute | solution.py:33
  9.9 0.0 collective-permute-start.2
  9.9 1.2 %collective-permute-start.4 = (bf16[8,3072]{1,0:T(8,128)(2,1)S(1)}, bf16[8,3072]{1,0:T(8,128)(2,1)S(1)}, u32[]{:S(2)}, u32[]{:S(2)}) collective-permute-start(bf16[8,3072]{1,0:T(8,128)(2,1)S(1)} %norm_both.1.own_ref), channel_id=1, source_target_pairs={{0,4},{2,6},{4,0},{6,2},{8,12},{10,14},{12,8},{14,10},{1,5},{3,7},... | collective-permute-start | bytes 147464 | tf_op jit(solution)/shard_map/ppermute | solution.py:28
  11.1 0.0 collective-permute-done.3.got_heads
  11.1 1.3 %collective-permute-done.1.last_ref = bf16[8,3072]{1,0:T(8,128)(2,1)S(1)} collective-permute-done((bf16[8,3072]{1,0:T(8,128)(2,1)S(1)}, bf16[8,3072]{1,0:T(8,128)(2,1)S(1)}, u32[]{:S(2)}, u32[]{:S(2)}) %collective-permute-start.1) | collective-permute-done | bytes 49184 | tf_op jit(solution)/shard_map/ppermute | solution.py:33
  12.4 3.1 %collective-permute-done.2.far_ref = bf16[8,3072]{1,0:T(8,128)(2,1)S(1)} collective-permute-done((bf16[8,3072]{1,0:T(8,128)(2,1)S(1)}, bf16[8,3072]{1,0:T(8,128)(2,1)S(1)}, u32[]{:S(2)}, u32[]{:S(2)}) %collective-permute-start.2) | collective-permute-done | bytes 49184 | tf_op jit(solution)/shard_map/ppermute | solution.py:33
  15.5 0.0 collective-permute-done.4.next_ref
  15.5 0.2 collective-permute-start.6
  15.7 1.4 %collective-permute-start.5 = (bf16[256,128]{1,0:T(8,128)(2,1)S(1)}, bf16[256,128]{1,0:T(8,128)(2,1)S(1)}, u32[]{:S(2)}, u32[]{:S(2)}) collective-permute-start(bf16[256,128]{1,0:T(8,128)(2,1)S(1)} %get-tuple-element.19.own_ref), channel_id=1, source_target_pairs={{0,8},{2,10},{4,12},{6,14},{8,0},{10,2},{12,4},{14,6},{1,9},{3,11}... | collective-permute-start | bytes 196616 | tf_op jit(solution)/shard_map/ppermute | solution.py:28
  17.1 0.0 collective-permute-done.6.other_ref
  17.1 0.0 slice-done
  17.1 0.0 slice-done.1
  17.1 0.0 slice-done.2
  17.1 4.8 %gate_all.1 = (bf16[32,1024]{1,0:T(8,128)(2,1)S(1)}, bf16[1024,3072]{1,0:T(8,128)(2,1)S(1)}, bf16[1024,3072]{1,0:T(8,128)(2,1)S(1)}) custom-call(bf16[32,3072]{1,0:T(8,128)(2,1)S(1)} %get-tuple-element.20.x_ref, bf16[32,3072]{1,0:T(8,128)(2,1)S(1)} %collective-permute-done.6.other_ref, bf16[1,6144,1024]{2,1,0:T(8,128)(2,1)S(1)} %bitcast.4, ...), custom_call_target="tpu_custom_call" | custom-call | flops 805306368 | bytes 37748736 | tf_op jit(solution)/shard_map/gate_all/pallas_call | solution.py:59
  21.9 0.5 %collective-permute-done.5.got_ref = bf16[256,128]{1,0:T(8,128)(2,1)S(1)} collective-permute-done((bf16[256,128]{1,0:T(8,128)(2,1)S(1)}, bf16[256,128]{1,0:T(8,128)(2,1)S(1)}, u32[]{:S(2)}, u32[]{:S(2)}) %collective-permute-start.5) | collective-permute-done | bytes 65568 | tf_op jit(solution)/shard_map/ppermute | solution.py:28
  22.4 0.0 copy-start.1
  22.5 0.0 copy-start.2
  22.5 0.0 copy-start.4
  22.5 0.0 copy-start.5
  22.5 1.3 %down.2.after = bf16[32,3072]{1,0:T(8,128)(2,1)S(1)} custom-call(bf16[32,1024]{1,0:T(8,128)(2,1)S(1)} %get-tuple-element.21.after.hidden_ref, bf16[1024,3072]{1,0:T(8,128)(2,1)S(1)} %get-tuple-element.23.down_ref, bf16[512,128]{1,0:T(8,128)(2,1)S(1)} %stack_after.1.after.near_ref.refs_0_), custom_call_target="tpu_custom_call" | custom-call | flops 201326592 | bytes 6291456 | tf_op jit(solution)/shard_map/down/pallas_call | solution.py:59
  23.8 0.0 collective-permute-start.8
  23.8 1.3 %collective-permute-start.7 = (bf16[512,128]{1,0:T(8,128)(2,1)S(1)}, bf16[512,128]{1,0:T(8,128)(2,1)S(1)}, u32[]{:S(2)}, u32[]{:S(2)}) collective-permute-start(bf16[512,128]{1,0:T(8,128)(2,1)S(1)} %stack_after.1.after.near_ref.refs_0_), channel_id=1, source_target_pairs={{0,2},{2,0},{4,6},{6,4},{8,10},{10,8},{12,14},{14,12},{1,3},{3,1},... | collective-permute-start | bytes 393224 | tf_op jit(solution)/shard_map/ppermute | solution.py:28
  25.1 1.3 %down.3.terms_ref = f32[32,3072]{1,0:T(8,128)S(1)} custom-call(bf16[32,1024]{1,0:T(8,128)(2,1)S(1)} %get-tuple-element.21.after.hidden_ref, bf16[1024,3072]{1,0:T(8,128)(2,1)S(1)} %get-tuple-element.22.down_ref, bf16[32,3072]{1,0:T(8,128)(2,1)S(1)} %down.2.after), custom_call_target="tpu_custom_call" | custom-call | flops 201326592 | bytes 6291456 | tf_op jit(solution)/shard_map/down/pallas_call | solution.py:59
  26.4 0.0 collective-permute-done.8.taken_ref
  26.4 2.0 %collective-permute-start.10 = (bf16[8,3072]{1,0:T(8,128)(2,1)S(1)}, bf16[8,3072]{1,0:T(8,128)(2,1)S(1)}, u32[]{:S(2)}, u32[]{:S(2)}) collective-permute-start(bf16[8,3072]{1,0:T(8,128)(2,1)S(1)} %get-tuple-element.26), channel_id=1, source_target_pairs={{0,13},{1,12},{2,15},{3,14},{4,9},{5,8},{6,11},{7,10},{8,5},{9,4},... | collective-permute-start | bytes 147464 | tf_op jit(solution)/shard_map/ppermute | solution.py:33
  28.4 0.2 collective-permute-start.11
  28.6 2.0 %collective-permute-start.9 = (bf16[8,3072]{1,0:T(8,128)(2,1)S(1)}, bf16[8,3072]{1,0:T(8,128)(2,1)S(1)}, u32[]{:S(2)}, u32[]{:S(2)}) collective-permute-start(bf16[8,3072]{1,0:T(8,128)(2,1)S(1)} %get-tuple-element.25), channel_id=1, source_target_pairs={{0,4},{2,6},{4,0},{6,2},{8,12},{10,14},{12,8},{14,10},{1,5},{3,7},... | collective-permute-start | bytes 147464 | tf_op jit(solution)/shard_map/ppermute | solution.py:28
  30.6 0.0 collective-permute-done.7.far_ref.refs_1_
  30.6 0.0 copy-done.4
  30.6 0.0 copy-done.5
  30.6 2.2 %attend.1.refs_4_.refs_7_ = f32[72,128]{1,0:T(8,128)S(1)} custom-call(bf16[512,128]{1,0:T(8,128)(2,1)S(1)} %stack_after.1.after.near_ref.refs_0_, bf16[512,128]{1,0:T(8,128)(2,1)S(1)} %collective-permute-done.7.far_ref.refs_1_, bf16[4,512,512]{2,1,0:T(8,128)(2,1)S(1)} %copy-done.1, bf16[4,512,512]{2,1,0:T(8,128)(2,1)S(1)} %copy-done.2, s32[4]{0:T(128)S(1)} %copy-done.4, ...), custom_call_target="tpu_custom_call" | custom-call | flops 12582912 | bytes 2097152 | tf_op jit(solution)/shard_map/attend/pallas_call | solution.py:59
  32.8 0.0 collective-permute-done.10.refs_2_
  32.9 1.5 %collective-permute-done.11.refs_3_ = bf16[8,3072]{1,0:T(8,128)(2,1)S(1)} collective-permute-done((bf16[8,3072]{1,0:T(8,128)(2,1)S(1)}, bf16[8,3072]{1,0:T(8,128)(2,1)S(1)}, u32[]{:S(2)}, u32[]{:S(2)}) %collective-permute-start.11) | collective-permute-done | bytes 49184 | tf_op jit(solution)/shard_map/ppermute | solution.py:33
  34.4 0.0 collective-permute-done.9.refs_1_
  34.4 0.9 %collective-permute-start.12 = (bf16[4,3072]{1,0:T(4,128)(2,1)S(1)}, bf16[4,3072]{1,0:T(4,128)(2,1)S(1)}, u32[]{:S(2)}, u32[]{:S(2)}) collective-permute-start(bf16[4,3072]{1,0:T(4,128)(2,1)S(1)} %get-tuple-element.28.refs_6_), channel_id=1, source_target_pairs={{0,2},{2,0},{4,6},{6,4},{8,10},{10,8},{12,14},{14,12},{1,3},{3,1},... | collective-permute-start | bytes 73736 | tf_op jit(solution)/shard_map/ppermute | solution.py:28
  35.3 0.0 collective-permute-start.13
  35.3 1.3 %collective-permute-start.14 = (bf16[4,3072]{1,0:T(4,128)(2,1)S(1)}, bf16[4,3072]{1,0:T(4,128)(2,1)S(1)}, u32[]{:S(2)}, u32[]{:S(2)}) collective-permute-start(bf16[4,3072]{1,0:T(4,128)(2,1)S(1)} %get-tuple-element.28.refs_6_), channel_id=1, source_target_pairs={{0,3},{1,2},{2,1},{3,0},{4,7},{5,6},{6,5},{7,4},{8,11},{9,10},{10,... | collective-permute-start | bytes 73736 | tf_op jit(solution)/shard_map/ppermute | solution.py:33
  36.6 1.8 %attend_last.1.after = bf16[4,3072]{1,0:T(4,128)(2,1)} custom-call(bf16[512,128]{1,0:T(8,128)(2,1)S(1)} %stack_after.1.after.near_ref.refs_0_, bf16[512,128]{1,0:T(8,128)(2,1)S(1)} %collective-permute-done.7.far_ref.refs_1_, bf16[4,512,512]{2,1,0:T(8,128)(2,1)S(1)} %copy-done.1, bf16[4,512,512]{2,1,0:T(8,128)(2,1)S(1)} %copy-done.2, s32[4]{0:T(128)S(1)} %copy-done.4, ...), custom_call_target="tpu_custom_call" | custom-call | flops 12582912 | bytes 2097152 | tf_op jit(solution)/shard_map/attend_last/pallas_call | solution.py:59
  38.4 0.0 collective-permute-done.12.taken_ref
  38.4 0.0 collective-permute-done.13.other_kept
  38.4 0.1 collective-permute-done.14.other_taken
  38.6 0.7 %finish.1 = bf16[4,6144]{1,0:T(4,128)(2,1)} custom-call(bf16[4,3072]{1,0:T(4,128)(2,1)S(1)} %get-tuple-element.29.kept_ref, bf16[4,3072]{1,0:T(4,128)(2,1)S(1)} %collective-permute-done.12.taken_ref, bf16[4,3072]{1,0:T(4,128)(2,1)S(1)} %collective-permute-done.13.other_kept, bf16[4,3072]{1,0:T(4,128)(2,1)S(1)} %collective-permute-done.14.other_taken, ...), custom_call_target="tpu_custom_call" | custom-call | bytes 98304 | tf_op jit(solution)/shard_map/finish/pallas_call | solution.py:59
  (15 shorter events, 0.1 us)
Async XLA Ops:
  0.6 6.1 %collective-permute-start = (bf16[4,6144]{1,0:T(4,128)(2,1)}, bf16[4,6144]{1,0:T(4,128)(2,1)S(1)}, u32[]{:S(2)}, u32[]{:S(2)}) collective-permute-start(bf16[4,6144]{1,0:T(4,128)(2,1)} %tokens_ref.1), channel_id=1, source_target_pairs={{0,3},{1,2},{2,1},{3,0},{4,7},{5,6},{6,5},{7,4},{8,11},{9,10},{10,... | collective-permute-start | bytes 147464 | tf_op jit(solution)/shard_map/ppermute | solution.py:33
  4.1 7.0 %collective-permute-start.3 = (bf16[192,128]{1,0:T(8,128)(2,1)S(1)}, bf16[192,128]{1,0:T(8,128)(2,1)S(1)}, u32[]{:S(2)}, u32[]{:S(2)}) collective-permute-start(bf16[192,128]{1,0:T(8,128)(2,1)S(1)} %widen.1), channel_id=1, source_target_pairs={{0,4},{2,6},{4,0},{6,2},{8,12},{10,14},{12,8},{14,10},{1,5},{3,7},... | collective-permute-start | bytes 147464 | tf_op jit(solution)/shard_map/ppermute | solution.py:28
  5.7 11.4 %slice-start = ((s8[12582912]{0:T(1024)(128)(4,1)}), s8[4194304]{0:T(1024)(128)(4,1)S(1)}, s32[]{:S(2)}) async-start(s8[12582912]{0:T(1024)(128)(4,1)} %bitcast.3), calls=%async_computation | async-start | bytes 8388608
  5.7 11.4 %slice-start.1 = ((s8[12582912]{0:T(1024)(128)(4,1)}), s8[4194304]{0:T(1024)(128)(4,1)S(1)}, s32[]{:S(2)}) async-start(s8[12582912]{0:T(1024)(128)(4,1)} %bitcast.3), calls=%async_computation.1 | async-start | bytes 8388608
  5.7 11.4 %slice-start.2 = ((s8[12582912]{0:T(1024)(128)(4,1)}), s8[4194304]{0:T(1024)(128)(4,1)S(1)}, s32[]{:S(2)}) async-start(s8[12582912]{0:T(1024)(128)(4,1)} %bitcast.3), calls=%async_computation.2 | async-start | bytes 8388608
  5.7 11.4 %copy-start = (bf16[1,6144,1024]{2,1,0:T(8,128)(2,1)S(1)}, bf16[1,6144,1024]{2,1,0:T(8,128)(2,1)}, u32[]{:S(2)}) copy-start(bf16[1,6144,1024]{2,1,0:T(8,128)(2,1)} %up_ref.1) | copy-start | bytes 37748740
  6.9 5.5 %collective-permute-start.1 = (bf16[8,3072]{1,0:T(8,128)(2,1)S(1)}, bf16[8,3072]{1,0:T(8,128)(2,1)S(1)}, u32[]{:S(2)}, u32[]{:S(2)}) collective-permute-start(bf16[8,3072]{1,0:T(8,128)(2,1)S(1)} %norm_both.1.own_ref), channel_id=1, source_target_pairs={{0,13},{1,12},{2,15},{3,14},{4,9},{5,8},{6,11},{7,10},{8,5},{9,4},... | collective-permute-start | bytes 147464 | tf_op jit(solution)/shard_map/ppermute | solution.py:33
  9.9 5.6 %collective-permute-start.2 = (bf16[8,3072]{1,0:T(8,128)(2,1)S(1)}, bf16[8,3072]{1,0:T(8,128)(2,1)S(1)}, u32[]{:S(2)}, u32[]{:S(2)}) collective-permute-start(bf16[8,3072]{1,0:T(8,128)(2,1)S(1)} %norm_both.1.own_ref), channel_id=1, source_target_pairs={{0,9},{1,8},{2,11},{3,10},{4,13},{5,12},{6,15},{7,14},{8,1},{9,0},... | collective-permute-start | bytes 147464 | tf_op jit(solution)/shard_map/ppermute | solution.py:33
  9.9 5.6 %collective-permute-start.4 = (bf16[8,3072]{1,0:T(8,128)(2,1)S(1)}, bf16[8,3072]{1,0:T(8,128)(2,1)S(1)}, u32[]{:S(2)}, u32[]{:S(2)}) collective-permute-start(bf16[8,3072]{1,0:T(8,128)(2,1)S(1)} %norm_both.1.own_ref), channel_id=1, source_target_pairs={{0,4},{2,6},{4,0},{6,2},{8,12},{10,14},{12,8},{14,10},{1,5},{3,7},... | collective-permute-start | bytes 147464 | tf_op jit(solution)/shard_map/ppermute | solution.py:28
  15.5 1.6 %collective-permute-start.6 = (bf16[32,3072]{1,0:T(8,128)(2,1)S(1)}, bf16[32,3072]{1,0:T(8,128)(2,1)S(1)}, u32[]{:S(2)}, u32[]{:S(2)}) collective-permute-start(bf16[32,3072]{1,0:T(8,128)(2,1)S(1)} %get-tuple-element.20.x_ref), channel_id=1, source_target_pairs={{0,1},{1,0},{2,3},{3,2},{4,5},{5,4},{6,7},{7,6},{8,9},{9,8},{10,11... | collective-permute-start | bytes 589832 | tf_op jit(solution)/shard_map/ppermute | solution.py:28
  15.7 6.7 %collective-permute-start.5 = (bf16[256,128]{1,0:T(8,128)(2,1)S(1)}, bf16[256,128]{1,0:T(8,128)(2,1)S(1)}, u32[]{:S(2)}, u32[]{:S(2)}) collective-permute-start(bf16[256,128]{1,0:T(8,128)(2,1)S(1)} %get-tuple-element.19.own_ref), channel_id=1, source_target_pairs={{0,8},{2,10},{4,12},{6,14},{8,0},{10,2},{12,4},{14,6},{1,9},{3,11}... | collective-permute-start | bytes 196616 | tf_op jit(solution)/shard_map/ppermute | solution.py:28
  22.4 8.2 %copy-start.1 = (bf16[4,512,512]{2,1,0:T(8,128)(2,1)S(1)}, bf16[4,512,512]{2,1,0:T(8,128)(2,1)}, u32[]{:S(2)}) copy-start(bf16[4,512,512]{2,1,0:T(8,128)(2,1)} %refs_2_.3) | copy-start | bytes 6291460
  22.5 8.2 %copy-start.2 = (bf16[4,512,512]{2,1,0:T(8,128)(2,1)S(1)}, bf16[4,512,512]{2,1,0:T(8,128)(2,1)}, u32[]{:S(2)}) copy-start(bf16[4,512,512]{2,1,0:T(8,128)(2,1)} %refs_3_.1) | copy-start | bytes 6291460
  22.5 8.2 %copy-start.4 = (s32[4]{0:T(128)S(1)}, s32[4]{0:T(128)}, u32[]{:S(2)}) copy-start(s32[4]{0:T(128)} %refs_4_.1) | copy-start | bytes 52
  22.5 8.1 %copy-start.5 = (s32[4]{0:T(128)S(1)}, s32[4]{0:T(128)}, u32[]{:S(2)}) copy-start(s32[4]{0:T(128)} %refs_5_.1) | copy-start | bytes 52
  23.8 2.6 %collective-permute-start.8 = (bf16[32,3072]{1,0:T(8,128)(2,1)S(1)}, bf16[32,3072]{1,0:T(8,128)(2,1)S(1)}, u32[]{:S(2)}, u32[]{:S(2)}) collective-permute-start(bf16[32,3072]{1,0:T(8,128)(2,1)S(1)} %down.2.after), channel_id=1, source_target_pairs={{0,1},{1,0},{2,3},{3,2},{4,5},{5,4},{6,7},{7,6},{8,9},{9,8},{10,11... | collective-permute-start | bytes 589832 | tf_op jit(solution)/shard_map/ppermute | solution.py:28
  23.8 6.8 %collective-permute-start.7 = (bf16[512,128]{1,0:T(8,128)(2,1)S(1)}, bf16[512,128]{1,0:T(8,128)(2,1)S(1)}, u32[]{:S(2)}, u32[]{:S(2)}) collective-permute-start(bf16[512,128]{1,0:T(8,128)(2,1)S(1)} %stack_after.1.after.near_ref.refs_0_), channel_id=1, source_target_pairs={{0,2},{2,0},{4,6},{6,4},{8,10},{10,8},{12,14},{14,12},{1,3},{3,1},... | collective-permute-start | bytes 393224 | tf_op jit(solution)/shard_map/ppermute | solution.py:28
  26.4 12.2 %copy-start.3 = (bf16[4,6144]{1,0:T(4,128)(2,1)S(1)}, bf16[4,6144]{1,0:T(4,128)(2,1)}, u32[]{:S(2)}) copy-start(bf16[4,6144]{1,0:T(4,128)(2,1)} %tokens_ref.1) | copy-start | bytes 147460
  26.4 6.4 %collective-permute-start.10 = (bf16[8,3072]{1,0:T(8,128)(2,1)S(1)}, bf16[8,3072]{1,0:T(8,128)(2,1)S(1)}, u32[]{:S(2)}, u32[]{:S(2)}) collective-permute-start(bf16[8,3072]{1,0:T(8,128)(2,1)S(1)} %get-tuple-element.26), channel_id=1, source_target_pairs={{0,13},{1,12},{2,15},{3,14},{4,9},{5,8},{6,11},{7,10},{8,5},{9,4},... | collective-permute-start | bytes 147464 | tf_op jit(solution)/shard_map/ppermute | solution.py:33
  28.4 6.0 %collective-permute-start.11 = (bf16[8,3072]{1,0:T(8,128)(2,1)S(1)}, bf16[8,3072]{1,0:T(8,128)(2,1)S(1)}, u32[]{:S(2)}, u32[]{:S(2)}) collective-permute-start(bf16[8,3072]{1,0:T(8,128)(2,1)S(1)} %get-tuple-element.27.after), channel_id=1, source_target_pairs={{0,9},{1,8},{2,11},{3,10},{4,13},{5,12},{6,15},{7,14},{8,1},{9,0},... | collective-permute-start | bytes 147464 | tf_op jit(solution)/shard_map/ppermute | solution.py:33
  28.6 5.8 %collective-permute-start.9 = (bf16[8,3072]{1,0:T(8,128)(2,1)S(1)}, bf16[8,3072]{1,0:T(8,128)(2,1)S(1)}, u32[]{:S(2)}, u32[]{:S(2)}) collective-permute-start(bf16[8,3072]{1,0:T(8,128)(2,1)S(1)} %get-tuple-element.25), channel_id=1, source_target_pairs={{0,4},{2,6},{4,0},{6,2},{8,12},{10,14},{12,8},{14,10},{1,5},{3,7},... | collective-permute-start | bytes 147464 | tf_op jit(solution)/shard_map/ppermute | solution.py:28
  34.4 4.0 %collective-permute-start.12 = (bf16[4,3072]{1,0:T(4,128)(2,1)S(1)}, bf16[4,3072]{1,0:T(4,128)(2,1)S(1)}, u32[]{:S(2)}, u32[]{:S(2)}) collective-permute-start(bf16[4,3072]{1,0:T(4,128)(2,1)S(1)} %get-tuple-element.28.refs_6_), channel_id=1, source_target_pairs={{0,2},{2,0},{4,6},{6,4},{8,10},{10,8},{12,14},{14,12},{1,3},{3,1},... | collective-permute-start | bytes 73736 | tf_op jit(solution)/shard_map/ppermute | solution.py:28
  35.3 3.1 %collective-permute-start.13 = (bf16[4,3072]{1,0:T(4,128)(2,1)S(1)}, bf16[4,3072]{1,0:T(4,128)(2,1)S(1)}, u32[]{:S(2)}, u32[]{:S(2)}) collective-permute-start(bf16[4,3072]{1,0:T(4,128)(2,1)S(1)} %get-tuple-element.29.kept_ref), channel_id=1, source_target_pairs={{0,1},{1,0},{2,3},{3,2},{4,5},{5,4},{6,7},{7,6},{8,9},{9,8},{10,11... | collective-permute-start | bytes 73736 | tf_op jit(solution)/shard_map/ppermute | solution.py:28
  35.3 3.3 %collective-permute-start.14 = (bf16[4,3072]{1,0:T(4,128)(2,1)S(1)}, bf16[4,3072]{1,0:T(4,128)(2,1)S(1)}, u32[]{:S(2)}, u32[]{:S(2)}) collective-permute-start(bf16[4,3072]{1,0:T(4,128)(2,1)S(1)} %get-tuple-element.28.refs_6_), channel_id=1, source_target_pairs={{0,3},{1,2},{2,1},{3,0},{4,7},{5,6},{6,5},{7,4},{8,11},{9,10},{10,... | collective-permute-start | bytes 73736 | tf_op jit(solution)/shard_map/ppermute | solution.py:33

commit v20 on v18

--- a/solution.py
+++ b/solution.py
@@ -245,7 +245,7 @@
     sent_ref[...] = total[kept:].astype(jnp.bfloat16)
 
 
-def finish(flip, kept_ref, taken_ref, other_kept, other_taken, tokens_ref, after, out_ref):
+def finish(flip, kept_ref, taken_ref, other_taken, other_kept, tokens_ref, after, out_ref):
     half = kept_ref.shape[1]
     first = side_of(flip) == 0
     own = kept_ref[...].astype(jnp.float32) + taken_ref[...].astype(jnp.float32)
@@ -512,7 +512,7 @@
         context = call(
             functools.partial(attend_last, head_steps, late_slots, heads_local),
             shape(queries.shape, bf16),
-            [heads, far_heads, *caches, sent, early],
+            [heads, far_heads, *caches, terms, early],
             [
                 pltpu.VMEM((len(late_slots) * heads_local, HD), f32),
                 pltpu.VMEM((slots * heads_local, HD), f32),
@@ -527,7 +527,7 @@
         mixed_out = call(
             functools.partial(finish, steps[-1]),
             shape((rows, width), bf16),
-            [terms, *taken, other_kept, other_taken, tokens, distant(context)],
+            [terms, *taken, other_taken, other_kept, tokens, distant(context)],
             size=terms.size * 8,
             far=(5,),
         )

time: 39.6 us -> 39.8 us (level)
    ppermute x9, starting transfers between devices: 6.05 us -> 6.61 us  [swap(): return lax.ppermute(block, axis, [(i, i ^ step) for i in range(count)])]
    ppermute x6, starting transfers between devices: 10.3 us -> 9.76 us  [cross(): return lax.ppermute(block, ('wide', 'narrow'), pairs)]
where the time goes in v20:
time: 39.8 us; the launch traced here: 39.6 us
  starting transfers between devices  16.4 us (41%)
  Pallas kernels  14.2 us (36%)
  waiting for transfers between devices  8.14 us (20%)
  between operations  0.83 us (2%)
    pallas_call x14, Pallas kernels, call(): pl.pallas_call(kernel, name=getattr(kernel, 'func', kernel).__name__, out...  14.2 us
    ppermute x6, starting transfers between devices, cross(): return lax.ppermute(block, ('wide', 'narrow'), pairs)  9.76 us
    ppermute x9, starting transfers between devices, swap(): return lax.ppermute(block, axis, [(i, i ^ step) for i in range(count)])  6.61 us
    ppermute x9, waiting for transfers between devices, swap(): return lax.ppermute(block, axis, [(i, i ^ step) for i in range(count)])  5.19 us
    ppermute x6, waiting for transfers between devices, cross(): return lax.ppermute(block, ('wide', 'narrow'), pairs)  2.95 us
  transfers between devices with their start and end apart: 15, of which 5 were waited for; matrix products, arithmetic and copies ran while one was open for 0% of the time, Pallas kernels for 31%

profile of v20, /device:TPU:0, one launch (start us, length us, event | category | flops | bytes accessed | tf_op | source)
XLA Modules:
  0.0 39.6 jit_solution(14596427778046334817)
XLA Ops:
  0.6 2.5 %collective-permute-start = (bf16[4,6144]{1,0:T(4,128)(2,1)}, bf16[4,6144]{1,0:T(4,128)(2,1)S(1)}, u32[]{:S(2)}, u32[]{:S(2)}) collective-permute-start(bf16[4,6144]{1,0:T(4,128)(2,1)} %tokens_ref.1), channel_id=1, source_target_pairs={{0,3},{1,2},{2,1},{3,0},{4,7},{5,6},{6,5},{7,4},{8,11},{9,10},{10,... | collective-permute-start | bytes 147464 | tf_op jit(solution)/shard_map/ppermute | solution.py:33
  3.1 1.0 %pack.1 = (bf16[128,128]{1,0:T(8,128)(2,1)S(1)}, bf16[4,6144]{1,0:T(4,128)(2,1)S(1)}, f32[1,6144]{1,0:T(1,128)S(1)}) custom-call(bf16[4,3072]{1,0:T(4,128)(2,1)} %far_query.1, bf16[4,512]{1,0:T(4,128)(2,1)} %far_key.1, bf16[4,512]{1,0:T(4,128)(2,1)} %far_value.1, bf16[4,6144]{1,0:T(4,128)(2,1)} %tokens_ref.1, f32[1,6144]{1,0:T(1,128)} %bitcast.5), custom_call_target="tpu_custom_call" | custom-call | bytes 100000 | tf_op jit(solution)/shard_map/pack/pallas_call | solution.py:59
  4.1 0.6 %collective-permute-start.3 = (bf16[192,128]{1,0:T(8,128)(2,1)S(1)}, bf16[192,128]{1,0:T(8,128)(2,1)S(1)}, u32[]{:S(2)}, u32[]{:S(2)}) collective-permute-start(bf16[192,128]{1,0:T(8,128)(2,1)S(1)} %widen.1), channel_id=1, source_target_pairs={{0,2},{2,0},{4,6},{6,4},{8,10},{10,8},{12,14},{14,12},{1,3},{3,1},... | collective-permute-start | bytes 147464 | tf_op jit(solution)/shard_map/ppermute | solution.py:28
  4.7 1.0 %shares.1.share.share_ref = f32[32,128]{1,0:T(8,128)S(1)} custom-call(s32[2,32]{1,0:T(2,128)} %bitcast.6, f32[2,32]{1,0:T(2,128)} %bitcast.7, bf16[128,128]{1,0:T(8,128)(2,1)S(1)} %get-tuple-element.18.refs_0_.heads.own_ref.own_heads, bf16[1,6144,1024]{2,1,0:T(8,128)(2,1)} %gate_ref.1, bf16[1,6144,1024]{2,1,0:T(8,128)(2,1)} %up_ref.1), custom_call_target="tpu_custom_call" | custom-call | bytes 100000 | tf_op jit(solution)/shard_map/shares/pallas_call | solution.py:59
  5.7 0.0 collective-permute-done.got_ref
  5.7 0.2 norm_both.1.own_ref
  5.9 4.0 %collective-permute-start.1 = (bf16[8,3072]{1,0:T(8,128)(2,1)S(1)}, bf16[8,3072]{1,0:T(8,128)(2,1)S(1)}, u32[]{:S(2)}, u32[]{:S(2)}) collective-permute-start(bf16[8,3072]{1,0:T(8,128)(2,1)S(1)} %norm_both.1.own_ref), channel_id=1, source_target_pairs={{0,13},{1,12},{2,15},{3,14},{4,9},{5,8},{6,11},{7,10},{8,5},{9,4},... | collective-permute-start | bytes 147464 | tf_op jit(solution)/shard_map/ppermute | solution.py:33
  9.9 0.0 collective-permute-start.2
  9.9 0.4 collective-permute-start.4
  10.2 0.0 collective-permute-done.3.got_heads
  10.2 1.8 %collective-permute-done.1.last_ref = bf16[8,3072]{1,0:T(8,128)(2,1)S(1)} collective-permute-done((bf16[8,3072]{1,0:T(8,128)(2,1)S(1)}, bf16[8,3072]{1,0:T(8,128)(2,1)S(1)}, u32[]{:S(2)}, u32[]{:S(2)}) %collective-permute-start.1) | collective-permute-done | bytes 49184 | tf_op jit(solution)/shard_map/ppermute | solution.py:33
  12.1 3.0 %collective-permute-done.2.far_ref = bf16[8,3072]{1,0:T(8,128)(2,1)S(1)} collective-permute-done((bf16[8,3072]{1,0:T(8,128)(2,1)S(1)}, bf16[8,3072]{1,0:T(8,128)(2,1)S(1)}, u32[]{:S(2)}, u32[]{:S(2)}) %collective-permute-start.2) | collective-permute-done | bytes 49184 | tf_op jit(solution)/shard_map/ppermute | solution.py:28
  15.0 0.0 collective-permute-done.4.next_ref
  15.0 0.1 collective-permute-start.6
  15.2 1.6 %collective-permute-start.5 = (bf16[256,128]{1,0:T(8,128)(2,1)S(1)}, bf16[256,128]{1,0:T(8,128)(2,1)S(1)}, u32[]{:S(2)}, u32[]{:S(2)}) collective-permute-start(bf16[256,128]{1,0:T(8,128)(2,1)S(1)} %get-tuple-element.19.own_ref), channel_id=1, source_target_pairs={{0,8},{2,10},{4,12},{6,14},{8,0},{10,2},{12,4},{14,6},{1,9},{3,11}... | collective-permute-start | bytes 196616 | tf_op jit(solution)/shard_map/ppermute | solution.py:28
  16.8 0.0 collective-permute-done.6.other_ref
  16.8 0.0 slice-done
  16.8 0.0 slice-done.1
  16.8 0.0 slice-done.2
  16.8 0.0 copy-done
  16.8 4.8 %gate_all.1 = (bf16[32,1024]{1,0:T(8,128)(2,1)S(1)}, bf16[1024,3072]{1,0:T(8,128)(2,1)S(1)}, bf16[1024,3072]{1,0:T(8,128)(2,1)S(1)}) custom-call(bf16[32,3072]{1,0:T(8,128)(2,1)S(1)} %get-tuple-element.20.x_ref, bf16[32,3072]{1,0:T(8,128)(2,1)S(1)} %collective-permute-done.6.other_ref, bf16[1,6144,1024]{2,1,0:T(8,128)(2,1)S(1)} %bitcast.4, ...), custom_call_target="tpu_custom_call" | custom-call | flops 805306368 | bytes 37748736 | tf_op jit(solution)/shard_map/gate_all/pallas_call | solution.py:59
  21.6 0.3 collective-permute-done.5.got_ref
  22.0 0.0 copy-start.1
  22.0 0.0 copy-start.2
  22.0 0.0 copy-start.4
  22.0 0.0 copy-start.5
  22.0 1.3 %down.2.after = bf16[32,3072]{1,0:T(8,128)(2,1)S(1)} custom-call(bf16[32,1024]{1,0:T(8,128)(2,1)S(1)} %get-tuple-element.21.after.hidden_ref, bf16[1024,3072]{1,0:T(8,128)(2,1)S(1)} %get-tuple-element.23.down_ref, bf16[512,128]{1,0:T(8,128)(2,1)S(1)} %stack_after.1.after.near_ref.refs_0_), custom_call_target="tpu_custom_call" | custom-call | flops 201326592 | bytes 6291456 | tf_op jit(solution)/shard_map/down/pallas_call | solution.py:59
  23.3 0.0 collective-permute-start.8
  23.3 1.1 %collective-permute-start.7 = (bf16[512,128]{1,0:T(8,128)(2,1)S(1)}, bf16[512,128]{1,0:T(8,128)(2,1)S(1)}, u32[]{:S(2)}, u32[]{:S(2)}) collective-permute-start(bf16[512,128]{1,0:T(8,128)(2,1)S(1)} %stack_after.1.after.near_ref.refs_0_), channel_id=1, source_target_pairs={{0,4},{2,6},{4,0},{6,2},{8,12},{10,14},{12,8},{14,10},{1,5},{3,7},... | collective-permute-start | bytes 393224 | tf_op jit(solution)/shard_map/ppermute | solution.py:28
  24.4 1.3 %down.3.terms_ref = f32[32,3072]{1,0:T(8,128)S(1)} custom-call(bf16[32,1024]{1,0:T(8,128)(2,1)S(1)} %get-tuple-element.21.after.hidden_ref, bf16[1024,3072]{1,0:T(8,128)(2,1)S(1)} %get-tuple-element.22.down_ref, bf16[32,3072]{1,0:T(8,128)(2,1)S(1)} %down.2.after), custom_call_target="tpu_custom_call" | custom-call | flops 201326592 | bytes 6291456 | tf_op jit(solution)/shard_map/down/pallas_call | solution.py:59
  25.7 0.0 collective-permute-done.8.taken_ref
  25.8 1.4 %collective-permute-start.10 = (bf16[8,3072]{1,0:T(8,128)(2,1)S(1)}, bf16[8,3072]{1,0:T(8,128)(2,1)S(1)}, u32[]{:S(2)}, u32[]{:S(2)}) collective-permute-start(bf16[8,3072]{1,0:T(8,128)(2,1)S(1)} %get-tuple-element.26), channel_id=1, source_target_pairs={{0,13},{1,12},{2,15},{3,14},{4,9},{5,8},{6,11},{7,10},{8,5},{9,4},... | collective-permute-start | bytes 147464 | tf_op jit(solution)/shard_map/ppermute | solution.py:33
  27.1 1.0 %collective-permute-start.11 = (bf16[8,3072]{1,0:T(8,128)(2,1)S(1)}, bf16[8,3072]{1,0:T(8,128)(2,1)S(1)}, u32[]{:S(2)}, u32[]{:S(2)}) collective-permute-start(bf16[8,3072]{1,0:T(8,128)(2,1)S(1)} %get-tuple-element.27.after), channel_id=1, source_target_pairs={{0,8},{2,10},{4,12},{6,14},{8,0},{10,2},{12,4},{14,6},{1,9},{3,11}... | collective-permute-start | bytes 147464 | tf_op jit(solution)/shard_map/ppermute | solution.py:28
  28.1 1.6 %collective-permute-start.9 = (bf16[8,3072]{1,0:T(8,128)(2,1)S(1)}, bf16[8,3072]{1,0:T(8,128)(2,1)S(1)}, u32[]{:S(2)}, u32[]{:S(2)}) collective-permute-start(bf16[8,3072]{1,0:T(8,128)(2,1)S(1)} %get-tuple-element.25), channel_id=1, source_target_pairs={{0,5},{1,4},{2,7},{3,6},{4,1},{5,0},{6,3},{7,2},{8,13},{9,12},{10,... | collective-permute-start | bytes 147464 | tf_op jit(solution)/shard_map/ppermute | solution.py:33
  29.7 0.0 collective-permute-done.7.far_ref.refs_1_
  29.7 0.0 copy-done.2
  29.7 2.2 %attend.1.refs_4_.refs_7_ = f32[72,128]{1,0:T(8,128)S(1)} custom-call(bf16[512,128]{1,0:T(8,128)(2,1)S(1)} %stack_after.1.after.near_ref.refs_0_, bf16[512,128]{1,0:T(8,128)(2,1)S(1)} %collective-permute-done.7.far_ref.refs_1_, bf16[4,512,512]{2,1,0:T(8,128)(2,1)S(1)} %copy-done.1, bf16[4,512,512]{2,1,0:T(8,128)(2,1)S(1)} %copy-done.2, s32[4]{0:T(128)S(1)} %copy-done.4, ...), custom_call_target="tpu_custom_call" | custom-call | flops 12582912 | bytes 2097152 | tf_op jit(solution)/shard_map/attend/pallas_call | solution.py:59
  31.9 0.0 collective-permute-done.10.refs_2_
  31.9 1.9 %collective-permute-done.11.refs_3_ = bf16[8,3072]{1,0:T(8,128)(2,1)S(1)} collective-permute-done((bf16[8,3072]{1,0:T(8,128)(2,1)S(1)}, bf16[8,3072]{1,0:T(8,128)(2,1)S(1)}, u32[]{:S(2)}, u32[]{:S(2)}) %collective-permute-start.11) | collective-permute-done | bytes 49184 | tf_op jit(solution)/shard_map/ppermute | solution.py:28
  33.8 0.0 collective-permute-done.9.refs_1_
  33.8 1.6 %collective-permute-start.12 = (bf16[4,3072]{1,0:T(4,128)(2,1)S(1)}, bf16[4,3072]{1,0:T(4,128)(2,1)S(1)}, u32[]{:S(2)}, u32[]{:S(2)}) collective-permute-start(bf16[4,3072]{1,0:T(4,128)(2,1)S(1)} %get-tuple-element.29), channel_id=1, source_target_pairs={{0,2},{2,0},{4,6},{6,4},{8,10},{10,8},{12,14},{14,12},{1,3},{3,1},... | collective-permute-start | bytes 73736 | tf_op jit(solution)/shard_map/ppermute | solution.py:28
  35.5 0.0 collective-permute-start.13
  35.5 0.6 %collective-permute-start.14 = (bf16[4,3072]{1,0:T(4,128)(2,1)S(1)}, bf16[4,3072]{1,0:T(4,128)(2,1)S(1)}, u32[]{:S(2)}, u32[]{:S(2)}) collective-permute-start(bf16[4,3072]{1,0:T(4,128)(2,1)S(1)} %get-tuple-element.28.refs_6_.kept_ref), channel_id=1, source_target_pairs={{0,1},{1,0},{2,3},{3,2},{4,5},{5,4},{6,7},{7,6},{8,9},{9,8},{10,11... | collective-permute-start | bytes 73736 | tf_op jit(solution)/shard_map/ppermute | solution.py:28
  36.0 1.8 %attend_last.1.after = bf16[4,3072]{1,0:T(4,128)(2,1)} custom-call(bf16[512,128]{1,0:T(8,128)(2,1)S(1)} %stack_after.1.after.near_ref.refs_0_, bf16[512,128]{1,0:T(8,128)(2,1)S(1)} %collective-permute-done.7.far_ref.refs_1_, bf16[4,512,512]{2,1,0:T(8,128)(2,1)S(1)} %copy-done.1, bf16[4,512,512]{2,1,0:T(8,128)(2,1)S(1)} %copy-done.2, s32[4]{0:T(128)S(1)} %copy-done.4, ...), custom_call_target="tpu_custom_call" | custom-call | flops 12582912 | bytes 2097152 | tf_op jit(solution)/shard_map/attend_last/pallas_call | solution.py:59
  37.8 0.0 collective-permute-done.12.taken_ref
  37.8 1.1 %collective-permute-done.13.other_taken = bf16[4,3072]{1,0:T(4,128)(2,1)S(1)} collective-permute-done((bf16[4,3072]{1,0:T(4,128)(2,1)S(1)}, bf16[4,3072]{1,0:T(4,128)(2,1)S(1)}, u32[]{:S(2)}, u32[]{:S(2)}) %collective-permute-start.13) | collective-permute-done | bytes 24608 | tf_op jit(solution)/shard_map/ppermute | solution.py:33
  38.9 0.0 collective-permute-done.14.other_kept
  38.9 0.7 %finish.1 = bf16[4,6144]{1,0:T(4,128)(2,1)} custom-call(bf16[4,3072]{1,0:T(4,128)(2,1)S(1)} %get-tuple-element.28.refs_6_.kept_ref, bf16[4,3072]{1,0:T(4,128)(2,1)S(1)} %collective-permute-done.12.taken_ref, bf16[4,3072]{1,0:T(4,128)(2,1)S(1)} %collective-permute-done.13.other_taken, bf16[4,3072]{1,0:T(4,128)(2,1)S(1)} %collective-permute-done.14.other_kept, ...), custom_call_target="tpu_custom_call" | custom-call | bytes 98304 | tf_op jit(solution)/shard_map/finish/pallas_call | solution.py:59
  (15 shorter events, 0.1 us)
Async XLA Ops:
  0.6 5.1 %collective-permute-start = (bf16[4,6144]{1,0:T(4,128)(2,1)}, bf16[4,6144]{1,0:T(4,128)(2,1)S(1)}, u32[]{:S(2)}, u32[]{:S(2)}) collective-permute-start(bf16[4,6144]{1,0:T(4,128)(2,1)} %tokens_ref.1), channel_id=1, source_target_pairs={{0,3},{1,2},{2,1},{3,0},{4,7},{5,6},{6,5},{7,4},{8,11},{9,10},{10,... | collective-permute-start | bytes 147464 | tf_op jit(solution)/shard_map/ppermute | solution.py:33
  4.1 6.2 %collective-permute-start.3 = (bf16[192,128]{1,0:T(8,128)(2,1)S(1)}, bf16[192,128]{1,0:T(8,128)(2,1)S(1)}, u32[]{:S(2)}, u32[]{:S(2)}) collective-permute-start(bf16[192,128]{1,0:T(8,128)(2,1)S(1)} %widen.1), channel_id=1, source_target_pairs={{0,2},{2,0},{4,6},{6,4},{8,10},{10,8},{12,14},{14,12},{1,3},{3,1},... | collective-permute-start | bytes 147464 | tf_op jit(solution)/shard_map/ppermute | solution.py:28
  4.7 12.1 %slice-start = ((s8[12582912]{0:T(1024)(128)(4,1)}), s8[4194304]{0:T(1024)(128)(4,1)S(1)}, s32[]{:S(2)}) async-start(s8[12582912]{0:T(1024)(128)(4,1)} %bitcast.3), calls=%async_computation | async-start | bytes 8388608
  4.7 12.1 %slice-start.1 = ((s8[12582912]{0:T(1024)(128)(4,1)}), s8[4194304]{0:T(1024)(128)(4,1)S(1)}, s32[]{:S(2)}) async-start(s8[12582912]{0:T(1024)(128)(4,1)} %bitcast.3), calls=%async_computation.1 | async-start | bytes 8388608
  4.7 12.1 %slice-start.2 = ((s8[12582912]{0:T(1024)(128)(4,1)}), s8[4194304]{0:T(1024)(128)(4,1)S(1)}, s32[]{:S(2)}) async-start(s8[12582912]{0:T(1024)(128)(4,1)} %bitcast.3), calls=%async_computation.2 | async-start | bytes 8388608
  4.7 12.1 %copy-start = (bf16[1,6144,1024]{2,1,0:T(8,128)(2,1)S(1)}, bf16[1,6144,1024]{2,1,0:T(8,128)(2,1)}, u32[]{:S(2)}) copy-start(bf16[1,6144,1024]{2,1,0:T(8,128)(2,1)} %up_ref.1) | copy-start | bytes 37748740
  5.9 6.2 %collective-permute-start.1 = (bf16[8,3072]{1,0:T(8,128)(2,1)S(1)}, bf16[8,3072]{1,0:T(8,128)(2,1)S(1)}, u32[]{:S(2)}, u32[]{:S(2)}) collective-permute-start(bf16[8,3072]{1,0:T(8,128)(2,1)S(1)} %norm_both.1.own_ref), channel_id=1, source_target_pairs={{0,13},{1,12},{2,15},{3,14},{4,9},{5,8},{6,11},{7,10},{8,5},{9,4},... | collective-permute-start | bytes 147464 | tf_op jit(solution)/shard_map/ppermute | solution.py:33
  9.9 5.1 %collective-permute-start.2 = (bf16[8,3072]{1,0:T(8,128)(2,1)S(1)}, bf16[8,3072]{1,0:T(8,128)(2,1)S(1)}, u32[]{:S(2)}, u32[]{:S(2)}) collective-permute-start(bf16[8,3072]{1,0:T(8,128)(2,1)S(1)} %norm_both.1.own_ref), channel_id=1, source_target_pairs={{0,8},{2,10},{4,12},{6,14},{8,0},{10,2},{12,4},{14,6},{1,9},{3,11}... | collective-permute-start | bytes 147464 | tf_op jit(solution)/shard_map/ppermute | solution.py:28
  9.9 5.1 %collective-permute-start.4 = (bf16[8,3072]{1,0:T(8,128)(2,1)S(1)}, bf16[8,3072]{1,0:T(8,128)(2,1)S(1)}, u32[]{:S(2)}, u32[]{:S(2)}) collective-permute-start(bf16[8,3072]{1,0:T(8,128)(2,1)S(1)} %norm_both.1.own_ref), channel_id=1, source_target_pairs={{0,5},{1,4},{2,7},{3,6},{4,1},{5,0},{6,3},{7,2},{8,13},{9,12},{10,... | collective-permute-start | bytes 147464 | tf_op jit(solution)/shard_map/ppermute | solution.py:33
  15.0 1.7 %collective-permute-start.6 = (bf16[32,3072]{1,0:T(8,128)(2,1)S(1)}, bf16[32,3072]{1,0:T(8,128)(2,1)S(1)}, u32[]{:S(2)}, u32[]{:S(2)}) collective-permute-start(bf16[32,3072]{1,0:T(8,128)(2,1)S(1)} %get-tuple-element.20.x_ref), channel_id=1, source_target_pairs={{0,1},{1,0},{2,3},{3,2},{4,5},{5,4},{6,7},{7,6},{8,9},{9,8},{10,11... | collective-permute-start | bytes 589832 | tf_op jit(solution)/shard_map/ppermute | solution.py:28
  15.2 6.8 %collective-permute-start.5 = (bf16[256,128]{1,0:T(8,128)(2,1)S(1)}, bf16[256,128]{1,0:T(8,128)(2,1)S(1)}, u32[]{:S(2)}, u32[]{:S(2)}) collective-permute-start(bf16[256,128]{1,0:T(8,128)(2,1)S(1)} %get-tuple-element.19.own_ref), channel_id=1, source_target_pairs={{0,8},{2,10},{4,12},{6,14},{8,0},{10,2},{12,4},{14,6},{1,9},{3,11}... | collective-permute-start | bytes 196616 | tf_op jit(solution)/shard_map/ppermute | solution.py:28
  22.0 7.7 %copy-start.1 = (bf16[4,512,512]{2,1,0:T(8,128)(2,1)S(1)}, bf16[4,512,512]{2,1,0:T(8,128)(2,1)}, u32[]{:S(2)}) copy-start(bf16[4,512,512]{2,1,0:T(8,128)(2,1)} %refs_2_.3) | copy-start | bytes 6291460
  22.0 7.7 %copy-start.2 = (bf16[4,512,512]{2,1,0:T(8,128)(2,1)S(1)}, bf16[4,512,512]{2,1,0:T(8,128)(2,1)}, u32[]{:S(2)}) copy-start(bf16[4,512,512]{2,1,0:T(8,128)(2,1)} %refs_3_.1) | copy-start | bytes 6291460
  22.0 7.7 %copy-start.4 = (s32[4]{0:T(128)S(1)}, s32[4]{0:T(128)}, u32[]{:S(2)}) copy-start(s32[4]{0:T(128)} %refs_4_.1) | copy-start | bytes 52
  22.0 7.7 %copy-start.5 = (s32[4]{0:T(128)S(1)}, s32[4]{0:T(128)}, u32[]{:S(2)}) copy-start(s32[4]{0:T(128)} %refs_5_.1) | copy-start | bytes 52
  23.3 2.4 %collective-permute-start.8 = (bf16[32,3072]{1,0:T(8,128)(2,1)S(1)}, bf16[32,3072]{1,0:T(8,128)(2,1)S(1)}, u32[]{:S(2)}, u32[]{:S(2)}) collective-permute-start(bf16[32,3072]{1,0:T(8,128)(2,1)S(1)} %down.2.after), channel_id=1, source_target_pairs={{0,1},{1,0},{2,3},{3,2},{4,5},{5,4},{6,7},{7,6},{8,9},{9,8},{10,11... | collective-permute-start | bytes 589832 | tf_op jit(solution)/shard_map/ppermute | solution.py:28
  23.3 6.3 %collective-permute-start.7 = (bf16[512,128]{1,0:T(8,128)(2,1)S(1)}, bf16[512,128]{1,0:T(8,128)(2,1)S(1)}, u32[]{:S(2)}, u32[]{:S(2)}) collective-permute-start(bf16[512,128]{1,0:T(8,128)(2,1)S(1)} %stack_after.1.after.near_ref.refs_0_), channel_id=1, source_target_pairs={{0,4},{2,6},{4,0},{6,2},{8,12},{10,14},{12,8},{14,10},{1,5},{3,7},... | collective-permute-start | bytes 393224 | tf_op jit(solution)/shard_map/ppermute | solution.py:28
  25.7 13.3 %copy-start.3 = (bf16[4,6144]{1,0:T(4,128)(2,1)S(1)}, bf16[4,6144]{1,0:T(4,128)(2,1)}, u32[]{:S(2)}) copy-start(bf16[4,6144]{1,0:T(4,128)(2,1)} %tokens_ref.1) | copy-start | bytes 147460
  25.8 6.1 %collective-permute-start.10 = (bf16[8,3072]{1,0:T(8,128)(2,1)S(1)}, bf16[8,3072]{1,0:T(8,128)(2,1)S(1)}, u32[]{:S(2)}, u32[]{:S(2)}) collective-permute-start(bf16[8,3072]{1,0:T(8,128)(2,1)S(1)} %get-tuple-element.26), channel_id=1, source_target_pairs={{0,13},{1,12},{2,15},{3,14},{4,9},{5,8},{6,11},{7,10},{8,5},{9,4},... | collective-permute-start | bytes 147464 | tf_op jit(solution)/shard_map/ppermute | solution.py:33
  27.1 6.7 %collective-permute-start.11 = (bf16[8,3072]{1,0:T(8,128)(2,1)S(1)}, bf16[8,3072]{1,0:T(8,128)(2,1)S(1)}, u32[]{:S(2)}, u32[]{:S(2)}) collective-permute-start(bf16[8,3072]{1,0:T(8,128)(2,1)S(1)} %get-tuple-element.27.after), channel_id=1, source_target_pairs={{0,8},{2,10},{4,12},{6,14},{8,0},{10,2},{12,4},{14,6},{1,9},{3,11}... | collective-permute-start | bytes 147464 | tf_op jit(solution)/shard_map/ppermute | solution.py:28
  28.1 5.7 %collective-permute-start.9 = (bf16[8,3072]{1,0:T(8,128)(2,1)S(1)}, bf16[8,3072]{1,0:T(8,128)(2,1)S(1)}, u32[]{:S(2)}, u32[]{:S(2)}) collective-permute-start(bf16[8,3072]{1,0:T(8,128)(2,1)S(1)} %get-tuple-element.25), channel_id=1, source_target_pairs={{0,5},{1,4},{2,7},{3,6},{4,1},{5,0},{6,3},{7,2},{8,13},{9,12},{10,... | collective-permute-start | bytes 147464 | tf_op jit(solution)/shard_map/ppermute | solution.py:33
  33.8 4.0 %collective-permute-start.12 = (bf16[4,3072]{1,0:T(4,128)(2,1)S(1)}, bf16[4,3072]{1,0:T(4,128)(2,1)S(1)}, u32[]{:S(2)}, u32[]{:S(2)}) collective-permute-start(bf16[4,3072]{1,0:T(4,128)(2,1)S(1)} %get-tuple-element.29), channel_id=1, source_target_pairs={{0,2},{2,0},{4,6},{6,4},{8,10},{10,8},{12,14},{14,12},{1,3},{3,1},... | collective-permute-start | bytes 73736 | tf_op jit(solution)/shard_map/ppermute | solution.py:28
  35.5 3.5 %collective-permute-start.13 = (bf16[4,3072]{1,0:T(4,128)(2,1)S(1)}, bf16[4,3072]{1,0:T(4,128)(2,1)S(1)}, u32[]{:S(2)}, u32[]{:S(2)}) collective-permute-start(bf16[4,3072]{1,0:T(4,128)(2,1)S(1)} %get-tuple-element.29), channel_id=1, source_target_pairs={{0,3},{1,2},{2,1},{3,0},{4,7},{5,6},{6,5},{7,4},{8,11},{9,10},{10,... | collective-permute-start | bytes 73736 | tf_op jit(solution)/shard_map/ppermute | solution.py:33
  35.5 3.5 %collective-permute-start.14 = (bf16[4,3072]{1,0:T(4,128)(2,1)S(1)}, bf16[4,3072]{1,0:T(4,128)(2,1)S(1)}, u32[]{:S(2)}, u32[]{:S(2)}) collective-permute-start(bf16[4,3072]{1,0:T(4,128)(2,1)S(1)} %get-tuple-element.28.refs_6_.kept_ref), channel_id=1, source_target_pairs={{0,1},{1,0},{2,3},{3,2},{4,5},{5,4},{6,7},{7,6},{8,9},{9,8},{10,11... | collective-permute-start | bytes 73736 | tf_op jit(solution)/shard_map/ppermute | solution.py:28

commit v21 on v14

--- a/solution.py
+++ b/solution.py
@@ -14,7 +14,7 @@
 GROUP = HQ // KVH
 SCALE = HD ** (-0.5)
 TILE = 512
-WIDE_TILE = 1536
+WIDE_TILE = 3072
 CUTS = 4
 MIB = 1024 * 1024
 

time: 39.6 us -> 39.3 us (level)
  no operation moved by 1% of the time
where the time goes in v21:
time: 39.3 us; the launch traced here: 39.1 us
  starting transfers between devices  17.7 us (45%)
  Pallas kernels  14 us (36%)
  waiting for transfers between devices  6.54 us (17%)
  between operations  0.83 us (2%)
    pallas_call x14, Pallas kernels, call(): pl.pallas_call(kernel, name=getattr(kernel, 'func', kernel).__name__, out...  14 us
    ppermute x6, starting transfers between devices, cross(): return lax.ppermute(block, ('wide', 'narrow'), pairs)  9.38 us
    ppermute x9, starting transfers between devices, swap(): return lax.ppermute(block, axis, [(i, i ^ step) for i in range(count)])  8.32 us
    ppermute x6, waiting for transfers between devices, cross(): return lax.ppermute(block, ('wide', 'narrow'), pairs)  6.51 us
  transfers between devices with their start and end apart: 15, of which 4 were waited for; matrix products, arithmetic and copies ran while one was open for 0% of the time, Pallas kernels for 31%

profile of v21, /device:TPU:0, one launch (start us, length us, event | category | flops | bytes accessed | tf_op | source)
XLA Modules:
  0.0 39.1 jit_solution(9679683242164257212)
XLA Ops:
  0.6 2.5 %collective-permute-start = (bf16[4,6144]{1,0:T(4,128)(2,1)}, bf16[4,6144]{1,0:T(4,128)(2,1)S(1)}, u32[]{:S(2)}, u32[]{:S(2)}) collective-permute-start(bf16[4,6144]{1,0:T(4,128)(2,1)} %tokens_ref.1), channel_id=1, source_target_pairs={{0,3},{1,2},{2,1},{3,0},{4,7},{5,6},{6,5},{7,4},{8,11},{9,10},{10,... | collective-permute-start | bytes 147464 | tf_op jit(solution)/shard_map/ppermute | solution.py:33
  3.1 1.0 %pack.1 = (bf16[128,128]{1,0:T(8,128)(2,1)S(1)}, bf16[4,6144]{1,0:T(4,128)(2,1)S(1)}, f32[1,6144]{1,0:T(1,128)S(1)}) custom-call(bf16[4,3072]{1,0:T(4,128)(2,1)} %far_query.1, bf16[4,512]{1,0:T(4,128)(2,1)} %far_key.1, bf16[4,512]{1,0:T(4,128)(2,1)} %far_value.1, bf16[4,6144]{1,0:T(4,128)(2,1)} %tokens_ref.1, f32[1,6144]{1,0:T(1,128)} %bitcast.5), custom_call_target="tpu_custom_call" | custom-call | bytes 100000 | tf_op jit(solution)/shard_map/pack/pallas_call | solution.py:59
  4.1 0.6 %collective-permute-start.3 = (bf16[192,128]{1,0:T(8,128)(2,1)S(1)}, bf16[192,128]{1,0:T(8,128)(2,1)S(1)}, u32[]{:S(2)}, u32[]{:S(2)}) collective-permute-start(bf16[192,128]{1,0:T(8,128)(2,1)S(1)} %widen.1), channel_id=1, source_target_pairs={{0,2},{2,0},{4,6},{6,4},{8,10},{10,8},{12,14},{14,12},{1,3},{3,1},... | collective-permute-start | bytes 147464 | tf_op jit(solution)/shard_map/ppermute | solution.py:28
  4.7 1.0 %shares.1.share.share_ref = f32[32,128]{1,0:T(8,128)S(1)} custom-call(s32[2,32]{1,0:T(2,128)} %bitcast.6, f32[2,32]{1,0:T(2,128)} %bitcast.7, bf16[128,128]{1,0:T(8,128)(2,1)S(1)} %get-tuple-element.18.refs_0_.heads.own_ref.own_heads, bf16[1,6144,1024]{2,1,0:T(8,128)(2,1)} %gate_ref.1, bf16[1,6144,1024]{2,1,0:T(8,128)(2,1)} %up_ref.1), custom_call_target="tpu_custom_call" | custom-call | bytes 100000 | tf_op jit(solution)/shard_map/shares/pallas_call | solution.py:59
  5.7 0.0 collective-permute-done.got_ref
  5.7 0.2 norm_both.1.own_ref
  5.9 4.0 %collective-permute-start.1 = (bf16[8,3072]{1,0:T(8,128)(2,1)S(1)}, bf16[8,3072]{1,0:T(8,128)(2,1)S(1)}, u32[]{:S(2)}, u32[]{:S(2)}) collective-permute-start(bf16[8,3072]{1,0:T(8,128)(2,1)S(1)} %norm_both.1.own_ref), channel_id=1, source_target_pairs={{0,13},{1,12},{2,15},{3,14},{4,9},{5,8},{6,11},{7,10},{8,5},{9,4},... | collective-permute-start | bytes 147464 | tf_op jit(solution)/shard_map/ppermute | solution.py:33
  9.9 0.0 collective-permute-start.2
  9.9 0.6 %collective-permute-start.4 = (bf16[8,3072]{1,0:T(8,128)(2,1)S(1)}, bf16[8,3072]{1,0:T(8,128)(2,1)S(1)}, u32[]{:S(2)}, u32[]{:S(2)}) collective-permute-start(bf16[8,3072]{1,0:T(8,128)(2,1)S(1)} %norm_both.1.own_ref), channel_id=1, source_target_pairs={{0,4},{2,6},{4,0},{6,2},{8,12},{10,14},{12,8},{14,10},{1,5},{3,7},... | collective-permute-start | bytes 147464 | tf_op jit(solution)/shard_map/ppermute | solution.py:28
  10.5 0.0 collective-permute-done.3.got_heads
  10.5 1.5 %collective-permute-done.1.last_ref = bf16[8,3072]{1,0:T(8,128)(2,1)S(1)} collective-permute-done((bf16[8,3072]{1,0:T(8,128)(2,1)S(1)}, bf16[8,3072]{1,0:T(8,128)(2,1)S(1)}, u32[]{:S(2)}, u32[]{:S(2)}) %collective-permute-start.1) | collective-permute-done | bytes 49184 | tf_op jit(solution)/shard_map/ppermute | solution.py:33
  12.1 2.5 %collective-permute-done.2.far_ref = bf16[8,3072]{1,0:T(8,128)(2,1)S(1)} collective-permute-done((bf16[8,3072]{1,0:T(8,128)(2,1)S(1)}, bf16[8,3072]{1,0:T(8,128)(2,1)S(1)}, u32[]{:S(2)}, u32[]{:S(2)}) %collective-permute-start.2) | collective-permute-done | bytes 49184 | tf_op jit(solution)/shard_map/ppermute | solution.py:33
  14.6 0.0 collective-permute-done.4.next_ref
  14.6 0.3 collective-permute-start.6
  14.9 2.2 %collective-permute-start.5 = (bf16[256,128]{1,0:T(8,128)(2,1)S(1)}, bf16[256,128]{1,0:T(8,128)(2,1)S(1)}, u32[]{:S(2)}, u32[]{:S(2)}) collective-permute-start(bf16[256,128]{1,0:T(8,128)(2,1)S(1)} %get-tuple-element.19.own_ref), channel_id=1, source_target_pairs={{0,8},{2,10},{4,12},{6,14},{8,0},{10,2},{12,4},{14,6},{1,9},{3,11}... | collective-permute-start | bytes 196616 | tf_op jit(solution)/shard_map/ppermute | solution.py:28
  17.1 0.0 collective-permute-done.6.other_ref
  17.1 0.0 slice-done.1
  17.1 0.0 slice-done.2
  17.1 0.0 copy-done
  17.1 4.8 %gate_all.1 = (bf16[32,1024]{1,0:T(8,128)(2,1)S(1)}, bf16[1024,3072]{1,0:T(8,128)(2,1)S(1)}, bf16[1024,3072]{1,0:T(8,128)(2,1)S(1)}) custom-call(bf16[32,3072]{1,0:T(8,128)(2,1)S(1)} %get-tuple-element.20.x_ref, bf16[32,3072]{1,0:T(8,128)(2,1)S(1)} %collective-permute-done.6.other_ref, bf16[1,6144,1024]{2,1,0:T(8,128)(2,1)S(1)} %bitcast.4, ...), custom_call_target="tpu_custom_call" | custom-call | flops 805306368 | bytes 37748736 | tf_op jit(solution)/shard_map/gate_all/pallas_call | solution.py:59
  21.9 0.0 collective-permute-done.5.got_ref
  22.0 0.0 copy-start.1
  22.0 0.0 copy-start.2
  22.0 0.0 copy-start.4
  22.0 0.0 copy-start.5
  22.0 1.2 %down.2.after = bf16[32,3072]{1,0:T(8,128)(2,1)S(1)} custom-call(bf16[32,1024]{1,0:T(8,128)(2,1)S(1)} %get-tuple-element.21.after.hidden_ref, bf16[1024,3072]{1,0:T(8,128)(2,1)S(1)} %get-tuple-element.23.down_ref, bf16[512,128]{1,0:T(8,128)(2,1)S(1)} %stack_after.1.after.near_ref.refs_0_), custom_call_target="tpu_custom_call" | custom-call | flops 201326592 | bytes 6291456 | tf_op jit(solution)/shard_map/down/pallas_call | solution.py:59
  23.2 0.2 collective-permute-start.8
  23.4 0.9 %collective-permute-start.7 = (bf16[512,128]{1,0:T(8,128)(2,1)S(1)}, bf16[512,128]{1,0:T(8,128)(2,1)S(1)}, u32[]{:S(2)}, u32[]{:S(2)}) collective-permute-start(bf16[512,128]{1,0:T(8,128)(2,1)S(1)} %stack_after.1.after.near_ref.refs_0_), channel_id=1, source_target_pairs={{0,4},{2,6},{4,0},{6,2},{8,12},{10,14},{12,8},{14,10},{1,5},{3,7},... | collective-permute-start | bytes 393224 | tf_op jit(solution)/shard_map/ppermute | solution.py:28
  24.3 1.2 %down.3.terms_ref = f32[32,3072]{1,0:T(8,128)S(1)} custom-call(bf16[32,1024]{1,0:T(8,128)(2,1)S(1)} %get-tuple-element.21.after.hidden_ref, bf16[1024,3072]{1,0:T(8,128)(2,1)S(1)} %get-tuple-element.22.down_ref, bf16[32,3072]{1,0:T(8,128)(2,1)S(1)} %down.2.after), custom_call_target="tpu_custom_call" | custom-call | flops 201326592 | bytes 6291456 | tf_op jit(solution)/shard_map/down/pallas_call | solution.py:59
  25.5 0.0 collective-permute-done.8.taken_ref
  25.5 1.6 %collective-permute-start.10 = (bf16[8,3072]{1,0:T(8,128)(2,1)S(1)}, bf16[8,3072]{1,0:T(8,128)(2,1)S(1)}, u32[]{:S(2)}, u32[]{:S(2)}) collective-permute-start(bf16[8,3072]{1,0:T(8,128)(2,1)S(1)} %get-tuple-element.26), channel_id=1, source_target_pairs={{0,13},{1,12},{2,15},{3,14},{4,9},{5,8},{6,11},{7,10},{8,5},{9,4},... | collective-permute-start | bytes 147464 | tf_op jit(solution)/shard_map/ppermute | solution.py:33
  27.2 0.7 %collective-permute-start.11 = (bf16[8,3072]{1,0:T(8,128)(2,1)S(1)}, bf16[8,3072]{1,0:T(8,128)(2,1)S(1)}, u32[]{:S(2)}, u32[]{:S(2)}) collective-permute-start(bf16[8,3072]{1,0:T(8,128)(2,1)S(1)} %get-tuple-element.27.after), channel_id=1, source_target_pairs={{0,9},{1,8},{2,11},{3,10},{4,13},{5,12},{6,15},{7,14},{8,1},{9,0},... | collective-permute-start | bytes 147464 | tf_op jit(solution)/shard_map/ppermute | solution.py:33
  27.9 1.8 %collective-permute-start.9 = (bf16[8,3072]{1,0:T(8,128)(2,1)S(1)}, bf16[8,3072]{1,0:T(8,128)(2,1)S(1)}, u32[]{:S(2)}, u32[]{:S(2)}) collective-permute-start(bf16[8,3072]{1,0:T(8,128)(2,1)S(1)} %get-tuple-element.25), channel_id=1, source_target_pairs={{0,4},{2,6},{4,0},{6,2},{8,12},{10,14},{12,8},{14,10},{1,5},{3,7},... | collective-permute-start | bytes 147464 | tf_op jit(solution)/shard_map/ppermute | solution.py:28
  29.7 0.0 collective-permute-done.7.far_ref.refs_1_
  29.7 0.0 copy-done.2
  29.7 2.2 %attend.1.refs_4_.refs_7_ = f32[72,128]{1,0:T(8,128)S(1)} custom-call(bf16[512,128]{1,0:T(8,128)(2,1)S(1)} %stack_after.1.after.near_ref.refs_0_, bf16[512,128]{1,0:T(8,128)(2,1)S(1)} %collective-permute-done.7.far_ref.refs_1_, bf16[4,512,512]{2,1,0:T(8,128)(2,1)S(1)} %copy-done.1, bf16[4,512,512]{2,1,0:T(8,128)(2,1)S(1)} %copy-done.2, s32[4]{0:T(128)S(1)} %copy-done.4, ...), custom_call_target="tpu_custom_call" | custom-call | flops 12582912 | bytes 2097152 | tf_op jit(solution)/shard_map/attend/pallas_call | solution.py:59
  31.9 0.0 collective-permute-done.10.refs_2_
  32.0 1.5 %collective-permute-done.11.refs_3_ = bf16[8,3072]{1,0:T(8,128)(2,1)S(1)} collective-permute-done((bf16[8,3072]{1,0:T(8,128)(2,1)S(1)}, bf16[8,3072]{1,0:T(8,128)(2,1)S(1)}, u32[]{:S(2)}, u32[]{:S(2)}) %collective-permute-start.11) | collective-permute-done | bytes 49184 | tf_op jit(solution)/shard_map/ppermute | solution.py:33
  33.5 0.0 collective-permute-done.9.refs_1_
  33.5 1.6 %collective-permute-start.12 = (bf16[4,3072]{1,0:T(4,128)(2,1)S(1)}, bf16[4,3072]{1,0:T(4,128)(2,1)S(1)}, u32[]{:S(2)}, u32[]{:S(2)}) collective-permute-start(bf16[4,3072]{1,0:T(4,128)(2,1)S(1)} %get-tuple-element.28.refs_6_), channel_id=1, source_target_pairs={{0,2},{2,0},{4,6},{6,4},{8,10},{10,8},{12,14},{14,12},{1,3},{3,1},... | collective-permute-start | bytes 73736 | tf_op jit(solution)/shard_map/ppermute | solution.py:28
  35.2 0.0 collective-permute-start.13
  35.2 0.6 %collective-permute-start.14 = (bf16[4,3072]{1,0:T(4,128)(2,1)S(1)}, bf16[4,3072]{1,0:T(4,128)(2,1)S(1)}, u32[]{:S(2)}, u32[]{:S(2)}) collective-permute-start(bf16[4,3072]{1,0:T(4,128)(2,1)S(1)} %get-tuple-element.28.refs_6_), channel_id=1, source_target_pairs={{0,3},{1,2},{2,1},{3,0},{4,7},{5,6},{6,5},{7,4},{8,11},{9,10},{10,... | collective-permute-start | bytes 73736 | tf_op jit(solution)/shard_map/ppermute | solution.py:33
  35.7 1.8 %attend_last.1.after = bf16[4,3072]{1,0:T(4,128)(2,1)} custom-call(bf16[512,128]{1,0:T(8,128)(2,1)S(1)} %stack_after.1.after.near_ref.refs_0_, bf16[512,128]{1,0:T(8,128)(2,1)S(1)} %collective-permute-done.7.far_ref.refs_1_, bf16[4,512,512]{2,1,0:T(8,128)(2,1)S(1)} %copy-done.1, bf16[4,512,512]{2,1,0:T(8,128)(2,1)S(1)} %copy-done.2, s32[4]{0:T(128)S(1)} %copy-done.4, ...), custom_call_target="tpu_custom_call" | custom-call | flops 12582912 | bytes 2097152 | tf_op jit(solution)/shard_map/attend_last/pallas_call | solution.py:59
  37.5 0.0 collective-permute-done.12.taken_ref
  37.5 0.0 collective-permute-done.13.other_kept
  37.5 0.9 %collective-permute-done.14.other_taken = bf16[4,3072]{1,0:T(4,128)(2,1)S(1)} collective-permute-done((bf16[4,3072]{1,0:T(4,128)(2,1)S(1)}, bf16[4,3072]{1,0:T(4,128)(2,1)S(1)}, u32[]{:S(2)}, u32[]{:S(2)}) %collective-permute-start.14) | collective-permute-done | bytes 24608 | tf_op jit(solution)/shard_map/ppermute | solution.py:33
  38.4 0.0 copy-done.3
  38.4 0.7 %finish.1 = bf16[4,6144]{1,0:T(4,128)(2,1)} custom-call(bf16[4,3072]{1,0:T(4,128)(2,1)S(1)} %get-tuple-element.29.kept_ref, bf16[4,3072]{1,0:T(4,128)(2,1)S(1)} %collective-permute-done.12.taken_ref, bf16[4,3072]{1,0:T(4,128)(2,1)S(1)} %collective-permute-done.13.other_kept, bf16[4,3072]{1,0:T(4,128)(2,1)S(1)} %collective-permute-done.14.other_taken, ...), custom_call_target="tpu_custom_call" | custom-call | bytes 98304 | tf_op jit(solution)/shard_map/finish/pallas_call | solution.py:59
  (15 shorter events, 0.1 us)
Async XLA Ops:
  0.6 5.1 %collective-permute-start = (bf16[4,6144]{1,0:T(4,128)(2,1)}, bf16[4,6144]{1,0:T(4,128)(2,1)S(1)}, u32[]{:S(2)}, u32[]{:S(2)}) collective-permute-start(bf16[4,6144]{1,0:T(4,128)(2,1)} %tokens_ref.1), channel_id=1, source_target_pairs={{0,3},{1,2},{2,1},{3,0},{4,7},{5,6},{6,5},{7,4},{8,11},{9,10},{10,... | collective-permute-start | bytes 147464 | tf_op jit(solution)/shard_map/ppermute | solution.py:33
  4.1 6.4 %collective-permute-start.3 = (bf16[192,128]{1,0:T(8,128)(2,1)S(1)}, bf16[192,128]{1,0:T(8,128)(2,1)S(1)}, u32[]{:S(2)}, u32[]{:S(2)}) collective-permute-start(bf16[192,128]{1,0:T(8,128)(2,1)S(1)} %widen.1), channel_id=1, source_target_pairs={{0,2},{2,0},{4,6},{6,4},{8,10},{10,8},{12,14},{14,12},{1,3},{3,1},... | collective-permute-start | bytes 147464 | tf_op jit(solution)/shard_map/ppermute | solution.py:28
  4.7 12.4 %slice-start = ((s8[12582912]{0:T(1024)(128)(4,1)}), s8[4194304]{0:T(1024)(128)(4,1)S(1)}, s32[]{:S(2)}) async-start(s8[12582912]{0:T(1024)(128)(4,1)} %bitcast.3), calls=%async_computation | async-start | bytes 8388608
  4.7 12.4 %slice-start.1 = ((s8[12582912]{0:T(1024)(128)(4,1)}), s8[4194304]{0:T(1024)(128)(4,1)S(1)}, s32[]{:S(2)}) async-start(s8[12582912]{0:T(1024)(128)(4,1)} %bitcast.3), calls=%async_computation.1 | async-start | bytes 8388608
  4.7 12.4 %slice-start.2 = ((s8[12582912]{0:T(1024)(128)(4,1)}), s8[4194304]{0:T(1024)(128)(4,1)S(1)}, s32[]{:S(2)}) async-start(s8[12582912]{0:T(1024)(128)(4,1)} %bitcast.3), calls=%async_computation.2 | async-start | bytes 8388608
  4.7 12.4 %copy-start = (bf16[1,6144,1024]{2,1,0:T(8,128)(2,1)S(1)}, bf16[1,6144,1024]{2,1,0:T(8,128)(2,1)}, u32[]{:S(2)}) copy-start(bf16[1,6144,1024]{2,1,0:T(8,128)(2,1)} %up_ref.1) | copy-start | bytes 37748740
  5.9 6.2 %collective-permute-start.1 = (bf16[8,3072]{1,0:T(8,128)(2,1)S(1)}, bf16[8,3072]{1,0:T(8,128)(2,1)S(1)}, u32[]{:S(2)}, u32[]{:S(2)}) collective-permute-start(bf16[8,3072]{1,0:T(8,128)(2,1)S(1)} %norm_both.1.own_ref), channel_id=1, source_target_pairs={{0,13},{1,12},{2,15},{3,14},{4,9},{5,8},{6,11},{7,10},{8,5},{9,4},... | collective-permute-start | bytes 147464 | tf_op jit(solution)/shard_map/ppermute | solution.py:33
  9.9 4.7 %collective-permute-start.2 = (bf16[8,3072]{1,0:T(8,128)(2,1)S(1)}, bf16[8,3072]{1,0:T(8,128)(2,1)S(1)}, u32[]{:S(2)}, u32[]{:S(2)}) collective-permute-start(bf16[8,3072]{1,0:T(8,128)(2,1)S(1)} %norm_both.1.own_ref), channel_id=1, source_target_pairs={{0,9},{1,8},{2,11},{3,10},{4,13},{5,12},{6,15},{7,14},{8,1},{9,0},... | collective-permute-start | bytes 147464 | tf_op jit(solution)/shard_map/ppermute | solution.py:33
  9.9 4.7 %collective-permute-start.4 = (bf16[8,3072]{1,0:T(8,128)(2,1)S(1)}, bf16[8,3072]{1,0:T(8,128)(2,1)S(1)}, u32[]{:S(2)}, u32[]{:S(2)}) collective-permute-start(bf16[8,3072]{1,0:T(8,128)(2,1)S(1)} %norm_both.1.own_ref), channel_id=1, source_target_pairs={{0,4},{2,6},{4,0},{6,2},{8,12},{10,14},{12,8},{14,10},{1,5},{3,7},... | collective-permute-start | bytes 147464 | tf_op jit(solution)/shard_map/ppermute | solution.py:28
  14.6 2.5 %collective-permute-start.6 = (bf16[32,3072]{1,0:T(8,128)(2,1)S(1)}, bf16[32,3072]{1,0:T(8,128)(2,1)S(1)}, u32[]{:S(2)}, u32[]{:S(2)}) collective-permute-start(bf16[32,3072]{1,0:T(8,128)(2,1)S(1)} %get-tuple-element.20.x_ref), channel_id=1, source_target_pairs={{0,1},{1,0},{2,3},{3,2},{4,5},{5,4},{6,7},{7,6},{8,9},{9,8},{10,11... | collective-permute-start | bytes 589832 | tf_op jit(solution)/shard_map/ppermute | solution.py:28
  14.9 7.0 %collective-permute-start.5 = (bf16[256,128]{1,0:T(8,128)(2,1)S(1)}, bf16[256,128]{1,0:T(8,128)(2,1)S(1)}, u32[]{:S(2)}, u32[]{:S(2)}) collective-permute-start(bf16[256,128]{1,0:T(8,128)(2,1)S(1)} %get-tuple-element.19.own_ref), channel_id=1, source_target_pairs={{0,8},{2,10},{4,12},{6,14},{8,0},{10,2},{12,4},{14,6},{1,9},{3,11}... | collective-permute-start | bytes 196616 | tf_op jit(solution)/shard_map/ppermute | solution.py:28
  22.0 7.7 %copy-start.1 = (bf16[4,512,512]{2,1,0:T(8,128)(2,1)S(1)}, bf16[4,512,512]{2,1,0:T(8,128)(2,1)}, u32[]{:S(2)}) copy-start(bf16[4,512,512]{2,1,0:T(8,128)(2,1)} %refs_2_.3) | copy-start | bytes 6291460
  22.0 7.7 %copy-start.2 = (bf16[4,512,512]{2,1,0:T(8,128)(2,1)S(1)}, bf16[4,512,512]{2,1,0:T(8,128)(2,1)}, u32[]{:S(2)}) copy-start(bf16[4,512,512]{2,1,0:T(8,128)(2,1)} %refs_3_.1) | copy-start | bytes 6291460
  22.0 7.7 %copy-start.4 = (s32[4]{0:T(128)S(1)}, s32[4]{0:T(128)}, u32[]{:S(2)}) copy-start(s32[4]{0:T(128)} %refs_4_.1) | copy-start | bytes 52
  22.0 7.7 %copy-start.5 = (s32[4]{0:T(128)S(1)}, s32[4]{0:T(128)}, u32[]{:S(2)}) copy-start(s32[4]{0:T(128)} %refs_5_.1) | copy-start | bytes 52
  23.2 2.3 %collective-permute-start.8 = (bf16[32,3072]{1,0:T(8,128)(2,1)S(1)}, bf16[32,3072]{1,0:T(8,128)(2,1)S(1)}, u32[]{:S(2)}, u32[]{:S(2)}) collective-permute-start(bf16[32,3072]{1,0:T(8,128)(2,1)S(1)} %down.2.after), channel_id=1, source_target_pairs={{0,1},{1,0},{2,3},{3,2},{4,5},{5,4},{6,7},{7,6},{8,9},{9,8},{10,11... | collective-permute-start | bytes 589832 | tf_op jit(solution)/shard_map/ppermute | solution.py:28
  23.4 6.3 %collective-permute-start.7 = (bf16[512,128]{1,0:T(8,128)(2,1)S(1)}, bf16[512,128]{1,0:T(8,128)(2,1)S(1)}, u32[]{:S(2)}, u32[]{:S(2)}) collective-permute-start(bf16[512,128]{1,0:T(8,128)(2,1)S(1)} %stack_after.1.after.near_ref.refs_0_), channel_id=1, source_target_pairs={{0,4},{2,6},{4,0},{6,2},{8,12},{10,14},{12,8},{14,10},{1,5},{3,7},... | collective-permute-start | bytes 393224 | tf_op jit(solution)/shard_map/ppermute | solution.py:28
  25.5 13.0 %copy-start.3 = (bf16[4,6144]{1,0:T(4,128)(2,1)S(1)}, bf16[4,6144]{1,0:T(4,128)(2,1)}, u32[]{:S(2)}) copy-start(bf16[4,6144]{1,0:T(4,128)(2,1)} %tokens_ref.1) | copy-start | bytes 147460
  25.5 6.4 %collective-permute-start.10 = (bf16[8,3072]{1,0:T(8,128)(2,1)S(1)}, bf16[8,3072]{1,0:T(8,128)(2,1)S(1)}, u32[]{:S(2)}, u32[]{:S(2)}) collective-permute-start(bf16[8,3072]{1,0:T(8,128)(2,1)S(1)} %get-tuple-element.26), channel_id=1, source_target_pairs={{0,13},{1,12},{2,15},{3,14},{4,9},{5,8},{6,11},{7,10},{8,5},{9,4},... | collective-permute-start | bytes 147464 | tf_op jit(solution)/shard_map/ppermute | solution.py:33
  27.2 6.3 %collective-permute-start.11 = (bf16[8,3072]{1,0:T(8,128)(2,1)S(1)}, bf16[8,3072]{1,0:T(8,128)(2,1)S(1)}, u32[]{:S(2)}, u32[]{:S(2)}) collective-permute-start(bf16[8,3072]{1,0:T(8,128)(2,1)S(1)} %get-tuple-element.27.after), channel_id=1, source_target_pairs={{0,9},{1,8},{2,11},{3,10},{4,13},{5,12},{6,15},{7,14},{8,1},{9,0},... | collective-permute-start | bytes 147464 | tf_op jit(solution)/shard_map/ppermute | solution.py:33
  27.9 5.6 %collective-permute-start.9 = (bf16[8,3072]{1,0:T(8,128)(2,1)S(1)}, bf16[8,3072]{1,0:T(8,128)(2,1)S(1)}, u32[]{:S(2)}, u32[]{:S(2)}) collective-permute-start(bf16[8,3072]{1,0:T(8,128)(2,1)S(1)} %get-tuple-element.25), channel_id=1, source_target_pairs={{0,4},{2,6},{4,0},{6,2},{8,12},{10,14},{12,8},{14,10},{1,5},{3,7},... | collective-permute-start | bytes 147464 | tf_op jit(solution)/shard_map/ppermute | solution.py:28
  33.5 4.0 %collective-permute-start.12 = (bf16[4,3072]{1,0:T(4,128)(2,1)S(1)}, bf16[4,3072]{1,0:T(4,128)(2,1)S(1)}, u32[]{:S(2)}, u32[]{:S(2)}) collective-permute-start(bf16[4,3072]{1,0:T(4,128)(2,1)S(1)} %get-tuple-element.28.refs_6_), channel_id=1, source_target_pairs={{0,2},{2,0},{4,6},{6,4},{8,10},{10,8},{12,14},{14,12},{1,3},{3,1},... | collective-permute-start | bytes 73736 | tf_op jit(solution)/shard_map/ppermute | solution.py:28
  35.2 2.4 %collective-permute-start.13 = (bf16[4,3072]{1,0:T(4,128)(2,1)S(1)}, bf16[4,3072]{1,0:T(4,128)(2,1)S(1)}, u32[]{:S(2)}, u32[]{:S(2)}) collective-permute-start(bf16[4,3072]{1,0:T(4,128)(2,1)S(1)} %get-tuple-element.29.kept_ref), channel_id=1, source_target_pairs={{0,1},{1,0},{2,3},{3,2},{4,5},{5,4},{6,7},{7,6},{8,9},{9,8},{10,11... | collective-permute-start | bytes 73736 | tf_op jit(solution)/shard_map/ppermute | solution.py:28
  35.2 3.3 %collective-permute-start.14 = (bf16[4,3072]{1,0:T(4,128)(2,1)S(1)}, bf16[4,3072]{1,0:T(4,128)(2,1)S(1)}, u32[]{:S(2)}, u32[]{:S(2)}) collective-permute-start(bf16[4,3072]{1,0:T(4,128)(2,1)S(1)} %get-tuple-element.28.refs_6_), channel_id=1, source_target_pairs={{0,3},{1,2},{2,1},{3,0},{4,7},{5,6},{6,5},{7,4},{8,11},{9,10},{10,... | collective-permute-start | bytes 73736 | tf_op jit(solution)/shard_map/ppermute | solution.py:33
